TPU v7x, 32 devices: a whole 2x2x4 slice. The times are simulated.
32 devices in a mesh: section: 2 (over x), mp: 2 (over core), dp: 8 (over z, y).
Axes of the slice: x: 2, y: 2, z: 4, core: 2. Of those that a mesh axis runs over, the one named last changes fastest.
Arguments:
- tokens: bfloat16 [16, 1024, 768], P('dp', ('section', 'mp')), may hold values from -6 to 6
- grad_out: bfloat16 [16, 1024, 768], P('dp', ('section', 'mp')), may hold values from -6 to 6
- attention_in: bfloat16 [2, 768, 3, 768], P('section', None, None, 'mp'), may hold values from -0.21875 to 0.21875
- attention_bias: float32 [2, 2, 768], P('section', None, 'mp'), may hold values from -0.75 to 0.75
- attention_out: bfloat16 [2, 768, 768], P('section', 'mp'), may hold values from -3.5 to 3.5
- up_weight: bfloat16 [2, 768, 3072], P('section', None, 'mp'), may hold values from -0.21875 to 0.21875
- up_bias: float32 [2, 3072], P('section', 'mp'), may hold values from -4 to 4
- down_weight: bfloat16 [2, 3072, 768], P('section', 'mp'), may hold values from -0.109375 to 0.109375
- norm_gains: float32 [2, 2, 768], P('section'), may hold values from 0.5 to 1.5
- layer_biases: float32 [2, 4, 768], P('section'), may hold values from -4 to 4
- block_counts: int32 [16], P('dp'), may hold values from 2 to 3
- lengths: int32 [16], P('dp'), may hold values from 512 to 1024
- head_shifts: int32 [2, 12], P('section', 'mp'), may hold values from 0 to 2
Outputs:
- layer_out: bfloat16 [16, 1024, 768], P('dp', ('section', 'mp'))
- grad_tokens: bfloat16 [16, 1024, 768], P('dp', ('section', 'mp'))
- grad_attention_in: float32 [2, 768, 3, 768], P('section', None, None, 'mp')
- grad_attention_bias: float32 [2, 2, 768], P('section', None, 'mp')
- grad_attention_out: float32 [2, 768, 768], P('section', 'mp')
- grad_up_weight: float32 [2, 768, 3072], P('section', None, 'mp')
- grad_up_bias: float32 [2, 3072], P('section', 'mp')
- grad_down_weight: float32 [2, 3072, 768], P('section', 'mp')
- grad_norm_gains: float32 [2, 2, 768], P('section')
- grad_layer_biases: float32 [2, 4, 768], P('section')
Inputs may be any that keep to these rules, and one draw needn't show every extreme that they name: The first lengths[s] positions of sequence s are live, the others padding.
All inputs are finite; a program needn't handle non-finite values.
Results may differ from a plain program's by a relative error of at most 0.03.
Values may be sent and summed in bfloat16 or wider, within the bound.
No kernel may reach another device: no remote copies, remote signals or barrier semaphores. Data moves between devices by JAX's collectives and lax.ppermute only.
A program may use at most 320 MiB of HBM per device.

v0:
```python
import math

import jax
import jax.numpy as jnp
from jax import lax
from jax.sharding import PartitionSpec as P

MICRO = 2


EPS = 1e-05
MASKED = -1000000000.0


def from_behind(array, axis, by):
    devices = lax.axis_size(axis)
    pairs = [(i, i + by) for i in range(devices) if 0 <= i + by < devices]
    return lax.ppermute(array, axis, pairs)


def norm_rows(residual, gain_row, offset_row):
    row_mean = jnp.mean(residual, axis=-1, keepdims=True)
    centred = residual - row_mean
    inverse = lax.rsqrt(jnp.mean(centred * centred, axis=-1, keepdims=True) + EPS)
    normed = centred * inverse
    return (normed * gain_row + offset_row, normed, inverse)


def norm_back(upstream, normed, inverse, gain_row):
    scaled = upstream * gain_row
    return inverse * (
        scaled
        - jnp.mean(scaled, axis=-1, keepdims=True)
        - normed * jnp.mean(scaled * normed, axis=-1, keepdims=True)
    )


def gelu_pair(pre_act):
    normal_cdf = 0.5 * (1.0 + jax.scipy.special.erf(pre_act * 2.0 ** (-0.5)))
    density = jnp.exp(-0.5 * pre_act * pre_act) * (2.0 * math.pi) ** (-0.5)
    return (pre_act * normal_cdf, normal_cdf + pre_act * density)


def masked_scores(query_tile, key_heads, first_row, block_count, length, shift_row, score_scale):
    scores = (
        jnp.einsum("qhd,khd->hqk", query_tile, key_heads, preferred_element_type=jnp.float32)
        * score_scale
    )
    query_pos = first_row + jnp.arange(query_tile.shape[0], dtype=jnp.int32)
    key_pos = jnp.arange(key_heads.shape[0], dtype=jnp.int32)
    query_block = jnp.minimum(query_pos * block_count // length, block_count - 1)
    key_block = jnp.minimum(key_pos * block_count // length, block_count - 1)
    target = (query_block[None, :] + shift_row[:, None]) % block_count
    allowed = (key_block[None, None, :] == target[:, :, None]) & (key_pos < length)[None, None, :]
    return jnp.where(allowed, scores, MASKED)


def tile_forward(
    query_tile, key_heads, values, first_row, block_count, length, shift_row, score_scale
):
    scores = masked_scores(
        query_tile, key_heads, first_row, block_count, length, shift_row, score_scale
    )
    row_max = jnp.max(scores, axis=-1, keepdims=True)
    exponent = jnp.exp(scores - row_max)
    normalizer = jnp.sum(exponent, axis=-1, keepdims=True)
    weights = (exponent / normalizer).astype(jnp.bfloat16)
    mixed_tile = jnp.einsum("hqk,khd->qhd", weights, values, preferred_element_type=jnp.float32)
    return (
        mixed_tile.reshape(query_tile.shape[0], -1).astype(jnp.bfloat16),
        (row_max + jnp.log(normalizer))[:, :, 0],
    )


def tile_backward(
    query_tile,
    grad_tile,
    norm_tile,
    key_heads,
    values,
    first_row,
    block_count,
    length,
    shift_row,
    score_scale,
):
    scores = masked_scores(
        query_tile, key_heads, first_row, block_count, length, shift_row, score_scale
    )
    weights = jnp.exp(scores - norm_tile[:, :, None])
    grad_weights = jnp.einsum("qhd,khd->hqk", grad_tile, values, preferred_element_type=jnp.float32)
    row_dot = jnp.sum(weights * grad_weights, axis=-1, keepdims=True)
    grad_scores = (weights * (grad_weights - row_dot)).astype(jnp.bfloat16)
    grad_queries = (
        jnp.einsum("hqk,khd->qhd", grad_scores, key_heads, preferred_element_type=jnp.float32)
        * score_scale
    )
    key_inc = (
        jnp.einsum("hqk,qhd->khd", grad_scores, query_tile, preferred_element_type=jnp.float32)
        * score_scale
    )
    value_inc = jnp.einsum(
        "hqk,qhd->khd", weights.astype(jnp.bfloat16), grad_tile, preferred_element_type=jnp.float32
    )
    return (grad_queries, key_inc, value_inc)


def attend_forward(sequence_qkv, block_count, length, shift_row, score_scale, tile_rows):
    queries = sequence_qkv[:, 0]
    key_heads = sequence_qkv[:, 1]
    values = sequence_qkv[:, 2]
    positions = queries.shape[0]
    head_count = queries.shape[1]

    def one_tile(first_row):
        query_tile = lax.dynamic_slice_in_dim(queries, first_row, tile_rows, 0)
        return tile_forward(
            query_tile, key_heads, values, first_row, block_count, length, shift_row, score_scale
        )

    tile_starts = jnp.arange(positions // tile_rows, dtype=jnp.int32) * tile_rows
    mixed_tiles, norm_tiles = lax.map(one_tile, tile_starts)
    return (
        mixed_tiles.reshape(positions, -1),
        jnp.transpose(norm_tiles, (1, 0, 2)).reshape(head_count, positions),
    )


def attend_backward(
    sequence_qkv, grad_mixed, log_norm, block_count, length, shift_row, score_scale, tile_rows
):
    queries = sequence_qkv[:, 0]
    key_heads = sequence_qkv[:, 1]
    values = sequence_qkv[:, 2]
    positions = queries.shape[0]

    def one_tile(carry, first_row):
        grad_keys, grad_values = carry
        query_tile = lax.dynamic_slice_in_dim(queries, first_row, tile_rows, 0)
        grad_tile = lax.dynamic_slice_in_dim(grad_mixed, first_row, tile_rows, 0)
        norm_tile = lax.dynamic_slice_in_dim(log_norm, first_row, tile_rows, 1)
        grad_queries, key_inc, value_inc = tile_backward(
            query_tile,
            grad_tile,
            norm_tile,
            key_heads,
            values,
            first_row,
            block_count,
            length,
            shift_row,
            score_scale,
        )
        return ((grad_keys + key_inc, grad_values + value_inc), grad_queries)

    tile_starts = jnp.arange(positions // tile_rows, dtype=jnp.int32) * tile_rows
    zero_heads = jnp.zeros(queries.shape, jnp.float32)
    (grad_keys, grad_values), grad_tiles = lax.scan(one_tile, (zero_heads, zero_heads), tile_starts)
    grad_queries = grad_tiles.reshape(queries.shape)
    return jnp.stack([grad_queries, grad_keys, grad_values], axis=1).astype(jnp.bfloat16)


def project(inputs_micro, attention_in, attention_bias):
    bias_rows = jnp.stack([attention_bias[0], jnp.zeros_like(attention_bias[0]), attention_bias[1]])
    projected = jnp.einsum(
        "rd,dcf->rcf", inputs_micro, attention_in, preferred_element_type=jnp.float32
    )
    return (projected + bias_rows).astype(jnp.bfloat16)


def on_device(
    tokens,
    grad_out,
    attention_in,
    attention_bias,
    attention_out,
    up_weight,
    up_bias,
    down_weight,
    norm_gains,
    layer_biases,
    block_counts,
    lengths,
    head_shifts,
):
    segment_count = lax.axis_size("section")
    segment_index = lax.axis_index("section")
    half_index = lax.axis_index("mp")
    pair_count = lax.axis_size("mp")
    attention_in = attention_in[0]
    attention_bias = attention_bias[0]
    attention_out = attention_out[0]
    up_weight = up_weight[0]
    up_bias = up_bias[0]
    down_weight = down_weight[0]
    norm_gains = norm_gains[0]
    layer_biases = layer_biases[0]
    shift_row = head_shifts[0]
    inputs_all, cotangent = (
        lax.all_gather(tokens, ("section", "mp"), axis=1, tiled=True),
        lax.all_gather(grad_out, ("section", "mp"), axis=1, tiled=True),
    )
    sequence_total = block_counts.shape[0]
    per_micro = sequence_total // MICRO
    positions = inputs_all.shape[1]
    model_width = inputs_all.shape[2]
    micro_rows = per_micro * positions
    share_rows = micro_rows // pair_count
    head_count = shift_row.shape[0]
    local_width = attention_out.shape[0]
    head_size = local_width // head_count
    score_scale = head_size ** (-0.5)
    tile_rows = min(positions, 512)
    tick_count = MICRO + segment_count - 1
    last_segment = segment_count - 1

    def own_rows(whole_array, micro_slot):
        picked = lax.dynamic_slice_in_dim(
            whole_array, micro_slot * per_micro, per_micro, 0
        ).reshape(micro_rows, model_width)
        return lax.dynamic_slice_in_dim(picked, half_index * share_rows, share_rows, 0)

    def all_rows(row_piece):
        return lax.all_gather(row_piece, "mp", axis=0, tiled=True)

    def summed_rows(live_tick, term):
        first_row = jnp.int32(0)
        return lax.psum_scatter(
            lax.cond(
                live_tick,
                lambda: term(first_row, share_rows * lax.axis_size("mp")),
                lambda: jnp.zeros((share_rows * lax.axis_size("mp"), model_width), jnp.float32),
            ).astype(jnp.bfloat16),
            "mp",
            scatter_dimension=0,
            tiled=True,
        ).astype(jnp.float32)

    def store_slot(buffer, new_value, micro_slot, live_tick):
        return jnp.where(
            live_tick, lax.dynamic_update_index_in_dim(buffer, new_value, micro_slot, 0), buffer
        )

    def fetch_slot(buffer, micro_slot):
        return lax.dynamic_index_in_dim(buffer, micro_slot, 0, keepdims=False)

    def micro_ints(values_all, micro_slot):
        return lax.dynamic_slice_in_dim(values_all, micro_slot * per_micro, per_micro, 0)

    def place_rows(buffer, share_value, micro_slot, live_tick):
        placed = lax.dynamic_update_slice_in_dim(
            fetch_slot(buffer, micro_slot), share_value, half_index * share_rows, 0
        )
        return store_slot(buffer, placed, micro_slot, live_tick)

    def attention_forward(inputs_micro, counts_micro, lengths_micro):
        heads_all = project(inputs_micro, attention_in, attention_bias).reshape(
            per_micro, positions, 3, head_count, head_size
        )

        def one_sequence(sequence_item):
            return attend_forward(
                sequence_item[0],
                sequence_item[1],
                sequence_item[2],
                shift_row,
                score_scale,
                tile_rows,
            )

        mixed_rows, log_norm = lax.map(one_sequence, (heads_all, counts_micro, lengths_micro))
        return (mixed_rows.reshape(micro_rows, local_width), log_norm)

    def feed_forward(row_piece):
        pre_act = jnp.dot(row_piece, up_weight, preferred_element_type=jnp.float32) + up_bias
        activation = gelu_pair(pre_act)[0].astype(jnp.bfloat16)
        return jnp.dot(activation, down_weight, preferred_element_type=jnp.float32)

    def feed_backward(normed_all, grad_two_all):
        pre_act = jnp.dot(normed_all, up_weight, preferred_element_type=jnp.float32) + up_bias
        activation, slope_rows = gelu_pair(pre_act)
        down_inc = jnp.einsum(
            "rf,rd->fd",
            activation.astype(jnp.bfloat16),
            grad_two_all,
            preferred_element_type=jnp.float32,
        )
        grad_act = jnp.einsum(
            "rd,fd->rf", grad_two_all, down_weight, preferred_element_type=jnp.float32
        )
        grad_pre = (grad_act * slope_rows).astype(jnp.bfloat16)
        up_inc = jnp.einsum("rd,rf->df", normed_all, grad_pre, preferred_element_type=jnp.float32)
        return (down_inc, up_inc, jnp.sum(grad_pre, axis=0, dtype=jnp.float32), grad_pre)

    def attention_backward(
        inputs_micro, mixed_rows, log_norm, grad_one_all, counts_micro, lengths_micro
    ):
        out_inc = jnp.einsum(
            "rf,rd->fd", mixed_rows, grad_one_all, preferred_element_type=jnp.float32
        )
        grad_mixed = jnp.einsum(
            "rd,fd->rf", grad_one_all, attention_out, preferred_element_type=jnp.float32
        ).astype(jnp.bfloat16)
        heads_all = project(inputs_micro, attention_in, attention_bias).reshape(
            per_micro, positions, 3, head_count, head_size
        )
        grad_split = grad_mixed.reshape(per_micro, positions, head_count, head_size)

        def one_sequence(sequence_item):
            return attend_backward(
                sequence_item[0],
                sequence_item[1],
                sequence_item[2],
                sequence_item[3],
                sequence_item[4],
                shift_row,
                score_scale,
                tile_rows,
            )

        grad_heads = lax.map(
            one_sequence, (heads_all, grad_split, log_norm, counts_micro, lengths_micro)
        )
        grad_heads = grad_heads.reshape(micro_rows, 3, local_width)
        in_inc = jnp.einsum(
            "rd,rcf->dcf", inputs_micro, grad_heads, preferred_element_type=jnp.float32
        )
        column_sums = jnp.sum(grad_heads, axis=0, dtype=jnp.float32)
        return (out_inc, in_inc, jnp.stack([column_sums[0], column_sums[2]]), grad_heads)

    norm_shape = (MICRO, per_micro, head_count, positions)
    saved_inputs = jnp.zeros((MICRO, micro_rows, model_width), jnp.bfloat16)
    saved_normed = jnp.zeros((MICRO, micro_rows, model_width), jnp.bfloat16)
    saved_mixed = jnp.zeros((MICRO, micro_rows, local_width), jnp.bfloat16)
    saved_norms = jnp.zeros(norm_shape, jnp.float32)
    saved_first = jnp.zeros((MICRO, share_rows, model_width), jnp.float32)
    saved_second = jnp.zeros((MICRO, share_rows, model_width), jnp.float32)
    out_rows = jnp.zeros((MICRO, micro_rows, model_width), jnp.float32)
    grad_rows = jnp.zeros((MICRO, micro_rows, model_width), jnp.float32)
    inbox = jnp.zeros((share_rows, model_width), jnp.bfloat16)
    for tick_step in range(tick_count):
        micro_index = tick_step - segment_index
        live_tick = (micro_index >= 0) & (micro_index < MICRO)
        micro_slot = jnp.clip(micro_index, 0, MICRO - 1)
        entering = jnp.where(segment_index == 0, own_rows(inputs_all, micro_slot), inbox)
        counts_micro = micro_ints(block_counts, micro_slot)
        lengths_micro = micro_ints(lengths, micro_slot)
        inputs_micro = all_rows(entering)
        mixed_rows, log_norm = lax.cond(
            live_tick,
            lambda: attention_forward(inputs_micro, counts_micro, lengths_micro),
            lambda: (
                jnp.zeros((micro_rows, local_width), jnp.bfloat16),
                jnp.zeros(norm_shape[1:], jnp.float32),
            ),
        )
        attention_sum = summed_rows(
            live_tick,
            lambda first_row, row_total: jnp.dot(
                mixed_rows, attention_out, preferred_element_type=jnp.float32
            ),
        )
        resid_one = entering.astype(jnp.float32) + attention_sum + layer_biases[0]
        normed_one = norm_rows(resid_one, norm_gains[0], layer_biases[1])[0]
        keep_normed = all_rows(normed_one.astype(jnp.bfloat16))
        feed_sum = summed_rows(live_tick, lambda first_row, row_total: feed_forward(keep_normed))
        keep_input = inputs_micro
        resid_two = normed_one + feed_sum + layer_biases[2]
        leaving = norm_rows(resid_two, norm_gains[1], layer_biases[3])[0].astype(jnp.bfloat16)
        saved_inputs = store_slot(saved_inputs, keep_input, micro_slot, live_tick)
        saved_normed = store_slot(saved_normed, keep_normed, micro_slot, live_tick)
        saved_mixed = store_slot(saved_mixed, mixed_rows, micro_slot, live_tick)
        saved_norms = store_slot(saved_norms, log_norm, micro_slot, live_tick)
        saved_first = store_slot(saved_first, resid_one, micro_slot, live_tick)
        saved_second = store_slot(saved_second, resid_two, micro_slot, live_tick)
        out_rows = place_rows(
            out_rows,
            leaving.astype(jnp.float32),
            micro_slot,
            live_tick & (segment_index == last_segment),
        )
        inbox = from_behind(leaving, "section", 1)
    acc_in = jnp.zeros(attention_in.shape, jnp.float32)
    acc_bias = jnp.zeros(attention_bias.shape, jnp.float32)
    acc_out = jnp.zeros(attention_out.shape, jnp.float32)
    acc_up = jnp.zeros(up_weight.shape, jnp.float32)
    acc_up_bias = jnp.zeros(up_bias.shape, jnp.float32)
    acc_down = jnp.zeros(down_weight.shape, jnp.float32)
    gain_grads = jnp.zeros((2, model_width), jnp.float32)
    bias_grads = jnp.zeros((4, model_width), jnp.float32)
    inbox = jnp.zeros((share_rows, model_width), jnp.bfloat16)
    for tick_step in range(tick_count):
        micro_index = tick_step - (last_segment - segment_index)
        live_tick = (micro_index >= 0) & (micro_index < MICRO)
        live_scale = live_tick.astype(jnp.float32)
        micro_slot = jnp.clip(micro_index, 0, MICRO - 1)
        arriving = jnp.where(
            segment_index == last_segment, own_rows(cotangent, micro_slot), inbox
        ).astype(jnp.float32)
        keep_input = fetch_slot(saved_inputs, micro_slot)
        keep_normed = fetch_slot(saved_normed, micro_slot)
        mixed_rows = fetch_slot(saved_mixed, micro_slot)
        log_norm = fetch_slot(saved_norms, micro_slot)
        resid_one = fetch_slot(saved_first, micro_slot)
        resid_two = fetch_slot(saved_second, micro_slot)
        counts_micro = micro_ints(block_counts, micro_slot)
        lengths_micro = micro_ints(lengths, micro_slot)
        unit_one, inverse_one = norm_rows(resid_one, norm_gains[0], layer_biases[1])[1:]
        unit_two, inverse_two = norm_rows(resid_two, norm_gains[1], layer_biases[3])[1:]
        grad_resid_two = norm_back(arriving, unit_two, inverse_two, norm_gains[1])
        grad_two_all = all_rows(grad_resid_two.astype(jnp.bfloat16))
        down_inc, up_inc, up_bias_inc, grad_pre = lax.cond(
            live_tick,
            lambda: feed_backward(keep_normed, grad_two_all),
            lambda: (
                jnp.zeros(down_weight.shape, jnp.float32),
                jnp.zeros(up_weight.shape, jnp.float32),
                jnp.zeros(up_bias.shape, jnp.float32),
                jnp.zeros((micro_rows, up_bias.shape[0]), jnp.bfloat16),
            ),
        )
        grad_normed = grad_resid_two + summed_rows(
            live_tick,
            lambda first_row, row_total: jnp.einsum(
                "rf,df->rd", grad_pre, up_weight, preferred_element_type=jnp.float32
            ),
        )
        grad_resid_one = norm_back(grad_normed, unit_one, inverse_one, norm_gains[0])
        grad_one_all = all_rows(grad_resid_one.astype(jnp.bfloat16))
        out_inc, in_inc, bias_inc, grad_heads = lax.cond(
            live_tick,
            lambda: attention_backward(
                keep_input, mixed_rows, log_norm, grad_one_all, counts_micro, lengths_micro
            ),
            lambda: (
                jnp.zeros(attention_out.shape, jnp.float32),
                jnp.zeros(attention_in.shape, jnp.float32),
                jnp.zeros(attention_bias.shape, jnp.float32),
                jnp.zeros((micro_rows, 3, local_width), jnp.bfloat16),
            ),
        )
        grad_entering = grad_resid_one + summed_rows(
            live_tick,
            lambda first_row, row_total: jnp.einsum(
                "rcf,dcf->rd", grad_heads, attention_in, preferred_element_type=jnp.float32
            ),
        )
        acc_down = acc_down + down_inc
        acc_up = acc_up + up_inc
        acc_up_bias = acc_up_bias + up_bias_inc
        acc_out = acc_out + out_inc
        acc_in = acc_in + in_inc
        acc_bias = acc_bias + bias_inc
        leaving_grad = grad_entering.astype(jnp.bfloat16)
        gain_grads = gain_grads + live_scale * jnp.stack(
            [jnp.sum(grad_normed * unit_one, axis=0), jnp.sum(arriving * unit_two, axis=0)]
        )
        bias_grads = bias_grads + live_scale * jnp.stack(
            [
                jnp.sum(grad_resid_one, axis=0),
                jnp.sum(grad_normed, axis=0),
                jnp.sum(grad_resid_two, axis=0),
                jnp.sum(arriving, axis=0),
            ]
        )
        grad_rows = place_rows(
            grad_rows,
            leaving_grad.astype(jnp.float32),
            micro_slot,
            live_tick & (segment_index == 0),
        )
        inbox = from_behind(leaving_grad, "section", -1)
    acc_in, acc_bias, acc_out, acc_up, acc_up_bias, acc_down = (
        lax.psum(acc_in.astype(jnp.bfloat16), "dp").astype(jnp.float32),
        lax.psum(acc_bias.astype(jnp.bfloat16), "dp").astype(jnp.float32),
        lax.psum(acc_out.astype(jnp.bfloat16), "dp").astype(jnp.float32),
        lax.psum(acc_up.astype(jnp.bfloat16), "dp").astype(jnp.float32),
        lax.psum(acc_up_bias.astype(jnp.bfloat16), "dp").astype(jnp.float32),
        lax.psum(acc_down.astype(jnp.bfloat16), "dp").astype(jnp.float32),
    )
    gain_grads, bias_grads = lax.psum((gain_grads, bias_grads), ("mp", "dp"))
    layer_sum, tokens_sum = (
        lax.psum_scatter(
            out_rows.astype(jnp.bfloat16), ("section", "mp"), scatter_dimension=1, tiled=True
        ).astype(jnp.float32),
        lax.psum_scatter(
            grad_rows.astype(jnp.bfloat16), ("section", "mp"), scatter_dimension=1, tiled=True
        ).astype(jnp.float32),
    )
    return (
        layer_sum.astype(jnp.bfloat16),
        tokens_sum.astype(jnp.bfloat16),
        acc_in[None],
        acc_bias[None],
        acc_out[None],
        acc_up[None],
        acc_up_bias[None],
        acc_down[None],
        gain_grads[None],
        bias_grads[None],
    )


def solution(mesh):
    return jax.shard_map(
        on_device,
        mesh=mesh,
        in_specs=(
            P("dp", ("section", "mp"), None),
            P("dp", ("section", "mp"), None),
            P("section", None, None, "mp"),
            P("section", None, "mp"),
            P("section", "mp", None),
            P("section", None, "mp"),
            P("section", "mp"),
            P("section", "mp", None),
            P("section", None, None),
            P("section", None, None),
            P("dp"),
            P("dp"),
            P("section", "mp"),
        ),
        out_specs=(
            P("dp", ("section", "mp"), None),
            P("dp", ("section", "mp"), None),
            P("section", None, None, "mp"),
            P("section", None, "mp"),
            P("section", "mp", None),
            P("section", None, "mp"),
            P("section", "mp"),
            P("section", "mp", None),
            P("section", None, None),
            P("section", None, None),
        ),
        check_vma=False,
    )
```

profile of v0, /device:TPU:14, one launch (start us, length us, event | category | flops | bytes accessed | tf_op | source)
XLA Modules:
  0.0 1437.5 jit_solution(12522428857821549632)
XLA Ops:
  8.0 30.3 %all-gather.16.cloned.1.call-done = bf16[2,1024,768]{2,1,0:T(8,128)(2,1)} async-done(((bf16[2,256,768]{2,1,0:T(8,128)(2,1)}), bf16[2,1024,768]{2,1,0:T(8,128)(2,1)}) %all-gather.16.cloned.1.call-update) | async-done | bytes 3145744 | tf_op jit(solution)/shard_map/all_gather | solution.py:200
  40.7 11.1 all-gather.42.cloned.1.call-done
  55.4 63.8 %reduce-scatter.15.cloned.1.call-done = bf16[512,768]{1,0:T(8,128)(2,1)} async-done(((bf16[1024,768]{1,0:T(8,128)(2,1)}), bf16[512,768]{1,0:T(8,128)(2,1)}) %reduce-scatter.15.cloned.1.call-update) | async-done | bytes 786448 | tf_op jit(solution)/shard_map/reduce_scatter | solution.py:228
  126.0 11.1 all-gather.18.cloned.1.call-done
  138.4 17.4 %reduce-scatter.17.cloned.1.call-done = bf16[512,768]{1,0:T(8,128)(2,1)} async-done(((bf16[1024,768]{1,0:T(8,128)(2,1)}), bf16[512,768]{1,0:T(8,128)(2,1)}) %reduce-scatter.17.cloned.1.call-update) | async-done | bytes 786448 | tf_op jit(solution)/shard_map/reduce_scatter | solution.py:228
  164.4 20.3 %collective-permute-done = bf16[512,768]{1,0:T(8,128)(2,1)S(1)} collective-permute-done((bf16[512,768]{1,0:T(8,128)(2,1)S(1)}, bf16[512,768]{1,0:T(8,128)(2,1)S(1)}, u32[]{:S(2)}, u32[]{:S(2)}) %collective-permute-start) | collective-permute-done | bytes 786464 | tf_op jit(solution)/shard_map/ppermute | solution.py:18
  187.2 10.9 all-gather.20.cloned.1.call-done
  198.1 57.4 %conditional.24 = (bf16[1024,384]{1,0:T(8,128)(2,1)}, bf16[1,1024,384]{2,1,0:T(8,128)(2,1)S(1)}, f32[1,1,6,1024]{3,2,1,0:T(8,128)}) conditional(s32[]{:T(128)} %convert_element_type.474, () %tuple.310, (bf16[1024,768]{1,0:T(8,128)(2,1)}, bf16[768,3,384]{2,0,1:T(8,128)(2,1)}, f32[2,384]{1,0:T(2,128)S(1)}, s32[2]{0:T(128)S(1)}, s32[]{:T(128)}, ...), branch_computations={%region_16.17_spmd, %region_17.22_spmd} | conditional | flops 2676465408 | bytes 53873216 | solution.py:349
  206.6 47.8 %while.181 = (s32[]{:T(128)}, bf16[2,512,384]{2,1,0:T(8,128)(2,1)}, f32[2,6,512]{2,1,0:T(8,128)}, s32[]{:T(128)}, s32[]{:T(128)}, /*index=5*/s32[]{:T(128)}, s32...) while((s32[]{:T(128)}, bf16[2,512,384]{2,1,0:T(8,128)(2,1)}, ...), condition=%wide.region_21.21_spmd, body=%wide.region_18.20_spmd.sunk | while | flops 862164480 | bytes 41861412 | solution.py:122
  222.8 6.0 fusion.493
  246.7 6.0 fusion.493
  260.0 10.3 reduce-scatter.19.cloned.1.call-done
  275.1 10.9 all-gather.22.cloned.1.call-done
  286.0 8.1 conditional.26
  286.0 8.0 fusion.160
  319.0 20.5 %collective-permute-done.1 = bf16[512,768]{1,0:T(8,128)(2,1)S(1)} collective-permute-done((bf16[512,768]{1,0:T(8,128)(2,1)}, bf16[512,768]{1,0:T(8,128)(2,1)S(1)}, u32[]{:S(2)}, u32[]{:S(2)}) %collective-permute-start.1) | collective-permute-done | bytes 786464 | tf_op jit(solution)/shard_map/ppermute | solution.py:18
  341.8 11.1 all-gather.24.cloned.1.call-done
  352.9 57.0 %conditional.27 = (bf16[1024,384]{1,0:T(8,128)(2,1)}, bf16[1,1024,384]{2,1,0:T(8,128)(2,1)S(1)}, f32[1,1,6,1024]{3,2,1,0:T(8,128)}) conditional(s32[]{:T(128)} %convert_element_type.482, () %tuple.316, (bf16[1024,768]{1,0:T(8,128)(2,1)}, bf16[768,3,384]{2,0,1:T(8,128)(2,1)}, f32[2,384]{1,0:T(2,128)S(1)}, s32[2]{0:T(128)S(1)}, s32[]{:T(128)}, ...), branch_computations={%region_32.33_spmd, %region_33.38_spmd} | conditional | flops 2676465408 | bytes 53873216 | solution.py:349
  361.7 47.1 %while.182 = (s32[]{:T(128)}, bf16[2,512,384]{2,1,0:T(8,128)(2,1)}, f32[2,6,512]{2,1,0:T(8,128)}, s32[]{:T(128)}, s32[]{:T(128)}, /*index=5*/s32[]{:T(128)}, s32...) while((s32[]{:T(128)}, bf16[2,512,384]{2,1,0:T(8,128)(2,1)}, ...), condition=%wide.region_37.37_spmd, body=%wide.region_34.36_spmd.sunk | while | flops 862164480 | bytes 41861412 | solution.py:122
  377.6 6.0 fusion.486
  414.3 10.4 reduce-scatter.23.cloned.1.call-done
  429.3 11.1 all-gather.26.cloned.1.call-done
  440.4 9.5 conditional.29
  440.6 9.3 fusion.164
  450.6 9.8 reduce-scatter.25.cloned.1.call-done
  471.2 19.1 %all-gather.28.cloned.1.call-done = bf16[2,1024,768]{2,1,0:T(8,128)(2,1)} async-done(((bf16[2,256,768]{2,1,0:T(8,128)(2,1)}), bf16[2,1024,768]{2,1,0:T(8,128)(2,1)}) %all-gather.28.cloned.1.call-update) | async-done | bytes 3145744 | tf_op jit(solution)/shard_map/all_gather | solution.py:201
  508.9 23.6 %conditional.30 = (f32[1536,768]{1,0:T(8,128)}, f32[768,1536]{1,0:T(8,128)}, f32[1536]{0:T(1024)S(1)}, bf16[1024,1536]{1,0:T(8,128)(2,1)}) conditional(s32[]{:T(128)} %convert_element_type.492, () %tuple.322, (bf16[2,1024,768]{2,1,0:T(8,128)(2,1)}, s32[]{:T(128)}, bf16[768,1536]{1,0:T(8,128)(2,1)}, f32[1,1536]{1,0:T(1,128)S(1)}, ...), branch_computations={%region_55.56_spmd, %region_56.58_spmd} | conditional | flops 9693558784 | bytes 61373532 | solution.py:412
  514.1 6.5 convert_reduce_fusion.3
  525.3 7.2 fusion.176
  533.1 6.4 conditional.31
  533.1 6.4 fusion.297
  567.8 94.8 %conditional.32 = (f32[384,768]{1,0:T(8,128)}, f32[768,3,384]{2,0,1:T(8,128)}, f32[2,384]{1,0:T(2,128)}, bf16[1024,3,384]{2,0,1:T(8,128)(2,1)}) conditional(s32[]{:T(128)} %convert_element_type.492, () %tuple.326, (bf16[2,1024,384]{2,1,0:T(8,128)(2,1)}, s32[]{:T(128)}, bf16[1024,768]{1,0:T(8,128)(2,1)}, bf16[2,1024,768]{2,1,0:T(8,128)(2,1)S(1)}, ...), branch_computations={%region_63.64_spmd, %region_64.69_spmd} | conditional | flops 6890168320 | bytes 263641728 | solution.py:430
  584.3 57.6 %while.183 = (s32[]{:T(128)}, f32[1024,6,64]{0,2,1:T(8,128)S(1)}, f32[1024,6,64]{0,2,1:T(8,128)}, bf16[2,512,6,64]{1,3,2,0:T(8,128)(2,1)}, s32[2]{0:T(128)S(1)},...) while((s32[]{:T(128)}, f32[1024,6,64]{0,2,1:T(8,128)S(1)}, ...), condition=%wide.region_67.67_spmd.clone, body=%wide.region_65.66_spmd.clone.sunk | while | flops 2050070016 | bytes 184126032 | solution.py:158
  594.4 7.5 multiply_reduce_fusion.29
  623.2 7.4 multiply_reduce_fusion.29
  668.3 10.4 reduce-scatter.31.cloned.1.call-done
  683.9 17.1 %collective-permute-done.2 = bf16[512,768]{1,0:T(8,128)(2,1)S(1)} collective-permute-done((bf16[512,768]{1,0:T(8,128)(2,1)S(1)}, bf16[512,768]{1,0:T(8,128)(2,1)S(1)}, u32[]{:S(2)}, u32[]{:S(2)}) %collective-permute-start.2) | collective-permute-done | bytes 786464 | tf_op jit(solution)/shard_map/ppermute | solution.py:18
  708.6 12.0 all-gather.34.cloned.1.call-done
  720.6 23.4 %conditional.34 = (f32[1536,768]{1,0:T(8,128)}, f32[768,1536]{1,0:T(8,128)}, f32[1536]{0:T(1024)S(1)}, bf16[1024,1536]{1,0:T(8,128)(2,1)}) conditional(s32[]{:T(128)} %convert_element_type.502, () %tuple.330, (bf16[2,1024,768]{2,1,0:T(8,128)(2,1)}, s32[]{:T(128)}, bf16[768,1536]{1,0:T(8,128)(2,1)}, f32[1,1536]{1,0:T(1,128)S(1)}, ...), branch_computations={%region_78.79_spmd, %region_79.81_spmd} | conditional | flops 9693558784 | bytes 51936320 | solution.py:412
  725.5 6.5 convert_reduce_fusion.4
  736.7 7.2 fusion.192
  744.5 6.5 conditional.35
  744.6 6.5 fusion.298
  751.2 10.3 reduce-scatter.33.cloned.1.call-done
  768.8 10.6 all-gather.36.cloned.1.call-done
  779.5 93.5 %conditional.36 = (f32[384,768]{1,0:T(8,128)}, f32[768,3,384]{2,0,1:T(8,128)}, f32[2,384]{1,0:T(2,128)}, bf16[1024,3,384]{2,0,1:T(8,128)(2,1)}) conditional(s32[]{:T(128)} %convert_element_type.502, () %tuple.334, (bf16[2,1024,384]{2,1,0:T(8,128)(2,1)}, s32[]{:T(128)}, bf16[1024,768]{1,0:T(8,128)(2,1)}, bf16[2,1024,768]{2,1,0:T(8,128)(2,1)}, ...), branch_computations={%region_86.87_spmd, %region_87.92_spmd} | conditional | flops 6890168320 | bytes 251058784 | solution.py:430
  795.3 57.3 %while.184 = (s32[]{:T(128)}, f32[1024,6,64]{0,2,1:T(8,128)S(1)}, f32[1024,6,64]{0,2,1:T(8,128)}, bf16[2,512,6,64]{1,3,2,0:T(8,128)(2,1)}, s32[2]{0:T(128)S(1)},...) while((s32[]{:T(128)}, f32[1024,6,64]{0,2,1:T(8,128)S(1)}, ...), condition=%wide.region_90.90_spmd.clone, body=%wide.region_88.89_spmd.clone.sunk | while | flops 2050070016 | bytes 184126032 | solution.py:158
  805.2 7.5 multiply_reduce_fusion.28
  833.8 7.4 multiply_reduce_fusion.28
  880.4 8.5 reduce-scatter.35.cloned.1.call-done
  895.4 16.6 %collective-permute-done.3 = bf16[512,768]{1,0:T(8,128)(2,1)} collective-permute-done((bf16[512,768]{1,0:T(8,128)(2,1)}, bf16[512,768]{1,0:T(8,128)(2,1)}, u32[]{:S(2)}, u32[]{:S(2)}) %collective-permute-start.3) | collective-permute-done | bytes 786464 | tf_op jit(solution)/shard_map/ppermute | solution.py:18
  918.7 12.3 all-gather.38.cloned.1.call-done
  931.1 7.3 conditional.38
  940.4 31.0 %reduce-scatter.37.cloned.1.call-done = bf16[512,768]{1,0:T(8,128)(2,1)} async-done(((bf16[1024,768]{1,0:T(8,128)(2,1)}), bf16[512,768]{1,0:T(8,128)(2,1)}) %reduce-scatter.37.cloned.1.call-update) | async-done | bytes 786448 | tf_op jit(solution)/shard_map/reduce_scatter | solution.py:228
  978.0 11.1 all-gather.40.cloned.1.call-done
  989.1 12.1 conditional.40
  1002.5 7.3 fusion.217
  1009.8 7.8 fusion.216
  1045.2 52.5 %reduce-scatter.39.cloned.1.call-done = bf16[512,768]{1,0:T(8,128)(2,1)} async-done(((bf16[1024,768]{1,0:T(8,128)(2,1)}), bf16[512,768]{1,0:T(8,128)(2,1)}) %reduce-scatter.39.cloned.1.call-update) | async-done | bytes 786448 | tf_op jit(solution)/shard_map/reduce_scatter | solution.py:228
  1109.2 59.3 %all-reduce = (f32[1,2,768]{2,1,0:T(2,128)}, f32[1,4,768]{2,1,0:T(4,128)}) all-reduce(f32[1,2,768]{2,1,0:T(2,128)S(1)} %fusion.271, f32[1,4,768]{2,1,0:T(4,128)S(1)} %fusion.268), channel_id=1, replica_groups=mesh['section'=2,'mp'=2,'dp'=8] {'mp','dp'}, use_global_device_ids=true, to_apply=%region_131.132 | all-reduce | flops 4608 | bytes 36864 | tf_op jit(solution)/shard_map/psum | solution.py:481
  1169.2 22.0 %all-reduce.1 = (bf16[1,2,384]{2,1,0:T(2,128)(2,1)S(1)}, bf16[1,1536]{1,0:T(2,128)(2,1)S(1)}) all-reduce(bf16[1,2,384]{2,1,0:T(2,128)(2,1)S(1)} %fusion.272, bf16[1,1536]{1,0:T(2,128)(2,1)S(1)} %broadcast_in_dim.351), channel_id=1, replica_groups=mesh['section'=2,'mp'=2,'dp'=8] {'dp'}, use_global_device_ids=true, to_apply=%region_120.121 | all-reduce | flops 2304 | bytes 9216 | tf_op jit(solution)/shard_map/psum | solution.py:475
  1192.3 156.4 %all-reduce.5.cloned.1.call-done = (bf16[1,768,3,384]{3,1,2,0:T(8,128)(2,1)}, bf16[1,384,768]{2,1,0:T(8,128)(2,1)}, bf16[1,768,1536]{2,1,0:T(8,128)(2,1)}, bf16[1,1536,768]{2,1,0:T(8,128)(2,1)}) async-done(((bf16[1,768,3,384]{3,1,2,0:T(8,128)(2,1)}, bf16[1,384,768]{2,1,0:T(8,128)(2,1)}, bf16[1,768,1536]{2,1,0:T(8,128)(2,1)}, bf16[1,1536,768]{2,1,0:T(8,128)(2,1)}), (bf16[1,768,3,384]{3,1,2,0:T(8,128)(2,1)}, ...) | async-done | bytes 7077904 | tf_op jit(solution)/shard_map/psum | solution.py:474
  1359.2 30.4 %reduce-scatter.27.cloned.1.call-done = bf16[2,256,768]{2,1,0:T(8,128)(2,1)} async-done(((bf16[2,1024,768]{2,1,0:T(8,128)(2,1)}), bf16[2,256,768]{2,1,0:T(8,128)(2,1)}) %reduce-scatter.27.cloned.1.call-update) | async-done | bytes 786448 | tf_op jit(solution)/shard_map/reduce_scatter | solution.py:483
  1389.6 41.1 %reduce-scatter.41.cloned.1.call-done = bf16[2,256,768]{2,1,0:T(8,128)(2,1)} async-done(((bf16[2,1024,768]{2,1,0:T(8,128)(2,1)}), bf16[2,256,768]{2,1,0:T(8,128)(2,1)}) %reduce-scatter.41.cloned.1.call-update) | async-done | bytes 786448 | tf_op jit(solution)/shard_map/reduce_scatter | solution.py:486
  (757 shorter events, 512.2 us)
Async XLA Ops:
  7.2 44.6 %copy-start.95 = (s32[1,6]{1,0:T(1,128)S(1)}, s32[1,6]{1,0:T(1,128)}, u32[]{:S(2)}) copy-start(s32[1,6]{1,0:T(1,128)} %param.79) | copy-start | bytes 76
  7.2 44.6 %copy-start.173 = (s32[2]{0:T(128)S(1)}, s32[2]{0:T(128)}, u32[]{:S(2)}) copy-start(s32[2]{0:T(128)} %param.78) | copy-start | bytes 28
  7.2 44.6 %copy-start.170 = (s32[2]{0:T(128)S(1)}, s32[2]{0:T(128)}, u32[]{:S(2)}) copy-start(s32[2]{0:T(128)} %param.77) | copy-start | bytes 28
  7.2 44.6 %copy-start.113 = (f32[1,2,384]{2,1,0:T(2,128)S(1)}, f32[1,2,384]{2,1,0:T(2,128)}, u32[]{:S(2)}) copy-start(f32[1,2,384]{2,1,0:T(2,128)} %param.70) | copy-start | bytes 9220
  7.2 44.6 %copy-start.164 = (bf16[1,768,3,384]{3,1,2,0:T(8,128)(2,1)S(1)}, bf16[1,768,3,384]{3,1,2,0:T(8,128)(2,1)}, u32[]{:S(2)}) copy-start(bf16[1,768,3,384]{3,1,2,0:T(8,128)(2,1)} %param.69) | copy-start | bytes 5308420
  7.2 31.1 %all-gather.16.cloned.1.call-start = ((), (), s32[]{:S(2)}) async-start(), calls=%async_computation.14 | async-start | bytes 3932160 | tf_op jit(solution)/shard_map/all_gather | solution.py:200
  8.0 43.8 %all-gather.42.cloned.1.call-start = ((), (), s32[]{:S(2)}) async-start(), calls=%async_computation.41 | async-start | bytes 2359296 | tf_op jit(solution)/shard_map/all_gather | solution.py:224
  40.7 78.5 %reduce-scatter.15.cloned.1.call-start = ((), (), s32[]{:S(2)}) async-start(), calls=%async_computation.15 | async-start | bytes 2359296 | tf_op jit(solution)/shard_map/reduce_scatter | solution.py:228
  54.7 82.4 %all-gather.18.cloned.1.call-start = ((), (), s32[]{:S(2)}) async-start(), calls=%async_computation.16 | async-start | bytes 2359296 | tf_op jit(solution)/shard_map/all_gather | solution.py:224
  55.2 102.5 %copy-start.90 = (f32[768]{0:T(1024)}, f32[768]{0:T(1024)S(1)}, u32[]{:S(2)}) copy-start(f32[768]{0:T(1024)S(1)} %get-tuple-element.2475) | copy-start | bytes 9220
  55.3 106.3 %copy-start.99 = (f32[768]{0:T(1024)}, f32[768]{0:T(1024)S(1)}, u32[]{:S(2)}) copy-start(f32[768]{0:T(1024)S(1)} %get-tuple-element.2474) | copy-start | bytes 9220
  55.3 102.4 %copy-start.80 = (f32[768]{0:T(1024)}, f32[768]{0:T(1024)S(1)}, u32[]{:S(2)}) copy-start(f32[768]{0:T(1024)S(1)} %get-tuple-element.2472) | copy-start | bytes 9220
  55.3 102.4 %copy-start.110 = (f32[768]{0:T(1024)}, f32[768]{0:T(1024)S(1)}, u32[]{:S(2)}) copy-start(f32[768]{0:T(1024)S(1)} %get-tuple-element.2471) | copy-start | bytes 9220
  55.3 102.4 %copy-start.116 = (f32[768]{0:T(1024)}, f32[768]{0:T(1024)S(1)}, u32[]{:S(2)}) copy-start(f32[768]{0:T(1024)S(1)} %get-tuple-element.2473) | copy-start | bytes 9220
  55.3 106.2 %copy-start.119 = (f32[768]{0:T(1024)}, f32[768]{0:T(1024)S(1)}, u32[]{:S(2)}) copy-start(f32[768]{0:T(1024)S(1)} %get-tuple-element.2470) | copy-start | bytes 9220
  121.1 15.9 %copy-start.105 = (f32[1,1536]{1,0:T(1,128)S(1)}, f32[1,1536]{1,0:T(1,128)}, u32[]{:S(2)}) copy-start(f32[1,1536]{1,0:T(1,128)} %param.73) | copy-start | bytes 18436
  125.9 29.9 %reduce-scatter.17.cloned.1.call-start = ((), (), s32[]{:S(2)}) async-start(), calls=%async_computation.17 | async-start | bytes 2359296 | tf_op jit(solution)/shard_map/reduce_scatter | solution.py:228
  138.3 59.8 %all-gather.20.cloned.1.call-start = ((), (), s32[]{:S(2)}) async-start(), calls=%async_computation.18 | async-start | bytes 2359296 | tf_op jit(solution)/shard_map/all_gather | solution.py:224
  163.1 21.6 %collective-permute-start = (bf16[512,768]{1,0:T(8,128)(2,1)S(1)}, bf16[512,768]{1,0:T(8,128)(2,1)S(1)}, u32[]{:S(2)}, u32[]{:S(2)}) collective-permute-start(bf16[512,768]{1,0:T(8,128)(2,1)S(1)} %get-tuple-element.2703), channel_id=1, source_target_pairs={{0,16},{1,17},{2,18},{3,19},{4,20},{5,21},{6,22},{7,23},{8,24},{9,... | collective-permute-start | bytes 2359304 | tf_op jit(solution)/shard_map/ppermute | solution.py:18
  187.0 83.3 %reduce-scatter.19.cloned.1.call-start = ((), (), s32[]{:S(2)}) async-start(), calls=%async_computation.19 | async-start | bytes 2359296 | tf_op jit(solution)/shard_map/reduce_scatter | solution.py:228
  259.9 26.1 %all-gather.22.cloned.1.call-start = ((), (), s32[]{:S(2)}) async-start(), calls=%async_computation.20 | async-start | bytes 2359296 | tf_op jit(solution)/shard_map/all_gather | solution.py:224
  274.8 30.8 %reduce-scatter.21.cloned.1.call-start = ((), (), s32[]{:S(2)}) async-start(), calls=%async_computation.21 | async-start | bytes 2359296 | tf_op jit(solution)/shard_map/reduce_scatter | solution.py:228
  295.2 57.7 %all-gather.24.cloned.1.call-start = ((), (), s32[]{:S(2)}) async-start(), calls=%async_computation.22 | async-start | bytes 2359296 | tf_op jit(solution)/shard_map/all_gather | solution.py:224
  317.7 21.8 %collective-permute-start.1 = (bf16[512,768]{1,0:T(8,128)(2,1)}, bf16[512,768]{1,0:T(8,128)(2,1)S(1)}, u32[]{:S(2)}, u32[]{:S(2)}) collective-permute-start(bf16[512,768]{1,0:T(8,128)(2,1)} %get-tuple-element.2701), channel_id=1, source_target_pairs={{0,16},{1,17},{2,18},{3,19},{4,20},{5,21},{6,22},{7,23},{8,24},{9,... | collective-permute-start | bytes 2359304 | tf_op jit(solution)/shard_map/ppermute | solution.py:18
  341.8 82.9 %reduce-scatter.23.cloned.1.call-start = ((), (), s32[]{:S(2)}) async-start(), calls=%async_computation.23 | async-start | bytes 2359296 | tf_op jit(solution)/shard_map/reduce_scatter | solution.py:228
  414.3 26.1 %all-gather.26.cloned.1.call-start = ((), (), s32[]{:S(2)}) async-start(), calls=%async_computation.24 | async-start | bytes 2359296 | tf_op jit(solution)/shard_map/all_gather | solution.py:224
  429.2 31.1 %reduce-scatter.25.cloned.1.call-start = ((), (), s32[]{:S(2)}) async-start(), calls=%async_computation.25 | async-start | bytes 2359296 | tf_op jit(solution)/shard_map/reduce_scatter | solution.py:228
  440.4 20.0 %copy-start.4 = (f32[2,512,768]{2,1,0:T(8,128)S(1)}, f32[2,512,768]{2,1,0:T(8,128)}, u32[]{:S(2)}) copy-start(f32[2,512,768]{2,1,0:T(8,128)} %copy-done.3) | copy-start | bytes 9437188
  449.9 40.4 %all-gather.28.cloned.1.call-start = ((), (), s32[]{:S(2)}) async-start(), calls=%async_computation.27 | async-start | bytes 3932160 | tf_op jit(solution)/shard_map/all_gather | solution.py:201
  450.5 58.4 %all-gather.30.cloned.1.call-start = ((), (), s32[]{:S(2)}) async-start(), calls=%async_computation.28 | async-start | bytes 2359296 | tf_op jit(solution)/shard_map/all_gather | solution.py:224
  465.0 88.4 %copy-start.5 = (f32[2,512,768]{2,1,0:T(8,128)}, f32[2,512,768]{2,1,0:T(8,128)S(1)}, u32[]{:S(2)}) copy-start(f32[2,512,768]{2,1,0:T(8,128)S(1)} %get-tuple-element.2758) | copy-start | bytes 9437188
  465.0 25.4 %copy-start.101 = (f32[768]{0:T(1024)S(1)}, f32[768]{0:T(1024)}, u32[]{:S(2)}) copy-start(f32[768]{0:T(1024)} %copy-done.99) | copy-start | bytes 9220
  469.3 24.7 %copy-start.122 = (f32[512]{0:T(512)}, f32[512]{0:T(512)S(1)}, u32[]{:S(2)}) copy-start(f32[512]{0:T(512)S(1)} %get-tuple-element.2762) | copy-start | bytes 6148
  497.7 52.2 %reduce-scatter.29.cloned.1.call-start = ((), (), s32[]{:S(2)}) async-start(), calls=%async_computation.29 | async-start | bytes 2359296 | tf_op jit(solution)/shard_map/reduce_scatter | solution.py:228
  539.5 28.3 %all-gather.32.cloned.1.call-start = ((), (), s32[]{:S(2)}) async-start(), calls=%async_computation.30 | async-start | bytes 2359296 | tf_op jit(solution)/shard_map/all_gather | solution.py:224
  556.7 121.9 %reduce-scatter.31.cloned.1.call-start = ((), (), s32[]{:S(2)}) async-start(), calls=%async_computation.31 | async-start | bytes 2359296 | tf_op jit(solution)/shard_map/reduce_scatter | solution.py:228
  668.2 52.3 %all-gather.34.cloned.1.call-start = ((), (), s32[]{:S(2)}) async-start(), calls=%async_computation.32 | async-start | bytes 2359296 | tf_op jit(solution)/shard_map/all_gather | solution.py:224
  678.8 22.3 %copy-start.102 = (f32[768]{0:T(1024)S(1)}, f32[768]{0:T(1024)}, u32[]{:S(2)}) copy-start(f32[768]{0:T(1024)} %copy-done.99) | copy-start | bytes 9220
  678.8 22.3 %copy-start.123 = (f32[512]{0:T(512)S(1)}, f32[512]{0:T(512)}, u32[]{:S(2)}) copy-start(f32[512]{0:T(512)} %copy-done.122) | copy-start | bytes 6148
  681.3 19.7 %collective-permute-start.2 = (bf16[512,768]{1,0:T(8,128)(2,1)S(1)}, bf16[512,768]{1,0:T(8,128)(2,1)S(1)}, u32[]{:S(2)}, u32[]{:S(2)}) collective-permute-start(bf16[512,768]{1,0:T(8,128)(2,1)S(1)} %get-tuple-element.2691), channel_id=1, source_target_pairs={{16,0},{17,1},{18,2},{19,3},{20,4},{21,5},{22,6},{23,7},{24,8},{25... | collective-permute-start | bytes 2359304 | tf_op jit(solution)/shard_map/ppermute | solution.py:18
  683.9 21.1 %copy-start.126 = (f32[512]{0:T(512)}, f32[512]{0:T(512)S(1)}, u32[]{:S(2)}) copy-start(f32[512]{0:T(512)S(1)} %broadcast_multiply_fusion.4) | copy-start | bytes 6148
  705.0 15.5 %copy-start.108 = (f32[1,1536]{1,0:T(1,128)S(1)}, f32[1,1536]{1,0:T(1,128)}, u32[]{:S(2)}) copy-start(f32[1,1536]{1,0:T(1,128)} %param.73) | copy-start | bytes 18436
  705.0 15.5 %copy-start.161 = (bf16[1,1536,768]{2,1,0:T(8,128)(2,1)S(1)}, bf16[1,1536,768]{2,1,0:T(8,128)(2,1)}, u32[]{:S(2)}) copy-start(bf16[1,1536,768]{2,1,0:T(8,128)(2,1)} %param.74) | copy-start | bytes 7077892
  708.5 53.0 %reduce-scatter.33.cloned.1.call-start = ((), (), s32[]{:S(2)}) async-start(), calls=%async_computation.33 | async-start | bytes 2359296 | tf_op jit(solution)/shard_map/reduce_scatter | solution.py:228
  744.5 17.0 %copy-start.6 = (f32[2,512,768]{2,1,0:T(8,128)S(1)}, f32[2,512,768]{2,1,0:T(8,128)}, u32[]{:S(2)}) copy-start(f32[2,512,768]{2,1,0:T(8,128)} %copy-done.5) | copy-start | bytes 9437188
  744.5 17.0 %copy-start.93 = (f32[768]{0:T(1024)S(1)}, f32[768]{0:T(1024)}, u32[]{:S(2)}) copy-start(f32[768]{0:T(1024)} %copy-done.90) | copy-start | bytes 9220
  744.5 17.0 %copy-start.125 = (f32[512]{0:T(512)S(1)}, f32[512]{0:T(512)}, u32[]{:S(2)}) copy-start(f32[512]{0:T(512)} %copy-done.124) | copy-start | bytes 6148
  751.1 28.3 %all-gather.36.cloned.1.call-start = ((), (), s32[]{:S(2)}) async-start(), calls=%async_computation.34 | async-start | bytes 2359296 | tf_op jit(solution)/shard_map/all_gather | solution.py:224
  768.3 120.6 %reduce-scatter.35.cloned.1.call-start = ((), (), s32[]{:S(2)}) async-start(), calls=%async_computation.35 | async-start | bytes 2359296 | tf_op jit(solution)/shard_map/reduce_scatter | solution.py:228
  878.5 52.5 %all-gather.38.cloned.1.call-start = ((), (), s32[]{:S(2)}) async-start(), calls=%async_computation.36 | async-start | bytes 2359296 | tf_op jit(solution)/shard_map/all_gather | solution.py:224
  880.4 38.3 %copy-start.28 = (bf16[2,1024,768]{2,1,0:T(8,128)(2,1)}, bf16[2,1024,768]{2,1,0:T(8,128)(2,1)S(1)}, u32[]{:S(2)}) copy-start(bf16[2,1024,768]{2,1,0:T(8,128)(2,1)S(1)} %constant_dynamic-update-slice_fusion.3) | copy-start | bytes 9437188
  880.4 31.7 %copy-start.103 = (f32[768]{0:T(1024)S(1)}, f32[768]{0:T(1024)}, u32[]{:S(2)}) copy-start(f32[768]{0:T(1024)} %copy-done.99) | copy-start | bytes 9220
  880.4 31.6 %copy-start.127 = (f32[512]{0:T(512)S(1)}, f32[512]{0:T(512)}, u32[]{:S(2)}) copy-start(f32[512]{0:T(512)} %copy-done.126) | copy-start | bytes 6148
  892.1 20.0 %collective-permute-start.3 = (bf16[512,768]{1,0:T(8,128)(2,1)}, bf16[512,768]{1,0:T(8,128)(2,1)}, u32[]{:S(2)}, u32[]{:S(2)}) collective-permute-start(bf16[512,768]{1,0:T(8,128)(2,1)} %get-tuple-element.2686), channel_id=1, source_target_pairs={{16,0},{17,1},{18,2},{19,3},{20,4},{21,5},{22,6},{23,7},{24,8},{25... | collective-permute-start | bytes 2359304 | tf_op jit(solution)/shard_map/ppermute | solution.py:18
  915.3 15.7 %copy-start.109 = (f32[1,1536]{1,0:T(1,128)S(1)}, f32[1,1536]{1,0:T(1,128)}, u32[]{:S(2)}) copy-start(f32[1,1536]{1,0:T(1,128)} %param.73) | copy-start | bytes 18436
  918.7 52.7 %reduce-scatter.37.cloned.1.call-start = ((), (), s32[]{:S(2)}) async-start(), calls=%async_computation.37 | async-start | bytes 2359296 | tf_op jit(solution)/shard_map/reduce_scatter | solution.py:228
  939.0 32.4 %copy-start.7 = (f32[2,512,768]{2,1,0:T(8,128)S(1)}, f32[2,512,768]{2,1,0:T(8,128)}, u32[]{:S(2)}) copy-start(f32[2,512,768]{2,1,0:T(8,128)} %copy-done.5) | copy-start | bytes 9437188
  939.0 32.4 %copy-start.94 = (f32[768]{0:T(1024)S(1)}, f32[768]{0:T(1024)}, u32[]{:S(2)}) copy-start(f32[768]{0:T(1024)} %copy-done.90) | copy-start | bytes 9220
  939.0 32.4 %copy-start.129 = (f32[512]{0:T(512)S(1)}, f32[512]{0:T(512)}, u32[]{:S(2)}) copy-start(f32[512]{0:T(512)} %copy-done.128) | copy-start | bytes 6148
  940.3 48.7 %all-gather.40.cloned.1.call-start = ((), (), s32[]{:S(2)}) async-start(), calls=%async_computation.38 | async-start | bytes 2359296 | tf_op jit(solution)/shard_map/all_gather | solution.py:224
  977.9 119.8 %reduce-scatter.39.cloned.1.call-start = ((), (), s32[]{:S(2)}) async-start(), calls=%async_computation.39 | async-start | bytes 2359296 | tf_op jit(solution)/shard_map/reduce_scatter | solution.py:228
  1002.4 346.3 %all-reduce.5.cloned.1.call-start = ((), (), s32[]{:S(2)}) async-start(), calls=%async_computation.42 | async-start | bytes 14155776 | tf_op jit(solution)/shard_map/psum | solution.py:474
  1026.4 363.2 %reduce-scatter.27.cloned.1.call-start = ((), (), s32[]{:S(2)}) async-start(), calls=%async_computation.26 | async-start | bytes 3932160 | tf_op jit(solution)/shard_map/reduce_scatter | solution.py:483
  1040.0 390.7 %reduce-scatter.41.cloned.1.call-start = ((), (), s32[]{:S(2)}) async-start(), calls=%async_computation.40 | async-start | bytes 3932160 | tf_op jit(solution)/shard_map/reduce_scatter | solution.py:486
  (147 other events, 708.3 us)
Sparse Core Ops, SparseCore 0:
  9.6 28.6 all-gather.15
  40.8 10.9 all-gather.41
  54.8 64.3 reduce-scatter.14
  126.0 10.9 all-gather.17
  139.8 15.9 reduce-scatter.16
  187.1 10.9 all-gather.19
  260.0 10.2 reduce-scatter.18
  275.0 10.9 all-gather.21
  295.4 10.2 reduce-scatter.20
  341.9 10.9 all-gather.23
  414.4 10.2 reduce-scatter.22
  429.4 10.9 all-gather.25
  450.0 10.2 reduce-scatter.24
  461.8 28.5 all-gather.27
  497.9 11.0 all-gather.29
  539.6 10.2 reduce-scatter.28
  556.8 10.9 all-gather.31
  668.3 10.2 reduce-scatter.30
  708.7 11.8 all-gather.33
  751.2 10.2 reduce-scatter.32
  768.4 10.9 all-gather.35
  878.7 10.2 reduce-scatter.34
  918.8 12.2 all-gather.37
  940.4 30.9 reduce-scatter.36
  978.0 10.9 all-gather.39
  1002.6 95.1 reduce-scatter.38
  1102.6 246.1 all-reduce.4
  1352.0 37.5 reduce-scatter.26
  1392.7 37.9 reduce-scatter.40
where the time goes:
time: 1450 us; the launch traced here: 1440 us
  waiting for transfers between devices  705 us (49%)
  other arithmetic  248 us (17%)
  matrix products  233 us (16%)
  local copies, waits for them, and re-layouts  109 us (8%)
  blocking collectives  81.2 us (6%)
  loops' own time  35.4 us (2%)
  between operations  16.1 us (1%)
    reduce_scatter x12, waiting for transfers between devices, summed_rows(): lax.psum_scatter(lax.cond(live_tick, lambda: term(first_row, share_rows *...  235 us
    psum x1, waiting for transfers between devices, on_device(): lax.psum(acc_in.astype(jnp.bfloat16), 'dp').astype(jnp.float32)  156 us
    all_gather x12, waiting for transfers between devices, all_rows(): return lax.all_gather(row_piece, 'mp', axis=0, tiled=True)  117 us
    ppermute x4, waiting for transfers between devices, from_behind(): return lax.ppermute(array, axis, pairs)  74.5 us
    psum x1, blocking collectives, on_device(): gain_grads, bias_grads = lax.psum((gain_grads, bias_grads), ('mp', 'dp'))  59.3 us
    dot_general x8, matrix products, masked_scores(): jnp.einsum('qhd,khd->hqk', query_tile, key_heads, preferred_element_type=...  45.8 us
    select_n x22, other arithmetic, store_slot(): jnp.where(live_tick, lax.dynamic_update_index_in_dim(buffer, new_value, m...  44.2 us
    reduce_scatter x1, waiting for transfers between devices, on_device(): lax.psum_scatter(grad_rows.astype(jnp.bfloat16), ('section', 'mp'), scatt...  41.1 us
  transfers between devices with their start and end apart: 33, of which 33 were waited for; matrix products, arithmetic and copies ran while one was open for 7% of the time, Pallas kernels for 0%

commit v1 on v0

v1 whole, which is shorter than its diff:
```python
import math

import jax
import jax.numpy as jnp
from jax import lax
from jax.experimental import pallas as pl
from jax.experimental.pallas import tpu as pltpu
from jax.sharding import PartitionSpec as P

EPS = 1e-05
BF=jnp.bfloat16; F32=jnp.float32
NEG=-1e30
TQ=256
WINDOWS=(384,528)
UNROLL_F=3
UNROLL_B=2

def dotf(a,b):
    return lax.dot_general(a,b,(((1,),(0,)),((),())),preferred_element_type=F32)

def key_ext(th1,th2,n,rows):
    u=lax.broadcasted_iota(jnp.int32,(rows,128),0)
    col=lax.broadcasted_iota(jnp.int32,(rows,128),1)
    blk=(u>=th1).astype(jnp.int32)+(u>=th2).astype(jnp.int32)
    open_=(blk==col)&(u<n)
    one=jnp.where(col<8,1.0,0.0)
    return jnp.where(col<3,jnp.where(open_,0.0,NEG),one).astype(BF)

def query_rows(th1,th2,c,shift,r0):
    pos=r0+lax.broadcasted_iota(jnp.int32,(16,TQ),1)
    row=lax.broadcasted_iota(jnp.int32,(16,TQ),0)
    t=(pos>=th1).astype(jnp.int32)+(pos>=th2).astype(jnp.int32)+shift
    t=jnp.where(t>=c,t-c,t)
    return jnp.where(row==t,1.0,0.0), row

def split3(x):
    a=x.astype(BF).astype(F32); b=(x-a).astype(BF).astype(F32); cc=(x-a-b).astype(BF).astype(F32)
    return a,b,cc

def block_start(t,th1,th2):
    return jnp.where(t==0,0,jnp.where(t==1,th1,th2))

def tile_need(th1,th2,n,c,r0):
    last=r0+TQ-1
    whole=((r0<th1)==(last<th1))&((r0<th2)==(last<th2))
    end=jnp.minimum(th2,n)
    need=jnp.maximum(th1,jnp.maximum(end-(th1//16)*16,jnp.where(c==3,n-(th2//16)*16,0)))
    return jnp.where(whole,need,4096)

def head_base(th1,th2,c,shift,r0,limit):
    t=jnp.where(r0>=th1,1,0)+jnp.where(r0>=th2,1,0)+shift
    t=jnp.where(t>=c,t-c,t)
    ks=block_start(t,th1,th2)
    return pl.multiple_of(jnp.minimum((ks//16)*16,limit),16)

def run_window(need,length,body):
    prev=0
    for w in WINDOWS:
        if w>=length: continue
        @pl.when((need>prev)&(need<=w))
        def _(w=w):
            body(w)
        prev=w
    @pl.when(need>prev)
    def _():
        body(length)

def place(scr,pair_n,own_ref,peer_ref,own_off,peer_off,m,ext,half_pairs):
    for i in range(2):
        for who,(ref,off) in enumerate(((own_ref,own_off),(peer_ref,peer_off))):
            blk=2*i+jnp.where(m==who,0,1)
            dst=pl.ds(pl.multiple_of(blk*TQ,TQ),TQ)
            for p in range(pair_n):
                src=p if who==0 else (p+half_pairs)%pair_n
                scr[p,dst,0:128]=ref[i*TQ:(i+1)*TQ,off+src*128:off+(src+1)*128]
    for p in range(pair_n):
        scr[p,:,128:256]=ext

def attn_fwd_kernel(scal,q_ref,kv_ref,kvp_ref,mixed_ref,lse_ref,kb,vs):
    D=q_ref.shape[1]; pairs=D//128; length=kb.shape[1]
    th1=scal[0]; th2=scal[1]; n=scal[2]; c=scal[3]; m=scal[4]
    ext=key_ext(th1,th2,n,length)
    place(kb,pairs,kv_ref,kvp_ref,0,0,m,ext,pairs//2)
    for i in range(2):
        for who,ref in enumerate((kv_ref,kvp_ref)):
            blk=2*i+jnp.where(m==who,0,1)
            dst=pl.ds(pl.multiple_of(blk*TQ,TQ),TQ)
            for p in range(pairs):
                src=p if who==0 else (p+pairs//2)%pairs
                vs[p,dst,:]=ref[i*TQ:(i+1)*TQ,D+src*128:D+(src+1)*128]
    sub=lax.broadcasted_iota(jnp.int32,(128,TQ),0)
    for tile in range(2):
        r0=(2*tile+m)*TQ
        rows=slice(tile*TQ,(tile+1)*TQ)
        def body(w):
            @pl.loop(0,pairs,unroll=UNROLL_F if w<length else 1)
            def _(p):
                lanes=pl.ds(pl.multiple_of(p*128,128),128)
                qt=(q_ref[rows,lanes].astype(F32)*0.125).T
                outs=[]
                for hh in range(2):
                    shift=scal[8+2*p+hh]
                    oneh,_=query_rows(th1,th2,c,shift,r0)
                    qm=jnp.where((sub>=64)==(hh==1),qt,0.0).astype(BF)
                    rhs=jnp.concatenate([qm,oneh.astype(BF),jnp.zeros((112,TQ),BF)],axis=0)
                    win=pl.ds(head_base(th1,th2,c,shift,r0,length-w) if w<length else 0,w)
                    st=dotf(kb[p,win,:],rhs)
                    mx=jnp.max(st,axis=0,keepdims=True)
                    e=jnp.exp(st-mx).astype(BF)
                    vt=vs[p,win,:].T
                    vt=jnp.concatenate([vt[hh*64:(hh+1)*64],jnp.ones((16,w),BF)],axis=0)
                    o=dotf(vt,e)
                    l=o[64:65]
                    outs.append(o[:64]/l)
                    lse_ref[p,hh:hh+1,rows]=mx+jnp.log(l)
                mixed_ref[rows,lanes]=jnp.concatenate(outs,axis=0).T.astype(BF)
        run_window(tile_need(th1,th2,n,c,r0),length,body)

def attn_fwd(scal,q,kv,kvp):
    R,D=q.shape; pairs=D//128; L=2*R
    return pl.pallas_call(attn_fwd_kernel,
        out_shape=(jax.ShapeDtypeStruct((R,D),BF),jax.ShapeDtypeStruct((pairs,2,R),F32)),
        in_specs=[pl.BlockSpec(memory_space=pltpu.SMEM)]+[pl.BlockSpec(memory_space=pltpu.VMEM)]*3,
        out_specs=(pl.BlockSpec(memory_space=pltpu.VMEM),)*2,
        scratch_shapes=[pltpu.VMEM((pairs,L,256),BF),pltpu.VMEM((pairs,L,128),BF)],
        compiler_params=pltpu.CompilerParams(vmem_limit_bytes=48*2**20),
        cost_estimate=pl.CostEstimate(flops=4*R*512*D,bytes_accessed=R*D*10,transcendentals=R*512*12),
        name="attend_forward",
    )(scal,q,kv,kvp)

def attn_bwd_kernel(scal,q_ref,kv_ref,kvp_ref,do_ref,mixed_ref,lse_ref,dq_ref,own_ref,far_ref,kb,vb,dka,dva):
    D=q_ref.shape[1]; pairs=D//128; length=kb.shape[1]
    th1=scal[0]; th2=scal[1]; n=scal[2]; c=scal[3]; m=scal[4]
    ext=key_ext(th1,th2,n,length)
    place(kb,pairs,kv_ref,kvp_ref,0,0,m,ext,pairs//2)
    place(vb,pairs,kv_ref,kvp_ref,D,D,m,ext,pairs//2)
    dka[...]=jnp.zeros_like(dka); dva[...]=jnp.zeros_like(dva)
    sub=lax.broadcasted_iota(jnp.int32,(128,TQ),0)
    lane=lax.broadcasted_iota(jnp.int32,(TQ,128),1)
    for tile in range(2):
        r0=(2*tile+m)*TQ
        rows=slice(tile*TQ,(tile+1)*TQ)
        def body(w):
            @pl.loop(0,pairs,unroll=UNROLL_B if w<length else 1)
            def _(p):
                lanes=pl.ds(pl.multiple_of(p*128,128),128)
                qn=q_ref[rows,lanes].astype(F32)*0.125
                don=do_ref[rows,lanes].astype(F32)
                qt=qn.T; dot_=don.T
                prod=dot_*mixed_ref[rows,lanes].astype(F32).T
                outs=[]
                for hh in range(2):
                    shift=scal[8+2*p+hh]
                    oneh,row=query_rows(th1,th2,c,shift,r0)
                    la,lb,lc=split3(-lse_ref[p,hh:hh+1,rows])
                    oneh=oneh+jnp.where(row==3,la,jnp.where(row==4,lb,jnp.where(row==5,lc,0.0)))
                    keep=(sub>=64)==(hh==1)
                    zeros=jnp.zeros((112,TQ),BF)
                    rhs=jnp.concatenate([jnp.where(keep,qt,0.0).astype(BF),oneh.astype(BF),zeros],axis=0)
                    da,db,dc=split3(-jnp.sum(prod[hh*64:(hh+1)*64],axis=0,keepdims=True))
                    ext2=jnp.where(row==3,da,jnp.where(row==4,db,jnp.where(row==5,dc,0.0)))
                    rhs2=jnp.concatenate([jnp.where(keep,dot_,0.0).astype(BF),ext2.astype(BF),zeros],axis=0)
                    keepl=(lane>=64)==(hh==1)
                    qm=jnp.where(keepl,qn,0.0).astype(BF)
                    dom=jnp.where(keepl,don,0.0).astype(BF)
                    win=pl.ds(head_base(th1,th2,c,shift,r0,length-w) if w<length else 0,w)
                    kwin=kb[p,win,:]
                    pt=jnp.exp(dotf(kwin,rhs))
                    dst=(pt*dotf(vb[p,win,:],rhs2)).astype(BF)
                    dva[p,win,:]+=dotf(pt.astype(BF),dom)
                    dka[p,win,:]+=dotf(dst,qm)
                    kt=kwin[:,0:128].T[hh*64:(hh+1)*64]
                    outs.append(dotf(kt,dst))
                dq_ref[rows,lanes]=(jnp.concatenate(outs,axis=0)*0.125).T.astype(BF)
        run_window(tile_need(th1,th2,n,c,r0),length,body)
    for i in range(2):
        mine=pl.ds(pl.multiple_of((2*i+m)*TQ,TQ),TQ)
        theirs=pl.ds(pl.multiple_of((2*i+1-m)*TQ,TQ),TQ)
        for p in range(pairs):
            src=(p+pairs//2)%pairs
            for j,acc in enumerate((dka,dva)):
                own_ref[i*TQ:(i+1)*TQ,j*D+p*128:j*D+(p+1)*128]=acc[p,mine,:]
                far_ref[i*TQ:(i+1)*TQ,j*D+p*128:j*D+(p+1)*128]=acc[src,theirs,:].astype(BF)

def attn_bwd(scal,q,kv,kvp,do,mixed,lse):
    R,D=q.shape; pairs=D//128; L=2*R
    return pl.pallas_call(attn_bwd_kernel,
        out_shape=(jax.ShapeDtypeStruct((R,D),BF),jax.ShapeDtypeStruct((R,2*D),F32),jax.ShapeDtypeStruct((R,2*D),BF)),
        in_specs=[pl.BlockSpec(memory_space=pltpu.SMEM)]+[pl.BlockSpec(memory_space=pltpu.VMEM)]*6,
        out_specs=(pl.BlockSpec(memory_space=pltpu.VMEM),)*3,
        scratch_shapes=[pltpu.VMEM((pairs,L,256),BF),pltpu.VMEM((pairs,L,256),BF),pltpu.VMEM((pairs,L,128),F32),pltpu.VMEM((pairs,L,128),F32)],
        compiler_params=pltpu.CompilerParams(vmem_limit_bytes=48*2**20),
        cost_estimate=pl.CostEstimate(flops=10*R*512*D,bytes_accessed=R*D*26,transcendentals=R*512*12),
        name="attend_backward",
    )(scal,q,kv,kvp,do,mixed,lse)


SWAP = [(0, 1), (1, 0)]


def to_peer(x):
    return lax.ppermute(x, "mp", SWAP)


def forward_x(x):
    return lax.ppermute(x, "section", [(0, 1)])


def backward_x(x):
    return lax.ppermute(x, "section", [(1, 0)])


def dot_nn(a, b):
    return lax.dot_general(a, b, (((1,), (0,)), ((), ())), preferred_element_type=F32)


def dot_nt(a, b):
    return lax.dot_general(a, b, (((1,), (1,)), ((), ())), preferred_element_type=F32)


def dot_tn(a, b):
    return lax.dot_general(a, b, (((0,), (0,)), ((), ())), preferred_element_type=F32)


def norm_rows(residual):
    row_mean = jnp.mean(residual, axis=-1, keepdims=True)
    centred = residual - row_mean
    inverse = lax.rsqrt(jnp.mean(centred * centred, axis=-1, keepdims=True) + EPS)
    return centred * inverse, inverse


def norm_back(upstream, normed, inverse, gain_row):
    scaled = upstream * gain_row
    return inverse * (
        scaled
        - jnp.mean(scaled, axis=-1, keepdims=True)
        - normed * jnp.mean(scaled * normed, axis=-1, keepdims=True)
    )


def gelu_pair(pre_act):
    normal_cdf = 0.5 * (1.0 + lax.erf(pre_act * 2.0 ** (-0.5)))
    density = jnp.exp(-0.5 * pre_act * pre_act) * (2.0 * math.pi) ** (-0.5)
    return (pre_act * normal_cdf, normal_cdf + pre_act * density)


def swap_halves(x, parts):
    rows, width = x.shape
    y = x.reshape(rows, parts, 2, width // parts // 2)
    return jnp.concatenate([y[:, :, 1:], y[:, :, :1]], axis=2).reshape(rows, width)


def forward_tick(h, scal, w):
    q = (dot_nn(h, w["q"]) + w["bq"]).astype(BF)
    kv = (dot_nn(h, w["kv"]) + w["bkv"]).astype(BF)
    kvp = to_peer(kv)
    mixed, lse = attn_fwd(scal, q, kv, kvp)
    n1, inv1 = norm_rows(h.astype(F32) + dot_nn(mixed, w["out"]) + w["lb"][0])
    x1 = n1 * w["ng"][0] + w["lb"][1]
    x1_low = x1.astype(BF)
    act, slope = gelu_pair(dot_nn(x1_low, w["up"]) + w["bup"])
    act = act.astype(BF)
    slope = slope.astype(BF)
    n2, inv2 = norm_rows(x1 + dot_nn(act, w["down"]) + w["lb"][2])
    out = (n2 * w["ng"][1] + w["lb"][3]).astype(BF)
    return out, (h, q, kv, kvp, mixed, lse, n1, inv1, x1_low, act, slope, n2, inv2)


def backward_tick(g, scal, saved, w):
    h, q, kv, kvp, mixed, lse, n1, inv1, x1_low, act, slope, n2, inv2 = saved
    g = g.astype(F32)
    d2 = norm_back(g, n2, inv2, w["ng"][1])
    d2_low = d2.astype(BF)
    d_pre = (dot_nt(d2_low, w["down"]) * slope.astype(F32)).astype(BF)
    dx1 = d2 + dot_nt(d_pre, w["up"])
    d1 = norm_back(dx1, n1, inv1, w["ng"][0])
    d1_low = d1.astype(BF)
    d_mixed = dot_nt(d1_low, w["out"]).astype(BF)
    dq, own, far = attn_bwd(scal, q, kv, kvp, d_mixed, mixed, lse)
    near = to_peer(far)
    dkv = (own + near.astype(F32)).astype(BF)
    leaving = (d1 + dot_nt(dq, w["q"]) + dot_nt(dkv, w["kv"])).astype(BF)
    sums = jnp.stack(
        [
            jnp.sum(dx1 * n1, axis=0),
            jnp.sum(g * n2, axis=0),
            jnp.sum(d1, axis=0),
            jnp.sum(dx1, axis=0),
            jnp.sum(d2, axis=0),
            jnp.sum(g, axis=0),
        ]
    )
    return leaving, (h, mixed, x1_low, act, d2_low, d_pre, d1_low, dq, dkv), sums


def line_positions(size):
    half = size // 2
    inner = [(p, p + 1) for p in range(half - 1)]
    return half, inner


def reduce_dp(x, size):
    if size < 4 or size % 4:
        return lax.psum(x, "dp")
    rows = x.shape[0] // 2
    line = size // 2
    me = lax.axis_index("dp")
    side = lax.rem(me, 2)
    place = me // 2
    x = x.reshape((2, rows) + x.shape[1:])
    keep = lax.dynamic_index_in_dim(x, side, 0, keepdims=False)
    send = lax.dynamic_index_in_dim(x, 1 - side, 0, keepdims=False)
    add = lambda a, b: (a.astype(F32) + b.astype(F32)).astype(BF)
    total = add(keep, lax.ppermute(send, "dp", [(i, i ^ 1) for i in range(size)]))
    half = line // 2
    both = lambda pairs: [(2 * a + s, 2 * b + s) for a, b in pairs for s in range(2)]
    for k in range(half - 1):
        pairs = [(k, k + 1), (line - 1 - k, line - 2 - k)]
        total = add(total, lax.ppermute(total, "dp", both(pairs)))
    total = add(total, lax.ppermute(total, "dp", both([(half - 1, half), (half, half - 1)])))
    for k in reversed(range(half - 1)):
        pairs = [(k + 1, k), (line - 2 - k, line - 1 - k)]
        got = lax.ppermute(total, "dp", both(pairs))
        total = jnp.where((place == k) | (place == line - 1 - k), got, total)
    other = lax.ppermute(total, "dp", [(i, i ^ 1) for i in range(size)])
    first = jnp.where(side == 0, total, other)
    second = jnp.where(side == 0, other, total)
    return jnp.concatenate([first, second], axis=0).reshape((2 * rows,) + x.shape[2:])


def on_device(
    tokens,
    grad_out,
    attention_in,
    attention_bias,
    attention_out,
    up_weight,
    up_bias,
    down_weight,
    norm_gains,
    layer_biases,
    block_counts,
    lengths,
    head_shifts,
):
    dp_size = lax.axis_size("dp")
    section = lax.axis_index("section")
    core = lax.axis_index("mp")
    first = section == 0
    width = tokens.shape[2]
    half = attention_in.shape[3]
    hidden = up_weight.shape[2]
    rows = tokens.shape[1] * 2
    positions = rows * 2

    win, win_p = attention_in[0], to_peer(attention_in[0])
    shifts = jnp.concatenate([head_shifts[0], to_peer(head_shifts)[0]])
    ab, ab_p = attention_bias[0], to_peer(attention_bias)[0]
    bup = jnp.concatenate([up_bias[0], to_peer(up_bias)[0]])
    bv = jnp.concatenate([ab[1], ab_p[1]])
    w = {
        "q": jnp.concatenate([win[:, 0], win_p[:, 0]], axis=1),
        "kv": jnp.concatenate([win[:, 1], win_p[:, 1], win[:, 2], win_p[:, 2]], axis=1),
        "bq": jnp.concatenate([ab[0], ab_p[0]]),
        "bkv": jnp.concatenate([jnp.zeros_like(bv), bv]),
        "out": jnp.concatenate([attention_out[0], to_peer(attention_out)[0]], axis=0),
        "up": jnp.concatenate([up_weight[0], to_peer(up_weight)[0]], axis=1),
        "bup": bup,
        "down": jnp.concatenate([down_weight[0], to_peer(down_weight)[0]], axis=0),
        "ng": norm_gains[0],
        "lb": layer_biases[0],
    }

    def scalars(slot):
        count = lax.dynamic_index_in_dim(block_counts, slot, 0, keepdims=False)
        length = lax.dynamic_index_in_dim(lengths, slot, 0, keepdims=False)
        th1 = (length + count - 1) // count
        th2 = jnp.where(count == 3, (2 * length + 2) // 3, 1 << 20)
        zero = jnp.zeros_like(th1)
        return jnp.concatenate(
            [jnp.stack([th1, th2, length, count, core, zero, zero, zero]), shifts]
        ).astype(jnp.int32)

    tok = [jnp.concatenate([tokens[s], backward_x(tokens[s])], axis=0) for s in range(2)]
    cot = [jnp.concatenate([forward_x(grad_out[s]), grad_out[s]], axis=0) for s in range(2)]
    quarter = rows // 2

    scal_a = scalars(1 - section)
    scal_b = scalars(section)

    out1, _ = forward_tick(tok[0], scalars(jnp.int32(0)), w)
    in2 = jnp.where(first, tok[1], forward_x(out1))
    out2, saved2 = forward_tick(in2, scal_a, w)
    in4 = jnp.where(first, tok[0], forward_x(out2))
    g3, _, _ = backward_tick(cot[0], scal_a, saved2, w)
    out4, saved4 = forward_tick(in4, scal_b, w)
    g5, part5, sums5 = backward_tick(jnp.where(first, backward_x(g3), cot[1]), scal_b, saved4, w)
    g6, part6, sums6 = backward_tick(jnp.where(first, backward_x(g5), cot[0]), scal_a, saved2, w)

    layer_out = jnp.stack(
        [
            jnp.where(first, backward_x(out2[:quarter]), out2[quarter:]),
            jnp.where(first, backward_x(out4[:quarter]), out4[quarter:]),
        ]
    )
    grad_tokens = jnp.stack(
        [
            jnp.where(first, g5[:quarter], forward_x(g5[quarter:])),
            jnp.where(first, g6[:quarter], forward_x(g6[quarter:])),
        ]
    )

    def both(fn):
        return fn(part5) + fn(part6)

    def paired(fn):
        mine = both(lambda part: fn(part, 0))
        far = both(lambda part: fn(part, 1)).astype(BF)
        return mine, far

    h_, mixed_, x1_, act_, d2_, dpre_, d1_, dq_, dkv_ = range(9)
    cut = lambda x, which, size: lax.slice_in_dim(x, which * size, (which + 1) * size, axis=1)

    def add_peer(mine, far):
        return (mine + to_peer(far).astype(F32)).astype(BF)

    ones = jnp.ones((1, rows), BF)
    col = lambda x: jnp.sum(x.astype(F32), axis=0)
    down_g = add_peer(*paired(lambda p, i: dot_tn(cut(p[act_], i, hidden), p[d2_])))
    up_g = add_peer(*paired(lambda p, i: dot_tn(p[x1_], cut(p[dpre_], i, hidden))))
    out_g = add_peer(*paired(lambda p, i: dot_tn(cut(p[mixed_], i, half), p[d1_])))
    q_g = add_peer(*paired(lambda p, i: dot_tn(p[h_], cut(p[dq_], i, half))))
    k_g = add_peer(*paired(lambda p, i: dot_tn(p[h_], cut(p[dkv_], i, half))))
    v_g = add_peer(*paired(lambda p, i: dot_tn(p[h_], cut(p[dkv_], 2 + i, half))))
    ub = both(lambda p: col(p[dpre_]))
    qb = both(lambda p: col(p[dq_]))
    vb = both(lambda p: col(p[dkv_][:, width:]))
    mine_small = jnp.concatenate([ub[:hidden], qb[:half], vb[:half]])
    far_small = jnp.concatenate([ub[hidden:], qb[half:], vb[half:]])
    sums = (sums5 + sums6).reshape(-1)
    small = jnp.concatenate([mine_small, sums])
    small = small + to_peer(jnp.concatenate([far_small, sums]))
    count = small.shape[0]
    small_rows = -(-count // (width * 32)) * 32
    small = jnp.pad(small, (0, small_rows * width - count)).reshape(small_rows, width).astype(BF)

    down_g = reduce_dp(down_g, dp_size)
    up_g = reduce_dp(up_g, dp_size)
    in_g = reduce_dp(jnp.concatenate([q_g, k_g, v_g], axis=1), dp_size)
    out_g = reduce_dp(jnp.concatenate([out_g, small], axis=0), dp_size)
    small = out_g[half:].reshape(-1)[:count].astype(F32)
    ub, qb, vb = small[:hidden], small[hidden : hidden + half], small[hidden + half : hidden + 2 * half]
    sums = small[hidden + 2 * half :].reshape(6, width)
    return (
        layer_out,
        grad_tokens,
        in_g.reshape(width, 3, half).astype(F32)[None],
        jnp.stack([qb, vb])[None],
        out_g[:half].astype(F32)[None],
        up_g.astype(F32)[None],
        ub[None],
        down_g.astype(F32)[None],
        sums[:2][None],
        sums[2:][None],
    )


def solution(mesh):
    return jax.shard_map(
        on_device,
        mesh=mesh,
        in_specs=(
            P("dp", ("section", "mp"), None),
            P("dp", ("section", "mp"), None),
            P("section", None, None, "mp"),
            P("section", None, "mp"),
            P("section", "mp", None),
            P("section", None, "mp"),
            P("section", "mp"),
            P("section", "mp", None),
            P("section", None, None),
            P("section", None, None),
            P("dp"),
            P("dp"),
            P("section", "mp"),
        ),
        out_specs=(
            P("dp", ("section", "mp"), None),
            P("dp", ("section", "mp"), None),
            P("section", None, None, "mp"),
            P("section", None, "mp"),
            P("section", "mp", None),
            P("section", None, "mp"),
            P("section", "mp"),
            P("section", "mp", None),
            P("section", None, None),
            P("section", None, None),
        ),
        check_vma=False,
    )
```

time: 1450 us -> 669 us (0.46)
  waiting for transfers between devices: 705 us -> 183 us
  other arithmetic: 248 us -> 53.6 us
  Pallas kernels: 0 us -> 109 us
  blocking collectives: 81.2 us -> 0 us
  starting transfers between devices: 10.9 us -> 77.8 us
  matrix products: 233 us -> 167 us
  local copies, waits for them, and re-layouts: 109 us -> 48.4 us
  loops' own time: 35.4 us -> 0 us
    reduce_scatter x14 -> x0, waiting for transfers between devices: 306 us -> none  [the longest x12 235 us: summed_rows(): lax.psum_scatter(lax.cond(live_tick, lambda: term(first_row, share_rows *...]
    all_gather x14 -> x0, waiting for transfers between devices: 166 us -> none  [the longest x12 117 us: all_rows(): return lax.all_gather(row_piece, 'mp', axis=0, tiled=True)]
    psum x1 -> x0, waiting for transfers between devices: 156 us -> none  [on_device(): lax.psum(acc_in.astype(jnp.bfloat16), 'dp').astype(jnp.float32)]
    pallas_call x0 -> x6, Pallas kernels: none -> 109 us  [the longest x3 59.3 us: attn_bwd(): pl.pallas_call(attn_bwd_kernel, out_shape=(jax.ShapeDtypeStruct((R, D), B...]
    ppermute x4 -> x52, waiting for transfers between devices: 74.5 us -> 183 us  [the longest x4 62.6 us: reduce_dp(): other = lax.ppermute(total, 'dp', [(i, i ^ 1) for i in range(size)])]
    psum x2 -> x0, blocking collectives: 81.2 us -> none  [the longest x1 59.3 us: on_device(): gain_grads, bias_grads = lax.psum((gain_grads, bias_grads), ('mp', 'dp'))]
    ppermute x4 -> x52, starting transfers between devices: 8.43 us -> 77.8 us  [the longest x6 23 us: backward_x(): return lax.ppermute(x, 'section', [(1, 0)])]
    dot_general x54 -> x52, matrix products: 233 us -> 167 us  [the longest x14 58.1 us: dot_nt(): lax.dot_general(a, b, (((1,), (1,)), ((), ())), preferred_element_type=F32)]
  transfers between devices with their start and end apart: 33 -> 52, of which waited for: 33 -> 17; matrix products, arithmetic and copies ran while one was open for 7% -> 29% of each run, Pallas kernels for 0% -> 14%
where the time goes in v1:
time: 669 us; the launch traced here: 657 us
  waiting for transfers between devices  183 us (27%)
  matrix products  167 us (25%)
  Pallas kernels  109 us (16%)
  starting transfers between devices  77.8 us (12%)
  other arithmetic  53.6 us (8%)
  local copies, waits for them, and re-layouts  48.4 us (7%)
  between operations  16.9 us (3%)
    ppermute x4, waiting for transfers between devices, reduce_dp(): other = lax.ppermute(total, 'dp', [(i, i ^ 1) for i in range(size)])  62.6 us
    pallas_call x3, Pallas kernels, attn_bwd(): pl.pallas_call(attn_bwd_kernel, out_shape=(jax.ShapeDtypeStruct((R, D), B...  59.3 us
    dot_general x14, matrix products, dot_nt(): lax.dot_general(a, b, (((1,), (1,)), ((), ())), preferred_element_type=F32)  58.1 us
    dot_general x14, matrix products, dot_nn(): lax.dot_general(a, b, (((1,), (0,)), ((), ())), preferred_element_type=F32)  57.2 us
    dot_general x24, matrix products, dot_tn(): lax.dot_general(a, b, (((0,), (0,)), ((), ())), preferred_element_type=F32)  52.1 us
    pallas_call x3, Pallas kernels, attn_fwd(): pl.pallas_call(attn_fwd_kernel, out_shape=(jax.ShapeDtypeStruct((R, D), B...  50 us
    ppermute x4, waiting for transfers between devices, reduce_dp(): total = add(total, lax.ppermute(total, 'dp', both(pairs)))  37.5 us
    ppermute x6, starting transfers between devices, backward_x(): return lax.ppermute(x, 'section', [(1, 0)])  23 us
  transfers between devices with their start and end apart: 52, of which 17 were waited for; matrix products, arithmetic and copies ran while one was open for 29% of the time, Pallas kernels for 14%

profile of v1, /device:TPU:14, one launch (start us, length us, event | category | flops | bytes accessed | tf_op | source)
XLA Modules:
  0.0 656.6 jit_solution(561820382991947325)
XLA Ops:
  3.1 2.6 collective-permute-start.1
  5.7 2.4 slice_bitcast_fusion.3
  10.5 3.8 collective-permute-done.1
  34.4 2.1 add_convert_fusion.22.q_ref
  36.6 16.6 %attend_forward.3 = (bf16[512,768]{1,0:T(8,128)(2,1)S(1)}, f32[6,2,512]{2,1,0:T(2,128)}) custom-call(s32[20]{0:T(128)S(1)} %concatenate.97.scal, bf16[512,768]{1,0:T(8,128)(2,1)S(1)} %add_convert_fusion.22.q_ref, bf16[512,1536]{1,0:T(8,128)(2,1)S(1)} %fusion.12.kv_ref, bf16[512,1536]{1,0:T(8,128)(2,1)S(1)} %collective-permute-done.5.kvp_ref), custom_call_target="tpu_custom_call" | custom-call | flops 805306368 | bytes 3932160 | tf_op jit(solution)/shard_map/attend_forward/pallas_call | solution.py:121
  56.6 10.1 %fusion.155 = (f32[512]{0:T(512)S(1)}, f32[512,768]{1,0:T(8,128)S(1)}) fusion(f32[768]{0:T(1024)S(1)} %copy-done.110, bf16[1536,768]{1,0:T(8,128)(2,1)} %bitcast.21, bf16[1536,768]{1,0:T(8,128)(2,1)} %bitcast.20, f32[3072]{0:T(1024)S(1)} %copy-done.103, f32[768]{0:T(1024)S(1)} %copy-done.101, f32[768]{0:T(1024)S(1)} %get-tuple-element.153, ...), kind=kOutput, calls=%fused_computation.334 | convolution fusion | flops 4869586432 | bytes 13400064 | tf_op jit(solution)/shard_map/dot_general | solution.py:214
  69.2 4.6 collective-permute-start
  73.8 8.7 %collective-permute-done = bf16[256,768]{1,0:T(8,128)(2,1)S(1)} collective-permute-done((bf16[256,768]{1,0:T(8,128)(2,1)S(1)}, bf16[256,768]{1,0:T(8,128)(2,1)S(1)}, u32[]{:S(2)}, u32[]{:S(2)}) %collective-permute-start) | collective-permute-done | bytes 393248 | tf_op jit(solution)/shard_map/ppermute | solution.py:210
  82.5 7.2 %collective-permute-done.10 = bf16[512,768]{1,0:T(8,128)(2,1)S(1)} collective-permute-done((bf16[512,768]{1,0:T(8,128)(2,1)S(1)}, bf16[512,768]{1,0:T(8,128)(2,1)S(1)}, u32[]{:S(2)}, u32[]{:S(2)}) %collective-permute-start.10) | collective-permute-done | bytes 786464 | tf_op jit(solution)/shard_map/ppermute | solution.py:206
  89.9 3.1 fusion.13.kv_ref
  102.5 2.3 add_convert_fusion.20.q_ref
  107.3 15.9 %attend_forward.4 = (bf16[512,768]{1,0:T(8,128)(2,1)S(1)}, f32[6,2,512]{2,1,0:T(2,128)S(1)}) custom-call(s32[20]{0:T(128)S(1)} %concatenate.106.scal, bf16[512,768]{1,0:T(8,128)(2,1)S(1)} %add_convert_fusion.20.q_ref, bf16[512,1536]{1,0:T(8,128)(2,1)S(1)} %fusion.13.kv_ref, bf16[512,1536]{1,0:T(8,128)(2,1)S(1)} %copy-done.2), custom_call_target="tpu_custom_call" | custom-call | flops 805306368 | bytes 3932160 | tf_op jit(solution)/shard_map/attend_forward/pallas_call | solution.py:121
  127.6 8.8 %fusion.6 = (bf16[512,3072]{1,0:T(8,128)(2,1)}, bf16[512,3072]{1,0:T(8,128)(2,1)S(1)}) fusion(f32[3072]{0:T(1024)S(1)} %copy-done.104, bf16[512,768]{1,0:T(8,128)(2,1)S(1)} %get-tuple-element.88, bf16[768,1536]{1,0:T(8,128)(2,1)} %bitcast.19, bf16[768,1536]{1,0:T(8,128)(2,1)} %bitcast.18), kind=kOutput, calls=%fused_computation.10 | convolution fusion | flops 2444230656 | bytes 11808768 | tf_op jit(solution)/shard_map/dot_general | solution.py:214
  136.5 6.3 fusion.158
  143.1 2.8 fusion.45
  147.7 12.1 %fusion.142 = (f32[512]{0:T(512)S(1)}, f32[512]{0:T(512)S(1)}, f32[512,768]{1,0:T(8,128)}) fusion(f32[512,768]{1,0:T(8,128)} %copy-done.36, f32[768]{0:T(1024)S(1)} %get-tuple-element.153, bf16[768,1536]{1,0:T(8,128)(2,1)} %bitcast.19, bf16[768,1536]{1,0:T(8,128)(2,1)} %bitcast.18, bf16[512,3072]{1,0:T(8,128)(2,1)} %get-tuple-element.90, ...), kind=kOutput, calls=%fused_computation.323 | convolution fusion | flops 4866440192 | bytes 18106368 | tf_op jit(solution)/shard_map/dot_general | solution.py:218
  159.8 3.2 convolution_convert_fusion.2.do_ref
  163.0 19.9 %attend_backward.3 = (bf16[512,768]{1,0:T(8,128)(2,1)S(1)}, f32[512,1536]{1,0:T(8,128)}, bf16[512,1536]{1,0:T(8,128)(2,1)}) custom-call(s32[20]{0:T(128)S(1)} %concatenate.106.scal, bf16[512,768]{1,0:T(8,128)(2,1)S(1)} %copy-done.6, bf16[512,1536]{1,0:T(8,128)(2,1)} %copy-done, bf16[512,1536]{1,0:T(8,128)(2,1)} %copy-done.1, ...), custom_call_target="tpu_custom_call" | custom-call | flops 2013265920 | bytes 10223616 | tf_op jit(solution)/shard_map/attend_backward/pallas_call | solution.py:187
  185.4 6.6 %collective-permute-start.12 = (bf16[256,768]{1,0:T(8,128)(2,1)}, bf16[256,768]{1,0:T(8,128)(2,1)}, u32[]{:S(2)}, u32[]{:S(2)}) collective-permute-start(bf16[256,768]{1,0:T(8,128)(2,1)} %slice.326), channel_id=1, source_target_pairs={{16,0},{17,1},{18,2},{19,3},{20,4},{21,5},{22,6},{23,7},{24,8},{25... | collective-permute-start | bytes 1179656 | tf_op jit(solution)/shard_map/ppermute | solution.py:210
  193.5 3.1 fusion.14.kv_ref
  204.5 2.2 fusion.137
  211.2 3.1 add_convert_fusion.16
  214.3 5.5 collective-permute-start.18
  219.7 17.5 %attend_forward.5 = (bf16[512,768]{1,0:T(8,128)(2,1)S(1)}, f32[6,2,512]{2,1,0:T(2,128)S(1)}) custom-call(s32[20]{0:T(128)S(1)} %concatenate.107.scal, bf16[512,768]{1,0:T(8,128)(2,1)S(1)} %add_convert_fusion.18.q_ref, bf16[512,1536]{1,0:T(8,128)(2,1)} %fusion.14.kv_ref, bf16[512,1536]{1,0:T(8,128)(2,1)} %collective-permute-done.14.kvp_ref), custom_call_target="tpu_custom_call" | custom-call | flops 805306368 | bytes 3932160 | tf_op jit(solution)/shard_map/attend_forward/pallas_call | solution.py:121
  239.7 5.7 multiply_convert_fusion.1
  245.5 6.3 fusion.160
  254.8 3.6 fusion.34
  258.4 7.4 %convert_reduce_fusion.1 = (f32[3072]{0:T(1024)S(1)}, bf16[512,3072]{1,0:T(8,128)(2,1)S(1)}) fusion(f32[512,3072]{1,0:T(8,128)S(1)} %get-tuple-element.139, f32[3072]{0:T(1024)S(1)} %copy-done.104, bf16[1536,768]{1,0:T(8,128)(2,1)} %bitcast.21, bf16[1536,768]{1,0:T(8,128)(2,1)} %bitcast.20, f32[512,768]{1,0:T(8,128)S(1)} %get-tuple-element.83), kind=kOutput, calls=%fused_computation.17 | convolution fusion | flops 2449339392 | bytes 15753216 | tf_op jit(solution)/shard_map/dot_general | solution.py:218
  266.7 2.2 collective-permute-start.15
  269.0 6.2 multiply_reduce_fusion.1
  275.7 2.6 convolution_convert_fusion.1.do_ref
  278.4 20.0 %attend_backward.4 = (bf16[512,768]{1,0:T(8,128)(2,1)S(1)}, f32[512,1536]{1,0:T(8,128)}, bf16[512,1536]{1,0:T(8,128)(2,1)}) custom-call(s32[20]{0:T(128)S(1)} %concatenate.107.scal, bf16[512,768]{1,0:T(8,128)(2,1)S(1)} %add_convert_fusion.18.q_ref, bf16[512,1536]{1,0:T(8,128)(2,1)} %fusion.14.kv_ref, bf16[512,1536]{1,0:T(8,128)(2,1)} %collective-permute-done.14.kvp_ref, ...), custom_call_target="tpu_custom_call" | custom-call | flops 2013265920 | bytes 10223616 | tf_op jit(solution)/shard_map/attend_backward/pallas_call | solution.py:187
  300.7 5.2 fusion.37
  305.9 3.9 fusion.43
  309.7 3.9 fusion.40
  313.7 2.1 add_convert_fusion.5
  322.7 10.5 %collective-permute-done.21 = bf16[256,768]{1,0:T(8,128)(2,1)S(1)} collective-permute-done((bf16[256,768]{1,0:T(8,128)(2,1)S(1)}, bf16[256,768]{1,0:T(8,128)(2,1)S(1)}, u32[]{:S(2)}, u32[]{:S(2)}) %collective-permute-start.21) | collective-permute-done | bytes 393248 | tf_op jit(solution)/shard_map/ppermute | solution.py:206
  334.0 3.5 collective-permute-done.22
  342.0 5.2 convert_reduce_fusion
  347.2 6.6 %multiply_reduce_fusion = (f32[768]{0:T(1024)S(1)}, f32[512]{0:T(512)S(1)}, f32[512]{0:T(512)S(1)}, f32[768]{0:T(1024)S(1)}, f32[512,768]{1,0:T(8,128)S(1)}) fusion(f32[512,768]{1,0:T(8,128)S(1)} %copy-done.38, f32[768]{0:T(1024)S(1)} %get-tuple-element.153, f32[512,768]{1,0:T(8,128)S(1)} %get-tuple-element.79, ...), kind=kOutput, calls=%fused_computation.89 | convolution fusion | flops 2428499456 | bytes 12596224 | tf_op jit(solution)/shard_map/dot_general | solution.py:218
  354.2 2.6 convolution_convert_fusion.do_ref
  356.9 19.4 %attend_backward.5 = (bf16[512,768]{1,0:T(8,128)(2,1)S(1)}, f32[512,1536]{1,0:T(8,128)}, bf16[512,1536]{1,0:T(8,128)(2,1)S(1)}) custom-call(s32[20]{0:T(128)S(1)} %concatenate.106.scal, bf16[512,768]{1,0:T(8,128)(2,1)S(1)} %copy-done.7, bf16[512,1536]{1,0:T(8,128)(2,1)} %copy-done, bf16[512,1536]{1,0:T(8,128)(2,1)} %copy-done.1, ...), custom_call_target="tpu_custom_call" | custom-call | flops 2013265920 | bytes 10223616 | tf_op jit(solution)/shard_map/attend_backward/pallas_call | solution.py:187
  381.3 2.2 fusion.53
  385.1 5.8 add_convert_fusion.3
  391.4 2.8 add_convert_fusion.1
  414.9 6.3 collective-permute-done.35
  428.8 5.6 collective-permute-done.36
  435.5 4.9 collective-permute-start.37
  440.4 5.1 add_convert_fusion.2
  449.3 3.3 add_convert_fusion
  459.8 48.1 %collective-permute-done.39 = bf16[208,768]{1,0:T(8,128)(2,1)S(1)} collective-permute-done((bf16[208,768]{1,0:T(8,128)(2,1)S(1)}, bf16[208,768]{1,0:T(8,128)(2,1)S(1)}, u32[]{:S(2)}, u32[]{:S(2)}) %collective-permute-start.39) | collective-permute-done | bytes 319520 | tf_op jit(solution)/shard_map/ppermute | solution.py:325
  517.7 4.9 collective-permute-start.30
  522.6 17.8 %collective-permute-done.42 = bf16[384,1536]{1,0:T(8,128)(2,1)} collective-permute-done((bf16[384,1536]{1,0:T(8,128)(2,1)S(1)}, bf16[384,1536]{1,0:T(8,128)(2,1)}, u32[]{:S(2)}, u32[]{:S(2)}) %collective-permute-start.42) | collective-permute-done | bytes 1179680 | tf_op jit(solution)/shard_map/ppermute | solution.py:319
  541.9 4.8 collective-permute-start.43
  550.1 14.1 %collective-permute-done.48 = bf16[768,768]{1,0:T(8,128)(2,1)S(1)} collective-permute-done((bf16[768,768]{1,0:T(8,128)(2,1)S(1)}, bf16[768,768]{1,0:T(8,128)(2,1)S(1)}, u32[]{:S(2)}, u32[]{:S(2)}) %collective-permute-start.48) | collective-permute-done | bytes 1179680 | tf_op jit(solution)/shard_map/ppermute | solution.py:319
  564.5 4.7 collective-permute-start.49
  569.3 2.5 collective-permute-done.43
  576.2 19.4 %collective-permute-done.49 = bf16[768,768]{1,0:T(8,128)(2,1)S(1)} collective-permute-done((bf16[768,768]{1,0:T(8,128)(2,1)S(1)}, bf16[768,768]{1,0:T(8,128)(2,1)S(1)}, u32[]{:S(2)}, u32[]{:S(2)}) %collective-permute-start.49) | collective-permute-done | bytes 1179680 | tf_op jit(solution)/shard_map/ppermute | solution.py:320
  601.6 20.0 %collective-permute-done.50 = bf16[768,768]{1,0:T(8,128)(2,1)S(1)} collective-permute-done((bf16[768,768]{1,0:T(8,128)(2,1)S(1)}, bf16[768,768]{1,0:T(8,128)(2,1)S(1)}, u32[]{:S(2)}, u32[]{:S(2)}) %collective-permute-start.50) | collective-permute-done | bytes 1179680 | tf_op jit(solution)/shard_map/ppermute | solution.py:323
  626.5 3.3 copy.37
  629.8 2.9 copy.38
  634.5 2.8 maximum_convert_fusion
  637.4 14.4 %collective-permute-done.51 = bf16[768,768]{1,0:T(8,128)(2,1)} collective-permute-done((bf16[768,768]{1,0:T(8,128)(2,1)}, bf16[768,768]{1,0:T(8,128)(2,1)}, u32[]{:S(2)}, u32[]{:S(2)}) %collective-permute-start.51) | collective-permute-done | bytes 1179680 | tf_op jit(solution)/shard_map/ppermute | solution.py:325
  653.6 2.5 maximum_convert_fusion.1
  (487 shorter events, 153.5 us)
Async XLA Ops:
  0.6 8.8 %collective-permute-start.3 = (bf16[768,3,384]{2,0,1:T(8,128)(2,1)}, bf16[768,3,384]{2,0,1:T(8,128)(2,1)S(1)}, u32[]{:S(2)}, u32[]{:S(2)}) collective-permute-start(bf16[768,3,384]{2,0,1:T(8,128)(2,1)} %bitcast.142), channel_id=1, source_target_pairs={{0,8},{8,0},{1,9},{9,1},{2,10},{10,2},{3,11},{11,3},{4,12},{12,4},... | collective-permute-start | bytes 5308424 | tf_op jit(solution)/shard_map/ppermute | solution.py:202
  0.7 8.1 %collective-permute-start.4 = (f32[1,2,384]{2,1,0:T(2,128)}, f32[1,2,384]{2,1,0:T(2,128)S(1)}, u32[]{:S(2)}, u32[]{:S(2)}) collective-permute-start(f32[1,2,384]{2,1,0:T(2,128)} %param.16), channel_id=1, source_target_pairs={{0,8},{8,0},{1,9},{9,1},{2,10},{10,2},{3,11},{11,3},{4,12},{12,4},... | collective-permute-start | bytes 9224 | tf_op jit(solution)/shard_map/ppermute | solution.py:202
  3.1 53.3 %copy-start.43 = (bf16[256,768]{1,0:T(8,128)(2,1)}, bf16[256,768]{1,0:T(8,128)(2,1)S(1)}, u32[]{:S(2)}) copy-start(bf16[256,768]{1,0:T(8,128)(2,1)S(1)} %get-tuple-element.109) | copy-start | bytes 1179652
  3.1 11.2 %collective-permute-start.1 = (bf16[256,768]{1,0:T(8,128)(2,1)S(1)}, bf16[256,768]{1,0:T(8,128)(2,1)S(1)}, u32[]{:S(2)}, u32[]{:S(2)}) collective-permute-start(bf16[256,768]{1,0:T(8,128)(2,1)S(1)} %get-tuple-element.109), channel_id=1, source_target_pairs={{16,0},{17,1},{18,2},{19,3},{20,4},{21,5},{22,6},{23,7},{24,8},{25... | collective-permute-start | bytes 1179656 | tf_op jit(solution)/shard_map/ppermute | solution.py:210
  17.2 19.4 %collective-permute-start.5 = (bf16[512,1536]{1,0:T(8,128)(2,1)S(1)}, bf16[512,1536]{1,0:T(8,128)(2,1)S(1)}, u32[]{:S(2)}, u32[]{:S(2)}) collective-permute-start(bf16[512,1536]{1,0:T(8,128)(2,1)S(1)} %fusion.12.kv_ref), channel_id=1, source_target_pairs={{0,8},{8,0},{1,9},{9,1},{2,10},{10,2},{3,11},{11,3},{4,12},{12,4},... | collective-permute-start | bytes 4718600 | tf_op jit(solution)/shard_map/ppermute | solution.py:202
  17.3 38.5 %collective-permute-start.7 = (bf16[1,768,1536]{2,1,0:T(8,128)(2,1)}, bf16[1,768,1536]{2,1,0:T(8,128)(2,1)}, u32[]{:S(2)}, u32[]{:S(2)}) collective-permute-start(bf16[1,768,1536]{2,1,0:T(8,128)(2,1)} %param.18), channel_id=1, source_target_pairs={{0,8},{8,0},{1,9},{9,1},{2,10},{10,2},{3,11},{11,3},{4,12},{12,4},... | collective-permute-start | bytes 7077896 | tf_op jit(solution)/shard_map/ppermute | solution.py:202
  17.8 38.0 %collective-permute-start.9 = (bf16[1,1536,768]{2,1,0:T(8,128)(2,1)}, bf16[1,1536,768]{2,1,0:T(8,128)(2,1)}, u32[]{:S(2)}, u32[]{:S(2)}) collective-permute-start(bf16[1,1536,768]{2,1,0:T(8,128)(2,1)} %param.20), channel_id=1, source_target_pairs={{0,8},{8,0},{1,9},{9,1},{2,10},{10,2},{3,11},{11,3},{4,12},{12,4},... | collective-permute-start | bytes 7077896 | tf_op jit(solution)/shard_map/ppermute | solution.py:202
  17.8 9.9 %collective-permute-start.2 = (s32[1,6]{1,0:T(1,128)}, s32[1,6]{1,0:T(1,128)}, u32[]{:S(2)}, u32[]{:S(2)}) collective-permute-start(s32[1,6]{1,0:T(1,128)} %param.25), channel_id=1, source_target_pairs={{0,8},{8,0},{1,9},{9,1},{2,10},{10,2},{3,11},{11,3},{4,12},{12,4},... | collective-permute-start | bytes 80 | tf_op jit(solution)/shard_map/ppermute | solution.py:202
  18.3 34.9 %collective-permute-start.6 = (bf16[1,384,768]{2,1,0:T(8,128)(2,1)}, bf16[1,384,768]{2,1,0:T(8,128)(2,1)}, u32[]{:S(2)}, u32[]{:S(2)}) collective-permute-start(bf16[1,384,768]{2,1,0:T(8,128)(2,1)} %param.17), channel_id=1, source_target_pairs={{0,8},{8,0},{1,9},{9,1},{2,10},{10,2},{3,11},{11,3},{4,12},{12,4},... | collective-permute-start | bytes 1769480 | tf_op jit(solution)/shard_map/ppermute | solution.py:202
  27.8 4.0 collective-permute-start.8
  67.7 22.2 %copy-start.71 = (bf16[768,384]{1,0:T(8,128)(2,1)S(1)}, bf16[768,384]{1,0:T(8,128)(2,1)}, u32[]{:S(2)}) copy-start(bf16[768,384]{1,0:T(8,128)(2,1)} %copy-done.70) | copy-start | bytes 1769476
  67.7 22.2 %copy-start.106 = (f32[1536]{0:T(1024)S(1)}, f32[1536]{0:T(1024)}, u32[]{:S(2)}) copy-start(f32[1536]{0:T(1024)} %copy-done.105) | copy-start | bytes 18436
  67.7 22.0 %collective-permute-start.10 = (bf16[512,768]{1,0:T(8,128)(2,1)S(1)}, bf16[512,768]{1,0:T(8,128)(2,1)S(1)}, u32[]{:S(2)}, u32[]{:S(2)}) collective-permute-start(bf16[512,768]{1,0:T(8,128)(2,1)S(1)} %add_convert_fusion.21), channel_id=1, source_target_pairs={{0,16},{1,17},{2,18},{3,19},{4,20},{5,21},{6,22},{7,23},{8,24},{9,... | collective-permute-start | bytes 2359304 | tf_op jit(solution)/shard_map/ppermute | solution.py:206
  69.2 13.3 %collective-permute-start = (bf16[256,768]{1,0:T(8,128)(2,1)S(1)}, bf16[256,768]{1,0:T(8,128)(2,1)S(1)}, u32[]{:S(2)}, u32[]{:S(2)}) collective-permute-start(bf16[256,768]{1,0:T(8,128)(2,1)S(1)} %copy-done.61), channel_id=1, source_target_pairs={{16,0},{17,1},{18,2},{19,3},{20,4},{21,5},{22,6},{23,7},{24,8},{25... | collective-permute-start | bytes 1179656 | tf_op jit(solution)/shard_map/ppermute | solution.py:210
  93.1 11.6 %collective-permute-start.11 = (bf16[512,1536]{1,0:T(8,128)(2,1)S(1)}, bf16[512,1536]{1,0:T(8,128)(2,1)S(1)}, u32[]{:S(2)}, u32[]{:S(2)}) collective-permute-start(bf16[512,1536]{1,0:T(8,128)(2,1)S(1)} %fusion.13.kv_ref), channel_id=1, source_target_pairs={{0,8},{8,0},{1,9},{9,1},{2,10},{10,2},{3,11},{11,3},{4,12},{12,4},... | collective-permute-start | bytes 4718600 | tf_op jit(solution)/shard_map/ppermute | solution.py:202
  94.3 48.8 %collective-permute-start.16 = (bf16[256,768]{1,0:T(8,128)(2,1)}, bf16[256,768]{1,0:T(8,128)(2,1)}, u32[]{:S(2)}, u32[]{:S(2)}) collective-permute-start(bf16[256,768]{1,0:T(8,128)(2,1)} %get-tuple-element.107), channel_id=1, source_target_pairs={{0,16},{1,17},{2,18},{3,19},{4,20},{5,21},{6,22},{7,23},{8,24},{9,... | collective-permute-start | bytes 1179656 | tf_op jit(solution)/shard_map/ppermute | solution.py:206
  146.0 46.1 %collective-permute-start.13 = (bf16[512,768]{1,0:T(8,128)(2,1)}, bf16[512,768]{1,0:T(8,128)(2,1)}, u32[]{:S(2)}, u32[]{:S(2)}) collective-permute-start(bf16[512,768]{1,0:T(8,128)(2,1)} %get-tuple-element.105), channel_id=1, source_target_pairs={{0,16},{1,17},{2,18},{3,19},{4,20},{5,21},{6,22},{7,23},{8,24},{9,... | collective-permute-start | bytes 2359304 | tf_op jit(solution)/shard_map/ppermute | solution.py:206
  163.0 29.0 %copy-start.44 = (bf16[256,768]{1,0:T(8,128)(2,1)S(1)}, bf16[256,768]{1,0:T(8,128)(2,1)}, u32[]{:S(2)}) copy-start(bf16[256,768]{1,0:T(8,128)(2,1)} %copy-done.43) | copy-start | bytes 1179652
  163.0 29.0 %copy-start.58 = (bf16[256,768]{1,0:T(8,128)(2,1)S(1)}, bf16[256,768]{1,0:T(8,128)(2,1)}, u32[]{:S(2)}) copy-start(bf16[256,768]{1,0:T(8,128)(2,1)} %copy-done.55) | copy-start | bytes 1179652
  183.0 26.5 %collective-permute-start.17 = (bf16[512,1536]{1,0:T(8,128)(2,1)}, bf16[512,1536]{1,0:T(8,128)(2,1)}, u32[]{:S(2)}, u32[]{:S(2)}) collective-permute-start(bf16[512,1536]{1,0:T(8,128)(2,1)} %get-tuple-element.30), channel_id=1, source_target_pairs={{0,8},{8,0},{1,9},{9,1},{2,10},{10,2},{3,11},{11,3},{4,12},{12,4},... | collective-permute-start | bytes 4718600 | tf_op jit(solution)/shard_map/ppermute | solution.py:202
  185.4 21.4 %collective-permute-start.12 = (bf16[256,768]{1,0:T(8,128)(2,1)}, bf16[256,768]{1,0:T(8,128)(2,1)}, u32[]{:S(2)}, u32[]{:S(2)}) collective-permute-start(bf16[256,768]{1,0:T(8,128)(2,1)} %slice.326), channel_id=1, source_target_pairs={{16,0},{17,1},{18,2},{19,3},{20,4},{21,5},{22,6},{23,7},{24,8},{25... | collective-permute-start | bytes 1179656 | tf_op jit(solution)/shard_map/ppermute | solution.py:210
  193.4 43.9 %copy-start.12 = (bf16[512,768]{1,0:T(8,128)(2,1)}, bf16[512,768]{1,0:T(8,128)(2,1)S(1)}, u32[]{:S(2)}) copy-start(bf16[512,768]{1,0:T(8,128)(2,1)S(1)} %broadcast_select_fusion.6) | copy-start | bytes 2359300
  196.5 23.2 %collective-permute-start.14 = (bf16[512,1536]{1,0:T(8,128)(2,1)}, bf16[512,1536]{1,0:T(8,128)(2,1)}, u32[]{:S(2)}, u32[]{:S(2)}) collective-permute-start(bf16[512,1536]{1,0:T(8,128)(2,1)} %fusion.14.kv_ref), channel_id=1, source_target_pairs={{0,8},{8,0},{1,9},{9,1},{2,10},{10,2},{3,11},{11,3},{4,12},{12,4},... | collective-permute-start | bytes 4718600 | tf_op jit(solution)/shard_map/ppermute | solution.py:202
  196.7 55.4 %collective-permute-start.19 = (bf16[256,768]{1,0:T(8,128)(2,1)S(1)}, bf16[256,768]{1,0:T(8,128)(2,1)}, u32[]{:S(2)}, u32[]{:S(2)}) collective-permute-start(bf16[256,768]{1,0:T(8,128)(2,1)S(1)} %copy-done.60), channel_id=1, source_target_pairs={{0,16},{1,17},{2,18},{3,19},{4,20},{5,21},{6,22},{7,23},{8,24},{9,... | collective-permute-start | bytes 1179656 | tf_op jit(solution)/shard_map/ppermute | solution.py:206
  214.3 37.9 %collective-permute-start.18 = (bf16[512,768]{1,0:T(8,128)(2,1)S(1)}, bf16[512,768]{1,0:T(8,128)(2,1)S(1)}, u32[]{:S(2)}, u32[]{:S(2)}) collective-permute-start(bf16[512,768]{1,0:T(8,128)(2,1)S(1)} %add_convert_fusion.16), channel_id=1, source_target_pairs={{16,0},{17,1},{18,2},{19,3},{20,4},{21,5},{22,6},{23,7},{24,8},{25... | collective-permute-start | bytes 2359304 | tf_op jit(solution)/shard_map/ppermute | solution.py:210
  239.4 35.8 %copy-start.39 = (f32[512,768]{1,0:T(8,128)}, f32[512,768]{1,0:T(8,128)S(1)}, u32[]{:S(2)}) copy-start(f32[512,768]{1,0:T(8,128)S(1)} %get-tuple-element.137) | copy-start | bytes 4718596
  266.7 54.8 %collective-permute-start.15 = (bf16[256,768]{1,0:T(8,128)(2,1)}, bf16[256,768]{1,0:T(8,128)(2,1)}, u32[]{:S(2)}, u32[]{:S(2)}) collective-permute-start(bf16[256,768]{1,0:T(8,128)(2,1)} %slice.328), channel_id=1, source_target_pairs={{16,0},{17,1},{18,2},{19,3},{20,4},{21,5},{22,6},{23,7},{24,8},{25... | collective-permute-start | bytes 1179656 | tf_op jit(solution)/shard_map/ppermute | solution.py:210
  298.4 15.2 %collective-permute-start.20 = (bf16[512,1536]{1,0:T(8,128)(2,1)}, bf16[512,1536]{1,0:T(8,128)(2,1)}, u32[]{:S(2)}, u32[]{:S(2)}) collective-permute-start(bf16[512,1536]{1,0:T(8,128)(2,1)} %get-tuple-element.34), channel_id=1, source_target_pairs={{0,8},{8,0},{1,9},{9,1},{2,10},{10,2},{3,11},{11,3},{4,12},{12,4},... | collective-permute-start | bytes 4718600 | tf_op jit(solution)/shard_map/ppermute | solution.py:202
  318.3 19.2 %collective-permute-start.22 = (bf16[512,768]{1,0:T(8,128)(2,1)S(1)}, bf16[512,768]{1,0:T(8,128)(2,1)S(1)}, u32[]{:S(2)}, u32[]{:S(2)}) collective-permute-start(bf16[512,768]{1,0:T(8,128)(2,1)S(1)} %add_convert_fusion.15), channel_id=1, source_target_pairs={{16,0},{17,1},{18,2},{19,3},{20,4},{21,5},{22,6},{23,7},{24,8},{25... | collective-permute-start | bytes 2359304 | tf_op jit(solution)/shard_map/ppermute | solution.py:210
  319.7 13.4 %collective-permute-start.21 = (bf16[256,768]{1,0:T(8,128)(2,1)S(1)}, bf16[256,768]{1,0:T(8,128)(2,1)S(1)}, u32[]{:S(2)}, u32[]{:S(2)}) collective-permute-start(bf16[256,768]{1,0:T(8,128)(2,1)S(1)} %slice.331), channel_id=1, source_target_pairs={{0,16},{1,17},{2,18},{3,19},{4,20},{5,21},{6,22},{7,23},{8,24},{9,... | collective-permute-start | bytes 1179656 | tf_op jit(solution)/shard_map/ppermute | solution.py:206
  354.2 25.4 %copy-start.19 = (f32[512,768]{1,0:T(8,128)}, f32[512,768]{1,0:T(8,128)S(1)}, u32[]{:S(2)}) copy-start(f32[512,768]{1,0:T(8,128)S(1)} %get-tuple-element.81) | copy-start | bytes 4718596
  381.3 24.6 %copy-start.98 = (f32[4608]{0:T(1024)}, f32[4608]{0:T(1024)S(1)}, u32[]{:S(2)}) copy-start(f32[4608]{0:T(1024)S(1)} %add.523) | copy-start | bytes 55300
  383.5 12.8 %collective-permute-start.25 = (bf16[768,384]{0,1:T(8,128)(2,1)S(1)}, bf16[768,384]{0,1:T(8,128)(2,1)S(1)}, u32[]{:S(2)}, u32[]{:S(2)}) collective-permute-start(bf16[768,384]{0,1:T(8,128)(2,1)S(1)} %fusion.53), channel_id=1, source_target_pairs={{0,8},{8,0},{1,9},{9,1},{2,10},{10,2},{3,11},{11,3},{4,12},{12,4},... | collective-permute-start | bytes 1769480 | tf_op jit(solution)/shard_map/ppermute | solution.py:202
  384.1 14.3 %collective-permute-start.33 = (bf16[384,768]{1,0:T(8,128)(2,1)S(1)}, bf16[384,768]{1,0:T(8,128)(2,1)S(1)}, u32[]{:S(2)}, u32[]{:S(2)}) collective-permute-start(bf16[384,768]{1,0:T(8,128)(2,1)S(1)} %fusion.59), channel_id=1, source_target_pairs={{0,8},{8,0},{1,9},{9,1},{2,10},{10,2},{3,11},{11,3},{4,12},{12,4},... | collective-permute-start | bytes 1769480 | tf_op jit(solution)/shard_map/ppermute | solution.py:202
  384.9 14.8 %collective-permute-start.23 = (bf16[512,1536]{1,0:T(8,128)(2,1)S(1)}, bf16[512,1536]{1,0:T(8,128)(2,1)S(1)}, u32[]{:S(2)}, u32[]{:S(2)}) collective-permute-start(bf16[512,1536]{1,0:T(8,128)(2,1)S(1)} %copy-done.4), channel_id=1, source_target_pairs={{0,8},{8,0},{1,9},{9,1},{2,10},{10,2},{3,11},{11,3},{4,12},{12,4},... | collective-permute-start | bytes 4718600 | tf_op jit(solution)/shard_map/ppermute | solution.py:202
  390.9 49.5 %collective-permute-start.40 = (bf16[768,1536]{1,0:T(8,128)(2,1)}, bf16[768,1536]{1,0:T(8,128)(2,1)}, u32[]{:S(2)}, u32[]{:S(2)}) collective-permute-start(bf16[768,1536]{1,0:T(8,128)(2,1)} %add_convert_fusion.3), channel_id=1, source_target_pairs={{0,8},{8,0},{1,9},{9,1},{2,10},{10,2},{3,11},{11,3},{4,12},{12,4},... | collective-permute-start | bytes 7077896 | tf_op jit(solution)/shard_map/ppermute | solution.py:202
  394.3 54.9 %collective-permute-start.46 = (bf16[1536,768]{1,0:T(8,128)(2,1)}, bf16[1536,768]{1,0:T(8,128)(2,1)}, u32[]{:S(2)}, u32[]{:S(2)}) collective-permute-start(bf16[1536,768]{1,0:T(8,128)(2,1)} %add_convert_fusion.1), channel_id=1, source_target_pairs={{0,8},{8,0},{1,9},{9,1},{2,10},{10,2},{3,11},{11,3},{4,12},{12,4},... | collective-permute-start | bytes 7077896 | tf_op jit(solution)/shard_map/ppermute | solution.py:202
  405.8 5.6 collective-permute-start.34
  406.8 15.3 %collective-permute-start.24 = (bf16[256,768]{1,0:T(8,128)(2,1)}, bf16[256,768]{1,0:T(8,128)(2,1)}, u32[]{:S(2)}, u32[]{:S(2)}) collective-permute-start(bf16[256,768]{1,0:T(8,128)(2,1)} %slice.333), channel_id=1, source_target_pairs={{0,16},{1,17},{2,18},{3,19},{4,20},{5,21},{6,22},{7,23},{8,24},{9,... | collective-permute-start | bytes 1179656 | tf_op jit(solution)/shard_map/ppermute | solution.py:206
  409.6 15.9 %collective-permute-start.27 = (bf16[768,384]{0,1:T(8,128)(2,1)}, bf16[768,384]{0,1:T(8,128)(2,1)S(1)}, u32[]{:S(2)}, u32[]{:S(2)}) collective-permute-start(bf16[768,384]{0,1:T(8,128)(2,1)} %fusion.57), channel_id=1, source_target_pairs={{0,8},{8,0},{1,9},{9,1},{2,10},{10,2},{3,11},{11,3},{4,12},{12,4},... | collective-permute-start | bytes 1769480 | tf_op jit(solution)/shard_map/ppermute | solution.py:202
  411.7 9.6 %collective-permute-start.35 = (bf16[208,768]{1,0:T(8,128)(2,1)S(1)}, bf16[208,768]{1,0:T(8,128)(2,1)S(1)}, u32[]{:S(2)}, u32[]{:S(2)}) collective-permute-start(bf16[208,768]{1,0:T(8,128)(2,1)S(1)} %dynamic-slice_bitcast_fusion.3), channel_id=1, source_target_pairs={{0,1},{1,0},{2,3},{3,2},{4,5},{5,4},{6,7},{7,6},{8,9},{9,8},{10,11... | collective-permute-start | bytes 958472 | tf_op jit(solution)/shard_map/ppermute | solution.py:314
  421.3 4.8 collective-permute-start.26
  422.1 12.3 %collective-permute-start.36 = (bf16[208,768]{1,0:T(8,128)(2,1)}, bf16[208,768]{1,0:T(8,128)(2,1)}, u32[]{:S(2)}, u32[]{:S(2)}) collective-permute-start(bf16[208,768]{1,0:T(8,128)(2,1)} %fusion.82), channel_id=1, source_target_pairs={{0,2},{1,3},{6,4},{7,5},{8,10},{9,11},{14,12},{15,13},{16,18},{17,... | collective-permute-start | bytes 958472 | tf_op jit(solution)/shard_map/ppermute | solution.py:319
  428.3 20.9 %slice-start = ((s8[4718592]{0:T(1024)(128)(4,1)}), s8[4194304]{0:T(1024)(128)(4,1)S(1)}, s32[]{:S(2)}) async-start(s8[4718592]{0:T(1024)(128)(4,1)} %bitcast.129), calls=%async_computation | async-start | bytes 8388608
  428.4 29.0 %collective-permute-start.28 = (bf16[384,1152]{1,0:T(8,128)(2,1)S(1)}, bf16[384,1152]{1,0:T(8,128)(2,1)S(1)}, u32[]{:S(2)}, u32[]{:S(2)}) collective-permute-start(bf16[384,1152]{1,0:T(8,128)(2,1)S(1)} %dynamic-slice_bitcast_fusion.2), channel_id=1, source_target_pairs={{0,1},{1,0},{2,3},{3,2},{4,5},{5,4},{6,7},{7,6},{8,9},{9,8},{10,11... | collective-permute-start | bytes 2654216 | tf_op jit(solution)/shard_map/ppermute | solution.py:314
  435.5 12.3 %collective-permute-start.37 = (bf16[208,768]{1,0:T(8,128)(2,1)S(1)}, bf16[208,768]{1,0:T(8,128)(2,1)S(1)}, u32[]{:S(2)}, u32[]{:S(2)}) collective-permute-start(bf16[208,768]{1,0:T(8,128)(2,1)S(1)} %add_convert_fusion.24), channel_id=1, source_target_pairs={{2,4},{3,5},{4,2},{5,3},{10,12},{11,13},{12,10},{13,11},{18,20},{1... | collective-permute-start | bytes 958472 | tf_op jit(solution)/shard_map/ppermute | solution.py:320
  445.7 63.1 %collective-permute-start.41 = (bf16[384,1536]{1,0:T(8,128)(2,1)S(1)}, bf16[384,1536]{1,0:T(8,128)(2,1)S(1)}, u32[]{:S(2)}, u32[]{:S(2)}) collective-permute-start(bf16[384,1536]{1,0:T(8,128)(2,1)S(1)} %dynamic-slice_bitcast_fusion.1), channel_id=1, source_target_pairs={{0,1},{1,0},{2,3},{3,2},{4,5},{5,4},{6,7},{7,6},{8,9},{9,8},{10,11... | collective-permute-start | bytes 3538952 | tf_op jit(solution)/shard_map/ppermute | solution.py:314
  447.9 7.7 %collective-permute-start.38 = (bf16[208,768]{1,0:T(8,128)(2,1)S(1)}, bf16[208,768]{1,0:T(8,128)(2,1)S(1)}, u32[]{:S(2)}, u32[]{:S(2)}) collective-permute-start(bf16[208,768]{1,0:T(8,128)(2,1)S(1)} %add_convert_fusion.23), channel_id=1, source_target_pairs={{2,0},{3,1},{4,6},{5,7},{10,8},{11,9},{12,14},{13,15},{18,16},{19,... | collective-permute-start | bytes 958472 | tf_op jit(solution)/shard_map/ppermute | solution.py:323
  453.7 59.5 %collective-permute-start.47 = (bf16[768,768]{1,0:T(8,128)(2,1)}, bf16[768,768]{1,0:T(8,128)(2,1)}, u32[]{:S(2)}, u32[]{:S(2)}) collective-permute-start(bf16[768,768]{1,0:T(8,128)(2,1)} %dynamic-slice_bitcast_fusion), channel_id=1, source_target_pairs={{0,1},{1,0},{2,3},{3,2},{4,5},{5,4},{6,7},{7,6},{8,9},{9,8},{10,11... | collective-permute-start | bytes 3538952 | tf_op jit(solution)/shard_map/ppermute | solution.py:314
  455.6 52.4 %collective-permute-start.39 = (bf16[208,768]{1,0:T(8,128)(2,1)S(1)}, bf16[208,768]{1,0:T(8,128)(2,1)S(1)}, u32[]{:S(2)}, u32[]{:S(2)}) collective-permute-start(bf16[208,768]{1,0:T(8,128)(2,1)S(1)} %broadcast_select_fusion.7), channel_id=1, source_target_pairs={{0,1},{1,0},{2,3},{3,2},{4,5},{5,4},{6,7},{7,6},{8,9},{9,8},{10,11... | collective-permute-start | bytes 958472 | tf_op jit(solution)/shard_map/ppermute | solution.py:325
  458.5 57.5 %collective-permute-start.29 = (bf16[384,1152]{1,0:T(8,128)(2,1)}, bf16[384,1152]{1,0:T(8,128)(2,1)}, u32[]{:S(2)}, u32[]{:S(2)}) collective-permute-start(bf16[384,1152]{1,0:T(8,128)(2,1)} %fusion.23), channel_id=1, source_target_pairs={{0,2},{1,3},{6,4},{7,5},{8,10},{9,11},{14,12},{15,13},{16,18},{17,... | collective-permute-start | bytes 2654216 | tf_op jit(solution)/shard_map/ppermute | solution.py:319
  509.1 31.3 %collective-permute-start.42 = (bf16[384,1536]{1,0:T(8,128)(2,1)S(1)}, bf16[384,1536]{1,0:T(8,128)(2,1)}, u32[]{:S(2)}, u32[]{:S(2)}) collective-permute-start(bf16[384,1536]{1,0:T(8,128)(2,1)S(1)} %fusion.16), channel_id=1, source_target_pairs={{0,2},{1,3},{6,4},{7,5},{8,10},{9,11},{14,12},{15,13},{16,18},{17,... | collective-permute-start | bytes 3538952 | tf_op jit(solution)/shard_map/ppermute | solution.py:319
  514.7 49.5 %collective-permute-start.48 = (bf16[768,768]{1,0:T(8,128)(2,1)S(1)}, bf16[768,768]{1,0:T(8,128)(2,1)S(1)}, u32[]{:S(2)}, u32[]{:S(2)}) collective-permute-start(bf16[768,768]{1,0:T(8,128)(2,1)S(1)} %fusion.15), channel_id=1, source_target_pairs={{0,2},{1,3},{6,4},{7,5},{8,10},{9,11},{14,12},{15,13},{16,18},{17,... | collective-permute-start | bytes 3538952 | tf_op jit(solution)/shard_map/ppermute | solution.py:319
  517.7 29.1 %copy-start.65 = (bf16[208,768]{1,0:T(8,128)(2,1)S(1)}, bf16[208,768]{1,0:T(8,128)(2,1)}, u32[]{:S(2)}) copy-start(bf16[208,768]{1,0:T(8,128)(2,1)} %copy-done.64) | copy-start | bytes 958468
  517.7 29.1 %copy-start.66 = (bf16[208,768]{1,0:T(8,128)(2,1)S(1)}, bf16[208,768]{1,0:T(8,128)(2,1)}, u32[]{:S(2)}) copy-start(bf16[208,768]{1,0:T(8,128)(2,1)} %get-tuple-element.110) | copy-start | bytes 958468
  517.7 30.8 %collective-permute-start.30 = (bf16[384,1152]{1,0:T(8,128)(2,1)S(1)}, bf16[384,1152]{1,0:T(8,128)(2,1)S(1)}, u32[]{:S(2)}, u32[]{:S(2)}) collective-permute-start(bf16[384,1152]{1,0:T(8,128)(2,1)S(1)} %add_convert_fusion.12), channel_id=1, source_target_pairs={{2,4},{3,5},{4,2},{5,3},{10,12},{11,13},{12,10},{13,11},{18,20},{1... | collective-permute-start | bytes 2654216 | tf_op jit(solution)/shard_map/ppermute | solution.py:320
  541.9 29.9 %collective-permute-start.43 = (bf16[384,1536]{1,0:T(8,128)(2,1)S(1)}, bf16[384,1536]{1,0:T(8,128)(2,1)S(1)}, u32[]{:S(2)}, u32[]{:S(2)}) collective-permute-start(bf16[384,1536]{1,0:T(8,128)(2,1)S(1)} %add_convert_fusion.10), channel_id=1, source_target_pairs={{2,4},{3,5},{4,2},{5,3},{10,12},{11,13},{12,10},{13,11},{18,20},{1... | collective-permute-start | bytes 3538952 | tf_op jit(solution)/shard_map/ppermute | solution.py:320
  548.7 25.6 %collective-permute-start.31 = (bf16[384,1152]{1,0:T(8,128)(2,1)S(1)}, bf16[384,1152]{1,0:T(8,128)(2,1)S(1)}, u32[]{:S(2)}, u32[]{:S(2)}) collective-permute-start(bf16[384,1152]{1,0:T(8,128)(2,1)S(1)} %add_convert_fusion.11), channel_id=1, source_target_pairs={{2,0},{3,1},{4,6},{5,7},{10,8},{11,9},{12,14},{13,15},{18,16},{19,... | collective-permute-start | bytes 2654216 | tf_op jit(solution)/shard_map/ppermute | solution.py:323
  564.5 31.1 %collective-permute-start.49 = (bf16[768,768]{1,0:T(8,128)(2,1)S(1)}, bf16[768,768]{1,0:T(8,128)(2,1)S(1)}, u32[]{:S(2)}, u32[]{:S(2)}) collective-permute-start(bf16[768,768]{1,0:T(8,128)(2,1)S(1)} %add_convert_fusion.8), channel_id=1, source_target_pairs={{2,4},{3,5},{4,2},{5,3},{10,12},{11,13},{12,10},{13,11},{18,20},{1... | collective-permute-start | bytes 3538952 | tf_op jit(solution)/shard_map/ppermute | solution.py:320
  572.1 26.4 %collective-permute-start.44 = (bf16[384,1536]{1,0:T(8,128)(2,1)S(1)}, bf16[384,1536]{1,0:T(8,128)(2,1)S(1)}, u32[]{:S(2)}, u32[]{:S(2)}) collective-permute-start(bf16[384,1536]{1,0:T(8,128)(2,1)S(1)} %add_convert_fusion.9), channel_id=1, source_target_pairs={{2,0},{3,1},{4,6},{5,7},{10,8},{11,9},{12,14},{13,15},{18,16},{19,... | collective-permute-start | bytes 3538952 | tf_op jit(solution)/shard_map/ppermute | solution.py:323
  574.4 27.0 %collective-permute-start.32 = (bf16[384,1152]{1,0:T(8,128)(2,1)S(1)}, bf16[384,1152]{1,0:T(8,128)(2,1)S(1)}, u32[]{:S(2)}, u32[]{:S(2)}) collective-permute-start(bf16[384,1152]{1,0:T(8,128)(2,1)S(1)} %broadcast_select_fusion.2), channel_id=1, source_target_pairs={{0,1},{1,0},{2,3},{3,2},{4,5},{5,4},{6,7},{7,6},{8,9},{9,8},{10,11... | collective-permute-start | bytes 2654216 | tf_op jit(solution)/shard_map/ppermute | solution.py:325
  596.0 25.6 %collective-permute-start.50 = (bf16[768,768]{1,0:T(8,128)(2,1)S(1)}, bf16[768,768]{1,0:T(8,128)(2,1)S(1)}, u32[]{:S(2)}, u32[]{:S(2)}) collective-permute-start(bf16[768,768]{1,0:T(8,128)(2,1)S(1)} %add_convert_fusion.7), channel_id=1, source_target_pairs={{2,0},{3,1},{4,6},{5,7},{10,8},{11,9},{12,14},{13,15},{18,16},{19,... | collective-permute-start | bytes 3538952 | tf_op jit(solution)/shard_map/ppermute | solution.py:323
  599.7 33.1 %collective-permute-start.45 = (bf16[384,1536]{1,0:T(8,128)(2,1)}, bf16[384,1536]{1,0:T(8,128)(2,1)}, u32[]{:S(2)}, u32[]{:S(2)}) collective-permute-start(bf16[384,1536]{1,0:T(8,128)(2,1)} %broadcast_select_fusion.1), channel_id=1, source_target_pairs={{0,1},{1,0},{2,3},{3,2},{4,5},{5,4},{6,7},{7,6},{8,9},{9,8},{10,11... | collective-permute-start | bytes 3538952 | tf_op jit(solution)/shard_map/ppermute | solution.py:325
  622.8 29.1 %collective-permute-start.51 = (bf16[768,768]{1,0:T(8,128)(2,1)}, bf16[768,768]{1,0:T(8,128)(2,1)}, u32[]{:S(2)}, u32[]{:S(2)}) collective-permute-start(bf16[768,768]{1,0:T(8,128)(2,1)} %broadcast_select_fusion), channel_id=1, source_target_pairs={{0,1},{1,0},{2,3},{3,2},{4,5},{5,4},{6,7},{7,6},{8,9},{9,8},{10,11... | collective-permute-start | bytes 3538952 | tf_op jit(solution)/shard_map/ppermute | solution.py:325
  (110 other events, 572.8 us)

commit v2 on v1

v2 whole, which is shorter than its diff:
```python
import functools
import math
from typing import Any, NamedTuple

import jax
import jax.numpy as jnp
from jax import lax
from jax.experimental import pallas as pl
from jax.experimental.pallas import tpu as pltpu
from jax.sharding import PartitionSpec as P

BF = jnp.bfloat16
F32 = jnp.float32
EPS = 1e-05
SHUT = -1e30
TILE = 256
FORWARD_WINDOWS = (512, 528)
BACKWARD_WINDOWS = (528,)
CHUNK = 512
BLOCK = 64
VMEM_BYTES = 58 * 2**20
NO_COST = pl.CostEstimate(flops=1, bytes_accessed=1, transcendentals=0)


def dot_nn(a, b):
    return lax.dot_general(a, b, (((1,), (0,)), ((), ())), preferred_element_type=F32)


def dot_nt(a, b):
    return lax.dot_general(a, b, (((1,), (1,)), ((), ())), preferred_element_type=F32)


def dot_tn(a, b):
    return lax.dot_general(a, b, (((0,), (0,)), ((), ())), preferred_element_type=F32)


def mask_numbers(slot, counts, lengths):
    c = counts[slot]
    n = lengths[slot]
    third = (n + 2) // 3
    th1 = jnp.where(c == 3, third, (n + 1) // 2)
    th2 = jnp.where(c == 3, (2 * n + 2) // 3, 1 << 20)
    return th1, th2, n, c, lax.axis_index("mp")


def key_columns(nums, rows):
    th1, th2, n = nums[:3]
    u = lax.broadcasted_iota(jnp.int32, (rows, 128), 0)
    col = lax.broadcasted_iota(jnp.int32, (rows, 128), 1)
    blk = (u >= th1).astype(jnp.int32) + (u >= th2).astype(jnp.int32)
    open_ = (blk == col) & (u < n)
    one = jnp.where(col < 8, 1.0, 0.0)
    return jnp.where(col < 3, jnp.where(open_, 0.0, SHUT), one).astype(BF)


def query_rows(nums, shift, r0):
    th1, th2, _, c, _ = nums
    pos = r0 + lax.broadcasted_iota(jnp.int32, (16, TILE), 1)
    row = lax.broadcasted_iota(jnp.int32, (16, TILE), 0)
    t = (pos >= th1).astype(jnp.int32) + (pos >= th2).astype(jnp.int32) + shift
    t = jnp.where(t >= c, t - c, t)
    return jnp.where(row == t, 1.0, 0.0), row


def split3(x):
    a = x.astype(BF).astype(F32)
    b = (x - a).astype(BF).astype(F32)
    return a, b, (x - a - b).astype(BF).astype(F32)


def window_need(nums, r0):
    th1, th2, n, c, _ = nums
    last = r0 + TILE - 1
    whole = ((r0 < th1) == (last < th1)) & ((r0 < th2) == (last < th2))
    need = jnp.maximum(th1, jnp.minimum(th2, n) - (th1 // 16) * 16)
    need = jnp.maximum(need, jnp.where(c == 3, n - (th2 // 16) * 16, 0))
    return jnp.where(whole, need, 1 << 20)


def window_base(nums, shift, r0, limit):
    th1, th2, _, c, _ = nums
    t = jnp.where(r0 >= th1, 1, 0) + jnp.where(r0 >= th2, 1, 0) + shift
    t = jnp.where(t >= c, t - c, t)
    start = jnp.where(t == 0, 0, jnp.where(t == 1, th1, th2))
    return pl.multiple_of(jnp.minimum((start // 16) * 16, limit), 16)


def by_window(need, length, windows, body):
    prev = 0
    for width in windows:
        if width < length:

            @pl.when((need > prev) & (need <= width))
            def _(width=width):
                body(width)

            prev = width

    @pl.when(need > prev)
    def _():
        body(length)


def place_rows(dst, lanes, own, far, offset, core):
    pairs = dst.shape[0]
    for i in range(2):
        for who, ref in enumerate((own, far)):
            blk = 2 * i + jnp.where(core == who, 0, 1)
            rows = pl.ds(pl.multiple_of(blk * TILE, TILE), TILE)
            for p in range(pairs):
                src = offset + (p if who == 0 else (p + pairs // 2) % pairs) * 128
                dst[p, rows, lanes] = ref[i * TILE : (i + 1) * TILE, src : src + 128]


def place_values(v0, v1, own, far, offset, core):
    pairs = v0.shape[0]
    lane = lax.broadcasted_iota(jnp.int32, (TILE, 128), 1)
    ones = jnp.ones((TILE, 128), BF)
    for i in range(2):
        for who, ref in enumerate((own, far)):
            blk = 2 * i + jnp.where(core == who, 0, 1)
            rows = pl.ds(pl.multiple_of(blk * TILE, TILE), TILE)
            for p in range(pairs):
                src = offset + (p if who == 0 else (p + pairs // 2) % pairs) * 128
                x = ref[i * TILE : (i + 1) * TILE, src : src + 128]
                v0[p, rows, :] = jnp.where(lane < 64, x, ones)
                v1[p, rows, :] = jnp.where(lane < 64, ones, x)


def head_shift(own, far, j):
    heads = own.shape[1]
    if isinstance(j, int):
        return own[0, j] if j < heads else far[0, j - heads]
    return jnp.where(j < heads, own[0, jnp.minimum(j, heads - 1)], far[0, jnp.maximum(j - heads, 0)])


def attend(nums, shifts, q, kb, v0, v1, score, weight, top, mixed, lse):
    pairs, length = kb.shape[:2]
    th1, th2, _, c, core = nums
    heads = 2 * pairs
    lane = lax.broadcasted_iota(jnp.int32, (TILE, 128), 1)
    sub = lax.broadcasted_iota(jnp.int32, (TILE, 128), 0)

    @pl.loop(0, 2)
    def _(tile):
        r0 = (2 * tile + core) * TILE
        rows = pl.ds(pl.multiple_of(tile * TILE, TILE), TILE)
        behind = ((r0 + sub) >= th1).astype(jnp.int32) + ((r0 + sub) >= th2).astype(jnp.int32) - lane

        def body(width):
            outs = [None] * heads

            def window(j):
                shift = head_shift(*shifts, j)
                return pl.ds(window_base(nums, shift, r0, length - width) if width < length else 0, width)

            def scores(j):
                p, hh = divmod(j, 2)
                qn = q[rows, p * 128 : (p + 1) * 128].astype(F32) * 0.125
                d = behind + head_shift(*shifts, j)
                target = jnp.where((lane < c) & ((d == 0) | (d == c)), 1.0, 0.0)
                qm = jnp.where((lane >= 64) == (hh == 1), qn, 0.0)
                lhs = jnp.concatenate([qm.astype(BF), target.astype(BF)], axis=1)
                score[j % 2, :, 0:width] = dot_nt(lhs, kb[p, window(j), :])

            def softmax(j):
                for r in range(0, TILE, 128):
                    part = score[j % 2, r : r + 128, 0:width]
                    largest = jnp.max(part, axis=1, keepdims=True)
                    top[j % 4, r : r + 128, :] = jnp.broadcast_to(largest, (128, 128))
                    weight[j % 2, r : r + 128, 0:width] = jnp.exp(part - largest).astype(BF)

            def product(j):
                p, hh = divmod(j, 2)
                outs[j] = dot_nn(weight[j % 2, :, 0:width], (v0, v1)[hh][p, window(j), :])
                if hh == 1:
                    total = jnp.where(lane < 64, pltpu.roll(outs[j - 1], 64, 1), pltpu.roll(outs[j], 64, 1))
                    value = jnp.where(lane < 64, outs[j - 1], outs[j])
                    mixed[rows, p * 128 : (p + 1) * 128] = (value / total).astype(BF)
                    if lse is not None:
                        both = (jnp.where(lane < 64, top[(j - 1) % 4], top[j % 4]) + jnp.log(total)).T
                        lse[p, 0:1, rows] = both[0:1]
                        lse[p, 1:2, rows] = both[64:65]

            for step in range(heads + 2):
                if step < heads:
                    scores(step)
                if 1 <= step <= heads:
                    softmax(step - 1)
                if step >= 2:
                    product(step - 2)

        by_window(window_need(nums, r0), length, FORWARD_WINDOWS, body)


def attend_back(nums, shifts, q, do, mixed, lse, kb, vb, dka, dva, dq):
    pairs, length = kb.shape[:2]
    core = nums[4]
    sub = lax.broadcasted_iota(jnp.int32, (128, TILE), 0)
    lane = lax.broadcasted_iota(jnp.int32, (TILE, 128), 1)
    for tile in range(2):
        r0 = (2 * tile + core) * TILE
        rows = slice(tile * TILE, (tile + 1) * TILE)

        def body(width):
            @pl.loop(0, pairs, unroll=2 if width < length else 1)
            def _(p):
                lanes = pl.ds(pl.multiple_of(p * 128, 128), 128)
                qn = q[rows, lanes].astype(F32) * 0.125
                don = do[rows, lanes].astype(F32)
                qt = qn.T
                dot_ = don.T
                prod = dot_ * mixed[rows, lanes].astype(F32).T
                outs = []
                for hh in range(2):
                    shift = head_shift(*shifts, 2 * p + hh)
                    target, row = query_rows(nums, shift, r0)
                    la, lb, lc = split3(-lse[p, hh : hh + 1, rows])
                    target = target + jnp.where(row == 3, la, jnp.where(row == 4, lb, jnp.where(row == 5, lc, 0.0)))
                    keep = (sub >= 64) == (hh == 1)
                    zeros = jnp.zeros((112, TILE), BF)
                    rhs = jnp.concatenate([jnp.where(keep, qt, 0.0).astype(BF), target.astype(BF), zeros], axis=0)
                    da, db, dc = split3(-jnp.sum(prod[hh * 64 : (hh + 1) * 64], axis=0, keepdims=True))
                    minus = jnp.where(row == 3, da, jnp.where(row == 4, db, jnp.where(row == 5, dc, 0.0)))
                    rhs2 = jnp.concatenate([jnp.where(keep, dot_, 0.0).astype(BF), minus.astype(BF), zeros], axis=0)
                    keepl = (lane >= 64) == (hh == 1)
                    qm = jnp.where(keepl, qn, 0.0).astype(BF)
                    dom = jnp.where(keepl, don, 0.0).astype(BF)
                    start = window_base(nums, shift, r0, length - width) if width < length else 0
                    win = pl.ds(start, width)
                    kwin = kb[p, win, :]
                    pt = jnp.exp(dot_nn(kwin, rhs))
                    ds = (pt * dot_nn(vb[p, win, :], rhs2)).astype(BF)
                    dva[p, win, :] += dot_nn(pt.astype(BF), dom)
                    dka[p, win, :] += dot_nn(ds, qm)
                    kt = kwin[:, 0:128].T[hh * 64 : (hh + 1) * 64]
                    outs.append(dot_nn(kt, ds))
                dq[rows, lanes] = (jnp.concatenate(outs, axis=0) * 0.125).T.astype(BF)

        by_window(window_need(nums, r0), length, BACKWARD_WINDOWS, body)


def gelu_pair(x):
    density = jnp.exp(x * x * (-0.5)) * (2.0 * math.pi) ** (-0.5)
    cdf = 0.5 + 0.5 * lax.erf(x * (2.0 ** (-0.5)))
    return x * cdf, cdf + x * density


def norm_rows(x):
    scale = 1.0 / x.shape[-1]
    centred = x - jnp.sum(x, axis=-1, keepdims=True) * scale
    inv = lax.rsqrt(jnp.sum(centred * centred, axis=-1, keepdims=True) * scale + EPS)
    return centred * inv, inv


def norm_back(up, normed, inv, gain):
    scale = 1.0 / normed.shape[-1]
    e = up * gain
    a = jnp.sum(e, axis=-1, keepdims=True) * scale
    b = jnp.sum(e * normed, axis=-1, keepdims=True) * scale
    return inv * (e - a - normed * b)


def copier(sems):
    used = [0]

    def start(src, dst):
        copy = pltpu.make_async_copy(src, dst, sems.at[used[0]])
        used[0] += 1
        copy.start()
        return copy

    return start


class ForwardIn(NamedTuple):
    q: Any
    kv: Any
    kvp: Any
    h: Any
    wout: Any
    wup: Any
    wdown: Any
    wout_far: Any
    wup_far: Any
    wdown_far: Any


class ForwardOut(NamedTuple):
    out: Any
    mixed: Any
    lse: Any
    x1_low: Any
    act: Any
    slope: Any
    n1: Any
    inv1: Any
    n2: Any
    inv2: Any


class ForwardWork(NamedTuple):
    kb: Any
    v0: Any
    v1: Any
    score: Any
    weight: Any
    top: Any
    pre: Any
    x1: Any
    acc: Any


def weight_copies(start, src, x):
    c_out, c_up, c_down = [], [], []
    for j, (out, up, down) in enumerate(((src.wout, src.wup, src.wdown), (src.wout_far, src.wup_far, src.wdown_far))):
        rows, cols = out.shape[0], up.shape[1]
        c_out.append(start(out, x.wout.at[j * rows : (j + 1) * rows, :]))
        c_up.append(start(up, x.wup.at[:, j * cols : (j + 1) * cols]))
        c_down.append(start(down, x.wdown.at[j * cols : (j + 1) * cols, :]))
    return c_out, c_up, c_down


def forward_kernel(save, slot_of, tokens, counts, lengths, shift_own, shift_far, lb, ng, bup_own, bup_far, *refs):
    refs = list(refs[tokens:])
    take = lambda kind: kind(*[refs.pop(0) for _ in range(len(kind._fields))])
    src = take(ForwardIn)
    dst = take(ForwardOut) if save else ForwardOut(refs.pop(0), *[None] * 9)
    x = ForwardIn(*[refs.pop(0) for _ in range(7)], None, None, None)
    y = take(ForwardOut)
    t = take(ForwardWork)
    start = copier(refs[0])
    rows, width = x.h.shape
    hidden = x.wup.shape[1]
    half = hidden // 2
    load = ForwardIn(*[None] * 10)._replace(
        kv=start(src.kv, x.kv),
        kvp=start(src.kvp, x.kvp),
        q=start(src.q, x.q),
        h=start(src.h, x.h),
    )
    c_out, c_up, c_down = weight_copies(start, src, x)
    done = []

    def ship(a, b):
        if b is not None:
            done.append(start(a, b))

    def ship_part(a, b, part):
        if b is not None:
            done.append(start(a.at[:, part], b.at[:, part]))

    nums = mask_numbers(slot_of(lax.axis_index("section")), counts, lengths)
    core = nums[4]
    ext = key_columns(nums, t.kb.shape[1])
    for p in range(t.kb.shape[0]):
        t.kb[p, :, 128:256] = ext
    load.kv.wait()
    load.kvp.wait()
    place_rows(t.kb, slice(0, 128), x.kv, x.kvp, 0, core)
    place_values(t.v0, t.v1, x.kv, x.kvp, width, core)
    load.q.wait()
    attend(
        nums, (shift_own, shift_far), x.q, t.kb, t.v0, t.v1, t.score, t.weight, t.top, y.mixed, y.lse if save else None
    )
    ship(y.mixed, dst.mixed)
    ship(y.lse, dst.lse)
    for copy in c_out:
        copy.wait()
    t.acc[...] = dot_nn(y.mixed[...], x.wout[...])
    load.h.wait()
    for r in range(0, rows, BLOCK):
        rs = slice(r, r + BLOCK)
        normed, inv = norm_rows(x.h[rs, :].astype(F32) + t.acc[rs, :] + lb[0:1, :])
        if save:
            y.n1[rs, :] = normed
            y.inv1[rs, :] = jnp.broadcast_to(inv, (BLOCK, 128))
        full = normed * ng[0:1, :] + lb[1:2, :]
        t.x1[rs, :] = full
        y.x1_low[rs, :] = full.astype(BF)
    ship(y.x1_low, dst.x1_low)
    ship(y.n1, dst.n1)
    ship(y.inv1, dst.inv1)
    chunks = hidden // CHUNK

    def up(j):
        t.pre[j % 2] = dot_nn(y.x1_low[...], x.wup[:, j * CHUNK : (j + 1) * CHUNK])

    def activate(j):
        part = slice(j * CHUNK, (j + 1) * CHUNK)
        low = (j * CHUNK) % half
        bias = (bup_own if j < chunks // 2 else bup_far)[0:1, low : low + CHUNK]
        for r in range(0, rows, BLOCK):
            rs = slice(r, r + BLOCK)
            act, slope = gelu_pair(t.pre[j % 2, rs, :] + bias)
            y.act[rs, part] = act.astype(BF)
            if save:
                y.slope[rs, part] = slope.astype(BF)

    c_up[0].wait()
    up(0)
    for j in range(chunks // 2):
        if j + 1 == chunks // 2:
            c_up[1].wait()
        up(j + 1)
        activate(j)
    ship_part(y.act, dst.act, slice(0, half))
    ship_part(y.slope, dst.slope, slice(0, half))
    c_down[0].wait()
    t.acc[...] = dot_nn(y.act[:, :half], x.wdown[:half, :])
    for j in range(chunks // 2, chunks):
        if j + 1 < chunks:
            up(j + 1)
        activate(j)
    ship_part(y.act, dst.act, slice(half, hidden))
    ship_part(y.slope, dst.slope, slice(half, hidden))
    c_down[1].wait()
    t.acc[...] += dot_nn(y.act[:, half:], x.wdown[half:, :])
    for r in range(0, rows, BLOCK):
        rs = slice(r, r + BLOCK)
        normed, inv = norm_rows(t.x1[rs, :] + t.acc[rs, :] + lb[2:3, :])
        if save:
            y.n2[rs, :] = normed
            y.inv2[rs, :] = jnp.broadcast_to(inv, (BLOCK, 128))
        y.out[rs, :] = (normed * ng[1:2, :] + lb[3:4, :]).astype(BF)
    ship(y.out, dst.out)
    ship(y.n2, dst.n2)
    ship(y.inv2, dst.inv2)
    for copy in done:
        copy.wait()


def buffers(shapes):
    return [pltpu.VMEM(*s) for s in shapes]


def results(shapes):
    return tuple(jax.ShapeDtypeStruct(*s) for s in shapes)


IN_SMEM = pl.BlockSpec(memory_space=pltpu.SMEM)
IN_VMEM = pl.BlockSpec(memory_space=pltpu.VMEM)
IN_HBM = pl.BlockSpec(memory_space=pltpu.HBM)


def forward_call(save, slot_of, w, q, kv, kvp, h, tokens=()):
    rows, width = h.shape
    hidden = 2 * w.up.shape[1]
    pairs, length = width // 128, 2 * rows
    low, wide, full = ((rows, width), BF), ((rows, hidden), BF), ((rows, width), F32)
    one, twice = ((rows, 128), F32), ((rows, 2 * width), BF)
    shapes_in = (low, twice, twice, low, ((width, width), BF), ((width, hidden), BF), ((hidden, width), BF))
    shapes_out = ForwardOut(low, low, ((pairs, 2, rows), F32), low, wide, wide, full, one, full, one)
    if not save:
        gone = ((16, 128), BF)
        scratch_out = shapes_out._replace(lse=gone, slope=gone, n1=gone, inv1=gone, n2=gone, inv2=gone)
    else:
        scratch_out = shapes_out
    work = ForwardWork(
        ((pairs, length, 256), BF),
        ((pairs, length, 128), BF),
        ((pairs, length, 128), BF),
        ((2, TILE, length), F32),
        ((2, TILE, length), BF),
        ((4, TILE, 128), F32),
        ((2, rows, CHUNK), F32),
        full,
        full,
    )
    outs = shapes_out if save else shapes_out[:1]
    res = pl.pallas_call(
        functools.partial(forward_kernel, save, slot_of, len(tokens)),
        out_shape=results(outs),
        in_specs=[IN_SMEM] * 4 + [IN_VMEM] * 4 + [IN_HBM] * (10 + len(tokens)),
        out_specs=(IN_HBM,) * len(outs),
        scratch_shapes=buffers(shapes_in) + buffers(scratch_out) + buffers(work) + [pltpu.SemaphoreType.DMA((24,))],
        compiler_params=pltpu.CompilerParams(vmem_limit_bytes=VMEM_BYTES),
        cost_estimate=NO_COST,
        name="layer_forward",
    )(
        w.counts, w.lengths, w.shift_own, w.shift_far, w.lb, w.ng, w.bup_own, w.bup_far, *tokens,
        q, kv, kvp, h, w.out, w.up, w.down, w.out_far, w.up_far, w.down_far,
    )
    return ForwardOut(*res) if save else ForwardOut(res[0], *[None] * 9)


class RowsIn(NamedTuple):
    g: Any
    n2: Any
    inv2: Any
    n1: Any
    inv1: Any
    slope: Any
    wout: Any
    wup: Any
    wdown: Any
    wout_far: Any
    wup_far: Any
    wdown_far: Any


class RowsOut(NamedTuple):
    d2_low: Any
    d_pre: Any
    d1: Any
    d1_low: Any


class HeadsIn(NamedTuple):
    mixed: Any
    lse: Any
    q: Any
    kv: Any
    kvp: Any


class HeadsOut(NamedTuple):
    dq: Any
    near: Any
    far: Any


class HeadsWork(NamedTuple):
    kb: Any
    vb: Any
    dka: Any
    dva: Any


def rows_back(start, src, dst, x, y, d_mixed, dx, ng, sums, bias_sums, behind):
    rows, width = x.g.shape
    hidden = x.wup.shape[1]
    half = hidden // 2
    chunks = hidden // CHUNK
    early = [start(src.g, x.g), start(src.n2, x.n2), start(src.inv2, x.inv2)]
    c_slope = [
        start(src.slope.at[:, part], x.slope.at[:, part]) for part in (slice(0, half), slice(half, hidden))
    ]
    c_out, c_up, c_down = weight_copies(start, src, x)
    late = [start(src.n1, x.n1), start(src.inv1, x.inv1)]
    behind()
    done = []
    zero = jnp.zeros((1, width), F32)
    s_gn, s_g, s_d2 = zero, zero, zero
    for copy in early:
        copy.wait()
    for r in range(0, rows, BLOCK):
        rs = slice(r, r + BLOCK)
        g = x.g[rs, :].astype(F32)
        normed = x.n2[rs, :]
        d2 = norm_back(g, normed, x.inv2[rs, 0:1], ng[1:2, :])
        dx[rs, :] = d2
        y.d2_low[rs, :] = d2.astype(BF)
        s_gn += jnp.sum(g * normed, axis=0, keepdims=True)
        s_g += jnp.sum(g, axis=0, keepdims=True)
        s_d2 += jnp.sum(d2, axis=0, keepdims=True)
    done.append(start(y.d2_low, dst.d2_low))
    for k in range(2):
        c_down[k].wait()
        c_slope[k].wait()
        for j in range(k * chunks // 2, (k + 1) * chunks // 2):
            part = slice(j * CHUNK, (j + 1) * CHUNK)
            d_act = dot_nt(y.d2_low[...], x.wdown[part, :])
            d_pre = (d_act * x.slope[:, part].astype(F32)).astype(BF)
            y.d_pre[:, part] = d_pre
            bias_sums[0:1, part] = jnp.sum(d_pre.astype(F32), axis=0, keepdims=True)
        part = slice(k * half, (k + 1) * half)
        done.append(start(y.d_pre.at[:, part], dst.d_pre.at[:, part]))
        c_up[k].wait()
        dx[...] += dot_nt(y.d_pre[:, part], x.wup[:, part])
    s_dn, s_dx, s_d1 = zero, zero, zero
    late[0].wait()
    late[1].wait()
    for r in range(0, rows, BLOCK):
        rs = slice(r, r + BLOCK)
        g = dx[rs, :]
        normed = x.n1[rs, :]
        d1 = norm_back(g, normed, x.inv1[rs, 0:1], ng[0:1, :])
        y.d1[rs, :] = d1
        y.d1_low[rs, :] = d1.astype(BF)
        s_dn += jnp.sum(g * normed, axis=0, keepdims=True)
        s_dx += jnp.sum(g, axis=0, keepdims=True)
        s_d1 += jnp.sum(d1, axis=0, keepdims=True)
    done += [start(y.d1, dst.d1), start(y.d1_low, dst.d1_low)]
    for i, s in enumerate((s_dn, s_gn, s_d1, s_dx, s_d2, s_g)):
        sums[i : i + 1, :] = s
    sums[6:8, :] = jnp.zeros((2, width), F32)
    for copy in c_out:
        copy.wait()
    d_mixed[...] = dot_nt(y.d1_low[...], x.wout[...]).astype(BF)
    return done


def heads_back(start, load, dst, x, y, t, d_mixed, nums, shifts):
    width = x.q.shape[1]
    core = nums[4]
    pairs = t.kb.shape[0]
    ext = key_columns(nums, t.kb.shape[1])
    for p in range(pairs):
        t.kb[p, :, 128:256] = ext
        t.vb[p, :, 128:256] = ext
    for copy in load:
        copy.wait()
    place_rows(t.kb, slice(0, 128), x.kv, x.kvp, 0, core)
    place_rows(t.vb, slice(0, 128), x.kv, x.kvp, width, core)
    t.dka[...] = jnp.zeros_like(t.dka)
    t.dva[...] = jnp.zeros_like(t.dva)
    attend_back(nums, shifts, x.q, d_mixed, x.mixed, x.lse, t.kb, t.vb, t.dka, t.dva, y.dq)
    done = [start(y.dq, dst.dq)]
    for to, side, turn in ((y.far, 1 - core, pairs // 2), (y.near, core, 0)):
        for i in range(2):
            mine = pl.ds(pl.multiple_of((2 * i + side) * TILE, TILE), TILE)
            for p in range(pairs):
                for j, total in enumerate((t.dka, t.dva)):
                    lanes = slice(j * width + p * 128, j * width + (p + 1) * 128)
                    to[i * TILE : (i + 1) * TILE, lanes] = total[(p + turn) % pairs, mine, :].astype(to.dtype)
    done += [start(y.far, dst.far), start(y.near, dst.near)]
    return done


ALL, ROWS, HEADS = 3, 1, 2


def backward_kernel(which, slot_of, tokens, counts, lengths, shift_own, shift_far, ng, *refs):
    refs = list(refs[tokens:])
    take = lambda kind: kind(*[refs.pop(0) for _ in range(len(kind._fields))])
    rows_on, heads_on = which & ROWS, which & HEADS
    if rows_on:
        r_src = take(RowsIn)
    if heads_on:
        h_src = take(HeadsIn)
    if which == HEADS:
        mixed_src = refs.pop(0)
    if rows_on:
        r_dst = take(RowsOut)
        sums, bias_sums = refs.pop(0), refs.pop(0)
    if which == ROWS:
        mixed_dst = refs.pop(0)
    if heads_on:
        h_dst = take(HeadsOut)
    d_mixed = refs.pop(0)
    if rows_on:
        r_x = RowsIn(*[refs.pop(0) for _ in range(9)], None, None, None)
        r_y, dx = take(RowsOut), refs.pop(0)
    if heads_on:
        h_x, h_y, h_t = take(HeadsIn), take(HeadsOut), take(HeadsWork)
    start = copier(refs[0])
    load, done = [], []

    def load_heads():
        if heads_on:
            load.extend(start(a, b) for a, b in zip(h_src, h_x))

    if rows_on:
        done += rows_back(start, r_src, r_dst, r_x, r_y, d_mixed, dx, ng, sums, bias_sums, load_heads)
    else:
        load_heads()
        load.append(start(mixed_src, d_mixed))
    if which == ROWS:
        done.append(start(d_mixed, mixed_dst))
    if heads_on:
        nums = mask_numbers(slot_of(lax.axis_index("section")), counts, lengths)
        done += heads_back(start, load, h_dst, h_x, h_y, h_t, d_mixed, nums, (shift_own, shift_far))
    for copy in done:
        copy.wait()


def gradient_kernel(*refs):
    refs = list(refs)
    src = [refs.pop(0) for _ in range(9)]
    dst = [refs.pop(0) for _ in range(5)]
    col_sums = refs.pop(0)
    x = [refs.pop(0) for _ in range(9)]
    y = [refs.pop(0) for _ in range(5)]
    start = copier(refs[0])
    load = [start(a, b) for a, b in zip(src, x)]
    done = []
    act, d2_low, x1_low, d_pre, mixed, d1_low, h, dq, dkv = range(9)
    for k, (left, right) in enumerate(((act, d2_low), (x1_low, d_pre), (mixed, d1_low), (h, dq), (h, dkv))):
        for i in (left, right):
            if load[i] is not None:
                load[i].wait()
                load[i] = None
        tall, broad = y[k].shape
        slab = CHUNK if max(tall, broad) % CHUNK == 0 else TILE
        for j in range(max(tall, broad) // slab):
            part = slice(j * slab, (j + 1) * slab)
            if tall > broad:
                y[k][part, :] = dot_tn(x[left][:, part], x[right][...]).astype(BF)
                done.append(start(y[k].at[part, :], dst[k].at[part, :]))
            else:
                y[k][:, part] = dot_tn(x[left][...], x[right][:, part]).astype(BF)
                done.append(start(y[k].at[:, part], dst[k].at[:, part]))
    width = x[h].shape[1]
    col_sums[0:1, :] = jnp.sum(x[dq][...].astype(F32), axis=0, keepdims=True)
    col_sums[1:2, :] = jnp.sum(x[dkv][:, width:].astype(F32), axis=0, keepdims=True)
    for copy in done:
        copy.wait()


def gradient_call(s, b):
    f = s.f
    rows, width = s.h.shape
    hidden = f.act.shape[1]
    args = (f.act, b.d2_low, f.x1_low, b.d_pre, f.mixed, b.d1_low, s.h, b.dq, b.dkv)
    shapes = [
        ((hidden, width), BF), ((width, hidden), BF), ((width, width), BF), ((width, width), BF), ((width, 2 * width), BF),
    ]
    return pl.pallas_call(
        gradient_kernel,
        out_shape=results(shapes + [((2, width), F32)]),
        in_specs=[IN_HBM] * 9,
        out_specs=(IN_HBM,) * 5 + (IN_VMEM,),
        scratch_shapes=buffers([(a.shape, BF) for a in args]) + buffers(shapes) + [pltpu.SemaphoreType.DMA((40,))],
        compiler_params=pltpu.CompilerParams(vmem_limit_bytes=VMEM_BYTES),
        cost_estimate=NO_COST,
        name="layer_gradient",
    )(*args)


def half_gradient_kernel(k, by_rows, token, left_h, right_h, early_h, out_h, left, right, early, out, sems):
    start = copier(sems)
    tall, broad = out.shape
    if by_rows:
        load = [start(left_h.at[:, k * tall : (k + 1) * tall], left), start(right_h, right)]
        before = start(early_h.at[k * tall : (k + 1) * tall, :], early)
    else:
        load = [start(left_h, left), start(right_h.at[:, k * broad : (k + 1) * broad], right)]
        before = start(early_h.at[:, k * broad : (k + 1) * broad], early)
    for copy in load:
        copy.wait()
    before.wait()
    done = []
    for j in range(2):
        if by_rows:
            part = slice(j * tall // 2, (j + 1) * tall // 2)
            out[part, :] = (dot_tn(left[:, part], right[...]) + early[part, :].astype(F32)).astype(BF)
            done.append(start(out.at[part, :], out_h.at[part, :]))
        else:
            part = slice(j * broad // 2, (j + 1) * broad // 2)
            out[:, part] = (dot_tn(left[...], right[:, part]) + early[:, part].astype(F32)).astype(BF)
            done.append(start(out.at[:, part], out_h.at[:, part]))
    for copy in done:
        copy.wait()


def half_gradient_call(token, left, right, early, k, by_rows):
    rows = left.shape[0]
    tall, broad = early.shape
    tall, broad = (tall // 2, broad) if by_rows else (tall, broad // 2)
    out = ((tall, broad), BF)
    return pl.pallas_call(
        functools.partial(half_gradient_kernel, k, by_rows),
        out_shape=jax.ShapeDtypeStruct(*out),
        in_specs=[IN_HBM] * 4,
        out_specs=IN_HBM,
        scratch_shapes=buffers([((rows, tall), BF), ((rows, broad), BF), out, out]) + [pltpu.SemaphoreType.DMA((5,))],
        compiler_params=pltpu.CompilerParams(vmem_limit_bytes=VMEM_BYTES),
        cost_estimate=NO_COST,
        name="half_gradient",
    )(token, left, right, early)


def last_gradient_kernel(*refs):
    token, mixed_h, d1_h, h_h, dq_h, dkv_h, eo_h, eq_h, ekv_h, c5, s5, s6, u5, u6, *refs = refs
    outs, refs = refs[:4], refs[4:]
    small_own, small_far, mixed, d1, h, dq, dkv, eo, eq, ekv, oo, fo, oi, fi, sems = refs
    start = copier(sems)
    pairs = ((h_h, h), (dq_h, dq), (eq_h, eq), (dkv_h, dkv), (ekv_h, ekv), (mixed_h, mixed), (d1_h, d1), (eo_h, eo))
    load = [start(a, b) for a, b in pairs]
    width = h.shape[1]
    half = width // 2
    done = []
    for copy in load[:5]:
        copy.wait()
    for k, to, away in ((1, fi, outs[3]), (0, oi, outs[2])):
        for part in range(3):
            right, before, at = ((dq, eq, 0), (dkv, ekv, 0), (dkv, ekv, width))[part]
            lanes = slice(at + k * half, at + (k + 1) * half)
            total = dot_tn(h[...], right[:, lanes]) + before[:, lanes].astype(F32)
            to[part * width : (part + 1) * width, :] = total.astype(BF)
        done.append(start(to, away))
    for copy in load[5:]:
        copy.wait()
    for k, to, away in ((1, fo, outs[1]), (0, oo, outs[0])):
        lanes = slice(k * half, (k + 1) * half)
        to[...] = (dot_tn(mixed[:, lanes], d1[...]) + eo[lanes, :].astype(F32)).astype(BF)
        done.append(start(to, away))
    qb = c5[0:1, :] + jnp.sum(dq[...].astype(F32), axis=0, keepdims=True)
    vb = c5[1:2, :] + jnp.sum(dkv[:, width:].astype(F32), axis=0, keepdims=True)
    ub = u5[...] + u6[...]
    for k, to in ((0, small_own), (1, small_far)):
        to[...] = jnp.zeros_like(to)
        to[0:6, :] = s5[0:6, :] + s6[0:6, :]
        for j in range(2):
            to[6 + j : 7 + j, :] = ub[:, (2 * k + j) * width : (2 * k + j + 1) * width]
        to[8:9, :half] = qb[:, k * half : (k + 1) * half]
        to[8:9, half:] = vb[:, k * half : (k + 1) * half]
    for copy in done:
        copy.wait()


def last_gradient_call(token, s, b, early, b5):
    rows, width = s.h.shape
    half = width // 2
    args = (s.f.mixed, b.d1_low, s.h, b.dq, b.dkv, early[2], early[3], early[4])
    shapes = [((half, width), BF), ((half, width), BF), ((3 * width, half), BF), ((3 * width, half), BF)]
    return pl.pallas_call(
        last_gradient_kernel,
        out_shape=results(shapes + [((16, width), F32)] * 2),
        in_specs=[IN_HBM] * 9 + [IN_VMEM] * 5,
        out_specs=(IN_HBM,) * 4 + (IN_VMEM,) * 2,
        scratch_shapes=buffers([(a.shape, BF) for a in args]) + buffers(shapes) + [pltpu.SemaphoreType.DMA((16,))],
        compiler_params=pltpu.CompilerParams(vmem_limit_bytes=VMEM_BYTES),
        cost_estimate=NO_COST,
        name="last_gradient",
    )(token, *args, early[5], b5.sums, b.sums, b5.bias_sums, b.bias_sums)


class Back(NamedTuple):
    d2_low: Any
    d_pre: Any
    d1: Any
    d1_low: Any
    sums: Any
    bias_sums: Any
    dq: Any
    near: Any
    far: Any
    dkv: Any


def backward_call(which, slot_of, w, g, f, q, kv, kvp, d_mixed=None, tokens=()):
    rows, width = f.n1.shape
    hidden = 2 * w.up.shape[1]
    pairs, length = width // 128, 2 * rows
    low, wide, full = ((rows, width), BF), ((rows, hidden), BF), ((rows, width), F32)
    one = ((rows, 128), F32)
    twice = ((rows, 2 * width), BF)
    r_in = (low, full, one, full, one, wide, ((width, width), BF), ((width, hidden), BF), ((hidden, width), BF))
    r_out = RowsOut(low, wide, full, low)
    h_in = HeadsIn(low, ((pairs, 2, rows), F32), low, twice, twice)
    h_out = HeadsOut(low, ((rows, 2 * width), F32), twice)
    h_work = HeadsWork(*[((pairs, length, 256), BF)] * 2, *[((pairs, length, 128), F32)] * 2)
    args, outs, out_specs, scratch = [], [], [], [low]
    if which & ROWS:
        args += [g, f.n2, f.inv2, f.n1, f.inv1, f.slope, w.out, w.up, w.down, w.out_far, w.up_far, w.down_far]
        outs += list(r_out) + [((8, width), F32), ((1, hidden), F32)]
        out_specs += [IN_HBM] * len(r_out) + [IN_VMEM] * 2
        scratch += list(r_in) + list(r_out) + [full]
    if which & HEADS:
        args += [f.mixed, f.lse, q, kv, kvp]
        scratch += list(h_in) + list(h_out) + list(h_work)
    if which == HEADS:
        args.append(d_mixed)
    if which == ROWS:
        outs.append(low)
        out_specs.append(IN_HBM)
    if which & HEADS:
        outs += list(h_out)
        out_specs += [IN_HBM] * len(h_out)
    return pl.pallas_call(
        functools.partial(backward_kernel, which, slot_of, len(tokens)),
        out_shape=results(outs),
        in_specs=[IN_SMEM] * 4 + [IN_VMEM] + [IN_HBM] * (len(tokens) + len(args)),
        out_specs=tuple(out_specs),
        scratch_shapes=buffers(scratch) + [pltpu.SemaphoreType.DMA((32,))],
        compiler_params=pltpu.CompilerParams(vmem_limit_bytes=VMEM_BYTES),
        cost_estimate=NO_COST,
        name="layer_backward",
    )(w.counts, w.lengths, w.shift_own, w.shift_far, w.ng, *tokens, *args)


SWAP = [(0, 1), (1, 0)]


def to_peer(x):
    return lax.ppermute(x, "mp", SWAP)


def next_section(x):
    return lax.ppermute(x, "section", [(0, 1)])


def last_section(x):
    return lax.ppermute(x, "section", [(1, 0)])


def add_low(a, b):
    return (a.astype(F32) + b.astype(F32)).astype(BF)


def gate_kernel(*refs):
    pass


def tied(*xs):
    hbm = pl.BlockSpec(memory_space=pl.ANY)
    return pl.pallas_call(
        gate_kernel,
        out_shape=tuple(jax.ShapeDtypeStruct(x.shape, x.dtype) for x in xs),
        in_specs=[hbm] * len(xs),
        out_specs=(hbm,) * len(xs),
        input_output_aliases={i: i for i in range(len(xs))},
        cost_estimate=NO_COST,
        name="gate",
    )(*xs)


class Sum:
    def __init__(self, x, size):
        self.whole = None
        if size < 4 or size % 4:
            self.whole = self.sent = lax.psum(x, "dp")
            return
        self.size = size
        self.steps = self.walk(x)
        self.got = next(self.steps)

    def walk(self, x):
        size = self.size
        line = size // 2
        half = line // 2
        me = lax.axis_index("dp")
        side = lax.rem(me, 2)
        place = me // 2
        pairs = [(i, i ^ 1) for i in range(size)]
        on_line = lambda moves: [(2 * a + s, 2 * b + s) for a, b in moves for s in range(2)]
        rows = x.shape[0] // 2
        x = x.reshape((2, rows) + x.shape[1:])
        keep = lax.dynamic_index_in_dim(x, side, 0, keepdims=False)
        send = lax.dynamic_index_in_dim(x, 1 - side, 0, keepdims=False)
        self.sent = send
        total = add_low(keep, (yield lax.ppermute(send, "dp", pairs)))
        self.sent = total
        for k in range(half - 1):
            moves = on_line([(k, k + 1), (line - 1 - k, line - 2 - k)])
            total = add_low(total, (yield lax.ppermute(total, "dp", moves)))
            self.sent = total
        moves = on_line([(half - 1, half), (half, half - 1)])
        total = add_low(total, (yield lax.ppermute(total, "dp", moves)))
        self.sent = total
        for k in reversed(range(half - 1)):
            moves = on_line([(k + 1, k), (line - 2 - k, line - 1 - k)])
            total = jnp.where((place == k) | (place == line - 1 - k), (yield lax.ppermute(total, "dp", moves)), total)
        got = yield lax.ppermute(total, "dp", pairs)
        self.whole = jnp.concatenate([jnp.where(side == 0, total, got), jnp.where(side == 0, got, total)], axis=0)
        yield None

    def take(self, got):
        self.got = self.steps.send(got)


def step_sums(sums, *others):
    moving = [one for one in sums if one.whole is None]
    res = tied(*[one.got for one in moving], *others)
    for one, got in zip(moving, res):
        one.take(got)
    return res[len(moving) :]


class Layer(NamedTuple):
    q: Any
    kv: Any
    bq: Any
    bkv: Any
    out: Any
    up: Any
    down: Any
    out_far: Any
    up_far: Any
    down_far: Any
    bup_own: Any
    bup_far: Any
    ng: Any
    lb: Any
    counts: Any
    lengths: Any
    shift_own: Any
    shift_far: Any


class Saved(NamedTuple):
    h: Any
    q: Any
    kv: Any
    kvp: Any
    f: Any


def forward_tick(save, slot_of, h, w, beside=()):
    kv = (dot_nn(h, w.kv) + w.bkv).astype(BF)
    kvp = to_peer(kv)
    q = (dot_nn(h, w.q) + w.bq).astype(BF)
    q, *beside = tied(q, *beside) if beside else (q,)
    f = forward_call(save, slot_of, w, q, kv, kvp, h)
    return f.out, Saved(h, q, kv, kvp, f), beside


def backward_end(b, w):
    other = to_peer(b.far)
    from_q = dot_nt(b.dq, w.q)
    dkv = (b.near + other.astype(F32)).astype(BF)
    return (b.d1 + from_q + dot_nt(dkv, w.kv)).astype(BF), b._replace(dkv=dkv)


def backward_tick(slot_of, g, s, w):
    b = Back(*backward_call(ALL, slot_of, w, g, s.f, s.q, s.kv, s.kvp), None)
    return backward_end(b, w)


def cut(x, which, size):
    return lax.slice_in_dim(x, which * size, (which + 1) * size, axis=1)


def on_device(
    tokens,
    grad_out,
    attention_in,
    attention_bias,
    attention_out,
    up_weight,
    up_bias,
    down_weight,
    norm_gains,
    layer_biases,
    block_counts,
    lengths,
    head_shifts,
):
    dp_size = lax.axis_size("dp")
    first = lax.axis_index("section") == 0
    width = tokens.shape[2]
    quarter = tokens.shape[1]
    half = attention_in.shape[3]
    hidden = up_weight.shape[2]

    crossed = [lax.ppermute(jnp.where(first, grad_out[s], tokens[s]), "section", SWAP) for s in range(2)]
    from_rows = lambda x, s: jnp.concatenate([tokens[s], x], axis=0)
    cot_rows = lambda x, s: jnp.concatenate([x, grad_out[s]], axis=0)
    tok0, cot0 = from_rows(crossed[0], 0), cot_rows(crossed[0], 0)
    win, win_far = attention_in[0], to_peer(attention_in[0])
    ab, ab_far = attention_bias[0], to_peer(attention_bias)[0]
    bv = jnp.concatenate([ab[1], ab_far[1]])
    w = Layer(
        q=jnp.concatenate([win[:, 0], win_far[:, 0]], axis=1),
        kv=jnp.concatenate([win[:, 1], win_far[:, 1], win[:, 2], win_far[:, 2]], axis=1),
        bq=jnp.concatenate([ab[0], ab_far[0]]),
        bkv=jnp.concatenate([jnp.zeros_like(bv), bv]),
        out=attention_out[0],
        up=up_weight[0],
        down=down_weight[0],
        out_far=to_peer(attention_out[0]),
        up_far=to_peer(up_weight[0]),
        down_far=to_peer(down_weight[0]),
        bup_own=up_bias,
        bup_far=to_peer(up_bias),
        ng=norm_gains[0],
        lb=layer_biases[0],
        counts=block_counts,
        lengths=lengths,
        shift_own=head_shifts,
        shift_far=to_peer(head_shifts),
    )
    slot_one = lambda s: 0
    slot_a = lambda s: 1 - s
    slot_b = lambda s: s

    out1, _, (crossed1,) = forward_tick(False, slot_one, tok0, w, (crossed[1],))
    tok1, cot1 = from_rows(crossed1, 1), cot_rows(crossed1, 1)
    out2, saved2, _ = forward_tick(True, slot_a, jnp.where(first, tok1, next_section(out1)), w)
    away2 = next_section(out2)
    g3, b3 = backward_tick(slot_a, cot0, saved2, w)
    away2, _ = tied(away2, b3.d1_low)
    out4, saved4, _ = forward_tick(True, slot_b, jnp.where(first, tok0, away2), w)
    g5, b5 = backward_tick(slot_b, jnp.where(first, last_section(g3), cot1), saved4, w)

    early = gradient_call(saved4, b5)
    g6_in = jnp.where(first, last_section(g5), cot0)

    f6 = saved2.f
    d2_low = norm_back(g6_in.astype(F32), f6.n2, f6.inv2[:, :1], w.ng[1]).astype(BF)
    down_far = half_gradient_call(d2_low, f6.act, d2_low, early[0], 1, True)
    down_own = half_gradient_call(down_far, f6.act, d2_low, early[0], 0, True)
    down = Sum(add_low(down_own, to_peer(down_far)), dp_size)
    r6 = backward_call(ROWS, slot_a, w, g6_in, f6, None, None, None, None, (down.sent,))
    b6 = Back(*r6[:6], None, None, None, None)
    up_far = half_gradient_call(b6.d1_low, f6.x1_low, b6.d_pre, early[1], 1, False)
    (up_far,) = step_sums([down], up_far)
    up_in = to_peer(up_far)
    up_own = half_gradient_call(up_far, f6.x1_low, b6.d_pre, early[1], 0, False)
    up = Sum(add_low(up_own, up_in), dp_size)
    quarters = jnp.concatenate([out2[:quarter], out4[:quarter]], axis=0)
    dq, near, far = backward_call(
        HEADS, slot_a, w, None, f6, saved2.q, saved2.kv, saved2.kvp, r6[6], (down.sent, up.sent)
    )
    dq, near, far, quarters = step_sums([down, up], dq, near, far, quarters)
    layer_far = last_section(quarters)
    g6, b6 = backward_end(b6._replace(dq=dq, near=near, far=far), w)
    out_own, out_far, in_own, in_far, small_own, small_far = last_gradient_call(up.sent, saved2, b6, early, b5)
    out_far, in_far, small_far = step_sums([down, up], out_far, in_far, small_far)
    tokens_far = next_section(jnp.concatenate([g5[quarter:], g6[quarter:]], axis=0))
    in_g = add_low(in_own, to_peer(in_far))
    small = small_own + to_peer(small_far)
    out_g = jnp.concatenate(
        [add_low(out_own, to_peer(out_far)), small.astype(BF), jnp.zeros((16, width), BF)], axis=0
    )
    part = lambda x, i: x[i * x.shape[0] // 2 : (i + 1) * x.shape[0] // 2]
    in_a, in_b = Sum(part(in_g, 0), dp_size), Sum(part(in_g, 1), dp_size)
    last = Sum(out_g, dp_size)
    step_sums([down, up, in_a])
    step_sums([up, in_a, in_b])
    (layer_far,) = step_sums([down, in_a, in_b, last], layer_far)
    step_sums([up, in_a, in_b, last])
    (tokens_far,) = step_sums([in_a, in_b, last], tokens_far)
    sums = [down, up, in_a, in_b, last]
    while any(one.whole is None for one in sums):
        step_sums(sums)
    down_s = down.whole.astype(F32)
    up_s = up.whole.astype(F32)
    in_s = jnp.concatenate([in_a.whole, in_b.whole], axis=0).astype(F32)
    out_s = last.whole.astype(F32)
    small = out_s[half : half + 16]

    pair = lambda x, y: jnp.stack([x, y])
    layer_out = jnp.where(first, layer_far.reshape(tokens.shape), pair(out2[quarter:], out4[quarter:]))
    grad_tokens = jnp.where(first, pair(g5[:quarter], g6[:quarter]), tokens_far.reshape(tokens.shape))
    return (
        layer_out,
        grad_tokens,
        in_s.reshape(3, width, half).transpose(1, 0, 2)[None],
        small[8].reshape(1, 2, half),
        out_s[:half][None],
        up_s[None],
        small[6:8].reshape(1, hidden),
        down_s[None],
        small[:2][None],
        small[2:6][None],
    )


def solution(mesh):
    tokens = P("dp", ("section", "mp"), None)
    weights = (
        P("section", None, None, "mp"),
        P("section", None, "mp"),
        P("section", "mp", None),
        P("section", None, "mp"),
        P("section", "mp"),
        P("section", "mp", None),
        P("section", None, None),
        P("section", None, None),
    )
    return jax.shard_map(
        on_device,
        mesh=mesh,
        in_specs=(tokens, tokens) + weights + (P("dp"), P("dp"), P("section", "mp")),
        out_specs=(tokens, tokens) + weights,
        check_vma=False,
    )
```

time: 669 us -> 539 us (0.81); the launches traced: 657 us -> 534 us
  matrix products: 167 us -> 23.9 us
  Pallas kernels: 109 us -> 206 us
  waiting for transfers between devices: 183 us -> 143 us
  local copies, waits for them, and re-layouts: 48.4 us -> 31.6 us
  between operations: 16.9 us -> 2.8 us
  starting transfers between devices: 77.8 us -> 65.4 us
  other arithmetic: 53.6 us -> 60.8 us
    pallas_call x6 -> x25, Pallas kernels: 109 us -> 206 us  [the longest x4 96.6 us: backward_call(): pl.pallas_call(functools.partial(backward_kernel, which, slot_of, len(tok...]
    dot_general x24 -> x0, matrix products: 52.1 us -> none  [dot_tn(): lax.dot_general(a, b, (((0,), (0,)), ((), ())), preferred_element_type=F32)]
    dot_general x14 -> x6, matrix products: 58.1 us -> 11.6 us  [dot_nt(): lax.dot_general(a, b, (((1,), (1,)), ((), ())), preferred_element_type=F32)]
    ppermute x32 -> x33, waiting for transfers between devices: 183 us -> 136 us  [the longest x10 35.6 us: walk(): total = add_low(total, (yield lax.ppermute(total, 'dp', moves)))]
    dot_general x14 -> x6, matrix products: 57.2 us -> 12.3 us  [dot_nn(): lax.dot_general(a, b, (((1,), (0,)), ((), ())), preferred_element_type=F32)]
    convert_element_type x20 -> x26, other arithmetic: 20.7 us -> 38.9 us  [the longest x19 27.9 us: add_low(): return (a.astype(F32) + b.astype(F32)).astype(BF)]
    ppermute x32 -> x33, starting transfers between devices: 73.5 us -> 56.7 us  [the longest x10 22.6 us: walk(): total = add_low(total, (yield lax.ppermute(total, 'dp', moves)))]
    reduce_sum x17 -> x1, other arithmetic: 11.6 us -> 0.49 us  [norm_back(): a = jnp.sum(e, axis=-1, keepdims=True) * scale]
  transfers between devices with their start and end apart: 52 -> 51, of which waited for: 17 -> 27; matrix products, arithmetic and copies ran while one was open for 29% -> 15% of each run, Pallas kernels for 14% -> 23%
where the time goes in v2:
time: 539 us; the launch traced here: 534 us
  Pallas kernels  206 us (38%)
  waiting for transfers between devices  143 us (27%)
  starting transfers between devices  65.4 us (12%)
  other arithmetic  60.8 us (11%)
  local copies, waits for them, and re-layouts  31.6 us (6%)
  matrix products  23.9 us (4%)
    pallas_call x4, Pallas kernels, backward_call(): pl.pallas_call(functools.partial(backward_kernel, which, slot_of, len(tok...  96.6 us
    pallas_call x3, Pallas kernels, forward_call(): pl.pallas_call(functools.partial(forward_kernel, save, slot_of, len(token...  68.1 us
    ppermute x10, waiting for transfers between devices, walk(): total = add_low(total, (yield lax.ppermute(total, 'dp', moves)))  35.6 us
    convert_element_type x19, other arithmetic, add_low(): return (a.astype(F32) + b.astype(F32)).astype(BF)  27.9 us
    ppermute x5, waiting for transfers between devices, walk(): total = add_low(keep, (yield lax.ppermute(send, 'dp', pairs)))  26.3 us
    ppermute x10, starting transfers between devices, walk(): total = add_low(total, (yield lax.ppermute(total, 'dp', moves)))  22.6 us
    ppermute x3, waiting for transfers between devices, next_section(): return lax.ppermute(x, 'section', [(0, 1)])  21.2 us
    pallas_call x4, Pallas kernels, half_gradient_call(): pl.pallas_call(functools.partial(half_gradient_kernel, k, by_rows), out_s...  19.8 us
  transfers between devices with their start and end apart: 51, of which 27 were waited for; matrix products, arithmetic and copies ran while one was open for 15% of the time, Pallas kernels for 23%

profile of v2, /device:TPU:14, one launch (start us, length us, event | category | flops | bytes accessed | tf_op | source)
XLA Modules:
  0.0 533.9 jit_solution(2490955299676092751)
XLA Ops:
  6.5 1.8 slice_bitcast_fusion.3
  8.4 5.4 %collective-permute-done.2 = bf16[256,768]{1,0:T(8,128)(2,1)S(1)} collective-permute-done((bf16[256,768]{1,0:T(8,128)(2,1)S(1)}, bf16[256,768]{1,0:T(8,128)(2,1)S(1)}, u32[]{:S(2)}, u32[]{:S(2)}) %collective-permute-start.2) | collective-permute-done | bytes 393248 | tf_op jit(solution)/shard_map/ppermute | solution.py:1038
  13.8 3.0 fusion.refs_1_
  17.4 3.3 collective-permute-done.shift_far
  23.0 9.2 %collective-permute-done.5.refs_1_ = bf16[256,768]{1,0:T(8,128)(2,1)} collective-permute-done((bf16[256,768]{1,0:T(8,128)(2,1)S(1)}, bf16[256,768]{1,0:T(8,128)(2,1)}, u32[]{:S(2)}, u32[]{:S(2)}) %collective-permute-start.5) | collective-permute-done | bytes 393248 | tf_op jit(solution)/shard_map/ppermute | solution.py:1038
  34.3 20.9 %layer_forward.3 = bf16[512,768]{1,0:T(8,128)(2,1)} custom-call(s32[2]{0:T(128)} %counts.13, s32[2]{0:T(128)} %lengths.13, s32[1,6]{1,0:T(1,128)} %shift_own.13, s32[1,6]{1,0:T(1,128)} %copy-done.116, f32[4,768]{1,0:T(4,128)} %bitcast.148, f32[2,768]{1,0:T(2,128)} %bitcast.141, f32[1,1536]{1,0:T(1,128)} %bup_own.5, f32[1,1536]{1,0:T(1,128)} %copy-done.112, ...), custom_call_target="tpu_custom_call" | custom-call | flops 1 | bytes 1 | tf_op jit(solution)/shard_map/layer_forward/pallas_call | solution.py:471
  56.6 21.1 %collective-permute-done.10 = bf16[512,768]{1,0:T(8,128)(2,1)S(1)} collective-permute-done((bf16[512,768]{1,0:T(8,128)(2,1)}, bf16[512,768]{1,0:T(8,128)(2,1)S(1)}, u32[]{:S(2)}, u32[]{:S(2)}) %collective-permute-start.10) | collective-permute-done | bytes 786464 | tf_op jit(solution)/shard_map/ppermute | solution.py:882
  79.1 2.1 fusion.1.refs_1_.refs_15_.refs_5_
  85.9 22.5 %layer_forward.4 = (bf16[512,768]{1,0:T(8,128)(2,1)}, bf16[512,768]{1,0:T(8,128)(2,1)}, f32[6,2,512]{2,1,0:T(2,128)}, bf16[512,768]{1,0:T(8,128)(2,1)}, bf16[512...) custom-call(s32[2]{0:T(128)} %counts.13, ...), custom_call_target="tpu_custom_call" | custom-call | flops 1 | bytes 1 | tf_op jit(solution)/shard_map/layer_forward/pallas_call | solution.py:471
  109.9 29.6 %layer_backward.4 = (bf16[512,768]{1,0:T(8,128)(2,1)}, bf16[512,3072]{1,0:T(8,128)(2,1)}, f32[512,768]{1,0:T(8,128)}, bf16[512,768]{1,0:T(8,128)(2,1)}, f32[8,76...) custom-call(s32[2]{0:T(128)} %counts.13, ...), custom_call_target="tpu_custom_call" | custom-call | flops 1 | bytes 1 | tf_op jit(solution)/shard_map/layer_backward/pallas_call | solution.py:862
  139.6 6.6 %collective-permute-start.12 = (bf16[512,1536]{1,0:T(8,128)(2,1)}, bf16[512,1536]{1,0:T(8,128)(2,1)}, u32[]{:S(2)}, u32[]{:S(2)}) collective-permute-start(bf16[512,1536]{1,0:T(8,128)(2,1)} %get-tuple-element.114), channel_id=1, source_target_pairs={{0,8},{8,0},{1,9},{9,1},{2,10},{10,2},{3,11},{11,3},{4,12},{12,4},... | collective-permute-start | bytes 4718600 | tf_op jit(solution)/shard_map/ppermute | solution.py:878
  148.5 2.1 fusion.2.refs_1_.refs_15_
  153.1 3.8 add_convert_fusion.14
  156.9 4.2 collective-permute-start.13
  163.9 24.7 %layer_forward.5 = (bf16[512,768]{1,0:T(8,128)(2,1)}, bf16[512,768]{1,0:T(8,128)(2,1)}, f32[6,2,512]{2,1,0:T(2,128)}, bf16[512,768]{1,0:T(8,128)(2,1)}, bf16[512...) custom-call(s32[2]{0:T(128)} %counts.13, ...), custom_call_target="tpu_custom_call" | custom-call | flops 1 | bytes 1 | tf_op jit(solution)/shard_map/layer_forward/pallas_call | solution.py:471
  188.7 2.1 maximum_select_fusion.1.refs_0_
  190.7 33.9 %layer_backward.5 = (bf16[512,768]{1,0:T(8,128)(2,1)}, bf16[512,3072]{1,0:T(8,128)(2,1)}, f32[512,768]{1,0:T(8,128)}, bf16[512,768]{1,0:T(8,128)(2,1)}, f32[8,76...) custom-call(s32[2]{0:T(128)} %counts.13, ...), custom_call_target="tpu_custom_call" | custom-call | flops 1 | bytes 1 | tf_op jit(solution)/shard_map/layer_backward/pallas_call | solution.py:862
  224.8 2.1 fusion.11
  230.7 2.0 add_convert_fusion.12
  234.7 13.1 %layer_gradient.1 = (bf16[3072,768]{1,0:T(8,128)(2,1)}, bf16[768,3072]{1,0:T(8,128)(2,1)}, bf16[768,768]{1,0:T(8,128)(2,1)}, bf16[768,768]{1,0:T(8,128)(2,1)}, b...) custom-call(bf16[512,3072]{1,0:T(8,128)(2,1)} %get-tuple-element.130.refs_0_, bf16[512,768]{1,0:T(8,128)(2,1)} %get-tuple-element.131.refs_1_, ...), custom_call_target="tpu_custom_call" | custom-call | flops 1 | bytes 1 | tf_op jit(solution)/shard_map/layer_gradient/pallas_call | solution.py:709
  247.8 3.6 collective-permute-done.17
  253.2 4.9 half_gradient.4.token
  258.2 4.9 half_gradient.5
  263.1 3.0 add_convert_fusion.1
  267.2 16.1 %layer_backward.6 = (bf16[512,768]{1,0:T(8,128)(2,1)}, bf16[512,3072]{1,0:T(8,128)(2,1)}, f32[512,768]{1,0:T(8,128)}, bf16[512,768]{1,0:T(8,128)(2,1)}, f32[8,76...) custom-call(s32[2]{0:T(128)} %counts.13, s32[2]{0:T(128)} %lengths.13, s32[1,6]{1,0:T(1,128)} %shift_own.13, ...), custom_call_target="tpu_custom_call" | custom-call | flops 1 | bytes 1 | tf_op jit(solution)/shard_map/layer_backward/pallas_call | solution.py:862
  283.3 4.9 half_gradient.6.refs_1_
  288.2 6.4 %collective-permute-done.19.refs_0_ = bf16[768,768]{1,0:T(8,128)(2,1)S(1)} collective-permute-done((bf16[768,768]{1,0:T(8,128)(2,1)S(1)}, bf16[768,768]{1,0:T(8,128)(2,1)S(1)}, u32[]{:S(2)}, u32[]{:S(2)}) %collective-permute-start.19) | collective-permute-done | bytes 1179680 | tf_op jit(solution)/shard_map/ppermute | solution.py:934
  295.8 5.1 half_gradient.7
  302.9 2.3 add_convert_fusion
  309.2 17.0 %layer_backward.7 = (bf16[512,768]{1,0:T(8,128)(2,1)}, f32[512,1536]{1,0:T(8,128)}, bf16[512,1536]{1,0:T(8,128)(2,1)}) custom-call(s32[2]{0:T(128)} %counts.13, s32[2]{0:T(128)} %lengths.13, s32[1,6]{1,0:T(1,128)} %shift_own.13, s32[1,6]{1,0:T(1,128)} %copy-done.116, f32[2,768]{1,0:T(2,128)} %bitcast.147, bf16[768,768]{1,0:T(8,128)(2,1)} %copy-done.7, ...), custom_call_target="tpu_custom_call" | custom-call | flops 1 | bytes 1 | tf_op jit(solution)/shard_map/layer_backward/pallas_call | solution.py:862
  326.1 5.6 %collective-permute-done.20.refs_0_ = bf16[768,768]{1,0:T(8,128)(2,1)S(1)} collective-permute-done((bf16[768,768]{1,0:T(8,128)(2,1)S(1)}, bf16[768,768]{1,0:T(8,128)(2,1)S(1)}, u32[]{:S(2)}, u32[]{:S(2)}) %collective-permute-start.20) | collective-permute-done | bytes 1179680 | tf_op jit(solution)/shard_map/ppermute | solution.py:938
  331.7 2.2 collective-permute-done.22.refs_1_
  333.9 2.7 fusion.3.refs_0_
  339.3 4.3 collective-permute-start.23
  343.7 3.0 add_convert_fusion.3.refs_5_
  346.7 8.9 %last_gradient.1 = (bf16[384,768]{1,0:T(8,128)(2,1)}, bf16[384,768]{1,0:T(8,128)(2,1)}, bf16[2304,384]{1,0:T(8,128)(2,1)}, bf16[2304,384]{1,0:T(8,128)(2,1)}, f32[16,768]{1,0:T(8,128)}, /*index=5*/f32[16,768]{1,0:T(8,128)}) custom-call(bf16[384,1536]{1,0:T(8,128)(2,1)} %fusion.3.refs_0_, bf16[512,768]{1,0:T(8,128)(2,1)} %get-tuple-element.109.refs_12_.refs_2_.refs_1_, ...), custom_call_target="tpu_custom_call" | custom-call | flops 1 | bytes 1 | tf_op jit(solution)/shard_map/last_gradient/pallas_call | solution.py:808
  355.6 11.7 %collective-permute-done.24.refs_1_ = bf16[384,1536]{1,0:T(8,128)(2,1)} collective-permute-done((bf16[384,1536]{1,0:T(8,128)(2,1)}, bf16[384,1536]{1,0:T(8,128)(2,1)}, u32[]{:S(2)}, u32[]{:S(2)}) %collective-permute-start.24) | collective-permute-done | bytes 1179680 | tf_op jit(solution)/shard_map/ppermute | solution.py:938
  367.3 3.0 collective-permute-done.23.refs_0_
  372.2 5.3 collective-permute-start.39
  378.3 2.0 add_convert_fusion.7
  380.4 3.6 collective-permute-start.27
  384.1 2.1 add_convert_fusion.8
  387.6 2.1 add_convert_fusion.11
  394.5 15.2 %collective-permute-done.27.refs_1_ = bf16[384,1536]{1,0:T(8,128)(2,1)S(1)} collective-permute-done((bf16[384,1536]{1,0:T(8,128)(2,1)S(1)}, bf16[384,1536]{1,0:T(8,128)(2,1)S(1)}, u32[]{:S(2)}, u32[]{:S(2)}) %collective-permute-start.27) | collective-permute-done | bytes 1179680 | tf_op jit(solution)/shard_map/ppermute | solution.py:941
  409.7 2.5 collective-permute-done.26.refs_0_
  414.9 4.7 collective-permute-start.31
  427.7 6.4 %collective-permute-done.33.refs_2_ = bf16[576,384]{1,0:T(8,128)(2,1)S(1)} collective-permute-done((bf16[576,384]{1,0:T(8,128)(2,1)S(1)}, bf16[576,384]{1,0:T(8,128)(2,1)S(1)}, u32[]{:S(2)}, u32[]{:S(2)}) %collective-permute-start.33) | collective-permute-done | bytes 442400 | tf_op jit(solution)/shard_map/ppermute | solution.py:934
  435.7 7.8 %collective-permute-done.31.refs_0_ = bf16[384,1536]{1,0:T(8,128)(2,1)S(1)} collective-permute-done((bf16[384,1536]{1,0:T(8,128)(2,1)S(1)}, bf16[384,1536]{1,0:T(8,128)(2,1)S(1)}, u32[]{:S(2)}, u32[]{:S(2)}) %collective-permute-start.31) | collective-permute-done | bytes 1179680 | tf_op jit(solution)/shard_map/ppermute | solution.py:945
  448.3 2.5 collective-permute-start.34
  452.4 11.2 %collective-permute-done.38.refs_3_ = bf16[208,768]{1,0:T(8,128)(2,1)} collective-permute-done((bf16[208,768]{1,0:T(8,128)(2,1)}, bf16[208,768]{1,0:T(8,128)(2,1)}, u32[]{:S(2)}, u32[]{:S(2)}) %collective-permute-start.38) | collective-permute-done | bytes 319520 | tf_op jit(solution)/shard_map/ppermute | solution.py:934
  468.9 2.5 collective-permute-start.42
  472.6 2.7 collective-permute-start.41
  476.8 2.5 maximum_convert_fusion.1
  481.6 7.1 %collective-permute-done.40.refs_0_ = bf16[384,1536]{1,0:T(8,128)(2,1)S(1)} collective-permute-done((bf16[384,1536]{1,0:T(8,128)(2,1)S(1)}, bf16[384,1536]{1,0:T(8,128)(2,1)S(1)}, u32[]{:S(2)}, u32[]{:S(2)}) %collective-permute-start.40) | collective-permute-done | bytes 1179680 | tf_op jit(solution)/shard_map/ppermute | solution.py:946
  491.0 2.7 collective-permute-start.46
  496.9 2.8 maximum_convert_fusion
  499.9 2.5 collective-permute-done.45.refs_1_
  502.4 2.4 collective-permute-done.44.refs_0_
  506.7 2.8 collective-permute-start.49
  510.0 2.1 maximum_select_fusion.3
  512.2 1.8 collective-permute-done.49.refs_1_
  514.0 6.2 %collective-permute-done.48.refs_0_ = bf16[576,384]{1,0:T(8,128)(2,1)S(1)} collective-permute-done((bf16[576,384]{1,0:T(8,128)(2,1)S(1)}, bf16[576,384]{1,0:T(8,128)(2,1)S(1)}, u32[]{:S(2)}, u32[]{:S(2)}) %collective-permute-start.48) | collective-permute-done | bytes 442400 | tf_op jit(solution)/shard_map/ppermute | solution.py:946
  522.7 2.0 convert_bitcast_fusion
  524.7 3.4 collective-permute-done.50.refs_0_
  (408 shorter events, 98.9 us)
Async XLA Ops:
  0.7 5.9 %collective-permute-start.3 = (bf16[768,3,384]{2,0,1:T(8,128)(2,1)}, bf16[768,3,384]{2,0,1:T(8,128)(2,1)}, u32[]{:S(2)}, u32[]{:S(2)}) collective-permute-start(bf16[768,3,384]{2,0,1:T(8,128)(2,1)} %bitcast.139), channel_id=1, source_target_pairs={{0,8},{8,0},{1,9},{9,1},{2,10},{10,2},{3,11},{11,3},{4,12},{12,4},... | collective-permute-start | bytes 5308424 | tf_op jit(solution)/shard_map/ppermute | solution.py:878
  2.3 11.4 %collective-permute-start.2 = (bf16[256,768]{1,0:T(8,128)(2,1)S(1)}, bf16[256,768]{1,0:T(8,128)(2,1)S(1)}, u32[]{:S(2)}, u32[]{:S(2)}) collective-permute-start(bf16[256,768]{1,0:T(8,128)(2,1)S(1)} %get-tuple-element.214), channel_id=1, source_target_pairs={{0,16},{16,0},{1,17},{17,1},{2,18},{18,2},{3,19},{19,3},{4,20},{20... | collective-permute-start | bytes 1179656 | tf_op jit(solution)/shard_map/ppermute | solution.py:1038
  2.9 3.5 collective-permute-start.4
  3.0 30.5 %collective-permute-start.8 = (bf16[768,1536]{1,0:T(8,128)(2,1)S(1)}, bf16[768,1536]{1,0:T(8,128)(2,1)}, u32[]{:S(2)}, u32[]{:S(2)}) collective-permute-start(bf16[768,1536]{1,0:T(8,128)(2,1)S(1)} %bitcast.113), channel_id=1, source_target_pairs={{0,8},{8,0},{1,9},{9,1},{2,10},{10,2},{3,11},{11,3},{4,12},{12,4},... | collective-permute-start | bytes 7077896 | tf_op jit(solution)/shard_map/ppermute | solution.py:878
  3.5 30.0 %collective-permute-start.9 = (bf16[1536,768]{1,0:T(8,128)(2,1)}, bf16[1536,768]{1,0:T(8,128)(2,1)}, u32[]{:S(2)}, u32[]{:S(2)}) collective-permute-start(bf16[1536,768]{1,0:T(8,128)(2,1)} %bitcast.114), channel_id=1, source_target_pairs={{0,8},{8,0},{1,9},{9,1},{2,10},{10,2},{3,11},{11,3},{4,12},{12,4},... | collective-permute-start | bytes 7077896 | tf_op jit(solution)/shard_map/ppermute | solution.py:878
  6.4 25.8 %copy-start.40 = (bf16[256,768]{1,0:T(8,128)(2,1)}, bf16[256,768]{1,0:T(8,128)(2,1)S(1)}, u32[]{:S(2)}) copy-start(bf16[256,768]{1,0:T(8,128)(2,1)S(1)} %get-tuple-element.228) | copy-start | bytes 1179652
  6.4 25.8 %copy-start.42 = (bf16[256,768]{1,0:T(8,128)(2,1)}, bf16[256,768]{1,0:T(8,128)(2,1)S(1)}, u32[]{:S(2)}) copy-start(bf16[256,768]{1,0:T(8,128)(2,1)S(1)} %get-tuple-element.237) | copy-start | bytes 1179652
  13.8 18.5 %copy-start.38 = (bf16[256,768]{1,0:T(8,128)(2,1)}, bf16[256,768]{1,0:T(8,128)(2,1)S(1)}, u32[]{:S(2)}) copy-start(bf16[256,768]{1,0:T(8,128)(2,1)S(1)} %collective-permute-done.2) | copy-start | bytes 1179652
  16.8 16.7 %collective-permute-start.6 = (bf16[512,1536]{1,0:T(8,128)(2,1)}, bf16[512,1536]{1,0:T(8,128)(2,1)}, u32[]{:S(2)}, u32[]{:S(2)}) collective-permute-start(bf16[512,1536]{1,0:T(8,128)(2,1)} %fusion.refs_1_), channel_id=1, source_target_pairs={{0,8},{8,0},{1,9},{9,1},{2,10},{10,2},{3,11},{11,3},{4,12},{12,4},... | collective-permute-start | bytes 4718600 | tf_op jit(solution)/shard_map/ppermute | solution.py:878
  16.8 16.6 %collective-permute-start.7 = (bf16[384,768]{1,0:T(8,128)(2,1)S(1)}, bf16[384,768]{1,0:T(8,128)(2,1)S(1)}, u32[]{:S(2)}, u32[]{:S(2)}) collective-permute-start(bf16[384,768]{1,0:T(8,128)(2,1)S(1)} %bitcast.127), channel_id=1, source_target_pairs={{0,8},{8,0},{1,9},{9,1},{2,10},{10,2},{3,11},{11,3},{4,12},{12,4},... | collective-permute-start | bytes 1769480 | tf_op jit(solution)/shard_map/ppermute | solution.py:878
  17.3 3.4 collective-permute-start
  20.7 11.5 %collective-permute-start.5 = (bf16[256,768]{1,0:T(8,128)(2,1)S(1)}, bf16[256,768]{1,0:T(8,128)(2,1)}, u32[]{:S(2)}, u32[]{:S(2)}) collective-permute-start(bf16[256,768]{1,0:T(8,128)(2,1)S(1)} %get-tuple-element.213), channel_id=1, source_target_pairs={{0,16},{16,0},{1,17},{17,1},{2,18},{18,2},{3,19},{19,3},{4,20},{20... | collective-permute-start | bytes 1179656 | tf_op jit(solution)/shard_map/ppermute | solution.py:1038
  32.2 1.3 collective-permute-start.1
  34.3 43.5 %copy-start.68 = (bf16[256,768]{1,0:T(8,128)(2,1)S(1)}, bf16[256,768]{1,0:T(8,128)(2,1)}, u32[]{:S(2)}) copy-start(bf16[256,768]{1,0:T(8,128)(2,1)} %get-tuple-element.238) | copy-start | bytes 1179652
  34.3 44.7 %copy-start.118 = (f32[1536]{0:T(1024)S(1)}, f32[1536]{0:T(1024)}, u32[]{:S(2)}) copy-start(f32[1536]{0:T(1024)} %copy-done.117) | copy-start | bytes 18436
  55.2 23.9 %copy-start.85 = (bf16[768,384]{1,0:T(8,128)(2,1)S(1)}, bf16[768,384]{1,0:T(8,128)(2,1)}, u32[]{:S(2)}) copy-start(bf16[768,384]{1,0:T(8,128)(2,1)} %copy-done.84) | copy-start | bytes 1769476
  55.2 23.9 %copy-start.88 = (bf16[768,384]{1,0:T(8,128)(2,1)S(1)}, bf16[768,384]{1,0:T(8,128)(2,1)}, u32[]{:S(2)}) copy-start(bf16[768,384]{1,0:T(8,128)(2,1)} %copy-done.87) | copy-start | bytes 1769476
  55.2 23.9 %copy-start.94 = (bf16[768,384]{1,0:T(8,128)(2,1)S(1)}, bf16[768,384]{1,0:T(8,128)(2,1)}, u32[]{:S(2)}) copy-start(bf16[768,384]{1,0:T(8,128)(2,1)} %copy-done.93) | copy-start | bytes 1769476
  55.2 23.9 %copy-start.99 = (bf16[768,384]{1,0:T(8,128)(2,1)S(1)}, bf16[768,384]{1,0:T(8,128)(2,1)}, u32[]{:S(2)}) copy-start(bf16[768,384]{1,0:T(8,128)(2,1)} %copy-done.98) | copy-start | bytes 1769476
  55.2 22.6 %collective-permute-start.10 = (bf16[512,768]{1,0:T(8,128)(2,1)}, bf16[512,768]{1,0:T(8,128)(2,1)S(1)}, u32[]{:S(2)}, u32[]{:S(2)}) collective-permute-start(bf16[512,768]{1,0:T(8,128)(2,1)} %layer_forward.3), channel_id=1, source_target_pairs={{0,16},{1,17},{2,18},{3,19},{4,20},{5,21},{6,22},{7,23},{8,24},{9,... | collective-permute-start | bytes 2359304 | tf_op jit(solution)/shard_map/ppermute | solution.py:882
  81.3 3.5 collective-permute-start.11
  108.4 37.8 %collective-permute-start.14 = (bf16[512,768]{1,0:T(8,128)(2,1)}, bf16[512,768]{1,0:T(8,128)(2,1)S(1)}, u32[]{:S(2)}, u32[]{:S(2)}) collective-permute-start(bf16[512,768]{1,0:T(8,128)(2,1)} %get-tuple-element.115), channel_id=1, source_target_pairs={{0,16},{1,17},{2,18},{3,19},{4,20},{5,21},{6,22},{7,23},{8,24},{9,... | collective-permute-start | bytes 2359304 | tf_op jit(solution)/shard_map/ppermute | solution.py:882
  139.6 12.3 %collective-permute-start.12 = (bf16[512,1536]{1,0:T(8,128)(2,1)}, bf16[512,1536]{1,0:T(8,128)(2,1)}, u32[]{:S(2)}, u32[]{:S(2)}) collective-permute-start(bf16[512,1536]{1,0:T(8,128)(2,1)} %get-tuple-element.114), channel_id=1, source_target_pairs={{0,8},{8,0},{1,9},{9,1},{2,10},{10,2},{3,11},{11,3},{4,12},{12,4},... | collective-permute-start | bytes 4718600 | tf_op jit(solution)/shard_map/ppermute | solution.py:878
  150.7 12.1 %collective-permute-start.15 = (bf16[512,1536]{1,0:T(8,128)(2,1)S(1)}, bf16[512,1536]{1,0:T(8,128)(2,1)S(1)}, u32[]{:S(2)}, u32[]{:S(2)}) collective-permute-start(bf16[512,1536]{1,0:T(8,128)(2,1)S(1)} %fusion.2.refs_1_.refs_15_), channel_id=1, source_target_pairs={{0,8},{8,0},{1,9},{9,1},{2,10},{10,2},{3,11},{11,3},{4,12},{12,4},... | collective-permute-start | bytes 4718600 | tf_op jit(solution)/shard_map/ppermute | solution.py:878
  156.9 31.7 %collective-permute-start.13 = (bf16[512,768]{1,0:T(8,128)(2,1)}, bf16[512,768]{1,0:T(8,128)(2,1)S(1)}, u32[]{:S(2)}, u32[]{:S(2)}) collective-permute-start(bf16[512,768]{1,0:T(8,128)(2,1)} %add_convert_fusion.14), channel_id=1, source_target_pairs={{16,0},{17,1},{18,2},{19,3},{20,4},{21,5},{22,6},{23,7},{24,8},{25... | collective-permute-start | bytes 2359304 | tf_op jit(solution)/shard_map/ppermute | solution.py:886
  162.8 25.9 %copy-start.67 = (bf16[256,768]{1,0:T(8,128)(2,1)S(1)}, bf16[256,768]{1,0:T(8,128)(2,1)}, u32[]{:S(2)}) copy-start(bf16[256,768]{1,0:T(8,128)(2,1)} %get-tuple-element.227) | copy-start | bytes 1179652
  190.7 34.0 %copy-start.106 = (bf16[768,384]{1,0:T(8,128)(2,1)S(1)}, bf16[768,384]{1,0:T(8,128)(2,1)}, u32[]{:S(2)}) copy-start(bf16[768,384]{1,0:T(8,128)(2,1)} %copy-done.103) | copy-start | bytes 1769476
  224.7 3.7 collective-permute-start.16
  232.7 18.7 %collective-permute-start.17 = (bf16[512,768]{1,0:T(8,128)(2,1)S(1)}, bf16[512,768]{1,0:T(8,128)(2,1)S(1)}, u32[]{:S(2)}, u32[]{:S(2)}) collective-permute-start(bf16[512,768]{1,0:T(8,128)(2,1)S(1)} %add_convert_fusion.12), channel_id=1, source_target_pairs={{16,0},{17,1},{18,2},{19,3},{20,4},{21,5},{22,6},{23,7},{24,8},{25... | collective-permute-start | bytes 2359304 | tf_op jit(solution)/shard_map/ppermute | solution.py:886
  234.7 16.7 %copy-start.1 = (f32[512,768]{1,0:T(8,128)S(1)}, f32[512,768]{1,0:T(8,128)}, u32[]{:S(2)}) copy-start(f32[512,768]{1,0:T(8,128)} %get-tuple-element.105.refs_1_.refs_2_) | copy-start | bytes 4718596
  258.1 5.0 collective-permute-start.18
  266.2 28.4 %collective-permute-start.19 = (bf16[768,768]{1,0:T(8,128)(2,1)S(1)}, bf16[768,768]{1,0:T(8,128)(2,1)S(1)}, u32[]{:S(2)}, u32[]{:S(2)}) collective-permute-start(bf16[768,768]{1,0:T(8,128)(2,1)S(1)} %dynamic-slice_bitcast_fusion.1.refs_0_), channel_id=1, source_target_pairs={{0,1},{1,0},{2,3},{3,2},{4,5},{5,4},{6,7},{7,6},{8,9},{9,8},{10,11... | collective-permute-start | bytes 3538952 | tf_op jit(solution)/shard_map/ppermute | solution.py:934
  295.7 7.2 %collective-permute-start.21 = (bf16[768,1536]{1,0:T(8,128)(2,1)}, bf16[768,1536]{1,0:T(8,128)(2,1)}, u32[]{:S(2)}, u32[]{:S(2)}) collective-permute-start(bf16[768,1536]{1,0:T(8,128)(2,1)} %get-tuple-element.141.token), channel_id=1, source_target_pairs={{0,8},{8,0},{1,9},{9,1},{2,10},{10,2},{3,11},{11,3},{4,12},{12,4},... | collective-permute-start | bytes 7077896 | tf_op jit(solution)/shard_map/ppermute | solution.py:878
  301.1 30.5 %collective-permute-start.20 = (bf16[768,768]{1,0:T(8,128)(2,1)S(1)}, bf16[768,768]{1,0:T(8,128)(2,1)S(1)}, u32[]{:S(2)}, u32[]{:S(2)}) collective-permute-start(bf16[768,768]{1,0:T(8,128)(2,1)S(1)} %fusion.4.refs_0_), channel_id=1, source_target_pairs={{0,2},{1,3},{6,4},{7,5},{8,10},{9,11},{14,12},{15,13},{16,18},{17,... | collective-permute-start | bytes 3538952 | tf_op jit(solution)/shard_map/ppermute | solution.py:938
  305.4 28.6 %collective-permute-start.22 = (bf16[384,1536]{1,0:T(8,128)(2,1)S(1)}, bf16[384,1536]{1,0:T(8,128)(2,1)}, u32[]{:S(2)}, u32[]{:S(2)}) collective-permute-start(bf16[384,1536]{1,0:T(8,128)(2,1)S(1)} %dynamic-slice_bitcast_fusion.refs_1_), channel_id=1, source_target_pairs={{0,1},{1,0},{2,3},{3,2},{4,5},{5,4},{6,7},{7,6},{8,9},{9,8},{10,11... | collective-permute-start | bytes 3538952 | tf_op jit(solution)/shard_map/ppermute | solution.py:934
  333.9 9.8 %collective-permute-start.25 = (bf16[512,1536]{1,0:T(8,128)(2,1)}, bf16[512,1536]{1,0:T(8,128)(2,1)}, u32[]{:S(2)}, u32[]{:S(2)}) collective-permute-start(bf16[512,1536]{1,0:T(8,128)(2,1)} %get-tuple-element.151), channel_id=1, source_target_pairs={{0,8},{8,0},{1,9},{9,1},{2,10},{10,2},{3,11},{11,3},{4,12},{12,4},... | collective-permute-start | bytes 4718600 | tf_op jit(solution)/shard_map/ppermute | solution.py:878
  336.6 30.6 %collective-permute-start.24 = (bf16[384,1536]{1,0:T(8,128)(2,1)}, bf16[384,1536]{1,0:T(8,128)(2,1)}, u32[]{:S(2)}, u32[]{:S(2)}) collective-permute-start(bf16[384,1536]{1,0:T(8,128)(2,1)} %fusion.3.refs_0_), channel_id=1, source_target_pairs={{0,2},{1,3},{6,4},{7,5},{8,10},{9,11},{14,12},{15,13},{16,18},{17,... | collective-permute-start | bytes 3538952 | tf_op jit(solution)/shard_map/ppermute | solution.py:938
  339.3 30.9 %collective-permute-start.23 = (bf16[768,768]{1,0:T(8,128)(2,1)}, bf16[768,768]{1,0:T(8,128)(2,1)}, u32[]{:S(2)}, u32[]{:S(2)}) collective-permute-start(bf16[768,768]{1,0:T(8,128)(2,1)} %add_convert_fusion.9), channel_id=1, source_target_pairs={{2,4},{3,5},{4,2},{5,3},{10,12},{11,13},{12,10},{13,11},{18,20},{1... | collective-permute-start | bytes 3538952 | tf_op jit(solution)/shard_map/ppermute | solution.py:941
  370.3 19.4 %collective-permute-start.28 = (bf16[2304,384]{1,0:T(8,128)(2,1)}, bf16[2304,384]{1,0:T(8,128)(2,1)S(1)}, u32[]{:S(2)}, u32[]{:S(2)}) collective-permute-start(bf16[2304,384]{1,0:T(8,128)(2,1)} %get-tuple-element.166), channel_id=1, source_target_pairs={{0,8},{8,0},{1,9},{9,1},{2,10},{10,2},{3,11},{11,3},{4,12},{12,4},... | collective-permute-start | bytes 5308424 | tf_op jit(solution)/shard_map/ppermute | solution.py:878
  372.2 78.9 %collective-permute-start.39 = (bf16[512,768]{1,0:T(8,128)(2,1)}, bf16[512,768]{1,0:T(8,128)(2,1)}, u32[]{:S(2)}, u32[]{:S(2)}) collective-permute-start(bf16[512,768]{1,0:T(8,128)(2,1)} %get-tuple-element.176), channel_id=1, source_target_pairs={{16,0},{17,1},{18,2},{19,3},{20,4},{21,5},{22,6},{23,7},{24,8},{25... | collective-permute-start | bytes 2359304 | tf_op jit(solution)/shard_map/ppermute | solution.py:886
  380.4 29.4 %collective-permute-start.27 = (bf16[384,1536]{1,0:T(8,128)(2,1)S(1)}, bf16[384,1536]{1,0:T(8,128)(2,1)S(1)}, u32[]{:S(2)}, u32[]{:S(2)}) collective-permute-start(bf16[384,1536]{1,0:T(8,128)(2,1)S(1)} %add_convert_fusion.7), channel_id=1, source_target_pairs={{2,4},{3,5},{4,2},{5,3},{10,12},{11,13},{12,10},{13,11},{18,20},{1... | collective-permute-start | bytes 3538952 | tf_op jit(solution)/shard_map/ppermute | solution.py:941
  386.1 26.1 %collective-permute-start.26 = (bf16[768,768]{1,0:T(8,128)(2,1)S(1)}, bf16[768,768]{1,0:T(8,128)(2,1)S(1)}, u32[]{:S(2)}, u32[]{:S(2)}) collective-permute-start(bf16[768,768]{1,0:T(8,128)(2,1)S(1)} %add_convert_fusion.8), channel_id=1, source_target_pairs={{2,0},{3,1},{4,6},{5,7},{10,8},{11,9},{12,14},{13,15},{18,16},{19,... | collective-permute-start | bytes 3538952 | tf_op jit(solution)/shard_map/ppermute | solution.py:945
  391.3 22.0 %collective-permute-start.29 = (bf16[576,384]{1,0:T(8,128)(2,1)S(1)}, bf16[576,384]{1,0:T(8,128)(2,1)}, u32[]{:S(2)}, u32[]{:S(2)}) collective-permute-start(bf16[576,384]{1,0:T(8,128)(2,1)S(1)} %dynamic-slice_bitcast_fusion.3), channel_id=1, source_target_pairs={{0,1},{1,0},{2,3},{3,2},{4,5},{5,4},{6,7},{7,6},{8,9},{9,8},{10,11... | collective-permute-start | bytes 1327112 | tf_op jit(solution)/shard_map/ppermute | solution.py:934
  392.4 1.2 collective-permute-start.37
  393.7 26.0 %collective-permute-start.36 = (bf16[384,768]{1,0:T(8,128)(2,1)}, bf16[384,768]{1,0:T(8,128)(2,1)}, u32[]{:S(2)}, u32[]{:S(2)}) collective-permute-start(bf16[384,768]{1,0:T(8,128)(2,1)} %get-tuple-element.173), channel_id=1, source_target_pairs={{0,8},{8,0},{1,9},{9,1},{2,10},{10,2},{3,11},{11,3},{4,12},{12,4},... | collective-permute-start | bytes 1769480 | tf_op jit(solution)/shard_map/ppermute | solution.py:878
  414.9 28.5 %collective-permute-start.31 = (bf16[384,1536]{1,0:T(8,128)(2,1)S(1)}, bf16[384,1536]{1,0:T(8,128)(2,1)S(1)}, u32[]{:S(2)}, u32[]{:S(2)}) collective-permute-start(bf16[384,1536]{1,0:T(8,128)(2,1)S(1)} %add_convert_fusion.6), channel_id=1, source_target_pairs={{2,0},{3,1},{4,6},{5,7},{10,8},{11,9},{12,14},{13,15},{18,16},{19,... | collective-permute-start | bytes 3538952 | tf_op jit(solution)/shard_map/ppermute | solution.py:945
  421.0 13.2 %collective-permute-start.33 = (bf16[576,384]{1,0:T(8,128)(2,1)S(1)}, bf16[576,384]{1,0:T(8,128)(2,1)S(1)}, u32[]{:S(2)}, u32[]{:S(2)}) collective-permute-start(bf16[576,384]{1,0:T(8,128)(2,1)S(1)} %dynamic-slice_bitcast_fusion.2), channel_id=1, source_target_pairs={{0,1},{1,0},{2,3},{3,2},{4,5},{5,4},{6,7},{7,6},{8,9},{9,8},{10,11... | collective-permute-start | bytes 1327112 | tf_op jit(solution)/shard_map/ppermute | solution.py:934
  422.5 12.0 %collective-permute-start.32 = (bf16[576,384]{1,0:T(8,128)(2,1)S(1)}, bf16[576,384]{1,0:T(8,128)(2,1)S(1)}, u32[]{:S(2)}, u32[]{:S(2)}) collective-permute-start(bf16[576,384]{1,0:T(8,128)(2,1)S(1)} %fusion.8), channel_id=1, source_target_pairs={{0,2},{1,3},{6,4},{7,5},{8,10},{9,11},{14,12},{15,13},{16,18},{17,... | collective-permute-start | bytes 1327112 | tf_op jit(solution)/shard_map/ppermute | solution.py:938
  425.2 19.3 %copy-start.35 = (bf16[1152,384]{1,0:T(8,128)(2,1)S(1)}, bf16[1152,384]{1,0:T(8,128)(2,1)}, u32[]{:S(2)}) copy-start(bf16[1152,384]{1,0:T(8,128)(2,1)} %get-tuple-element.205) | copy-start | bytes 2654212
  425.2 38.7 %collective-permute-start.30 = (bf16[768,768]{1,0:T(8,128)(2,1)}, bf16[768,768]{1,0:T(8,128)(2,1)S(1)}, u32[]{:S(2)}, u32[]{:S(2)}) collective-permute-start(bf16[768,768]{1,0:T(8,128)(2,1)} %broadcast_select_fusion.1), channel_id=1, source_target_pairs={{0,1},{1,0},{2,3},{3,2},{4,5},{5,4},{6,7},{7,6},{8,9},{9,8},{10,11... | collective-permute-start | bytes 3538952 | tf_op jit(solution)/shard_map/ppermute | solution.py:946
  434.1 29.4 %collective-permute-start.38 = (bf16[208,768]{1,0:T(8,128)(2,1)}, bf16[208,768]{1,0:T(8,128)(2,1)}, u32[]{:S(2)}, u32[]{:S(2)}) collective-permute-start(bf16[208,768]{1,0:T(8,128)(2,1)} %dynamic-slice_bitcast_fusion.4), channel_id=1, source_target_pairs={{0,1},{1,0},{2,3},{3,2},{4,5},{5,4},{6,7},{7,6},{8,9},{9,8},{10,11... | collective-permute-start | bytes 958472 | tf_op jit(solution)/shard_map/ppermute | solution.py:934
  445.7 18.1 %collective-permute-start.35 = (bf16[576,384]{1,0:T(8,128)(2,1)S(1)}, bf16[576,384]{1,0:T(8,128)(2,1)S(1)}, u32[]{:S(2)}, u32[]{:S(2)}) collective-permute-start(bf16[576,384]{1,0:T(8,128)(2,1)S(1)} %fusion.7), channel_id=1, source_target_pairs={{0,2},{1,3},{6,4},{7,5},{8,10},{9,11},{14,12},{15,13},{16,18},{17,... | collective-permute-start | bytes 1327112 | tf_op jit(solution)/shard_map/ppermute | solution.py:938
  448.3 16.4 %collective-permute-start.34 = (bf16[576,384]{1,0:T(8,128)(2,1)S(1)}, bf16[576,384]{1,0:T(8,128)(2,1)}, u32[]{:S(2)}, u32[]{:S(2)}) collective-permute-start(bf16[576,384]{1,0:T(8,128)(2,1)S(1)} %add_convert_fusion.21), channel_id=1, source_target_pairs={{2,4},{3,5},{4,2},{5,3},{10,12},{11,13},{12,10},{13,11},{18,20},{1... | collective-permute-start | bytes 1327112 | tf_op jit(solution)/shard_map/ppermute | solution.py:941
  451.1 48.7 %collective-permute-start.47 = (bf16[512,768]{1,0:T(8,128)(2,1)}, bf16[512,768]{1,0:T(8,128)(2,1)}, u32[]{:S(2)}, u32[]{:S(2)}) collective-permute-start(bf16[512,768]{1,0:T(8,128)(2,1)} %pad_maximum_fusion.6), channel_id=1, source_target_pairs={{0,16},{1,17},{2,18},{3,19},{4,20},{5,21},{6,22},{7,23},{8,24},{9,... | collective-permute-start | bytes 2359304 | tf_op jit(solution)/shard_map/ppermute | solution.py:882
  463.6 25.2 %collective-permute-start.40 = (bf16[384,1536]{1,0:T(8,128)(2,1)S(1)}, bf16[384,1536]{1,0:T(8,128)(2,1)S(1)}, u32[]{:S(2)}, u32[]{:S(2)}) collective-permute-start(bf16[384,1536]{1,0:T(8,128)(2,1)S(1)} %broadcast_select_fusion), channel_id=1, source_target_pairs={{0,1},{1,0},{2,3},{3,2},{4,5},{5,4},{6,7},{7,6},{8,9},{9,8},{10,11... | collective-permute-start | bytes 3538952 | tf_op jit(solution)/shard_map/ppermute | solution.py:946
  466.3 14.0 %collective-permute-start.43 = (bf16[208,768]{1,0:T(8,128)(2,1)S(1)}, bf16[208,768]{1,0:T(8,128)(2,1)S(1)}, u32[]{:S(2)}, u32[]{:S(2)}) collective-permute-start(bf16[208,768]{1,0:T(8,128)(2,1)S(1)} %fusion.9), channel_id=1, source_target_pairs={{0,2},{1,3},{6,4},{7,5},{8,10},{9,11},{14,12},{15,13},{16,18},{17,... | collective-permute-start | bytes 958472 | tf_op jit(solution)/shard_map/ppermute | solution.py:938
  468.9 11.5 %collective-permute-start.42 = (bf16[576,384]{1,0:T(8,128)(2,1)S(1)}, bf16[576,384]{1,0:T(8,128)(2,1)S(1)}, u32[]{:S(2)}, u32[]{:S(2)}) collective-permute-start(bf16[576,384]{1,0:T(8,128)(2,1)S(1)} %add_convert_fusion.19), channel_id=1, source_target_pairs={{2,4},{3,5},{4,2},{5,3},{10,12},{11,13},{12,10},{13,11},{18,20},{1... | collective-permute-start | bytes 1327112 | tf_op jit(solution)/shard_map/ppermute | solution.py:941
  472.6 9.0 %collective-permute-start.41 = (bf16[576,384]{1,0:T(8,128)(2,1)S(1)}, bf16[576,384]{1,0:T(8,128)(2,1)S(1)}, u32[]{:S(2)}, u32[]{:S(2)}) collective-permute-start(bf16[576,384]{1,0:T(8,128)(2,1)S(1)} %add_convert_fusion.20), channel_id=1, source_target_pairs={{2,0},{3,1},{4,6},{5,7},{10,8},{11,9},{12,14},{13,15},{18,16},{19,... | collective-permute-start | bytes 1327112 | tf_op jit(solution)/shard_map/ppermute | solution.py:945
  491.0 8.9 %collective-permute-start.46 = (bf16[208,768]{1,0:T(8,128)(2,1)S(1)}, bf16[208,768]{1,0:T(8,128)(2,1)S(1)}, u32[]{:S(2)}, u32[]{:S(2)}) collective-permute-start(bf16[208,768]{1,0:T(8,128)(2,1)S(1)} %add_convert_fusion.23), channel_id=1, source_target_pairs={{2,4},{3,5},{4,2},{5,3},{10,12},{11,13},{12,10},{13,11},{18,20},{1... | collective-permute-start | bytes 958472 | tf_op jit(solution)/shard_map/ppermute | solution.py:941
  495.0 7.4 %collective-permute-start.45 = (bf16[576,384]{1,0:T(8,128)(2,1)S(1)}, bf16[576,384]{1,0:T(8,128)(2,1)S(1)}, u32[]{:S(2)}, u32[]{:S(2)}) collective-permute-start(bf16[576,384]{1,0:T(8,128)(2,1)S(1)} %add_convert_fusion.18), channel_id=1, source_target_pairs={{2,0},{3,1},{4,6},{5,7},{10,8},{11,9},{12,14},{13,15},{18,16},{19,... | collective-permute-start | bytes 1327112 | tf_op jit(solution)/shard_map/ppermute | solution.py:945
  496.4 8.4 %collective-permute-start.44 = (bf16[576,384]{1,0:T(8,128)(2,1)S(1)}, bf16[576,384]{1,0:T(8,128)(2,1)S(1)}, u32[]{:S(2)}, u32[]{:S(2)}) collective-permute-start(bf16[576,384]{1,0:T(8,128)(2,1)S(1)} %broadcast_select_fusion.9), channel_id=1, source_target_pairs={{0,1},{1,0},{2,3},{3,2},{4,5},{5,4},{6,7},{7,6},{8,9},{9,8},{10,11... | collective-permute-start | bytes 1327112 | tf_op jit(solution)/shard_map/ppermute | solution.py:946
  506.7 7.3 %collective-permute-start.49 = (bf16[208,768]{1,0:T(8,128)(2,1)S(1)}, bf16[208,768]{1,0:T(8,128)(2,1)S(1)}, u32[]{:S(2)}, u32[]{:S(2)}) collective-permute-start(bf16[208,768]{1,0:T(8,128)(2,1)S(1)} %add_convert_fusion.22), channel_id=1, source_target_pairs={{2,0},{3,1},{4,6},{5,7},{10,8},{11,9},{12,14},{13,15},{18,16},{19,... | collective-permute-start | bytes 958472 | tf_op jit(solution)/shard_map/ppermute | solution.py:945
  509.6 10.6 %collective-permute-start.48 = (bf16[576,384]{1,0:T(8,128)(2,1)S(1)}, bf16[576,384]{1,0:T(8,128)(2,1)S(1)}, u32[]{:S(2)}, u32[]{:S(2)}) collective-permute-start(bf16[576,384]{1,0:T(8,128)(2,1)S(1)} %broadcast_select_fusion.8), channel_id=1, source_target_pairs={{0,1},{1,0},{2,3},{3,2},{4,5},{5,4},{6,7},{7,6},{8,9},{9,8},{10,11... | collective-permute-start | bytes 1327112 | tf_op jit(solution)/shard_map/ppermute | solution.py:946
  521.0 7.1 %collective-permute-start.50 = (bf16[208,768]{1,0:T(8,128)(2,1)S(1)}, bf16[208,768]{1,0:T(8,128)(2,1)S(1)}, u32[]{:S(2)}, u32[]{:S(2)}) collective-permute-start(bf16[208,768]{1,0:T(8,128)(2,1)S(1)} %broadcast_select_fusion.12), channel_id=1, source_target_pairs={{0,1},{1,0},{2,3},{3,2},{4,5},{5,4},{6,7},{7,6},{8,9},{9,8},{10,11... | collective-permute-start | bytes 958472 | tf_op jit(solution)/shard_map/ppermute | solution.py:946
  (114 other events, 479.9 us)

commit v3 on v2

--- a/solution.py
+++ b/solution.py
@@ -203,7 +203,7 @@
         rows = slice(tile * TILE, (tile + 1) * TILE)
 
         def body(width):
-            @pl.loop(0, pairs, unroll=2 if width < length else 1)
+            @pl.loop(0, pairs, unroll=2)
             def _(p):
                 lanes = pl.ds(pl.multiple_of(p * 128, 128), 128)
                 qn = q[rows, lanes].astype(F32) * 0.125
@@ -373,7 +373,7 @@
         rs = slice(r, r + BLOCK)
         normed, inv = norm_rows(x.h[rs, :].astype(F32) + t.acc[rs, :] + lb[0:1, :])
         if save:
-            y.n1[rs, :] = normed
+            y.n1[rs, :] = normed.astype(BF)
             y.inv1[rs, :] = jnp.broadcast_to(inv, (BLOCK, 128))
         full = normed * ng[0:1, :] + lb[1:2, :]
         t.x1[rs, :] = full
@@ -420,7 +420,7 @@
         rs = slice(r, r + BLOCK)
         normed, inv = norm_rows(t.x1[rs, :] + t.acc[rs, :] + lb[2:3, :])
         if save:
-            y.n2[rs, :] = normed
+            y.n2[rs, :] = normed.astype(BF)
             y.inv2[rs, :] = jnp.broadcast_to(inv, (BLOCK, 128))
         y.out[rs, :] = (normed * ng[1:2, :] + lb[3:4, :]).astype(BF)
     ship(y.out, dst.out)
@@ -450,7 +450,7 @@
     low, wide, full = ((rows, width), BF), ((rows, hidden), BF), ((rows, width), F32)
     one, twice = ((rows, 128), F32), ((rows, 2 * width), BF)
     shapes_in = (low, twice, twice, low, ((width, width), BF), ((width, hidden), BF), ((hidden, width), BF))
-    shapes_out = ForwardOut(low, low, ((pairs, 2, rows), F32), low, wide, wide, full, one, full, one)
+    shapes_out = ForwardOut(low, low, ((pairs, 2, rows), F32), low, wide, wide, low, one, low, one)
     if not save:
         gone = ((16, 128), BF)
         scratch_out = shapes_out._replace(lse=gone, slope=gone, n1=gone, inv1=gone, n2=gone, inv2=gone)
@@ -502,7 +502,6 @@
 class RowsOut(NamedTuple):
     d2_low: Any
     d_pre: Any
-    d1: Any
     d1_low: Any
 
 
@@ -527,27 +526,30 @@
     dva: Any
 
 
-def rows_back(start, src, dst, x, y, d_mixed, dx, ng, sums, bias_sums, behind):
+def rows_back(start, src, dst, x, y, d_mixed, dx, ng, sums, bias_sums, behind, up_refs):
     rows, width = x.g.shape
     hidden = x.wup.shape[1]
     half = hidden // 2
     chunks = hidden // CHUNK
-    early = [start(src.g, x.g), start(src.n2, x.n2), start(src.inv2, x.inv2)]
+    soon = [start(src.g, x.g), start(src.n2, x.n2), start(src.inv2, x.inv2)]
     c_slope = [
         start(src.slope.at[:, part], x.slope.at[:, part]) for part in (slice(0, half), slice(half, hidden))
     ]
     c_out, c_up, c_down = weight_copies(start, src, x)
     late = [start(src.n1, x.n1), start(src.inv1, x.inv1)]
+    if up_refs:
+        x1_h, early_h, outs_h, x1, early, outs = up_refs
+        up_load = [start(x1_h, x1), start(early_h, early)]
     behind()
     done = []
     zero = jnp.zeros((1, width), F32)
     s_gn, s_g, s_d2 = zero, zero, zero
-    for copy in early:
+    for copy in soon:
         copy.wait()
     for r in range(0, rows, BLOCK):
         rs = slice(r, r + BLOCK)
         g = x.g[rs, :].astype(F32)
-        normed = x.n2[rs, :]
+        normed = x.n2[rs, :].astype(F32)
         d2 = norm_back(g, normed, x.inv2[rs, 0:1], ng[1:2, :])
         dx[rs, :] = d2
         y.d2_low[rs, :] = d2.astype(BF)
@@ -568,26 +570,38 @@
         done.append(start(y.d_pre.at[:, part], dst.d_pre.at[:, part]))
         c_up[k].wait()
         dx[...] += dot_nt(y.d_pre[:, part], x.wup[:, part])
+    def up_gradient(k):
+        if up_refs:
+            for j in range(2):
+                to = slice(j * half // 2, (j + 1) * half // 2)
+                at = slice(k * half + j * half // 2, k * half + (j + 1) * half // 2)
+                outs[k][:, to] = (dot_tn(x1[...], y.d_pre[:, at]) + early[:, at].astype(F32)).astype(BF)
+            done.append(start(outs[k], outs_h[k]))
+
+    if up_refs:
+        for copy in up_load:
+            copy.wait()
+    up_gradient(1)
     s_dn, s_dx, s_d1 = zero, zero, zero
     late[0].wait()
     late[1].wait()
     for r in range(0, rows, BLOCK):
         rs = slice(r, r + BLOCK)
         g = dx[rs, :]
-        normed = x.n1[rs, :]
+        normed = x.n1[rs, :].astype(F32)
         d1 = norm_back(g, normed, x.inv1[rs, 0:1], ng[0:1, :])
-        y.d1[rs, :] = d1
         y.d1_low[rs, :] = d1.astype(BF)
         s_dn += jnp.sum(g * normed, axis=0, keepdims=True)
         s_dx += jnp.sum(g, axis=0, keepdims=True)
         s_d1 += jnp.sum(d1, axis=0, keepdims=True)
-    done += [start(y.d1, dst.d1), start(y.d1_low, dst.d1_low)]
+    done.append(start(y.d1_low, dst.d1_low))
     for i, s in enumerate((s_dn, s_gn, s_d1, s_dx, s_d2, s_g)):
         sums[i : i + 1, :] = s
     sums[6:8, :] = jnp.zeros((2, width), F32)
     for copy in c_out:
         copy.wait()
     d_mixed[...] = dot_nt(y.d1_low[...], x.wout[...]).astype(BF)
+    up_gradient(0)
     return done
 
 
@@ -631,17 +645,22 @@
         h_src = take(HeadsIn)
     if which == HEADS:
         mixed_src = refs.pop(0)
+    if which == ROWS:
+        up_refs = [refs.pop(0), refs.pop(0)]
     if rows_on:
         r_dst = take(RowsOut)
         sums, bias_sums = refs.pop(0), refs.pop(0)
     if which == ROWS:
         mixed_dst = refs.pop(0)
+        up_refs.append([refs.pop(0), refs.pop(0)])
     if heads_on:
         h_dst = take(HeadsOut)
     d_mixed = refs.pop(0)
     if rows_on:
         r_x = RowsIn(*[refs.pop(0) for _ in range(9)], None, None, None)
         r_y, dx = take(RowsOut), refs.pop(0)
+    if which == ROWS:
+        up_refs += [refs.pop(0), refs.pop(0), [refs.pop(0), refs.pop(0)]]
     if heads_on:
         h_x, h_y, h_t = take(HeadsIn), take(HeadsOut), take(HeadsWork)
     start = copier(refs[0])
@@ -652,7 +671,8 @@
             load.extend(start(a, b) for a, b in zip(h_src, h_x))
 
     if rows_on:
-        done += rows_back(start, r_src, r_dst, r_x, r_y, d_mixed, dx, ng, sums, bias_sums, load_heads)
+        up_refs = up_refs if which == ROWS else None
+        done += rows_back(start, r_src, r_dst, r_x, r_y, d_mixed, dx, ng, sums, bias_sums, load_heads, up_refs)
     else:
         load_heads()
         load.append(start(mixed_src, d_mixed))
@@ -820,7 +840,6 @@
 class Back(NamedTuple):
     d2_low: Any
     d_pre: Any
-    d1: Any
     d1_low: Any
     sums: Any
     bias_sums: Any
@@ -830,17 +849,17 @@
     dkv: Any
 
 
-def backward_call(which, slot_of, w, g, f, q, kv, kvp, d_mixed=None, tokens=()):
+def backward_call(which, slot_of, w, g, f, q, kv, kvp, d_mixed=None, tokens=(), early=None):
     rows, width = f.n1.shape
     hidden = 2 * w.up.shape[1]
     pairs, length = width // 128, 2 * rows
     low, wide, full = ((rows, width), BF), ((rows, hidden), BF), ((rows, width), F32)
     one = ((rows, 128), F32)
     twice = ((rows, 2 * width), BF)
-    r_in = (low, full, one, full, one, wide, ((width, width), BF), ((width, hidden), BF), ((hidden, width), BF))
-    r_out = RowsOut(low, wide, full, low)
+    r_in = (low, low, one, low, one, wide, ((width, width), BF), ((width, hidden), BF), ((hidden, width), BF))
+    r_out = RowsOut(low, wide, low)
     h_in = HeadsIn(low, ((pairs, 2, rows), F32), low, twice, twice)
-    h_out = HeadsOut(low, ((rows, 2 * width), F32), twice)
+    h_out = HeadsOut(low, twice, twice)
     h_work = HeadsWork(*[((pairs, length, 256), BF)] * 2, *[((pairs, length, 128), F32)] * 2)
     args, outs, out_specs, scratch = [], [], [], [low]
     if which & ROWS:
@@ -854,8 +873,11 @@
     if which == HEADS:
         args.append(d_mixed)
     if which == ROWS:
-        outs.append(low)
-        out_specs.append(IN_HBM)
+        half_up = ((width, hidden // 2), BF)
+        args += [f.x1_low, early]
+        outs += [low, half_up, half_up]
+        out_specs += [IN_HBM] * 3
+        scratch += [low, ((width, hidden), BF), half_up, half_up]
     if which & HEADS:
         outs += list(h_out)
         out_specs += [IN_HBM] * len(h_out)
@@ -988,20 +1010,19 @@
     f: Any
 
 
-def forward_tick(save, slot_of, h, w, beside=()):
+def forward_tick(save, slot_of, h, w):
     kv = (dot_nn(h, w.kv) + w.bkv).astype(BF)
     kvp = to_peer(kv)
     q = (dot_nn(h, w.q) + w.bq).astype(BF)
-    q, *beside = tied(q, *beside) if beside else (q,)
     f = forward_call(save, slot_of, w, q, kv, kvp, h)
-    return f.out, Saved(h, q, kv, kvp, f), beside
+    return f.out, Saved(h, q, kv, kvp, f)
 
 
 def backward_end(b, w):
     other = to_peer(b.far)
     from_q = dot_nt(b.dq, w.q)
-    dkv = (b.near + other.astype(F32)).astype(BF)
-    return (b.d1 + from_q + dot_nt(dkv, w.kv)).astype(BF), b._replace(dkv=dkv)
+    dkv = add_low(b.near, other)
+    return (b.d1_low.astype(F32) + from_q + dot_nt(dkv, w.kv)).astype(BF), b._replace(dkv=dkv)
 
 
 def backward_tick(slot_of, g, s, w):
@@ -1035,10 +1056,10 @@
     half = attention_in.shape[3]
     hidden = up_weight.shape[2]
 
-    crossed = [lax.ppermute(jnp.where(first, grad_out[s], tokens[s]), "section", SWAP) for s in range(2)]
+    crossed = lax.ppermute(jnp.where(first, grad_out[0], tokens[0]), "section", SWAP)
     from_rows = lambda x, s: jnp.concatenate([tokens[s], x], axis=0)
     cot_rows = lambda x, s: jnp.concatenate([x, grad_out[s]], axis=0)
-    tok0, cot0 = from_rows(crossed[0], 0), cot_rows(crossed[0], 0)
+    tok0, cot0 = from_rows(crossed, 0), cot_rows(crossed, 0)
     win, win_far = attention_in[0], to_peer(attention_in[0])
     ab, ab_far = attention_bias[0], to_peer(attention_bias)[0]
     bv = jnp.concatenate([ab[1], ab_far[1]])
@@ -1066,39 +1087,39 @@
     slot_a = lambda s: 1 - s
     slot_b = lambda s: s
 
-    out1, _, (crossed1,) = forward_tick(False, slot_one, tok0, w, (crossed[1],))
-    tok1, cot1 = from_rows(crossed1, 1), cot_rows(crossed1, 1)
-    out2, saved2, _ = forward_tick(True, slot_a, jnp.where(first, tok1, next_section(out1)), w)
+    out1, _ = forward_tick(False, slot_one, tok0, w)
+    tok1 = from_rows(last_section(tokens[1]), 1)
+    out2, saved2 = forward_tick(True, slot_a, jnp.where(first, tok1, next_section(out1)), w)
     away2 = next_section(out2)
     g3, b3 = backward_tick(slot_a, cot0, saved2, w)
-    away2, _ = tied(away2, b3.d1_low)
-    out4, saved4, _ = forward_tick(True, slot_b, jnp.where(first, tok0, away2), w)
+    away2, rows1, _ = tied(away2, grad_out[1], b3.d2_low)
+    cot1 = cot_rows(next_section(rows1), 1)
+    out4, saved4 = forward_tick(True, slot_b, jnp.where(first, tok0, away2), w)
     g5, b5 = backward_tick(slot_b, jnp.where(first, last_section(g3), cot1), saved4, w)
 
     early = gradient_call(saved4, b5)
     g6_in = jnp.where(first, last_section(g5), cot0)
 
     f6 = saved2.f
-    d2_low = norm_back(g6_in.astype(F32), f6.n2, f6.inv2[:, :1], w.ng[1]).astype(BF)
+    d2_low = norm_back(g6_in.astype(F32), f6.n2.astype(F32), f6.inv2[:, :1], w.ng[1]).astype(BF)
     down_far = half_gradient_call(d2_low, f6.act, d2_low, early[0], 1, True)
     down_own = half_gradient_call(down_far, f6.act, d2_low, early[0], 0, True)
     down = Sum(add_low(down_own, to_peer(down_far)), dp_size)
-    r6 = backward_call(ROWS, slot_a, w, g6_in, f6, None, None, None, None, (down.sent,))
-    b6 = Back(*r6[:6], None, None, None, None)
-    up_far = half_gradient_call(b6.d1_low, f6.x1_low, b6.d_pre, early[1], 1, False)
+    r6 = backward_call(ROWS, slot_a, w, g6_in, f6, None, None, None, None, (down.sent,), early[1])
+    b6 = Back(*r6[:5], None, None, None, None)
+    d_mixed, up_own, up_far = r6[5:]
     (up_far,) = step_sums([down], up_far)
     up_in = to_peer(up_far)
-    up_own = half_gradient_call(up_far, f6.x1_low, b6.d_pre, early[1], 0, False)
     up = Sum(add_low(up_own, up_in), dp_size)
     quarters = jnp.concatenate([out2[:quarter], out4[:quarter]], axis=0)
     dq, near, far = backward_call(
-        HEADS, slot_a, w, None, f6, saved2.q, saved2.kv, saved2.kvp, r6[6], (down.sent, up.sent)
+        HEADS, slot_a, w, None, f6, saved2.q, saved2.kv, saved2.kvp, d_mixed, (down.sent, up.sent)
     )
     dq, near, far, quarters = step_sums([down, up], dq, near, far, quarters)
     layer_far = last_section(quarters)
     g6, b6 = backward_end(b6._replace(dq=dq, near=near, far=far), w)
     out_own, out_far, in_own, in_far, small_own, small_far = last_gradient_call(up.sent, saved2, b6, early, b5)
-    out_far, in_far, small_far = step_sums([down, up], out_far, in_far, small_far)
+    out_far, in_far, small_far, tick = step_sums([down, up], out_far, in_far, small_far, b6.bias_sums)
     tokens_far = next_section(jnp.concatenate([g5[quarter:], g6[quarter:]], axis=0))
     in_g = add_low(in_own, to_peer(in_far))
     small = small_own + to_peer(small_far)
@@ -1108,14 +1129,19 @@
     part = lambda x, i: x[i * x.shape[0] // 2 : (i + 1) * x.shape[0] // 2]
     in_a, in_b = Sum(part(in_g, 0), dp_size), Sum(part(in_g, 1), dp_size)
     last = Sum(out_g, dp_size)
-    step_sums([down, up, in_a])
-    step_sums([up, in_a, in_b])
-    (layer_far,) = step_sums([down, in_a, in_b, last], layer_far)
-    step_sums([up, in_a, in_b, last])
-    (tokens_far,) = step_sums([in_a, in_b, last], tokens_far)
-    sums = [down, up, in_a, in_b, last]
+    (tick,) = step_sums([in_a], tick)
+    (tick,) = step_sums([in_b], tick)
+    (tick,) = step_sums([down, up], tick)
+    (tick,) = step_sums([in_a, last], tick)
+    tick, layer_far = step_sums([in_b], tick, layer_far)
+    (tick,) = step_sums([in_a, last], tick)
+    (tick,) = step_sums([up, in_b], tick)
+    (tick,) = step_sums([in_a, last], tick)
+    (tick,) = step_sums([down, in_b], tick)
+    tick, tokens_far = step_sums([last], tick, tokens_far)
+    sums = [up, in_a, in_b, last, down]
     while any(one.whole is None for one in sums):
-        step_sums(sums)
+        (tick,) = step_sums(sums, tick)
     down_s = down.whole.astype(F32)
     up_s = up.whole.astype(F32)
     in_s = jnp.concatenate([in_a.whole, in_b.whole], axis=0).astype(F32)

time: 539 us -> 525 us (0.974)
  waiting for transfers between devices: 143 us -> 107 us
  starting transfers between devices: 65.4 us -> 82.3 us
  other arithmetic: 60.8 us -> 71.6 us
  Pallas kernels: 206 us -> 197 us
    ppermute x3 -> x4, waiting for transfers between devices: 21.2 us -> 7.1 us  [next_section(): return lax.ppermute(x, 'section', [(0, 1)])]
    ppermute x10, waiting for transfers between devices: 35.6 us -> 22.1 us  [walk(): total = add_low(total, (yield lax.ppermute(total, 'dp', moves)))]
    ppermute x5, waiting for transfers between devices: 15.8 us -> 2.36 us  [walk(): lax.ppermute(total, 'dp', moves)]
    pallas_call x4 -> x2, Pallas kernels: 19.8 us -> 9.85 us  [half_gradient_call(): pl.pallas_call(functools.partial(half_gradient_kernel, k, by_rows), out_s...]
    ppermute x3 -> x4, waiting for transfers between devices: 3.65 us -> 13 us  [last_section(): return lax.ppermute(x, 'section', [(1, 0)])]
    convert_element_type x19 -> x21, other arithmetic: 27.9 us -> 36.7 us  [add_low(): return (a.astype(F32) + b.astype(F32)).astype(BF)]
    ppermute x2 -> x1, waiting for transfers between devices: 14.6 us -> 6.47 us  [on_device(): lax.ppermute(jnp.where(first, grad_out[0], tokens[0]), 'section', SWAP)]
    ppermute x3 -> x4, starting transfers between devices: 11.2 us -> 18.1 us  [last_section(): return lax.ppermute(x, 'section', [(1, 0)])]
  transfers between devices with their start and end apart: 51 -> 52, of which waited for: 27 -> 23; matrix products, arithmetic and copies ran while one was open for 15% -> 16% of each run, Pallas kernels for 23% -> 23%
where the time goes in v3:
time: 525 us; the launch traced here: 516 us
  Pallas kernels  197 us (38%)
  waiting for transfers between devices  107 us (20%)
  starting transfers between devices  82.3 us (16%)
  other arithmetic  71.6 us (14%)
  local copies, waits for them, and re-layouts  30.7 us (6%)
  matrix products  25.4 us (5%)
    pallas_call x4, Pallas kernels, backward_call(): pl.pallas_call(functools.partial(backward_kernel, which, slot_of, len(tok...  97.6 us
    pallas_call x3, Pallas kernels, forward_call(): pl.pallas_call(functools.partial(forward_kernel, save, slot_of, len(token...  67.8 us
    convert_element_type x21, other arithmetic, add_low(): return (a.astype(F32) + b.astype(F32)).astype(BF)  36.7 us
    ppermute x5, waiting for transfers between devices, walk(): total = add_low(keep, (yield lax.ppermute(send, 'dp', pairs)))  26.7 us
    ppermute x10, starting transfers between devices, walk(): total = add_low(total, (yield lax.ppermute(total, 'dp', moves)))  22.6 us
    ppermute x10, waiting for transfers between devices, walk(): total = add_low(total, (yield lax.ppermute(total, 'dp', moves)))  22.1 us
    ppermute x5, waiting for transfers between devices, walk(): got = (yield lax.ppermute(total, 'dp', pairs))  21.7 us
    unnamed x206, local copies, waits for them, and re-layouts  19.1 us
  transfers between devices with their start and end apart: 52, of which 23 were waited for; matrix products, arithmetic and copies ran while one was open for 16% of the time, Pallas kernels for 23%

profile of v3, /device:TPU:14, one launch (start us, length us, event | category | flops | bytes accessed | tf_op | source)
XLA Modules:
  0.0 516.1 jit_solution(2476443664244619096)
XLA Ops:
  4.9 2.2 slice_bitcast_fusion.3
  7.1 6.5 %collective-permute-done.3 = bf16[256,768]{1,0:T(8,128)(2,1)S(1)} collective-permute-done((bf16[256,768]{1,0:T(8,128)(2,1)S(1)}, bf16[256,768]{1,0:T(8,128)(2,1)S(1)}, u32[]{:S(2)}, u32[]{:S(2)}) %collective-permute-start.3) | collective-permute-done | bytes 393248 | tf_op jit(solution)/shard_map/ppermute | solution.py:1059
  13.6 2.2 fusion.refs_1_
  17.9 2.3 collective-permute-done.shift_far
  24.9 21.3 %layer_forward.3 = bf16[512,768]{1,0:T(8,128)(2,1)} custom-call(s32[2]{0:T(128)} %counts.13, s32[2]{0:T(128)} %lengths.13, s32[1,6]{1,0:T(1,128)} %shift_own.13, s32[1,6]{1,0:T(1,128)} %copy-done.96, f32[4,768]{1,0:T(4,128)} %bitcast.144, f32[2,768]{1,0:T(2,128)} %bitcast.137, f32[1,1536]{1,0:T(1,128)} %bup_own.5, f32[1,1536]{1,0:T(1,128)} %copy-done.92, ...), custom_call_target="tpu_custom_call" | custom-call | flops 1 | bytes 1 | tf_op jit(solution)/shard_map/layer_forward/pallas_call | solution.py:471
  47.6 4.6 collective-permute-start.2
  52.2 9.3 %collective-permute-done.2 = bf16[256,768]{1,0:T(8,128)(2,1)S(1)} collective-permute-done((bf16[256,768]{1,0:T(8,128)(2,1)}, bf16[256,768]{1,0:T(8,128)(2,1)S(1)}, u32[]{:S(2)}, u32[]{:S(2)}) %collective-permute-start.2) | collective-permute-done | bytes 393248 | tf_op jit(solution)/shard_map/ppermute | solution.py:908
  61.5 7.1 %collective-permute-done.10 = bf16[512,768]{1,0:T(8,128)(2,1)S(1)} collective-permute-done((bf16[512,768]{1,0:T(8,128)(2,1)}, bf16[512,768]{1,0:T(8,128)(2,1)S(1)}, u32[]{:S(2)}, u32[]{:S(2)}) %collective-permute-start.10) | collective-permute-done | bytes 786464 | tf_op jit(solution)/shard_map/ppermute | solution.py:904
  69.9 2.2 fusion.1.refs_1_.refs_15_.refs_5_
  76.7 22.0 %layer_forward.4 = (bf16[512,768]{1,0:T(8,128)(2,1)}, bf16[512,768]{1,0:T(8,128)(2,1)}, f32[6,2,512]{2,1,0:T(2,128)}, bf16[512,768]{1,0:T(8,128)(2,1)}, bf16[512...) custom-call(s32[2]{0:T(128)} %counts.13, ...), custom_call_target="tpu_custom_call" | custom-call | flops 1 | bytes 1 | tf_op jit(solution)/shard_map/layer_forward/pallas_call | solution.py:471
  100.4 28.8 %layer_backward.4 = (bf16[512,768]{1,0:T(8,128)(2,1)}, bf16[512,3072]{1,0:T(8,128)(2,1)}, bf16[512,768]{1,0:T(8,128)(2,1)}, f32[8,768]{1,0:T(8,128)}, f32[1,3072...) custom-call(s32[2]{0:T(128)} %counts.13, s32[2]{0:T(128)} %lengths.13, ...), custom_call_target="tpu_custom_call" | custom-call | flops 1 | bytes 1 | tf_op jit(solution)/shard_map/layer_backward/pallas_call | solution.py:884
  129.2 5.8 %collective-permute-start.12 = (bf16[512,1536]{1,0:T(8,128)(2,1)}, bf16[512,1536]{1,0:T(8,128)(2,1)}, u32[]{:S(2)}, u32[]{:S(2)}) collective-permute-start(bf16[512,1536]{1,0:T(8,128)(2,1)} %get-tuple-element.122), channel_id=1, source_target_pairs={{0,8},{8,0},{1,9},{9,1},{2,10},{10,2},{3,11},{11,3},{4,12},{12,4},... | collective-permute-start | bytes 4718600 | tf_op jit(solution)/shard_map/ppermute | solution.py:900
  138.2 2.1 fusion.2.refs_1_.refs_15_
  142.5 3.8 add_convert_fusion.14
  146.3 4.0 collective-permute-start.13
  154.5 24.5 %layer_forward.5 = (bf16[512,768]{1,0:T(8,128)(2,1)}, bf16[512,768]{1,0:T(8,128)(2,1)}, f32[6,2,512]{2,1,0:T(2,128)}, bf16[512,768]{1,0:T(8,128)(2,1)}, bf16[512...) custom-call(s32[2]{0:T(128)} %counts.13, ...), custom_call_target="tpu_custom_call" | custom-call | flops 1 | bytes 1 | tf_op jit(solution)/shard_map/layer_forward/pallas_call | solution.py:471
  180.1 32.5 %layer_backward.5 = (bf16[512,768]{1,0:T(8,128)(2,1)}, bf16[512,3072]{1,0:T(8,128)(2,1)}, bf16[512,768]{1,0:T(8,128)(2,1)}, f32[8,768]{1,0:T(8,128)}, f32[1,3072...) custom-call(s32[2]{0:T(128)} %counts.13, s32[2]{0:T(128)} %lengths.13, ...), custom_call_target="tpu_custom_call" | custom-call | flops 1 | bytes 1 | tf_op jit(solution)/shard_map/layer_backward/pallas_call | solution.py:884
  212.7 2.0 fusion.15
  217.6 2.1 add_convert_fusion.12
  219.7 4.2 collective-permute-start.18
  224.1 12.9 %layer_gradient.1 = (bf16[3072,768]{1,0:T(8,128)(2,1)}, bf16[768,3072]{1,0:T(8,128)(2,1)}, bf16[768,768]{1,0:T(8,128)(2,1)}, bf16[768,768]{1,0:T(8,128)(2,1)}, b...) custom-call(bf16[512,3072]{1,0:T(8,128)(2,1)} %get-tuple-element.139.refs_0_, bf16[512,768]{1,0:T(8,128)(2,1)} %get-tuple-element.140.refs_1_, ...), custom_call_target="tpu_custom_call" | custom-call | flops 1 | bytes 1 | tf_op jit(solution)/shard_map/layer_gradient/pallas_call | solution.py:729
  237.0 3.7 collective-permute-done.18
  242.7 4.9 half_gradient.2.token
  247.7 4.9 half_gradient.3
  252.6 3.0 add_convert_fusion.1
  256.7 19.7 %layer_backward.6 = (bf16[512,768]{1,0:T(8,128)(2,1)}, bf16[512,3072]{1,0:T(8,128)(2,1)}, bf16[512,768]{1,0:T(8,128)(2,1)}, f32[8,768]{1,0:T(8,128)}, f32[1,3072...) custom-call(s32[2]{0:T(128)} %counts.13, s32[2]{0:T(128)} %lengths.13, ...), custom_call_target="tpu_custom_call" | custom-call | flops 1 | bytes 1 | tf_op jit(solution)/shard_map/layer_backward/pallas_call | solution.py:884
  276.5 7.7 %collective-permute-done.20.refs_0_ = bf16[768,768]{1,0:T(8,128)(2,1)S(1)} collective-permute-done((bf16[768,768]{1,0:T(8,128)(2,1)S(1)}, bf16[768,768]{1,0:T(8,128)(2,1)S(1)}, u32[]{:S(2)}, u32[]{:S(2)}) %collective-permute-start.20) | collective-permute-done | bytes 1179680 | tf_op jit(solution)/shard_map/ppermute | solution.py:956
  290.0 2.3 add_convert_fusion
  296.6 16.5 %layer_backward.7 = (bf16[512,768]{1,0:T(8,128)(2,1)}, bf16[512,1536]{1,0:T(8,128)(2,1)}, bf16[512,1536]{1,0:T(8,128)(2,1)}) custom-call(s32[2]{0:T(128)} %counts.13, s32[2]{0:T(128)} %lengths.13, s32[1,6]{1,0:T(1,128)} %shift_own.13, s32[1,6]{1,0:T(1,128)} %copy-done.96, f32[2,768]{1,0:T(2,128)} %bitcast.143, bf16[768,768]{1,0:T(8,128)(2,1)} %copy-done.9, ...), custom_call_target="tpu_custom_call" | custom-call | flops 1 | bytes 1 | tf_op jit(solution)/shard_map/layer_backward/pallas_call | solution.py:884
  313.1 4.0 collective-permute-done.22.refs_0_
  317.1 3.4 collective-permute-done.23.refs_1_
  327.0 4.4 collective-permute-start.25
  331.5 2.1 slice_bitcast_fusion.8
  333.6 5.3 %collective-permute-start.37 = (bf16[512,768]{1,0:T(8,128)(2,1)}, bf16[512,768]{1,0:T(8,128)(2,1)}, u32[]{:S(2)}, u32[]{:S(2)}) collective-permute-start(bf16[512,768]{1,0:T(8,128)(2,1)} %get-tuple-element.187), channel_id=1, source_target_pairs={{16,0},{17,1},{18,2},{19,3},{20,4},{21,5},{22,6},{23,7},{24,8},{25... | collective-permute-start | bytes 2359304 | tf_op jit(solution)/shard_map/ppermute | solution.py:908
  338.9 3.2 fusion.14
  342.1 2.9 add_convert_fusion.3.refs_5_
  345.0 8.9 %last_gradient.1 = (bf16[384,768]{1,0:T(8,128)(2,1)}, bf16[384,768]{1,0:T(8,128)(2,1)}, bf16[2304,384]{1,0:T(8,128)(2,1)}, bf16[2304,384]{1,0:T(8,128)(2,1)}, f32[16,768]{1,0:T(8,128)}, /*index=5*/f32[16,768]{1,0:T(8,128)}) custom-call(bf16[384,1536]{1,0:T(8,128)(2,1)} %copy-done.7, bf16[512,768]{1,0:T(8,128)(2,1)} %get-tuple-element.117.refs_12_.refs_2_.refs_1_, ...), custom_call_target="tpu_custom_call" | custom-call | flops 1 | bytes 1 | tf_op jit(solution)/shard_map/last_gradient/pallas_call | solution.py:828
  354.0 2.9 collective-permute-done.25.refs_0_
  359.9 3.6 collective-permute-start.36
  363.6 2.7 add_convert_fusion.8
  367.8 2.1 add_convert_fusion.11
  377.8 8.4 %collective-permute-done.29.refs_0_ = bf16[576,384]{1,0:T(8,128)(2,1)} collective-permute-done((bf16[576,384]{1,0:T(8,128)(2,1)S(1)}, bf16[576,384]{1,0:T(8,128)(2,1)}, u32[]{:S(2)}, u32[]{:S(2)}) %collective-permute-start.29) | collective-permute-done | bytes 442400 | tf_op jit(solution)/shard_map/ppermute | solution.py:956
  387.5 7.3 %collective-permute-done.28.refs_0_ = bf16[576,384]{1,0:T(8,128)(2,1)} collective-permute-done((bf16[576,384]{1,0:T(8,128)(2,1)}, bf16[576,384]{1,0:T(8,128)(2,1)}, u32[]{:S(2)}, u32[]{:S(2)}) %collective-permute-start.28) | collective-permute-done | bytes 442400 | tf_op jit(solution)/shard_map/ppermute | solution.py:956
  395.3 2.1 fusion.11
  405.1 5.8 %collective-permute-start.42 = (bf16[384,1536]{1,0:T(8,128)(2,1)S(1)}, bf16[384,1536]{1,0:T(8,128)(2,1)}, u32[]{:S(2)}, u32[]{:S(2)}) collective-permute-start(bf16[384,1536]{1,0:T(8,128)(2,1)S(1)} %add_convert_fusion.6), channel_id=1, source_target_pairs={{2,0},{3,1},{4,6},{5,7},{10,8},{11,9},{12,14},{13,15},{18,16},{19,... | collective-permute-start | bytes 3538952 | tf_op jit(solution)/shard_map/ppermute | solution.py:967
  410.9 3.8 collective-permute-done.31.refs_0_
  421.3 2.3 collective-permute-done.30.refs_0_
  423.6 2.2 collective-permute-start.38
  425.8 2.1 add_convert_fusion.19
  429.2 3.4 collective-permute-start.43
  432.5 5.8 %collective-permute-done.38.refs_0_ = bf16[576,384]{1,0:T(8,128)(2,1)} collective-permute-done((bf16[576,384]{1,0:T(8,128)(2,1)}, bf16[576,384]{1,0:T(8,128)(2,1)}, u32[]{:S(2)}, u32[]{:S(2)}) %collective-permute-start.38) | collective-permute-done | bytes 442400 | tf_op jit(solution)/shard_map/ppermute | solution.py:963
  442.1 2.0 add_convert_fusion.20
  444.1 3.0 collective-permute-done.43.refs_1_
  447.2 2.1 collective-permute-start.40
  451.2 2.1 collective-permute-start.46
  456.3 2.3 collective-permute-done.40.refs_0_
  460.5 5.2 %collective-permute-start.44 = (bf16[208,768]{1,0:T(8,128)(2,1)}, bf16[208,768]{1,0:T(8,128)(2,1)}, u32[]{:S(2)}, u32[]{:S(2)}) collective-permute-start(bf16[208,768]{1,0:T(8,128)(2,1)} %add_convert_fusion.22), channel_id=1, source_target_pairs={{2,0},{3,1},{4,6},{5,7},{10,8},{11,9},{12,14},{13,15},{18,16},{19,... | collective-permute-start | bytes 958472 | tf_op jit(solution)/shard_map/ppermute | solution.py:967
  467.6 2.1 collective-permute-start.49
  474.9 2.5 maximum_convert_fusion.1
  477.5 2.1 maximum_select_fusion.3
  479.6 13.6 %collective-permute-done.49.refs_1_ = bf16[576,384]{1,0:T(8,128)(2,1)} collective-permute-done((bf16[576,384]{1,0:T(8,128)(2,1)}, bf16[576,384]{1,0:T(8,128)(2,1)}, u32[]{:S(2)}, u32[]{:S(2)}) %collective-permute-start.49) | collective-permute-done | bytes 442400 | tf_op jit(solution)/shard_map/ppermute | solution.py:968
  493.2 8.1 %collective-permute-done.51.refs_3_ = bf16[208,768]{1,0:T(8,128)(2,1)S(1)} collective-permute-done((bf16[208,768]{1,0:T(8,128)(2,1)S(1)}, bf16[208,768]{1,0:T(8,128)(2,1)S(1)}, u32[]{:S(2)}, u32[]{:S(2)}) %collective-permute-start.51) | collective-permute-done | bytes 319520 | tf_op jit(solution)/shard_map/ppermute | solution.py:968
  511.1 2.0 convert_bitcast_fusion
  513.1 2.8 maximum_convert_fusion
  (362 shorter events, 110.0 us)
Async XLA Ops:
  0.7 4.3 collective-permute-start.4
  2.1 11.5 %collective-permute-start.3 = (bf16[256,768]{1,0:T(8,128)(2,1)S(1)}, bf16[256,768]{1,0:T(8,128)(2,1)S(1)}, u32[]{:S(2)}, u32[]{:S(2)}) collective-permute-start(bf16[256,768]{1,0:T(8,128)(2,1)S(1)} %broadcast_select_fusion.10), channel_id=1, source_target_pairs={{0,16},{16,0},{1,17},{17,1},{2,18},{18,2},{3,19},{19,3},{4,20},{20... | collective-permute-start | bytes 1179656 | tf_op jit(solution)/shard_map/ppermute | solution.py:1059
  2.7 2.2 collective-permute-start.5
  2.8 19.2 %collective-permute-start.8 = (bf16[768,1536]{1,0:T(8,128)(2,1)}, bf16[768,1536]{1,0:T(8,128)(2,1)S(1)}, u32[]{:S(2)}, u32[]{:S(2)}) collective-permute-start(bf16[768,1536]{1,0:T(8,128)(2,1)} %bitcast.103), channel_id=1, source_target_pairs={{0,8},{8,0},{1,9},{9,1},{2,10},{10,2},{3,11},{11,3},{4,12},{12,4},... | collective-permute-start | bytes 7077896 | tf_op jit(solution)/shard_map/ppermute | solution.py:900
  3.2 18.9 %collective-permute-start.9 = (bf16[1536,768]{1,0:T(8,128)(2,1)}, bf16[1536,768]{1,0:T(8,128)(2,1)S(1)}, u32[]{:S(2)}, u32[]{:S(2)}) collective-permute-start(bf16[1536,768]{1,0:T(8,128)(2,1)} %bitcast.110), channel_id=1, source_target_pairs={{0,8},{8,0},{1,9},{9,1},{2,10},{10,2},{3,11},{11,3},{4,12},{12,4},... | collective-permute-start | bytes 7077896 | tf_op jit(solution)/shard_map/ppermute | solution.py:900
  4.9 15.4 %copy-start.79 = (bf16[768,384]{1,0:T(8,128)(2,1)}, bf16[768,384]{1,0:T(8,128)(2,1)S(1)}, u32[]{:S(2)}) copy-start(bf16[768,384]{1,0:T(8,128)(2,1)S(1)} %get-tuple-element.229) | copy-start | bytes 1769476
  7.1 13.2 %copy-start.84 = (bf16[768,384]{1,0:T(8,128)(2,1)}, bf16[768,384]{1,0:T(8,128)(2,1)S(1)}, u32[]{:S(2)}) copy-start(bf16[768,384]{1,0:T(8,128)(2,1)S(1)} %get-tuple-element.232) | copy-start | bytes 1769476
  15.8 6.2 %collective-permute-start.6 = (bf16[512,1536]{1,0:T(8,128)(2,1)S(1)}, bf16[512,1536]{1,0:T(8,128)(2,1)S(1)}, u32[]{:S(2)}, u32[]{:S(2)}) collective-permute-start(bf16[512,1536]{1,0:T(8,128)(2,1)S(1)} %fusion.refs_1_), channel_id=1, source_target_pairs={{0,8},{8,0},{1,9},{9,1},{2,10},{10,2},{3,11},{11,3},{4,12},{12,4},... | collective-permute-start | bytes 4718600 | tf_op jit(solution)/shard_map/ppermute | solution.py:900
  15.9 6.1 %collective-permute-start.7 = (bf16[384,768]{1,0:T(8,128)(2,1)S(1)}, bf16[384,768]{1,0:T(8,128)(2,1)S(1)}, u32[]{:S(2)}, u32[]{:S(2)}) collective-permute-start(bf16[384,768]{1,0:T(8,128)(2,1)S(1)} %bitcast.123), channel_id=1, source_target_pairs={{0,8},{8,0},{1,9},{9,1},{2,10},{10,2},{3,11},{11,3},{4,12},{12,4},... | collective-permute-start | bytes 1769480 | tf_op jit(solution)/shard_map/ppermute | solution.py:900
  16.4 3.7 collective-permute-start
  20.2 1.8 collective-permute-start.1
  46.1 23.7 %copy-start.65 = (bf16[768,384]{1,0:T(8,128)(2,1)S(1)}, bf16[768,384]{1,0:T(8,128)(2,1)}, u32[]{:S(2)}) copy-start(bf16[768,384]{1,0:T(8,128)(2,1)} %copy-done.64) | copy-start | bytes 1769476
  46.1 23.7 %copy-start.68 = (bf16[768,384]{1,0:T(8,128)(2,1)S(1)}, bf16[768,384]{1,0:T(8,128)(2,1)}, u32[]{:S(2)}) copy-start(bf16[768,384]{1,0:T(8,128)(2,1)} %copy-done.67) | copy-start | bytes 1769476
  46.2 23.7 %copy-start.71 = (bf16[768,384]{1,0:T(8,128)(2,1)S(1)}, bf16[768,384]{1,0:T(8,128)(2,1)}, u32[]{:S(2)}) copy-start(bf16[768,384]{1,0:T(8,128)(2,1)} %copy-done.70) | copy-start | bytes 1769476
  46.2 23.7 %copy-start.75 = (bf16[768,384]{1,0:T(8,128)(2,1)S(1)}, bf16[768,384]{1,0:T(8,128)(2,1)}, u32[]{:S(2)}) copy-start(bf16[768,384]{1,0:T(8,128)(2,1)} %copy-done.74) | copy-start | bytes 1769476
  46.2 22.4 %collective-permute-start.10 = (bf16[512,768]{1,0:T(8,128)(2,1)}, bf16[512,768]{1,0:T(8,128)(2,1)S(1)}, u32[]{:S(2)}, u32[]{:S(2)}) collective-permute-start(bf16[512,768]{1,0:T(8,128)(2,1)} %layer_forward.3), channel_id=1, source_target_pairs={{0,16},{1,17},{2,18},{3,19},{4,20},{5,21},{6,22},{7,23},{8,24},{9,... | collective-permute-start | bytes 2359304 | tf_op jit(solution)/shard_map/ppermute | solution.py:904
  47.6 13.9 %collective-permute-start.2 = (bf16[256,768]{1,0:T(8,128)(2,1)}, bf16[256,768]{1,0:T(8,128)(2,1)S(1)}, u32[]{:S(2)}, u32[]{:S(2)}) collective-permute-start(bf16[256,768]{1,0:T(8,128)(2,1)} %get-tuple-element.247), channel_id=1, source_target_pairs={{16,0},{17,1},{18,2},{19,3},{20,4},{21,5},{22,6},{23,7},{24,8},{25... | collective-permute-start | bytes 1179656 | tf_op jit(solution)/shard_map/ppermute | solution.py:908
  72.0 3.5 collective-permute-start.11
  98.7 37.1 %collective-permute-start.14 = (bf16[512,768]{1,0:T(8,128)(2,1)}, bf16[512,768]{1,0:T(8,128)(2,1)S(1)}, u32[]{:S(2)}, u32[]{:S(2)}) collective-permute-start(bf16[512,768]{1,0:T(8,128)(2,1)} %get-tuple-element.123), channel_id=1, source_target_pairs={{0,16},{1,17},{2,18},{3,19},{4,20},{5,21},{6,22},{7,23},{8,24},{9,... | collective-permute-start | bytes 2359304 | tf_op jit(solution)/shard_map/ppermute | solution.py:904
  129.2 12.3 %collective-permute-start.12 = (bf16[512,1536]{1,0:T(8,128)(2,1)}, bf16[512,1536]{1,0:T(8,128)(2,1)}, u32[]{:S(2)}, u32[]{:S(2)}) collective-permute-start(bf16[512,1536]{1,0:T(8,128)(2,1)} %get-tuple-element.122), channel_id=1, source_target_pairs={{0,8},{8,0},{1,9},{9,1},{2,10},{10,2},{3,11},{11,3},{4,12},{12,4},... | collective-permute-start | bytes 4718600 | tf_op jit(solution)/shard_map/ppermute | solution.py:900
  138.1 13.5 %copy-start.14 = (bf16[512,768]{1,0:T(8,128)(2,1)}, bf16[512,768]{1,0:T(8,128)(2,1)S(1)}, u32[]{:S(2)}) copy-start(bf16[512,768]{1,0:T(8,128)(2,1)S(1)} %broadcast_select_fusion.3.refs_3_.refs_6_) | copy-start | bytes 2359300
  140.3 13.0 %collective-permute-start.16 = (bf16[512,1536]{1,0:T(8,128)(2,1)S(1)}, bf16[512,1536]{1,0:T(8,128)(2,1)S(1)}, u32[]{:S(2)}, u32[]{:S(2)}) collective-permute-start(bf16[512,1536]{1,0:T(8,128)(2,1)S(1)} %fusion.2.refs_1_.refs_15_), channel_id=1, source_target_pairs={{0,8},{8,0},{1,9},{9,1},{2,10},{10,2},{3,11},{11,3},{4,12},{12,4},... | collective-permute-start | bytes 4718600 | tf_op jit(solution)/shard_map/ppermute | solution.py:900
  146.3 32.7 %collective-permute-start.13 = (bf16[512,768]{1,0:T(8,128)(2,1)}, bf16[512,768]{1,0:T(8,128)(2,1)S(1)}, u32[]{:S(2)}, u32[]{:S(2)}) collective-permute-start(bf16[512,768]{1,0:T(8,128)(2,1)} %add_convert_fusion.14), channel_id=1, source_target_pairs={{16,0},{17,1},{18,2},{19,3},{20,4},{21,5},{22,6},{23,7},{24,8},{25... | collective-permute-start | bytes 2359304 | tf_op jit(solution)/shard_map/ppermute | solution.py:908
  150.4 28.7 %collective-permute-start.15 = (bf16[256,768]{1,0:T(8,128)(2,1)S(1)}, bf16[256,768]{1,0:T(8,128)(2,1)S(1)}, u32[]{:S(2)}, u32[]{:S(2)}) collective-permute-start(bf16[256,768]{1,0:T(8,128)(2,1)S(1)} %copy-done.55), channel_id=1, source_target_pairs={{0,16},{1,17},{2,18},{3,19},{4,20},{5,21},{6,22},{7,23},{8,24},{9,... | collective-permute-start | bytes 1179656 | tf_op jit(solution)/shard_map/ppermute | solution.py:904
  180.1 32.6 %copy-start.82 = (bf16[768,384]{1,0:T(8,128)(2,1)S(1)}, bf16[768,384]{1,0:T(8,128)(2,1)}, u32[]{:S(2)}) copy-start(bf16[768,384]{1,0:T(8,128)(2,1)} %copy-done.79) | copy-start | bytes 1769476
  180.1 32.6 %copy-start.87 = (bf16[768,384]{1,0:T(8,128)(2,1)S(1)}, bf16[768,384]{1,0:T(8,128)(2,1)}, u32[]{:S(2)}) copy-start(bf16[768,384]{1,0:T(8,128)(2,1)} %copy-done.84) | copy-start | bytes 1769476
  212.6 3.7 collective-permute-start.17
  219.7 17.3 %copy-start.62 = (bf16[512,768]{1,0:T(8,128)(2,1)}, bf16[512,768]{1,0:T(8,128)(2,1)S(1)}, u32[]{:S(2)}) copy-start(bf16[512,768]{1,0:T(8,128)(2,1)S(1)} %add_convert_fusion.12) | copy-start | bytes 2359300
  219.7 21.1 %collective-permute-start.18 = (bf16[512,768]{1,0:T(8,128)(2,1)S(1)}, bf16[512,768]{1,0:T(8,128)(2,1)S(1)}, u32[]{:S(2)}, u32[]{:S(2)}) collective-permute-start(bf16[512,768]{1,0:T(8,128)(2,1)S(1)} %add_convert_fusion.12), channel_id=1, source_target_pairs={{16,0},{17,1},{18,2},{19,3},{20,4},{21,5},{22,6},{23,7},{24,8},{25... | collective-permute-start | bytes 2359304 | tf_op jit(solution)/shard_map/ppermute | solution.py:908
  224.1 16.7 %copy-start.6 = (bf16[512,768]{1,0:T(8,128)(2,1)S(1)}, bf16[512,768]{1,0:T(8,128)(2,1)}, u32[]{:S(2)}) copy-start(bf16[512,768]{1,0:T(8,128)(2,1)} %get-tuple-element.113.refs_1_.refs_2_) | copy-start | bytes 2359300
  224.1 16.7 %copy-start.39 = (bf16[256,768]{1,0:T(8,128)(2,1)S(1)}, bf16[256,768]{1,0:T(8,128)(2,1)}, u32[]{:S(2)}) copy-start(bf16[256,768]{1,0:T(8,128)(2,1)} %copy-done.38) | copy-start | bytes 1179652
  247.6 5.0 collective-permute-start.19
  255.7 28.4 %collective-permute-start.20 = (bf16[768,768]{1,0:T(8,128)(2,1)S(1)}, bf16[768,768]{1,0:T(8,128)(2,1)S(1)}, u32[]{:S(2)}, u32[]{:S(2)}) collective-permute-start(bf16[768,768]{1,0:T(8,128)(2,1)S(1)} %dynamic-slice_bitcast_fusion.1.refs_0_), channel_id=1, source_target_pairs={{0,1},{1,0},{2,3},{3,2},{4,5},{5,4},{6,7},{7,6},{8,9},{9,8},{10,11... | collective-permute-start | bytes 3538952 | tf_op jit(solution)/shard_map/ppermute | solution.py:956
  285.1 4.9 collective-permute-start.21
  286.9 30.3 %collective-permute-start.22 = (bf16[768,768]{1,0:T(8,128)(2,1)S(1)}, bf16[768,768]{1,0:T(8,128)(2,1)S(1)}, u32[]{:S(2)}, u32[]{:S(2)}) collective-permute-start(bf16[768,768]{1,0:T(8,128)(2,1)S(1)} %fusion.3.refs_0_), channel_id=1, source_target_pairs={{0,2},{1,3},{6,4},{7,5},{8,10},{9,11},{14,12},{15,13},{16,18},{17,... | collective-permute-start | bytes 3538952 | tf_op jit(solution)/shard_map/ppermute | solution.py:960
  292.4 28.1 %collective-permute-start.23 = (bf16[384,1536]{1,0:T(8,128)(2,1)S(1)}, bf16[384,1536]{1,0:T(8,128)(2,1)S(1)}, u32[]{:S(2)}, u32[]{:S(2)}) collective-permute-start(bf16[384,1536]{1,0:T(8,128)(2,1)S(1)} %dynamic-slice_bitcast_fusion.refs_1_), channel_id=1, source_target_pairs={{0,1},{1,0},{2,3},{3,2},{4,5},{5,4},{6,7},{7,6},{8,9},{9,8},{10,11... | collective-permute-start | bytes 3538952 | tf_op jit(solution)/shard_map/ppermute | solution.py:956
  321.5 20.5 %collective-permute-start.24 = (bf16[512,1536]{1,0:T(8,128)(2,1)}, bf16[512,1536]{1,0:T(8,128)(2,1)}, u32[]{:S(2)}, u32[]{:S(2)}) collective-permute-start(bf16[512,1536]{1,0:T(8,128)(2,1)} %get-tuple-element.159), channel_id=1, source_target_pairs={{0,8},{8,0},{1,9},{9,1},{2,10},{10,2},{3,11},{11,3},{4,12},{12,4},... | collective-permute-start | bytes 4718600 | tf_op jit(solution)/shard_map/ppermute | solution.py:900
  324.9 29.1 %collective-permute-start.26 = (bf16[384,1536]{1,0:T(8,128)(2,1)S(1)}, bf16[384,1536]{1,0:T(8,128)(2,1)S(1)}, u32[]{:S(2)}, u32[]{:S(2)}) collective-permute-start(bf16[384,1536]{1,0:T(8,128)(2,1)S(1)} %fusion.4.refs_0_), channel_id=1, source_target_pairs={{0,2},{1,3},{6,4},{7,5},{8,10},{9,11},{14,12},{15,13},{16,18},{17,... | collective-permute-start | bytes 3538952 | tf_op jit(solution)/shard_map/ppermute | solution.py:960
  327.0 29.9 %collective-permute-start.25 = (bf16[768,768]{1,0:T(8,128)(2,1)S(1)}, bf16[768,768]{1,0:T(8,128)(2,1)}, u32[]{:S(2)}, u32[]{:S(2)}) collective-permute-start(bf16[768,768]{1,0:T(8,128)(2,1)S(1)} %add_convert_fusion.9), channel_id=1, source_target_pairs={{2,4},{3,5},{4,2},{5,3},{10,12},{11,13},{12,10},{13,11},{18,20},{1... | collective-permute-start | bytes 3538952 | tf_op jit(solution)/shard_map/ppermute | solution.py:963
  333.6 86.3 %collective-permute-start.37 = (bf16[512,768]{1,0:T(8,128)(2,1)}, bf16[512,768]{1,0:T(8,128)(2,1)}, u32[]{:S(2)}, u32[]{:S(2)}) collective-permute-start(bf16[512,768]{1,0:T(8,128)(2,1)} %get-tuple-element.187), channel_id=1, source_target_pairs={{16,0},{17,1},{18,2},{19,3},{20,4},{21,5},{22,6},{23,7},{24,8},{25... | collective-permute-start | bytes 2359304 | tf_op jit(solution)/shard_map/ppermute | solution.py:908
  356.9 15.3 %collective-permute-start.27 = (bf16[2304,384]{1,0:T(8,128)(2,1)}, bf16[2304,384]{1,0:T(8,128)(2,1)S(1)}, u32[]{:S(2)}, u32[]{:S(2)}) collective-permute-start(bf16[2304,384]{1,0:T(8,128)(2,1)} %get-tuple-element.173), channel_id=1, source_target_pairs={{0,8},{8,0},{1,9},{9,1},{2,10},{10,2},{3,11},{11,3},{4,12},{12,4},... | collective-permute-start | bytes 5308424 | tf_op jit(solution)/shard_map/ppermute | solution.py:900
  359.9 39.4 %collective-permute-start.36 = (bf16[384,1536]{1,0:T(8,128)(2,1)S(1)}, bf16[384,1536]{1,0:T(8,128)(2,1)S(1)}, u32[]{:S(2)}, u32[]{:S(2)}) collective-permute-start(bf16[384,1536]{1,0:T(8,128)(2,1)S(1)} %add_convert_fusion.7), channel_id=1, source_target_pairs={{2,4},{3,5},{4,2},{5,3},{10,12},{11,13},{12,10},{13,11},{18,20},{1... | collective-permute-start | bytes 3538952 | tf_op jit(solution)/shard_map/ppermute | solution.py:963
  366.3 34.3 %collective-permute-start.35 = (bf16[768,768]{1,0:T(8,128)(2,1)}, bf16[768,768]{1,0:T(8,128)(2,1)S(1)}, u32[]{:S(2)}, u32[]{:S(2)}) collective-permute-start(bf16[768,768]{1,0:T(8,128)(2,1)} %add_convert_fusion.8), channel_id=1, source_target_pairs={{2,0},{3,1},{4,6},{5,7},{10,8},{11,9},{12,14},{13,15},{18,16},{19,... | collective-permute-start | bytes 3538952 | tf_op jit(solution)/shard_map/ppermute | solution.py:967
  367.7 4.0 collective-permute-start.33
  371.7 2.8 collective-permute-start.32
  373.0 13.2 %collective-permute-start.29 = (bf16[576,384]{1,0:T(8,128)(2,1)S(1)}, bf16[576,384]{1,0:T(8,128)(2,1)}, u32[]{:S(2)}, u32[]{:S(2)}) collective-permute-start(bf16[576,384]{1,0:T(8,128)(2,1)S(1)} %dynamic-slice_bitcast_fusion.2), channel_id=1, source_target_pairs={{0,1},{1,0},{2,3},{3,2},{4,5},{5,4},{6,7},{7,6},{8,9},{9,8},{10,11... | collective-permute-start | bytes 1327112 | tf_op jit(solution)/shard_map/ppermute | solution.py:956
  374.4 20.3 %collective-permute-start.28 = (bf16[576,384]{1,0:T(8,128)(2,1)}, bf16[576,384]{1,0:T(8,128)(2,1)}, u32[]{:S(2)}, u32[]{:S(2)}) collective-permute-start(bf16[576,384]{1,0:T(8,128)(2,1)} %dynamic-slice_bitcast_fusion.3), channel_id=1, source_target_pairs={{0,1},{1,0},{2,3},{3,2},{4,5},{5,4},{6,7},{7,6},{8,9},{9,8},{10,11... | collective-permute-start | bytes 1327112 | tf_op jit(solution)/shard_map/ppermute | solution.py:956
  386.2 86.6 %collective-permute-start.47 = (bf16[512,768]{1,0:T(8,128)(2,1)}, bf16[512,768]{1,0:T(8,128)(2,1)}, u32[]{:S(2)}, u32[]{:S(2)}) collective-permute-start(bf16[512,768]{1,0:T(8,128)(2,1)} %pad_maximum_fusion.6), channel_id=1, source_target_pairs={{0,16},{1,17},{2,18},{3,19},{4,20},{5,21},{6,22},{7,23},{8,24},{9,... | collective-permute-start | bytes 2359304 | tf_op jit(solution)/shard_map/ppermute | solution.py:904
  394.7 10.3 %collective-permute-start.34 = (bf16[208,768]{1,0:T(8,128)(2,1)}, bf16[208,768]{1,0:T(8,128)(2,1)}, u32[]{:S(2)}, u32[]{:S(2)}) collective-permute-start(bf16[208,768]{1,0:T(8,128)(2,1)} %dynamic-slice_bitcast_fusion.4), channel_id=1, source_target_pairs={{0,1},{1,0},{2,3},{3,2},{4,5},{5,4},{6,7},{7,6},{8,9},{9,8},{10,11... | collective-permute-start | bytes 958472 | tf_op jit(solution)/shard_map/ppermute | solution.py:956
  399.3 15.3 %collective-permute-start.31 = (bf16[576,384]{1,0:T(8,128)(2,1)}, bf16[576,384]{1,0:T(8,128)(2,1)}, u32[]{:S(2)}, u32[]{:S(2)}) collective-permute-start(bf16[576,384]{1,0:T(8,128)(2,1)} %fusion.11), channel_id=1, source_target_pairs={{0,2},{1,3},{6,4},{7,5},{8,10},{9,11},{14,12},{15,13},{16,18},{17,... | collective-permute-start | bytes 1327112 | tf_op jit(solution)/shard_map/ppermute | solution.py:960
  400.6 22.9 %collective-permute-start.30 = (bf16[576,384]{1,0:T(8,128)(2,1)}, bf16[576,384]{1,0:T(8,128)(2,1)}, u32[]{:S(2)}, u32[]{:S(2)}) collective-permute-start(bf16[576,384]{1,0:T(8,128)(2,1)} %fusion.12), channel_id=1, source_target_pairs={{0,2},{1,3},{6,4},{7,5},{8,10},{9,11},{14,12},{15,13},{16,18},{17,... | collective-permute-start | bytes 1327112 | tf_op jit(solution)/shard_map/ppermute | solution.py:960
  405.1 44.2 %collective-permute-start.42 = (bf16[384,1536]{1,0:T(8,128)(2,1)S(1)}, bf16[384,1536]{1,0:T(8,128)(2,1)}, u32[]{:S(2)}, u32[]{:S(2)}) collective-permute-start(bf16[384,1536]{1,0:T(8,128)(2,1)S(1)} %add_convert_fusion.6), channel_id=1, source_target_pairs={{2,0},{3,1},{4,6},{5,7},{10,8},{11,9},{12,14},{13,15},{18,16},{19,... | collective-permute-start | bytes 3538952 | tf_op jit(solution)/shard_map/ppermute | solution.py:967
  414.6 53.0 %collective-permute-start.45 = (bf16[768,768]{1,0:T(8,128)(2,1)S(1)}, bf16[768,768]{1,0:T(8,128)(2,1)S(1)}, u32[]{:S(2)}, u32[]{:S(2)}) collective-permute-start(bf16[768,768]{1,0:T(8,128)(2,1)S(1)} %broadcast_select_fusion.1), channel_id=1, source_target_pairs={{0,1},{1,0},{2,3},{3,2},{4,5},{5,4},{6,7},{7,6},{8,9},{9,8},{10,11... | collective-permute-start | bytes 3538952 | tf_op jit(solution)/shard_map/ppermute | solution.py:968
  420.0 9.2 %collective-permute-start.39 = (bf16[208,768]{1,0:T(8,128)(2,1)}, bf16[208,768]{1,0:T(8,128)(2,1)}, u32[]{:S(2)}, u32[]{:S(2)}) collective-permute-start(bf16[208,768]{1,0:T(8,128)(2,1)} %fusion.13), channel_id=1, source_target_pairs={{0,2},{1,3},{6,4},{7,5},{8,10},{9,11},{14,12},{15,13},{16,18},{17,... | collective-permute-start | bytes 958472 | tf_op jit(solution)/shard_map/ppermute | solution.py:960
  423.6 14.7 %collective-permute-start.38 = (bf16[576,384]{1,0:T(8,128)(2,1)}, bf16[576,384]{1,0:T(8,128)(2,1)}, u32[]{:S(2)}, u32[]{:S(2)}) collective-permute-start(bf16[576,384]{1,0:T(8,128)(2,1)} %add_convert_fusion.21), channel_id=1, source_target_pairs={{2,4},{3,5},{4,2},{5,3},{10,12},{11,13},{12,10},{13,11},{18,20},{1... | collective-permute-start | bytes 1327112 | tf_op jit(solution)/shard_map/ppermute | solution.py:963
  429.2 18.0 %collective-permute-start.43 = (bf16[576,384]{1,0:T(8,128)(2,1)}, bf16[576,384]{1,0:T(8,128)(2,1)}, u32[]{:S(2)}, u32[]{:S(2)}) collective-permute-start(bf16[576,384]{1,0:T(8,128)(2,1)} %add_convert_fusion.19), channel_id=1, source_target_pairs={{2,4},{3,5},{4,2},{5,3},{10,12},{11,13},{12,10},{13,11},{18,20},{1... | collective-permute-start | bytes 1327112 | tf_op jit(solution)/shard_map/ppermute | solution.py:963
  440.2 14.3 %collective-permute-start.41 = (bf16[208,768]{1,0:T(8,128)(2,1)}, bf16[208,768]{1,0:T(8,128)(2,1)}, u32[]{:S(2)}, u32[]{:S(2)}) collective-permute-start(bf16[208,768]{1,0:T(8,128)(2,1)} %add_convert_fusion.23), channel_id=1, source_target_pairs={{2,4},{3,5},{4,2},{5,3},{10,12},{11,13},{12,10},{13,11},{18,20},{1... | collective-permute-start | bytes 958472 | tf_op jit(solution)/shard_map/ppermute | solution.py:963
  447.2 11.5 %collective-permute-start.40 = (bf16[576,384]{1,0:T(8,128)(2,1)}, bf16[576,384]{1,0:T(8,128)(2,1)}, u32[]{:S(2)}, u32[]{:S(2)}) collective-permute-start(bf16[576,384]{1,0:T(8,128)(2,1)} %add_convert_fusion.20), channel_id=1, source_target_pairs={{2,0},{3,1},{4,6},{5,7},{10,8},{11,9},{12,14},{13,15},{18,16},{19,... | collective-permute-start | bytes 1327112 | tf_op jit(solution)/shard_map/ppermute | solution.py:967
  451.2 18.4 %collective-permute-start.46 = (bf16[576,384]{1,0:T(8,128)(2,1)}, bf16[576,384]{1,0:T(8,128)(2,1)}, u32[]{:S(2)}, u32[]{:S(2)}) collective-permute-start(bf16[576,384]{1,0:T(8,128)(2,1)} %add_convert_fusion.18), channel_id=1, source_target_pairs={{2,0},{3,1},{4,6},{5,7},{10,8},{11,9},{12,14},{13,15},{18,16},{19,... | collective-permute-start | bytes 1327112 | tf_op jit(solution)/shard_map/ppermute | solution.py:967
  454.5 46.8 %collective-permute-start.48 = (bf16[384,1536]{1,0:T(8,128)(2,1)}, bf16[384,1536]{1,0:T(8,128)(2,1)}, u32[]{:S(2)}, u32[]{:S(2)}) collective-permute-start(bf16[384,1536]{1,0:T(8,128)(2,1)} %broadcast_select_fusion), channel_id=1, source_target_pairs={{0,1},{1,0},{2,3},{3,2},{4,5},{5,4},{6,7},{7,6},{8,9},{9,8},{10,11... | collective-permute-start | bytes 3538952 | tf_op jit(solution)/shard_map/ppermute | solution.py:968
  460.5 12.3 %collective-permute-start.44 = (bf16[208,768]{1,0:T(8,128)(2,1)}, bf16[208,768]{1,0:T(8,128)(2,1)}, u32[]{:S(2)}, u32[]{:S(2)}) collective-permute-start(bf16[208,768]{1,0:T(8,128)(2,1)} %add_convert_fusion.22), channel_id=1, source_target_pairs={{2,0},{3,1},{4,6},{5,7},{10,8},{11,9},{12,14},{13,15},{18,16},{19,... | collective-permute-start | bytes 958472 | tf_op jit(solution)/shard_map/ppermute | solution.py:967
  467.6 25.5 %collective-permute-start.49 = (bf16[576,384]{1,0:T(8,128)(2,1)}, bf16[576,384]{1,0:T(8,128)(2,1)}, u32[]{:S(2)}, u32[]{:S(2)}) collective-permute-start(bf16[576,384]{1,0:T(8,128)(2,1)} %broadcast_select_fusion.5), channel_id=1, source_target_pairs={{0,1},{1,0},{2,3},{3,2},{4,5},{5,4},{6,7},{7,6},{8,9},{9,8},{10,11... | collective-permute-start | bytes 1327112 | tf_op jit(solution)/shard_map/ppermute | solution.py:968
  471.6 29.7 %collective-permute-start.50 = (bf16[576,384]{1,0:T(8,128)(2,1)}, bf16[576,384]{1,0:T(8,128)(2,1)}, u32[]{:S(2)}, u32[]{:S(2)}) collective-permute-start(bf16[576,384]{1,0:T(8,128)(2,1)} %broadcast_select_fusion.4), channel_id=1, source_target_pairs={{0,1},{1,0},{2,3},{3,2},{4,5},{5,4},{6,7},{7,6},{8,9},{9,8},{10,11... | collective-permute-start | bytes 1327112 | tf_op jit(solution)/shard_map/ppermute | solution.py:968
  473.8 27.5 %collective-permute-start.51 = (bf16[208,768]{1,0:T(8,128)(2,1)S(1)}, bf16[208,768]{1,0:T(8,128)(2,1)S(1)}, u32[]{:S(2)}, u32[]{:S(2)}) collective-permute-start(bf16[208,768]{1,0:T(8,128)(2,1)S(1)} %broadcast_select_fusion.13), channel_id=1, source_target_pairs={{0,1},{1,0},{2,3},{3,2},{4,5},{5,4},{6,7},{7,6},{8,9},{9,8},{10,11... | collective-permute-start | bytes 958472 | tf_op jit(solution)/shard_map/ppermute | solution.py:968
  (90 other events, 305.8 us)

commit v4 on v3

--- a/solution.py
+++ b/solution.py
@@ -18,7 +18,7 @@
 BACKWARD_WINDOWS = (528,)
 CHUNK = 512
 BLOCK = 64
-VMEM_BYTES = 58 * 2**20
+VMEM_BYTES = 50 * 2**20
 NO_COST = pl.CostEstimate(flops=1, bytes_accessed=1, transcendentals=0)
 
 
@@ -794,17 +794,20 @@
     for copy in load[:5]:
         copy.wait()
     for k, to, away in ((1, fi, outs[3]), (0, oi, outs[2])):
-        for part in range(3):
-            right, before, at = ((dq, eq, 0), (dkv, ekv, 0), (dkv, ekv, width))[part]
-            lanes = slice(at + k * half, at + (k + 1) * half)
+        for part, (right, before) in enumerate(((dq, eq), (dkv, ekv))):
+            lanes = slice(k * half, (k + 1) * half)
             total = dot_tn(h[...], right[:, lanes]) + before[:, lanes].astype(F32)
             to[part * width : (part + 1) * width, :] = total.astype(BF)
         done.append(start(to, away))
     for copy in load[5:]:
         copy.wait()
     for k, to, away in ((1, fo, outs[1]), (0, oo, outs[0])):
+        lanes = slice(width + k * half, width + (k + 1) * half)
+        total = (dot_tn(h[...], dkv[:, lanes]) + ekv[:, lanes].astype(F32)).astype(BF)
+        to[0:half, 0:half] = total[0:half]
+        to[0:half, half:] = total[half:]
         lanes = slice(k * half, (k + 1) * half)
-        to[...] = (dot_tn(mixed[:, lanes], d1[...]) + eo[lanes, :].astype(F32)).astype(BF)
+        to[half : 2 * half, :] = (dot_tn(mixed[:, lanes], d1[...]) + eo[lanes, :].astype(F32)).astype(BF)
         done.append(start(to, away))
     qb = c5[0:1, :] + jnp.sum(dq[...].astype(F32), axis=0, keepdims=True)
     vb = c5[1:2, :] + jnp.sum(dkv[:, width:].astype(F32), axis=0, keepdims=True)
@@ -824,7 +827,7 @@
     rows, width = s.h.shape
     half = width // 2
     args = (s.f.mixed, b.d1_low, s.h, b.dq, b.dkv, early[2], early[3], early[4])
-    shapes = [((half, width), BF), ((half, width), BF), ((3 * width, half), BF), ((3 * width, half), BF)]
+    shapes = [((2 * half, width), BF)] * 2 + [((2 * width, half), BF)] * 2
     return pl.pallas_call(
         last_gradient_kernel,
         out_shape=results(shapes + [((16, width), F32)] * 2),
@@ -916,17 +919,17 @@
     pass
 
 
-def tied(*xs):
+def tied(*xs, unread=()):
     hbm = pl.BlockSpec(memory_space=pl.ANY)
     return pl.pallas_call(
         gate_kernel,
         out_shape=tuple(jax.ShapeDtypeStruct(x.shape, x.dtype) for x in xs),
-        in_specs=[hbm] * len(xs),
+        in_specs=[hbm] * (len(xs) + len(unread)),
         out_specs=(hbm,) * len(xs),
         input_output_aliases={i: i for i in range(len(xs))},
         cost_estimate=NO_COST,
         name="gate",
-    )(*xs)
+    )(*xs, *unread)
 
 
 class Sum:
@@ -973,9 +976,9 @@
         self.got = self.steps.send(got)
 
 
-def step_sums(sums, *others):
+def step_sums(sums, *others, unread=()):
     moving = [one for one in sums if one.whole is None]
-    res = tied(*[one.got for one in moving], *others)
+    res = tied(*[one.got for one in moving], *others, unread=unread)
     for one, got in zip(moving, res):
         one.take(got)
     return res[len(moving) :]
@@ -1018,16 +1021,14 @@
     return f.out, Saved(h, q, kv, kvp, f)
 
 
-def backward_end(b, w):
-    other = to_peer(b.far)
-    from_q = dot_nt(b.dq, w.q)
-    dkv = add_low(b.near, other)
-    return (b.d1_low.astype(F32) + from_q + dot_nt(dkv, w.kv)).astype(BF), b._replace(dkv=dkv)
+def rows_gradient(b, dq, dkv, w):
+    return (b.d1_low.astype(F32) + dot_nt(dq, w.q) + dot_nt(dkv, w.kv)).astype(BF)
 
 
 def backward_tick(slot_of, g, s, w):
     b = Back(*backward_call(ALL, slot_of, w, g, s.f, s.q, s.kv, s.kvp), None)
-    return backward_end(b, w)
+    b = b._replace(dkv=add_low(b.near, to_peer(b.far)))
+    return rows_gradient(b, b.dq, b.dkv, w), b
 
 
 def cut(x, which, size):
@@ -1090,12 +1091,14 @@
     out1, _ = forward_tick(False, slot_one, tok0, w)
     tok1 = from_rows(last_section(tokens[1]), 1)
     out2, saved2 = forward_tick(True, slot_a, jnp.where(first, tok1, next_section(out1)), w)
-    away2 = next_section(out2)
+    away2 = next_section(jnp.concatenate([out2, grad_out[1]], axis=0))
     g3, b3 = backward_tick(slot_a, cot0, saved2, w)
-    away2, rows1, _ = tied(away2, grad_out[1], b3.d2_low)
-    cot1 = cot_rows(next_section(rows1), 1)
+    away2, _ = tied(away2, b3.d2_low)
+    away2, rows1 = away2[: 2 * quarter], away2[2 * quarter :]
+    cot1 = cot_rows(rows1, 1)
     out4, saved4 = forward_tick(True, slot_b, jnp.where(first, tok0, away2), w)
-    g5, b5 = backward_tick(slot_b, jnp.where(first, last_section(g3), cot1), saved4, w)
+    (away3,) = tied(last_section(g3), unread=(out4,))
+    g5, b5 = backward_tick(slot_b, jnp.where(first, away3, cot1), saved4, w)
 
     early = gradient_call(saved4, b5)
     g6_in = jnp.where(first, last_section(g5), cot0)
@@ -1111,52 +1114,54 @@
     (up_far,) = step_sums([down], up_far)
     up_in = to_peer(up_far)
     up = Sum(add_low(up_own, up_in), dp_size)
-    quarters = jnp.concatenate([out2[:quarter], out4[:quarter]], axis=0)
     dq, near, far = backward_call(
         HEADS, slot_a, w, None, f6, saved2.q, saved2.kv, saved2.kvp, d_mixed, (down.sent, up.sent)
     )
-    dq, near, far, quarters = step_sums([down, up], dq, near, far, quarters)
-    layer_far = last_section(quarters)
-    g6, b6 = backward_end(b6._replace(dq=dq, near=near, far=far), w)
+    dq, near, far = step_sums([down, up], dq, near, far)
+    b6 = b6._replace(dq=dq, dkv=add_low(near, to_peer(far)))
     out_own, out_far, in_own, in_far, small_own, small_far = last_gradient_call(up.sent, saved2, b6, early, b5)
     out_far, in_far, small_far, tick = step_sums([down, up], out_far, in_far, small_far, b6.bias_sums)
-    tokens_far = next_section(jnp.concatenate([g5[quarter:], g6[quarter:]], axis=0))
-    in_g = add_low(in_own, to_peer(in_far))
+    inner = Sum(add_low(in_own, to_peer(in_far)), dp_size)
     small = small_own + to_peer(small_far)
     out_g = jnp.concatenate(
         [add_low(out_own, to_peer(out_far)), small.astype(BF), jnp.zeros((16, width), BF)], axis=0
     )
-    part = lambda x, i: x[i * x.shape[0] // 2 : (i + 1) * x.shape[0] // 2]
-    in_a, in_b = Sum(part(in_g, 0), dp_size), Sum(part(in_g, 1), dp_size)
     last = Sum(out_g, dp_size)
-    (tick,) = step_sums([in_a], tick)
-    (tick,) = step_sums([in_b], tick)
-    (tick,) = step_sums([down, up], tick)
-    (tick,) = step_sums([in_a, last], tick)
-    tick, layer_far = step_sums([in_b], tick, layer_far)
-    (tick,) = step_sums([in_a, last], tick)
-    (tick,) = step_sums([up, in_b], tick)
-    (tick,) = step_sums([in_a, last], tick)
-    (tick,) = step_sums([down, in_b], tick)
-    tick, tokens_far = step_sums([last], tick, tokens_far)
-    sums = [up, in_a, in_b, last, down]
-    while any(one.whole is None for one in sums):
-        (tick,) = step_sums(sums, tick)
-    down_s = down.whole.astype(F32)
-    up_s = up.whole.astype(F32)
-    in_s = jnp.concatenate([in_a.whole, in_b.whole], axis=0).astype(F32)
-    out_s = last.whole.astype(F32)
-    small = out_s[half : half + 16]
-
+    (tick,) = step_sums([inner], tick, unread=(last.sent,))
+    (tick,) = step_sums([down, up, last], tick)
+    (tick,) = step_sums([inner], tick)
+    (tick,) = step_sums([last], tick)
+    tick, dq, dkv = step_sums([up, inner], tick, b6.dq, b6.dkv)
+    quarters = jnp.concatenate([out2[:quarter], out4[:quarter]], axis=0)
+    tick, quarters = tied(tick, quarters, unread=(inner.sent, up.sent))
+    layer_far = last_section(quarters)
+    g6 = rows_gradient(b6, dq, dkv, w)
+    tokens_far = next_section(jnp.concatenate([g5[quarter:], g6[quarter:]], axis=0))
+    tick, layer_far = step_sums([last], tick, layer_far)
+    tick, tokens_far = step_sums([down, inner], tick, tokens_far)
+    (tick,) = step_sums([last], tick)
+    while up.whole is None or down.whole is None:
+        (tick,) = step_sums([up, down], tick)
     pair = lambda x, y: jnp.stack([x, y])
     layer_out = jnp.where(first, layer_far.reshape(tokens.shape), pair(out2[quarter:], out4[quarter:]))
     grad_tokens = jnp.where(first, pair(g5[:quarter], g6[:quarter]), tokens_far.reshape(tokens.shape))
+    down_s = down.whole.astype(F32)
+    up_s = up.whole.astype(F32)
+    while inner.whole is None or last.whole is None:
+        tick, down_s, up_s, layer_out, grad_tokens = step_sums(
+            [inner, last], tick, down_s, up_s, layer_out, grad_tokens
+        )
+    out_s = last.whole
+    in_s = jnp.concatenate([inner.whole, out_s[:half, :half], out_s[:half, half:]], axis=0).astype(F32)
+    small = out_s[2 * half : 2 * half + 16].astype(F32)
+    out_s = out_s[half : 2 * half].astype(F32)
+
     return (
         layer_out,
         grad_tokens,
         in_s.reshape(3, width, half).transpose(1, 0, 2)[None],
         small[8].reshape(1, 2, half),
-        out_s[:half][None],
+        out_s[None],
         up_s[None],
         small[6:8].reshape(1, hidden),
         down_s[None],

time: 525 us -> 519 us (0.989)
  Pallas kernels: 197 us -> 182 us
  waiting for transfers between devices: 107 us -> 120 us
  local copies, waits for them, and re-layouts: 30.7 us -> 42.3 us
  starting transfers between devices: 82.3 us -> 73.1 us
  other arithmetic: 71.6 us -> 66.2 us
    unnamed x206 -> x271, local copies, waits for them, and re-layouts: 19.1 us -> 31.9 us
    pallas_call x4, Pallas kernels: 97.6 us -> 90.2 us  [backward_call(): pl.pallas_call(functools.partial(backward_kernel, which, slot_of, len(tok...]
    ppermute x4, waiting for transfers between devices: 13 us -> 20.4 us  [last_section(): return lax.ppermute(x, 'section', [(1, 0)])]
    ppermute x5 -> x4, waiting for transfers between devices: 21.7 us -> 15.7 us  [walk(): got = (yield lax.ppermute(total, 'dp', pairs))]
    ppermute x4 -> x3, waiting for transfers between devices: 7.1 us -> 12.9 us  [next_section(): return lax.ppermute(x, 'section', [(0, 1)])]
    ppermute x10 -> x8, waiting for transfers between devices: 22.1 us -> 27.8 us  [walk(): total = add_low(total, (yield lax.ppermute(total, 'dp', moves)))]
    ppermute x18, starting transfers between devices: 8.23 us -> 13.7 us  [to_peer(): return lax.ppermute(x, 'mp', SWAP)]
    ppermute x10 -> x8, starting transfers between devices: 22.6 us -> 17.7 us  [walk(): total = add_low(total, (yield lax.ppermute(total, 'dp', moves)))]
  transfers between devices with their start and end apart: 52 -> 46, of which waited for: 23 -> 24; matrix products, arithmetic and copies ran while one was open for 16% -> 16% of each run, Pallas kernels for 23% -> 21%
where the time goes in v4:
time: 519 us; the launch traced here: 511 us
  Pallas kernels  182 us (35%)
  waiting for transfers between devices  120 us (23%)
  starting transfers between devices  73.1 us (14%)
  other arithmetic  66.2 us (13%)
  local copies, waits for them, and re-layouts  42.3 us (8%)
  matrix products  24.8 us (5%)
    pallas_call x4, Pallas kernels, backward_call(): pl.pallas_call(functools.partial(backward_kernel, which, slot_of, len(tok...  90.2 us
    pallas_call x3, Pallas kernels, forward_call(): pl.pallas_call(functools.partial(forward_kernel, save, slot_of, len(token...  62.9 us
    convert_element_type x18, other arithmetic, add_low(): return (a.astype(F32) + b.astype(F32)).astype(BF)  34.5 us
    unnamed x271, local copies, waits for them, and re-layouts  31.9 us
    ppermute x8, waiting for transfers between devices, walk(): total = add_low(total, (yield lax.ppermute(total, 'dp', moves)))  27.8 us
    ppermute x4, waiting for transfers between devices, walk(): total = add_low(keep, (yield lax.ppermute(send, 'dp', pairs)))  24.6 us
    ppermute x4, waiting for transfers between devices, last_section(): return lax.ppermute(x, 'section', [(1, 0)])  20.4 us
    ppermute x4, starting transfers between devices, last_section(): return lax.ppermute(x, 'section', [(1, 0)])  17.8 us
  transfers between devices with their start and end apart: 46, of which 24 were waited for; matrix products, arithmetic and copies ran while one was open for 16% of the time, Pallas kernels for 21%

profile of v4, /device:TPU:14, one launch (start us, length us, event | category | flops | bytes accessed | tf_op | source)
XLA Modules:
  0.0 510.6 jit_solution(14222781918483283698)
XLA Ops:
  5.2 2.2 slice_bitcast_fusion.2
  7.4 6.1 %collective-permute-done.3 = bf16[256,768]{1,0:T(8,128)(2,1)S(1)} collective-permute-done((bf16[256,768]{1,0:T(8,128)(2,1)S(1)}, bf16[256,768]{1,0:T(8,128)(2,1)S(1)}, u32[]{:S(2)}, u32[]{:S(2)}) %collective-permute-start.3) | collective-permute-done | bytes 393248 | tf_op jit(solution)/shard_map/ppermute | solution.py:1060
  13.5 2.1 fusion.refs_1_
  17.4 2.6 collective-permute-done.shift_far
  23.9 20.3 %layer_forward.3 = bf16[512,768]{1,0:T(8,128)(2,1)S(1)} custom-call(s32[2]{0:T(128)S(1)} %copy-done.33, s32[2]{0:T(128)S(1)} %copy-done.36, s32[1,6]{1,0:T(1,128)S(1)} %copy-done.39, s32[1,6]{1,0:T(1,128)S(1)} %collective-permute-done.shift_far, f32[4,768]{1,0:T(4,128)S(1)} %bitcast.108, f32[2,768]{1,0:T(2,128)S(1)} %bitcast.101, f32[1,1536]{1,0:T(1,128)S(1)} %copy-done.28, ...), custom_call_target="tpu_custom_call" | custom-call | flops 1 | bytes 1 | tf_op jit(solution)/shard_map/layer_forward/pallas_call | solution.py:471
  45.7 4.6 collective-permute-start.2
  50.3 8.7 %collective-permute-done.2 = bf16[256,768]{1,0:T(8,128)(2,1)S(1)} collective-permute-done((bf16[256,768]{1,0:T(8,128)(2,1)S(1)}, bf16[256,768]{1,0:T(8,128)(2,1)S(1)}, u32[]{:S(2)}, u32[]{:S(2)}) %collective-permute-start.2) | collective-permute-done | bytes 393248 | tf_op jit(solution)/shard_map/ppermute | solution.py:911
  59.0 7.2 %collective-permute-done.10 = bf16[512,768]{1,0:T(8,128)(2,1)S(1)} collective-permute-done((bf16[512,768]{1,0:T(8,128)(2,1)S(1)}, bf16[512,768]{1,0:T(8,128)(2,1)S(1)}, u32[]{:S(2)}, u32[]{:S(2)}) %collective-permute-start.10) | collective-permute-done | bytes 786464 | tf_op jit(solution)/shard_map/ppermute | solution.py:907
  66.4 2.1 fusion.1.refs_1_.refs_15_.refs_5_
  73.3 21.3 %layer_forward.4 = (bf16[512,768]{1,0:T(8,128)(2,1)S(1)}, bf16[512,768]{1,0:T(8,128)(2,1)S(1)}, f32[6,2,512]{2,1,0:T(2,128)S(1)}, bf16[512,768]{1,0:T(8,128)(2,1...) custom-call(s32[2]{0:T(128)S(1)} %copy-done.33, ...), custom_call_target="tpu_custom_call" | custom-call | flops 1 | bytes 1 | tf_op jit(solution)/shard_map/layer_forward/pallas_call | solution.py:471
  96.8 28.2 %layer_backward.4 = (bf16[512,768]{1,0:T(8,128)(2,1)S(1)}, bf16[512,3072]{1,0:T(8,128)(2,1)}, bf16[512,768]{1,0:T(8,128)(2,1)S(1)}, f32[8,768]{1,0:T(8,128)}, f3...) custom-call(s32[2]{0:T(128)S(1)} %copy-done.33, ...), custom_call_target="tpu_custom_call" | custom-call | flops 1 | bytes 1 | tf_op jit(solution)/shard_map/layer_backward/pallas_call | solution.py:887
  126.8 5.9 %collective-permute-start.12 = (bf16[512,1536]{1,0:T(8,128)(2,1)}, bf16[512,1536]{1,0:T(8,128)(2,1)}, u32[]{:S(2)}, u32[]{:S(2)}) collective-permute-start(bf16[512,1536]{1,0:T(8,128)(2,1)} %get-tuple-element.122), channel_id=1, source_target_pairs={{0,8},{8,0},{1,9},{9,1},{2,10},{10,2},{3,11},{11,3},{4,12},{12,4},... | collective-permute-start | bytes 4718600 | tf_op jit(solution)/shard_map/ppermute | solution.py:903
  134.8 2.1 fusion.2.refs_1_.refs_15_
  139.2 2.8 add_convert_fusion.15
  142.0 6.1 %collective-permute-start.13 = (bf16[512,768]{1,0:T(8,128)(2,1)S(1)}, bf16[512,768]{1,0:T(8,128)(2,1)}, u32[]{:S(2)}, u32[]{:S(2)}) collective-permute-start(bf16[512,768]{1,0:T(8,128)(2,1)S(1)} %add_convert_fusion.15), channel_id=1, source_target_pairs={{16,0},{17,1},{18,2},{19,3},{20,4},{21,5},{22,6},{23,7},{24,8},{25... | collective-permute-start | bytes 2359304 | tf_op jit(solution)/shard_map/ppermute | solution.py:911
  152.8 21.3 %layer_forward.5 = (bf16[512,768]{1,0:T(8,128)(2,1)S(1)}, bf16[512,768]{1,0:T(8,128)(2,1)S(1)}, f32[6,2,512]{2,1,0:T(2,128)S(1)}, bf16[512,768]{1,0:T(8,128)(2,1...) custom-call(s32[2]{0:T(128)S(1)} %copy-done.34, ...), custom_call_target="tpu_custom_call" | custom-call | flops 1 | bytes 1 | tf_op jit(solution)/shard_map/layer_forward/pallas_call | solution.py:471
  177.3 2.2 maximum_select_fusion.1.refs_0_
  179.6 27.6 %layer_backward.5 = (bf16[512,768]{1,0:T(8,128)(2,1)S(1)}, bf16[512,3072]{1,0:T(8,128)(2,1)}, bf16[512,768]{1,0:T(8,128)(2,1)S(1)}, f32[8,768]{1,0:T(8,128)S(1)}...) custom-call(s32[2]{0:T(128)S(1)} %copy-done.35, ...), custom_call_target="tpu_custom_call" | custom-call | flops 1 | bytes 1 | tf_op jit(solution)/shard_map/layer_backward/pallas_call | solution.py:887
  207.2 5.6 %collective-permute-start.16 = (bf16[512,1536]{1,0:T(8,128)(2,1)}, bf16[512,1536]{1,0:T(8,128)(2,1)S(1)}, u32[]{:S(2)}, u32[]{:S(2)}) collective-permute-start(bf16[512,1536]{1,0:T(8,128)(2,1)} %get-tuple-element.137), channel_id=1, source_target_pairs={{0,8},{8,0},{1,9},{9,1},{2,10},{10,2},{3,11},{11,3},{4,12},{12,4},... | collective-permute-start | bytes 4718600 | tf_op jit(solution)/shard_map/ppermute | solution.py:903
  212.8 2.1 fusion.16
  218.2 2.1 add_convert_fusion.13
  222.3 12.1 %layer_gradient.1 = (bf16[3072,768]{1,0:T(8,128)(2,1)}, bf16[768,3072]{1,0:T(8,128)(2,1)}, bf16[768,768]{1,0:T(8,128)(2,1)}, bf16[768,768]{1,0:T(8,128)(2,1)}, b...) custom-call(bf16[512,3072]{1,0:T(8,128)(2,1)} %get-tuple-element.139.refs_0_, ...), custom_call_target="tpu_custom_call" | custom-call | flops 1 | bytes 1 | tf_op jit(solution)/shard_map/layer_gradient/pallas_call | solution.py:729
  234.4 4.8 collective-permute-done.17
  240.2 4.7 half_gradient.2.token
  245.1 4.9 half_gradient.3
  250.0 2.3 add_convert_fusion.1
  253.5 18.6 %layer_backward.6 = (bf16[512,768]{1,0:T(8,128)(2,1)}, bf16[512,3072]{1,0:T(8,128)(2,1)}, bf16[512,768]{1,0:T(8,128)(2,1)S(1)}, f32[8,768]{1,0:T(8,128)S(1)}, f3...) custom-call(s32[2]{0:T(128)S(1)} %copy-done.35, ...), custom_call_target="tpu_custom_call" | custom-call | flops 1 | bytes 1 | tf_op jit(solution)/shard_map/layer_backward/pallas_call | solution.py:887
  273.9 6.9 %collective-permute-done.19.refs_0_ = bf16[768,768]{1,0:T(8,128)(2,1)S(1)} collective-permute-done((bf16[768,768]{1,0:T(8,128)(2,1)S(1)}, bf16[768,768]{1,0:T(8,128)(2,1)S(1)}, u32[]{:S(2)}, u32[]{:S(2)}) %collective-permute-start.19) | collective-permute-done | bytes 1179680 | tf_op jit(solution)/shard_map/ppermute | solution.py:959
  286.7 2.3 add_convert_fusion
  291.9 15.8 %layer_backward.7 = (bf16[512,768]{1,0:T(8,128)(2,1)S(1)}, bf16[512,1536]{1,0:T(8,128)(2,1)}, bf16[512,1536]{1,0:T(8,128)(2,1)}) custom-call(s32[2]{0:T(128)S(1)} %copy-done.35, s32[2]{0:T(128)S(1)} %copy-done.38, s32[1,6]{1,0:T(1,128)S(1)} %copy-done.42, s32[1,6]{1,0:T(1,128)S(1)} %copy-done.46, f32[2,768]{1,0:T(2,128)S(1)} %bitcast.107, ...), custom_call_target="tpu_custom_call" | custom-call | flops 1 | bytes 1 | tf_op jit(solution)/shard_map/layer_backward/pallas_call | solution.py:887
  308.6 5.6 %collective-permute-done.20.refs_0_ = bf16[768,768]{1,0:T(8,128)(2,1)S(1)} collective-permute-done((bf16[768,768]{1,0:T(8,128)(2,1)S(1)}, bf16[768,768]{1,0:T(8,128)(2,1)S(1)}, u32[]{:S(2)}, u32[]{:S(2)}) %collective-permute-start.20) | collective-permute-done | bytes 1179680 | tf_op jit(solution)/shard_map/ppermute | solution.py:963
  318.3 3.1 fusion.3.refs_0_
  324.4 3.9 collective-permute-start.23
  328.4 3.6 add_convert_fusion.2.refs_5_.refs_4_
  332.0 7.3 %last_gradient.1 = (bf16[768,768]{1,0:T(8,128)(2,1)}, bf16[768,768]{1,0:T(8,128)(2,1)}, bf16[1536,384]{1,0:T(8,128)(2,1)}, bf16[1536,384]{1,0:T(8,128)(2,1)}, f3...) custom-call(bf16[384,1536]{1,0:T(8,128)(2,1)} %fusion.3.refs_0_, bf16[512,768]{1,0:T(8,128)(2,1)S(1)} %copy-done.8, ...), custom_call_target="tpu_custom_call" | custom-call | flops 1 | bytes 1 | tf_op jit(solution)/shard_map/last_gradient/pallas_call | solution.py:831
  340.0 12.0 %collective-permute-done.24.refs_1_ = bf16[384,1536]{1,0:T(8,128)(2,1)} collective-permute-done((bf16[384,1536]{1,0:T(8,128)(2,1)}, bf16[384,1536]{1,0:T(8,128)(2,1)}, u32[]{:S(2)}, u32[]{:S(2)}) %collective-permute-start.24) | collective-permute-done | bytes 1179680 | tf_op jit(solution)/shard_map/ppermute | solution.py:963
  351.9 3.3 collective-permute-done.23.refs_0_
  357.2 2.9 add_convert_fusion.8
  360.1 3.6 collective-permute-start.27
  363.7 3.0 add_convert_fusion.9
  366.7 2.3 collective-permute-start.26
  374.2 11.7 %collective-permute-done.32.refs_0_ = bf16[768,384]{1,0:T(8,128)(2,1)S(1)} collective-permute-done((bf16[768,384]{1,0:T(8,128)(2,1)S(1)}, bf16[768,384]{1,0:T(8,128)(2,1)S(1)}, u32[]{:S(2)}, u32[]{:S(2)}) %collective-permute-start.32) | collective-permute-done | bytes 589856 | tf_op jit(solution)/shard_map/ppermute | solution.py:959
  390.2 3.6 collective-permute-done.26.refs_0_
  393.7 4.0 collective-permute-done.30.refs_2_
  400.6 2.3 collective-permute-start.35
  404.4 2.3 add_convert_fusion.21
  406.7 2.2 collective-permute-start.36
  409.9 2.4 broadcast_select_fusion.5
  412.9 6.8 %collective-permute-done.37.refs_0_ = bf16[400,768]{1,0:T(8,128)(2,1)S(1)} collective-permute-done((bf16[400,768]{1,0:T(8,128)(2,1)S(1)}, bf16[400,768]{1,0:T(8,128)(2,1)S(1)}, u32[]{:S(2)}, u32[]{:S(2)}) %collective-permute-start.37) | collective-permute-done | bytes 614432 | tf_op jit(solution)/shard_map/ppermute | solution.py:963
  420.5 2.1 add_convert_fusion.19
  422.6 2.2 collective-permute-start.39
  427.7 3.1 fusion.15
  430.8 2.2 add_convert_fusion.20.refs_2_
  433.0 5.5 %collective-permute-start.38 = (bf16[768,384]{1,0:T(8,128)(2,1)}, bf16[768,384]{1,0:T(8,128)(2,1)}, u32[]{:S(2)}, u32[]{:S(2)}) collective-permute-start(bf16[768,384]{1,0:T(8,128)(2,1)} %add_convert_fusion.20.refs_2_), channel_id=1, source_target_pairs={{2,0},{3,1},{4,6},{5,7},{10,8},{11,9},{12,14},{13,15},{18,16},{19,... | collective-permute-start | bytes 1769480 | tf_op jit(solution)/shard_map/ppermute | solution.py:970
  438.5 5.3 %collective-permute-start.40 = (bf16[512,768]{1,0:T(8,128)(2,1)}, bf16[512,768]{1,0:T(8,128)(2,1)}, u32[]{:S(2)}, u32[]{:S(2)}) collective-permute-start(bf16[512,768]{1,0:T(8,128)(2,1)} %get-tuple-element.193), channel_id=1, source_target_pairs={{16,0},{17,1},{18,2},{19,3},{20,4},{21,5},{22,6},{23,7},{24,8},{25... | collective-permute-start | bytes 2359304 | tf_op jit(solution)/shard_map/ppermute | solution.py:911
  443.8 3.4 add_convert_fusion.12
  451.3 6.9 %collective-permute-done.40.refs_2_ = bf16[512,768]{1,0:T(8,128)(2,1)} collective-permute-done((bf16[512,768]{1,0:T(8,128)(2,1)}, bf16[512,768]{1,0:T(8,128)(2,1)}, u32[]{:S(2)}, u32[]{:S(2)}) %collective-permute-start.40) | collective-permute-done | bytes 786464 | tf_op jit(solution)/shard_map/ppermute | solution.py:911
  458.2 2.2 add_convert_fusion.18
  460.4 2.3 collective-permute-start.43
  462.7 5.7 %collective-permute-done.41.refs_3_ = bf16[512,768]{1,0:T(8,128)(2,1)S(1)} collective-permute-done((bf16[512,768]{1,0:T(8,128)(2,1)}, bf16[512,768]{1,0:T(8,128)(2,1)S(1)}, u32[]{:S(2)}, u32[]{:S(2)}) %collective-permute-start.41) | collective-permute-done | bytes 786464 | tf_op jit(solution)/shard_map/ppermute | solution.py:907
  476.0 2.5 maximum_convert_fusion.refs_3_
  483.6 2.8 maximum_convert_fusion.1.refs_4_
  486.4 5.9 %collective-permute-done.42.refs_0_ = bf16[768,384]{1,0:T(8,128)(2,1)} collective-permute-done((bf16[768,384]{1,0:T(8,128)(2,1)}, bf16[768,384]{1,0:T(8,128)(2,1)}, u32[]{:S(2)}, u32[]{:S(2)}) %collective-permute-start.42) | collective-permute-done | bytes 589856 | tf_op jit(solution)/shard_map/ppermute | solution.py:971
  492.3 9.9 %collective-permute-done.44.refs_1_ = bf16[400,768]{1,0:T(8,128)(2,1)} collective-permute-done((bf16[400,768]{1,0:T(8,128)(2,1)S(1)}, bf16[400,768]{1,0:T(8,128)(2,1)}, u32[]{:S(2)}, u32[]{:S(2)}) %collective-permute-start.44) | collective-permute-done | bytes 614432 | tf_op jit(solution)/shard_map/ppermute | solution.py:971
  (412 shorter events, 104.8 us)
Async XLA Ops:
  0.7 4.6 collective-permute-start.4
  2.0 11.5 %collective-permute-start.3 = (bf16[256,768]{1,0:T(8,128)(2,1)S(1)}, bf16[256,768]{1,0:T(8,128)(2,1)S(1)}, u32[]{:S(2)}, u32[]{:S(2)}) collective-permute-start(bf16[256,768]{1,0:T(8,128)(2,1)S(1)} %broadcast_select_fusion.13), channel_id=1, source_target_pairs={{0,16},{16,0},{1,17},{17,1},{2,18},{18,2},{3,19},{19,3},{4,20},{20... | collective-permute-start | bytes 1179656 | tf_op jit(solution)/shard_map/ppermute | solution.py:1060
  2.6 2.5 collective-permute-start.5
  2.7 18.5 %collective-permute-start.8 = (bf16[768,1536]{1,0:T(8,128)(2,1)}, bf16[768,1536]{1,0:T(8,128)(2,1)S(1)}, u32[]{:S(2)}, u32[]{:S(2)}) collective-permute-start(bf16[768,1536]{1,0:T(8,128)(2,1)} %bitcast.111), channel_id=1, source_target_pairs={{0,8},{8,0},{1,9},{9,1},{2,10},{10,2},{3,11},{11,3},{4,12},{12,4},... | collective-permute-start | bytes 7077896 | tf_op jit(solution)/shard_map/ppermute | solution.py:903
  3.1 18.1 %collective-permute-start.9 = (bf16[1536,768]{1,0:T(8,128)(2,1)}, bf16[1536,768]{1,0:T(8,128)(2,1)S(1)}, u32[]{:S(2)}, u32[]{:S(2)}) collective-permute-start(bf16[1536,768]{1,0:T(8,128)(2,1)} %bitcast.118), channel_id=1, source_target_pairs={{0,8},{8,0},{1,9},{9,1},{2,10},{10,2},{3,11},{11,3},{4,12},{12,4},... | collective-permute-start | bytes 7077896 | tf_op jit(solution)/shard_map/ppermute | solution.py:903
  4.4 15.7 %copy-start.80 = (bf16[256,768]{1,0:T(8,128)(2,1)}, bf16[256,768]{1,0:T(8,128)(2,1)S(1)}, u32[]{:S(2)}) copy-start(bf16[256,768]{1,0:T(8,128)(2,1)S(1)} %get-tuple-element.246) | copy-start | bytes 1179652
  5.1 15.0 %copy-start.116 = (bf16[768,384]{1,0:T(8,128)(2,1)}, bf16[768,384]{1,0:T(8,128)(2,1)S(1)}, u32[]{:S(2)}) copy-start(bf16[768,384]{1,0:T(8,128)(2,1)S(1)} %get-tuple-element.227) | copy-start | bytes 1769476
  7.4 59.0 %copy-start.121 = (bf16[768,384]{1,0:T(8,128)(2,1)}, bf16[768,384]{1,0:T(8,128)(2,1)S(1)}, u32[]{:S(2)}) copy-start(bf16[768,384]{1,0:T(8,128)(2,1)S(1)} %get-tuple-element.228) | copy-start | bytes 1769476
  7.4 59.0 %copy-start.124 = (bf16[768,384]{1,0:T(8,128)(2,1)}, bf16[768,384]{1,0:T(8,128)(2,1)S(1)}, u32[]{:S(2)}) copy-start(bf16[768,384]{1,0:T(8,128)(2,1)S(1)} %get-tuple-element.229) | copy-start | bytes 1769476
  15.7 5.5 %collective-permute-start.6 = (bf16[512,1536]{1,0:T(8,128)(2,1)S(1)}, bf16[512,1536]{1,0:T(8,128)(2,1)S(1)}, u32[]{:S(2)}, u32[]{:S(2)}) collective-permute-start(bf16[512,1536]{1,0:T(8,128)(2,1)S(1)} %fusion.refs_1_), channel_id=1, source_target_pairs={{0,8},{8,0},{1,9},{9,1},{2,10},{10,2},{3,11},{11,3},{4,12},{12,4},... | collective-permute-start | bytes 4718600 | tf_op jit(solution)/shard_map/ppermute | solution.py:903
  15.8 5.4 %collective-permute-start.7 = (bf16[384,768]{1,0:T(8,128)(2,1)S(1)}, bf16[384,768]{1,0:T(8,128)(2,1)S(1)}, u32[]{:S(2)}, u32[]{:S(2)}) collective-permute-start(bf16[384,768]{1,0:T(8,128)(2,1)S(1)} %bitcast.94), channel_id=1, source_target_pairs={{0,8},{8,0},{1,9},{9,1},{2,10},{10,2},{3,11},{11,3},{4,12},{12,4},... | collective-permute-start | bytes 1769480 | tf_op jit(solution)/shard_map/ppermute | solution.py:903
  16.3 3.7 collective-permute-start
  20.0 76.8 %copy-start.43 = (s32[1,6]{1,0:T(1,128)}, s32[1,6]{1,0:T(1,128)S(1)}, u32[]{:S(2)}) copy-start(s32[1,6]{1,0:T(1,128)S(1)} %collective-permute-done.shift_far) | copy-start | bytes 76
  20.0 1.2 collective-permute-start.1
  21.2 50.9 %copy-start.29 = (f32[1,1536]{1,0:T(1,128)}, f32[1,1536]{1,0:T(1,128)S(1)}, u32[]{:S(2)}) copy-start(f32[1,1536]{1,0:T(1,128)S(1)} %collective-permute-done.1.bup_far) | copy-start | bytes 18436
  44.2 22.2 %copy-start.108 = (bf16[768,384]{1,0:T(8,128)(2,1)S(1)}, bf16[768,384]{1,0:T(8,128)(2,1)}, u32[]{:S(2)}) copy-start(bf16[768,384]{1,0:T(8,128)(2,1)} %copy-done.107) | copy-start | bytes 1769476
  44.2 22.2 %copy-start.113 = (bf16[768,384]{1,0:T(8,128)(2,1)S(1)}, bf16[768,384]{1,0:T(8,128)(2,1)}, u32[]{:S(2)}) copy-start(bf16[768,384]{1,0:T(8,128)(2,1)} %copy-done.112) | copy-start | bytes 1769476
  44.2 21.9 %collective-permute-start.10 = (bf16[512,768]{1,0:T(8,128)(2,1)S(1)}, bf16[512,768]{1,0:T(8,128)(2,1)S(1)}, u32[]{:S(2)}, u32[]{:S(2)}) collective-permute-start(bf16[512,768]{1,0:T(8,128)(2,1)S(1)} %layer_forward.3), channel_id=1, source_target_pairs={{0,16},{1,17},{2,18},{3,19},{4,20},{5,21},{6,22},{7,23},{8,24},{9,... | collective-permute-start | bytes 2359304 | tf_op jit(solution)/shard_map/ppermute | solution.py:907
  45.7 13.3 %collective-permute-start.2 = (bf16[256,768]{1,0:T(8,128)(2,1)S(1)}, bf16[256,768]{1,0:T(8,128)(2,1)S(1)}, u32[]{:S(2)}, u32[]{:S(2)}) collective-permute-start(bf16[256,768]{1,0:T(8,128)(2,1)S(1)} %get-tuple-element.245), channel_id=1, source_target_pairs={{16,0},{17,1},{18,2},{19,3},{20,4},{21,5},{22,6},{23,7},{24,8},{25... | collective-permute-start | bytes 1179656 | tf_op jit(solution)/shard_map/ppermute | solution.py:911
  68.6 3.5 collective-permute-start.11
  95.4 29.6 %copy-start.26 = (f32[6,2,512]{2,1,0:T(2,128)}, f32[6,2,512]{2,1,0:T(2,128)S(1)}, u32[]{:S(2)}) copy-start(f32[6,2,512]{2,1,0:T(2,128)S(1)} %get-tuple-element.118.refs_13_.refs_3_) | copy-start | bytes 73732
  95.5 37.2 %collective-permute-start.14 = (bf16[768,768]{1,0:T(8,128)(2,1)S(1)}, bf16[768,768]{1,0:T(8,128)(2,1)}, u32[]{:S(2)}, u32[]{:S(2)}) collective-permute-start(bf16[768,768]{1,0:T(8,128)(2,1)S(1)} %pad_maximum_fusion.3), channel_id=1, source_target_pairs={{0,16},{1,17},{2,18},{3,19},{4,20},{5,21},{6,22},{7,23},{8,24},{9,... | collective-permute-start | bytes 3538952 | tf_op jit(solution)/shard_map/ppermute | solution.py:907
  126.8 11.4 %collective-permute-start.12 = (bf16[512,1536]{1,0:T(8,128)(2,1)}, bf16[512,1536]{1,0:T(8,128)(2,1)}, u32[]{:S(2)}, u32[]{:S(2)}) collective-permute-start(bf16[512,1536]{1,0:T(8,128)(2,1)} %get-tuple-element.122), channel_id=1, source_target_pairs={{0,8},{8,0},{1,9},{9,1},{2,10},{10,2},{3,11},{11,3},{4,12},{12,4},... | collective-permute-start | bytes 4718600 | tf_op jit(solution)/shard_map/ppermute | solution.py:903
  134.8 15.1 %copy-start.5 = (bf16[512,768]{1,0:T(8,128)(2,1)}, bf16[512,768]{1,0:T(8,128)(2,1)S(1)}, u32[]{:S(2)}) copy-start(bf16[512,768]{1,0:T(8,128)(2,1)S(1)} %slice_select_fusion.refs_3_.refs_6_) | copy-start | bytes 2359300
  137.0 14.7 %collective-permute-start.15 = (bf16[512,1536]{1,0:T(8,128)(2,1)S(1)}, bf16[512,1536]{1,0:T(8,128)(2,1)S(1)}, u32[]{:S(2)}, u32[]{:S(2)}) collective-permute-start(bf16[512,1536]{1,0:T(8,128)(2,1)S(1)} %fusion.2.refs_1_.refs_15_), channel_id=1, source_target_pairs={{0,8},{8,0},{1,9},{9,1},{2,10},{10,2},{3,11},{11,3},{4,12},{12,4},... | collective-permute-start | bytes 4718600 | tf_op jit(solution)/shard_map/ppermute | solution.py:903
  142.0 35.2 %collective-permute-start.13 = (bf16[512,768]{1,0:T(8,128)(2,1)S(1)}, bf16[512,768]{1,0:T(8,128)(2,1)}, u32[]{:S(2)}, u32[]{:S(2)}) collective-permute-start(bf16[512,768]{1,0:T(8,128)(2,1)S(1)} %add_convert_fusion.15), channel_id=1, source_target_pairs={{16,0},{17,1},{18,2},{19,3},{20,4},{21,5},{22,6},{23,7},{24,8},{25... | collective-permute-start | bytes 2359304 | tf_op jit(solution)/shard_map/ppermute | solution.py:911
  179.5 33.3 %copy-start.119 = (bf16[768,384]{1,0:T(8,128)(2,1)S(1)}, bf16[768,384]{1,0:T(8,128)(2,1)}, u32[]{:S(2)}) copy-start(bf16[768,384]{1,0:T(8,128)(2,1)} %copy-done.116) | copy-start | bytes 1769476
  179.5 33.3 %copy-start.130 = (bf16[768,384]{1,0:T(8,128)(2,1)S(1)}, bf16[768,384]{1,0:T(8,128)(2,1)}, u32[]{:S(2)}) copy-start(bf16[768,384]{1,0:T(8,128)(2,1)} %copy-done.127) | copy-start | bytes 1769476
  207.2 8.9 %collective-permute-start.16 = (bf16[512,1536]{1,0:T(8,128)(2,1)}, bf16[512,1536]{1,0:T(8,128)(2,1)S(1)}, u32[]{:S(2)}, u32[]{:S(2)}) collective-permute-start(bf16[512,1536]{1,0:T(8,128)(2,1)} %get-tuple-element.137), channel_id=1, source_target_pairs={{0,8},{8,0},{1,9},{9,1},{2,10},{10,2},{3,11},{11,3},{4,12},{12,4},... | collective-permute-start | bytes 4718600 | tf_op jit(solution)/shard_map/ppermute | solution.py:903
  220.3 14.1 %copy-start.105 = (bf16[512,768]{1,0:T(8,128)(2,1)}, bf16[512,768]{1,0:T(8,128)(2,1)S(1)}, u32[]{:S(2)}) copy-start(bf16[512,768]{1,0:T(8,128)(2,1)S(1)} %add_convert_fusion.13) | copy-start | bytes 2359300
  220.3 18.9 %collective-permute-start.17 = (bf16[512,768]{1,0:T(8,128)(2,1)S(1)}, bf16[512,768]{1,0:T(8,128)(2,1)S(1)}, u32[]{:S(2)}, u32[]{:S(2)}) collective-permute-start(bf16[512,768]{1,0:T(8,128)(2,1)S(1)} %add_convert_fusion.13), channel_id=1, source_target_pairs={{16,0},{17,1},{18,2},{19,3},{20,4},{21,5},{22,6},{23,7},{24,8},{25... | collective-permute-start | bytes 2359304 | tf_op jit(solution)/shard_map/ppermute | solution.py:911
  222.3 17.0 %copy-start.60 = (bf16[512,768]{1,0:T(8,128)(2,1)S(1)}, bf16[512,768]{1,0:T(8,128)(2,1)}, u32[]{:S(2)}) copy-start(bf16[512,768]{1,0:T(8,128)(2,1)} %get-tuple-element.113.refs_1_.refs_2_) | copy-start | bytes 2359300
  222.3 16.9 %copy-start.82 = (bf16[256,768]{1,0:T(8,128)(2,1)S(1)}, bf16[256,768]{1,0:T(8,128)(2,1)}, u32[]{:S(2)}) copy-start(bf16[256,768]{1,0:T(8,128)(2,1)} %copy-done.81) | copy-start | bytes 1179652
  222.3 16.9 %copy-start.84 = (bf16[256,768]{1,0:T(8,128)(2,1)S(1)}, bf16[256,768]{1,0:T(8,128)(2,1)}, u32[]{:S(2)}) copy-start(bf16[256,768]{1,0:T(8,128)(2,1)} %copy-done.83) | copy-start | bytes 1179652
  245.0 5.0 collective-permute-start.18
  252.3 19.9 %copy-start.65 = (bf16[1536,768]{1,0:T(8,128)(2,1)}, bf16[1536,768]{1,0:T(8,128)(2,1)S(1)}, u32[]{:S(2)}) copy-start(bf16[1536,768]{1,0:T(8,128)(2,1)S(1)} %add_convert_fusion.1) | copy-start | bytes 7077892
  252.4 28.4 %collective-permute-start.19 = (bf16[768,768]{1,0:T(8,128)(2,1)S(1)}, bf16[768,768]{1,0:T(8,128)(2,1)S(1)}, u32[]{:S(2)}, u32[]{:S(2)}) collective-permute-start(bf16[768,768]{1,0:T(8,128)(2,1)S(1)} %dynamic-slice_bitcast_fusion.1.refs_0_), channel_id=1, source_target_pairs={{0,1},{1,0},{2,3},{3,2},{4,5},{5,4},{6,7},{7,6},{8,9},{9,8},{10,11... | collective-permute-start | bytes 3538952 | tf_op jit(solution)/shard_map/ppermute | solution.py:959
  273.9 58.1 %copy-start.14 = (f32[1,3072]{1,0:T(1,128)}, f32[1,3072]{1,0:T(1,128)S(1)}, u32[]{:S(2)}) copy-start(f32[1,3072]{1,0:T(1,128)S(1)} %get-tuple-element.167.refs_13_.refs_5_) | copy-start | bytes 36868
  281.8 4.9 collective-permute-start.21
  283.9 30.3 %collective-permute-start.20 = (bf16[768,768]{1,0:T(8,128)(2,1)S(1)}, bf16[768,768]{1,0:T(8,128)(2,1)S(1)}, u32[]{:S(2)}, u32[]{:S(2)}) collective-permute-start(bf16[768,768]{1,0:T(8,128)(2,1)S(1)} %fusion.4.refs_0_), channel_id=1, source_target_pairs={{0,2},{1,3},{6,4},{7,5},{8,10},{9,11},{14,12},{15,13},{16,18},{17,... | collective-permute-start | bytes 3538952 | tf_op jit(solution)/shard_map/ppermute | solution.py:963
  289.2 28.1 %collective-permute-start.22 = (bf16[384,1536]{1,0:T(8,128)(2,1)S(1)}, bf16[384,1536]{1,0:T(8,128)(2,1)S(1)}, u32[]{:S(2)}, u32[]{:S(2)}) collective-permute-start(bf16[384,1536]{1,0:T(8,128)(2,1)S(1)} %dynamic-slice_bitcast_fusion.refs_1_), channel_id=1, source_target_pairs={{0,1},{1,0},{2,3},{3,2},{4,5},{5,4},{6,7},{7,6},{8,9},{9,8},{10,11... | collective-permute-start | bytes 3538952 | tf_op jit(solution)/shard_map/ppermute | solution.py:959
  318.3 10.1 %collective-permute-start.25 = (bf16[512,1536]{1,0:T(8,128)(2,1)}, bf16[512,1536]{1,0:T(8,128)(2,1)}, u32[]{:S(2)}, u32[]{:S(2)}) collective-permute-start(bf16[512,1536]{1,0:T(8,128)(2,1)} %get-tuple-element.159), channel_id=1, source_target_pairs={{0,8},{8,0},{1,9},{9,1},{2,10},{10,2},{3,11},{11,3},{4,12},{12,4},... | collective-permute-start | bytes 4718600 | tf_op jit(solution)/shard_map/ppermute | solution.py:903
  321.4 30.6 %collective-permute-start.24 = (bf16[384,1536]{1,0:T(8,128)(2,1)}, bf16[384,1536]{1,0:T(8,128)(2,1)}, u32[]{:S(2)}, u32[]{:S(2)}) collective-permute-start(bf16[384,1536]{1,0:T(8,128)(2,1)} %fusion.3.refs_0_), channel_id=1, source_target_pairs={{0,2},{1,3},{6,4},{7,5},{8,10},{9,11},{14,12},{15,13},{16,18},{17,... | collective-permute-start | bytes 3538952 | tf_op jit(solution)/shard_map/ppermute | solution.py:963
  324.4 30.8 %collective-permute-start.23 = (bf16[768,768]{1,0:T(8,128)(2,1)}, bf16[768,768]{1,0:T(8,128)(2,1)}, u32[]{:S(2)}, u32[]{:S(2)}) collective-permute-start(bf16[768,768]{1,0:T(8,128)(2,1)} %add_convert_fusion.10), channel_id=1, source_target_pairs={{2,4},{3,5},{4,2},{5,3},{10,12},{11,13},{12,10},{13,11},{18,20},{1... | collective-permute-start | bytes 3538952 | tf_op jit(solution)/shard_map/ppermute | solution.py:966
  355.2 13.9 %collective-permute-start.31 = (bf16[1536,384]{1,0:T(8,128)(2,1)}, bf16[1536,384]{1,0:T(8,128)(2,1)S(1)}, u32[]{:S(2)}, u32[]{:S(2)}) collective-permute-start(bf16[1536,384]{1,0:T(8,128)(2,1)} %get-tuple-element.178), channel_id=1, source_target_pairs={{0,8},{8,0},{1,9},{9,1},{2,10},{10,2},{3,11},{11,3},{4,12},{12,4},... | collective-permute-start | bytes 3538952 | tf_op jit(solution)/shard_map/ppermute | solution.py:903
  356.6 13.6 %collective-permute-start.28 = (bf16[768,768]{1,0:T(8,128)(2,1)S(1)}, bf16[768,768]{1,0:T(8,128)(2,1)S(1)}, u32[]{:S(2)}, u32[]{:S(2)}) collective-permute-start(bf16[768,768]{1,0:T(8,128)(2,1)S(1)} %copy-done.104), channel_id=1, source_target_pairs={{0,8},{8,0},{1,9},{9,1},{2,10},{10,2},{3,11},{11,3},{4,12},{12,4},... | collective-permute-start | bytes 3538952 | tf_op jit(solution)/shard_map/ppermute | solution.py:903
  356.7 12.4 %collective-permute-start.29 = (f32[16,768]{1,0:T(8,128)S(1)}, f32[16,768]{1,0:T(8,128)S(1)}, u32[]{:S(2)}, u32[]{:S(2)}) collective-permute-start(f32[16,768]{1,0:T(8,128)S(1)} %copy-done.32), channel_id=1, source_target_pairs={{0,8},{8,0},{1,9},{9,1},{2,10},{10,2},{3,11},{11,3},{4,12},{12,4},... | collective-permute-start | bytes 147464 | tf_op jit(solution)/shard_map/ppermute | solution.py:903
  360.1 30.1 %collective-permute-start.27 = (bf16[384,1536]{1,0:T(8,128)(2,1)}, bf16[384,1536]{1,0:T(8,128)(2,1)}, u32[]{:S(2)}, u32[]{:S(2)}) collective-permute-start(bf16[384,1536]{1,0:T(8,128)(2,1)} %add_convert_fusion.8), channel_id=1, source_target_pairs={{2,4},{3,5},{4,2},{5,3},{10,12},{11,13},{12,10},{13,11},{18,20},{1... | collective-permute-start | bytes 3538952 | tf_op jit(solution)/shard_map/ppermute | solution.py:966
  366.7 27.0 %collective-permute-start.26 = (bf16[768,768]{1,0:T(8,128)(2,1)}, bf16[768,768]{1,0:T(8,128)(2,1)}, u32[]{:S(2)}, u32[]{:S(2)}) collective-permute-start(bf16[768,768]{1,0:T(8,128)(2,1)} %add_convert_fusion.9), channel_id=1, source_target_pairs={{2,0},{3,1},{4,6},{5,7},{10,8},{11,9},{12,14},{13,15},{18,16},{19,... | collective-permute-start | bytes 3538952 | tf_op jit(solution)/shard_map/ppermute | solution.py:970
  369.5 16.3 %collective-permute-start.32 = (bf16[768,384]{1,0:T(8,128)(2,1)S(1)}, bf16[768,384]{1,0:T(8,128)(2,1)S(1)}, u32[]{:S(2)}, u32[]{:S(2)}) collective-permute-start(bf16[768,384]{1,0:T(8,128)(2,1)S(1)} %dynamic-slice_bitcast_fusion.3), channel_id=1, source_target_pairs={{0,1},{1,0},{2,3},{3,2},{4,5},{5,4},{6,7},{7,6},{8,9},{9,8},{10,11... | collective-permute-start | bytes 1769480 | tf_op jit(solution)/shard_map/ppermute | solution.py:959
  371.0 26.7 %collective-permute-start.30 = (bf16[400,768]{1,0:T(8,128)(2,1)S(1)}, bf16[400,768]{1,0:T(8,128)(2,1)S(1)}, u32[]{:S(2)}, u32[]{:S(2)}) collective-permute-start(bf16[400,768]{1,0:T(8,128)(2,1)S(1)} %dynamic-slice_bitcast_fusion.2.refs_2_), channel_id=1, source_target_pairs={{0,1},{1,0},{2,3},{3,2},{4,5},{5,4},{6,7},{7,6},{8,9},{9,8},{10,11... | collective-permute-start | bytes 1843208 | tf_op jit(solution)/shard_map/ppermute | solution.py:959
  388.7 15.7 %collective-permute-start.34 = (bf16[768,384]{1,0:T(8,128)(2,1)}, bf16[768,384]{1,0:T(8,128)(2,1)}, u32[]{:S(2)}, u32[]{:S(2)}) collective-permute-start(bf16[768,384]{1,0:T(8,128)(2,1)} %fusion.12), channel_id=1, source_target_pairs={{0,2},{1,3},{6,4},{7,5},{8,10},{9,11},{14,12},{15,13},{16,18},{17,... | collective-permute-start | bytes 1769480 | tf_op jit(solution)/shard_map/ppermute | solution.py:963
  400.6 25.9 %collective-permute-start.35 = (bf16[384,1536]{1,0:T(8,128)(2,1)S(1)}, bf16[384,1536]{1,0:T(8,128)(2,1)}, u32[]{:S(2)}, u32[]{:S(2)}) collective-permute-start(bf16[384,1536]{1,0:T(8,128)(2,1)S(1)} %add_convert_fusion.5.refs_3_), channel_id=1, source_target_pairs={{2,0},{3,1},{4,6},{5,7},{10,8},{11,9},{12,14},{13,15},{18,16},{19,... | collective-permute-start | bytes 3538952 | tf_op jit(solution)/shard_map/ppermute | solution.py:970
  403.1 16.6 %collective-permute-start.37 = (bf16[400,768]{1,0:T(8,128)(2,1)S(1)}, bf16[400,768]{1,0:T(8,128)(2,1)S(1)}, u32[]{:S(2)}, u32[]{:S(2)}) collective-permute-start(bf16[400,768]{1,0:T(8,128)(2,1)S(1)} %fusion.11), channel_id=1, source_target_pairs={{0,2},{1,3},{6,4},{7,5},{8,10},{9,11},{14,12},{15,13},{16,18},{17,... | collective-permute-start | bytes 1843208 | tf_op jit(solution)/shard_map/ppermute | solution.py:963
  406.7 18.1 %collective-permute-start.36 = (bf16[768,384]{1,0:T(8,128)(2,1)}, bf16[768,384]{1,0:T(8,128)(2,1)}, u32[]{:S(2)}, u32[]{:S(2)}) collective-permute-start(bf16[768,384]{1,0:T(8,128)(2,1)} %add_convert_fusion.21), channel_id=1, source_target_pairs={{2,4},{3,5},{4,2},{5,3},{10,12},{11,13},{12,10},{13,11},{18,20},{1... | collective-permute-start | bytes 1769480 | tf_op jit(solution)/shard_map/ppermute | solution.py:966
  412.3 50.4 %collective-permute-start.33 = (bf16[768,768]{1,0:T(8,128)(2,1)}, bf16[768,768]{1,0:T(8,128)(2,1)}, u32[]{:S(2)}, u32[]{:S(2)}) collective-permute-start(bf16[768,768]{1,0:T(8,128)(2,1)} %broadcast_select_fusion.5), channel_id=1, source_target_pairs={{0,1},{1,0},{2,3},{3,2},{4,5},{5,4},{6,7},{7,6},{8,9},{9,8},{10,11... | collective-permute-start | bytes 3538952 | tf_op jit(solution)/shard_map/ppermute | solution.py:971
  422.6 28.0 %collective-permute-start.39 = (bf16[400,768]{1,0:T(8,128)(2,1)}, bf16[400,768]{1,0:T(8,128)(2,1)}, u32[]{:S(2)}, u32[]{:S(2)}) collective-permute-start(bf16[400,768]{1,0:T(8,128)(2,1)} %add_convert_fusion.19), channel_id=1, source_target_pairs={{2,4},{3,5},{4,2},{5,3},{10,12},{11,13},{12,10},{13,11},{18,20},{1... | collective-permute-start | bytes 1843208 | tf_op jit(solution)/shard_map/ppermute | solution.py:966
  433.0 29.6 %collective-permute-start.38 = (bf16[768,384]{1,0:T(8,128)(2,1)}, bf16[768,384]{1,0:T(8,128)(2,1)}, u32[]{:S(2)}, u32[]{:S(2)}) collective-permute-start(bf16[768,384]{1,0:T(8,128)(2,1)} %add_convert_fusion.20.refs_2_), channel_id=1, source_target_pairs={{2,0},{3,1},{4,6},{5,7},{10,8},{11,9},{12,14},{13,15},{18,16},{19,... | collective-permute-start | bytes 1769480 | tf_op jit(solution)/shard_map/ppermute | solution.py:970
  438.5 19.7 %collective-permute-start.40 = (bf16[512,768]{1,0:T(8,128)(2,1)}, bf16[512,768]{1,0:T(8,128)(2,1)}, u32[]{:S(2)}, u32[]{:S(2)}) collective-permute-start(bf16[512,768]{1,0:T(8,128)(2,1)} %get-tuple-element.193), channel_id=1, source_target_pairs={{16,0},{17,1},{18,2},{19,3},{20,4},{21,5},{22,6},{23,7},{24,8},{25... | collective-permute-start | bytes 2359304 | tf_op jit(solution)/shard_map/ppermute | solution.py:911
  449.1 19.3 %collective-permute-start.41 = (bf16[512,768]{1,0:T(8,128)(2,1)}, bf16[512,768]{1,0:T(8,128)(2,1)S(1)}, u32[]{:S(2)}, u32[]{:S(2)}) collective-permute-start(bf16[512,768]{1,0:T(8,128)(2,1)} %pad_maximum_fusion.7), channel_id=1, source_target_pairs={{0,16},{1,17},{2,18},{3,19},{4,20},{5,21},{6,22},{7,23},{8,24},{9,... | collective-permute-start | bytes 2359304 | tf_op jit(solution)/shard_map/ppermute | solution.py:907
  450.6 30.6 %collective-permute-start.45 = (bf16[384,1536]{1,0:T(8,128)(2,1)S(1)}, bf16[384,1536]{1,0:T(8,128)(2,1)S(1)}, u32[]{:S(2)}, u32[]{:S(2)}) collective-permute-start(bf16[384,1536]{1,0:T(8,128)(2,1)S(1)} %broadcast_select_fusion.4), channel_id=1, source_target_pairs={{0,1},{1,0},{2,3},{3,2},{4,5},{5,4},{6,7},{7,6},{8,9},{9,8},{10,11... | collective-permute-start | bytes 3538952 | tf_op jit(solution)/shard_map/ppermute | solution.py:971
  460.4 18.2 %collective-permute-start.43 = (bf16[400,768]{1,0:T(8,128)(2,1)}, bf16[400,768]{1,0:T(8,128)(2,1)}, u32[]{:S(2)}, u32[]{:S(2)}) collective-permute-start(bf16[400,768]{1,0:T(8,128)(2,1)} %add_convert_fusion.18), channel_id=1, source_target_pairs={{2,0},{3,1},{4,6},{5,7},{10,8},{11,9},{12,14},{13,15},{18,16},{19,... | collective-permute-start | bytes 1843208 | tf_op jit(solution)/shard_map/ppermute | solution.py:970
  471.2 21.1 %collective-permute-start.42 = (bf16[768,384]{1,0:T(8,128)(2,1)}, bf16[768,384]{1,0:T(8,128)(2,1)}, u32[]{:S(2)}, u32[]{:S(2)}) collective-permute-start(bf16[768,384]{1,0:T(8,128)(2,1)} %broadcast_select_fusion.12), channel_id=1, source_target_pairs={{0,1},{1,0},{2,3},{3,2},{4,5},{5,4},{6,7},{7,6},{8,9},{9,8},{10,11... | collective-permute-start | bytes 1769480 | tf_op jit(solution)/shard_map/ppermute | solution.py:971
  479.7 22.4 %collective-permute-start.44 = (bf16[400,768]{1,0:T(8,128)(2,1)S(1)}, bf16[400,768]{1,0:T(8,128)(2,1)}, u32[]{:S(2)}, u32[]{:S(2)}) collective-permute-start(bf16[400,768]{1,0:T(8,128)(2,1)S(1)} %broadcast_select_fusion.9), channel_id=1, source_target_pairs={{0,1},{1,0},{2,3},{3,2},{4,5},{5,4},{6,7},{7,6},{8,9},{9,8},{10,11... | collective-permute-start | bytes 1843208 | tf_op jit(solution)/shard_map/ppermute | solution.py:971
  (117 other events, 328.3 us)

commit v5 on v4

--- a/solution.py
+++ b/solution.py
@@ -1131,15 +1131,15 @@
     (tick,) = step_sums([down, up, last], tick)
     (tick,) = step_sums([inner], tick)
     (tick,) = step_sums([last], tick)
-    tick, dq, dkv = step_sums([up, inner], tick, b6.dq, b6.dkv)
+    (tick,) = step_sums([up, inner], tick)
+    (tick,) = step_sums([last], tick)
+    (tick,) = step_sums([down, inner], tick)
+    tick, dq, dkv = step_sums([last], tick, b6.dq, b6.dkv)
     quarters = jnp.concatenate([out2[:quarter], out4[:quarter]], axis=0)
-    tick, quarters = tied(tick, quarters, unread=(inner.sent, up.sent))
+    tick, quarters = tied(tick, quarters, unread=(last.sent,))
     layer_far = last_section(quarters)
     g6 = rows_gradient(b6, dq, dkv, w)
     tokens_far = next_section(jnp.concatenate([g5[quarter:], g6[quarter:]], axis=0))
-    tick, layer_far = step_sums([last], tick, layer_far)
-    tick, tokens_far = step_sums([down, inner], tick, tokens_far)
-    (tick,) = step_sums([last], tick)
     while up.whole is None or down.whole is None:
         (tick,) = step_sums([up, down], tick)
     pair = lambda x, y: jnp.stack([x, y])

time: 519 us -> 510 us (0.983)
  waiting for transfers between devices: 120 us -> 111 us
  starting transfers between devices: 73.1 us -> 65.4 us
  Pallas kernels: 182 us -> 188 us
    ppermute x4, waiting for transfers between devices: 15.7 us -> 2.56 us  [walk(): got = (yield lax.ppermute(total, 'dp', pairs))]
    ppermute x4, waiting for transfers between devices: 5.29 us -> 15.8 us  [walk(): lax.ppermute(total, 'dp', moves)]
    ppermute x4, waiting for transfers between devices: 20.4 us -> 13.7 us  [last_section(): return lax.ppermute(x, 'section', [(1, 0)])]
    ppermute x18, starting transfers between devices: 13.7 us -> 8.19 us  [to_peer(): return lax.ppermute(x, 'mp', SWAP)]
    unnamed x271 -> x279, local copies, waits for them, and re-layouts: 31.9 us -> 32.4 us
  transfers between devices with their start and end apart: 46 -> 46, of which waited for: 24 -> 26; matrix products, arithmetic and copies ran while one was open for 16% -> 17% of each run, Pallas kernels for 21% -> 22%
where the time goes in v5:
time: 510 us; the launch traced here: 501 us
  Pallas kernels  188 us (37%)
  waiting for transfers between devices  111 us (22%)
  other arithmetic  68 us (13%)
  starting transfers between devices  65.4 us (13%)
  local copies, waits for them, and re-layouts  43.6 us (9%)
  matrix products  22.6 us (4%)
    pallas_call x4, Pallas kernels, backward_call(): pl.pallas_call(functools.partial(backward_kernel, which, slot_of, len(tok...  93.8 us
    pallas_call x3, Pallas kernels, forward_call(): pl.pallas_call(functools.partial(forward_kernel, save, slot_of, len(token...  64.8 us
    convert_element_type x18, other arithmetic, add_low(): return (a.astype(F32) + b.astype(F32)).astype(BF)  33.7 us
    unnamed x279, local copies, waits for them, and re-layouts  32.4 us
    ppermute x8, waiting for transfers between devices, walk(): total = add_low(total, (yield lax.ppermute(total, 'dp', moves)))  28.4 us
    ppermute x4, waiting for transfers between devices, walk(): total = add_low(keep, (yield lax.ppermute(send, 'dp', pairs)))  24.6 us
    ppermute x4, starting transfers between devices, last_section(): return lax.ppermute(x, 'section', [(1, 0)])  18.6 us
    ppermute x8, starting transfers between devices, walk(): total = add_low(total, (yield lax.ppermute(total, 'dp', moves)))  17.6 us
  transfers between devices with their start and end apart: 46, of which 26 were waited for; matrix products, arithmetic and copies ran while one was open for 17% of the time, Pallas kernels for 22%

profile of v5, /device:TPU:14, one launch (start us, length us, event | category | flops | bytes accessed | tf_op | source)
XLA Modules:
  0.0 500.5 jit_solution(1475153445409890272)
XLA Ops:
  5.2 2.2 slice_bitcast_fusion.2
  7.4 6.1 %collective-permute-done.3 = bf16[256,768]{1,0:T(8,128)(2,1)S(1)} collective-permute-done((bf16[256,768]{1,0:T(8,128)(2,1)S(1)}, bf16[256,768]{1,0:T(8,128)(2,1)S(1)}, u32[]{:S(2)}, u32[]{:S(2)}) %collective-permute-start.3) | collective-permute-done | bytes 393248 | tf_op jit(solution)/shard_map/ppermute | solution.py:1060
  13.5 2.1 fusion.refs_1_
  17.4 2.6 collective-permute-done.shift_far
  23.9 20.1 %layer_forward.3 = bf16[512,768]{1,0:T(8,128)(2,1)S(1)} custom-call(s32[2]{0:T(128)S(1)} %copy-done.33, s32[2]{0:T(128)S(1)} %copy-done.36, s32[1,6]{1,0:T(1,128)S(1)} %copy-done.39, s32[1,6]{1,0:T(1,128)S(1)} %collective-permute-done.shift_far, f32[4,768]{1,0:T(4,128)S(1)} %bitcast.108, f32[2,768]{1,0:T(2,128)S(1)} %bitcast.101, f32[1,1536]{1,0:T(1,128)S(1)} %copy-done.28, ...), custom_call_target="tpu_custom_call" | custom-call | flops 1 | bytes 1 | tf_op jit(solution)/shard_map/layer_forward/pallas_call | solution.py:471
  45.5 4.6 collective-permute-start.2
  50.1 8.9 %collective-permute-done.2 = bf16[256,768]{1,0:T(8,128)(2,1)S(1)} collective-permute-done((bf16[256,768]{1,0:T(8,128)(2,1)S(1)}, bf16[256,768]{1,0:T(8,128)(2,1)S(1)}, u32[]{:S(2)}, u32[]{:S(2)}) %collective-permute-start.2) | collective-permute-done | bytes 393248 | tf_op jit(solution)/shard_map/ppermute | solution.py:911
  59.0 7.2 %collective-permute-done.10 = bf16[512,768]{1,0:T(8,128)(2,1)S(1)} collective-permute-done((bf16[512,768]{1,0:T(8,128)(2,1)S(1)}, bf16[512,768]{1,0:T(8,128)(2,1)S(1)}, u32[]{:S(2)}, u32[]{:S(2)}) %collective-permute-start.10) | collective-permute-done | bytes 786464 | tf_op jit(solution)/shard_map/ppermute | solution.py:907
  66.4 2.1 fusion.1.refs_1_.refs_15_.refs_5_
  73.3 21.4 %layer_forward.4 = (bf16[512,768]{1,0:T(8,128)(2,1)S(1)}, bf16[512,768]{1,0:T(8,128)(2,1)S(1)}, f32[6,2,512]{2,1,0:T(2,128)S(1)}, bf16[512,768]{1,0:T(8,128)(2,1...) custom-call(s32[2]{0:T(128)S(1)} %copy-done.33, ...), custom_call_target="tpu_custom_call" | custom-call | flops 1 | bytes 1 | tf_op jit(solution)/shard_map/layer_forward/pallas_call | solution.py:471
  96.9 28.1 %layer_backward.4 = (bf16[512,768]{1,0:T(8,128)(2,1)S(1)}, bf16[512,3072]{1,0:T(8,128)(2,1)}, bf16[512,768]{1,0:T(8,128)(2,1)S(1)}, f32[8,768]{1,0:T(8,128)}, f3...) custom-call(s32[2]{0:T(128)S(1)} %copy-done.33, ...), custom_call_target="tpu_custom_call" | custom-call | flops 1 | bytes 1 | tf_op jit(solution)/shard_map/layer_backward/pallas_call | solution.py:887
  126.8 5.9 %collective-permute-start.12 = (bf16[512,1536]{1,0:T(8,128)(2,1)}, bf16[512,1536]{1,0:T(8,128)(2,1)}, u32[]{:S(2)}, u32[]{:S(2)}) collective-permute-start(bf16[512,1536]{1,0:T(8,128)(2,1)} %get-tuple-element.120), channel_id=1, source_target_pairs={{0,8},{8,0},{1,9},{9,1},{2,10},{10,2},{3,11},{11,3},{4,12},{12,4},... | collective-permute-start | bytes 4718600 | tf_op jit(solution)/shard_map/ppermute | solution.py:903
  134.9 2.1 fusion.2.refs_1_.refs_15_
  139.3 2.8 add_convert_fusion.15
  142.1 6.2 %collective-permute-start.13 = (bf16[512,768]{1,0:T(8,128)(2,1)S(1)}, bf16[512,768]{1,0:T(8,128)(2,1)}, u32[]{:S(2)}, u32[]{:S(2)}) collective-permute-start(bf16[512,768]{1,0:T(8,128)(2,1)S(1)} %add_convert_fusion.15), channel_id=1, source_target_pairs={{16,0},{17,1},{18,2},{19,3},{20,4},{21,5},{22,6},{23,7},{24,8},{25... | collective-permute-start | bytes 2359304 | tf_op jit(solution)/shard_map/ppermute | solution.py:911
  152.9 23.3 %layer_forward.5 = (bf16[512,768]{1,0:T(8,128)(2,1)S(1)}, bf16[512,768]{1,0:T(8,128)(2,1)S(1)}, f32[6,2,512]{2,1,0:T(2,128)S(1)}, bf16[512,768]{1,0:T(8,128)(2,1...) custom-call(s32[2]{0:T(128)S(1)} %copy-done.34, ...), custom_call_target="tpu_custom_call" | custom-call | flops 1 | bytes 1 | tf_op jit(solution)/shard_map/layer_forward/pallas_call | solution.py:471
  179.4 2.2 maximum_select_fusion.1.refs_0_
  181.7 31.4 %layer_backward.5 = (bf16[512,768]{1,0:T(8,128)(2,1)S(1)}, bf16[512,3072]{1,0:T(8,128)(2,1)}, bf16[512,768]{1,0:T(8,128)(2,1)S(1)}, f32[8,768]{1,0:T(8,128)S(1)}...) custom-call(s32[2]{0:T(128)S(1)} %copy-done.35, ...), custom_call_target="tpu_custom_call" | custom-call | flops 1 | bytes 1 | tf_op jit(solution)/shard_map/layer_backward/pallas_call | solution.py:887
  213.2 2.1 fusion.16
  222.8 12.1 %layer_gradient.1 = (bf16[3072,768]{1,0:T(8,128)(2,1)}, bf16[768,3072]{1,0:T(8,128)(2,1)}, bf16[768,768]{1,0:T(8,128)(2,1)}, bf16[768,768]{1,0:T(8,128)(2,1)}, b...) custom-call(bf16[512,3072]{1,0:T(8,128)(2,1)} %get-tuple-element.137.refs_0_, ...), custom_call_target="tpu_custom_call" | custom-call | flops 1 | bytes 1 | tf_op jit(solution)/shard_map/layer_gradient/pallas_call | solution.py:729
  234.9 4.8 collective-permute-done.17
  240.7 4.8 half_gradient.2.token
  245.6 4.9 half_gradient.3
  250.5 2.3 add_convert_fusion.1
  254.1 18.6 %layer_backward.6 = (bf16[512,768]{1,0:T(8,128)(2,1)}, bf16[512,3072]{1,0:T(8,128)(2,1)}, bf16[512,768]{1,0:T(8,128)(2,1)S(1)}, f32[8,768]{1,0:T(8,128)S(1)}, f3...) custom-call(s32[2]{0:T(128)S(1)} %copy-done.35, ...), custom_call_target="tpu_custom_call" | custom-call | flops 1 | bytes 1 | tf_op jit(solution)/shard_map/layer_backward/pallas_call | solution.py:887
  274.5 6.9 %collective-permute-done.19.refs_0_ = bf16[768,768]{1,0:T(8,128)(2,1)S(1)} collective-permute-done((bf16[768,768]{1,0:T(8,128)(2,1)S(1)}, bf16[768,768]{1,0:T(8,128)(2,1)S(1)}, u32[]{:S(2)}, u32[]{:S(2)}) %collective-permute-start.19) | collective-permute-done | bytes 1179680 | tf_op jit(solution)/shard_map/ppermute | solution.py:959
  282.4 2.1 fusion.4.refs_0_
  287.2 2.3 add_convert_fusion
  292.4 15.7 %layer_backward.7 = (bf16[512,768]{1,0:T(8,128)(2,1)S(1)}, bf16[512,1536]{1,0:T(8,128)(2,1)}, bf16[512,1536]{1,0:T(8,128)(2,1)}) custom-call(s32[2]{0:T(128)S(1)} %copy-done.35, s32[2]{0:T(128)S(1)} %copy-done.38, s32[1,6]{1,0:T(1,128)S(1)} %copy-done.42, s32[1,6]{1,0:T(1,128)S(1)} %copy-done.46, f32[2,768]{1,0:T(2,128)S(1)} %bitcast.107, ...), custom_call_target="tpu_custom_call" | custom-call | flops 1 | bytes 1 | tf_op jit(solution)/shard_map/layer_backward/pallas_call | solution.py:887
  309.1 5.7 %collective-permute-done.20.refs_0_ = bf16[768,768]{1,0:T(8,128)(2,1)S(1)} collective-permute-done((bf16[768,768]{1,0:T(8,128)(2,1)S(1)}, bf16[768,768]{1,0:T(8,128)(2,1)S(1)}, u32[]{:S(2)}, u32[]{:S(2)}) %collective-permute-start.20) | collective-permute-done | bytes 1179680 | tf_op jit(solution)/shard_map/ppermute | solution.py:963
  318.8 3.1 fusion.3.refs_0_
  324.7 3.5 collective-permute-start.23
  328.4 3.6 add_convert_fusion.2.refs_5_.refs_3_
  332.0 7.3 %last_gradient.1 = (bf16[768,768]{1,0:T(8,128)(2,1)}, bf16[768,768]{1,0:T(8,128)(2,1)}, bf16[1536,384]{1,0:T(8,128)(2,1)}, bf16[1536,384]{1,0:T(8,128)(2,1)}, f3...) custom-call(bf16[384,1536]{1,0:T(8,128)(2,1)} %fusion.3.refs_0_, bf16[512,768]{1,0:T(8,128)(2,1)S(1)} %copy-done.8, ...), custom_call_target="tpu_custom_call" | custom-call | flops 1 | bytes 1 | tf_op jit(solution)/shard_map/last_gradient/pallas_call | solution.py:831
  339.9 12.6 %collective-permute-done.24.refs_1_ = bf16[384,1536]{1,0:T(8,128)(2,1)} collective-permute-done((bf16[384,1536]{1,0:T(8,128)(2,1)}, bf16[384,1536]{1,0:T(8,128)(2,1)}, u32[]{:S(2)}, u32[]{:S(2)}) %collective-permute-start.24) | collective-permute-done | bytes 1179680 | tf_op jit(solution)/shard_map/ppermute | solution.py:963
  352.5 2.8 collective-permute-done.23.refs_0_
  357.2 2.9 add_convert_fusion.8
  360.1 3.5 collective-permute-start.27
  363.6 3.0 add_convert_fusion.9
  366.6 2.3 collective-permute-start.26
  374.1 11.6 %collective-permute-done.32.refs_0_ = bf16[768,384]{1,0:T(8,128)(2,1)S(1)} collective-permute-done((bf16[768,384]{1,0:T(8,128)(2,1)S(1)}, bf16[768,384]{1,0:T(8,128)(2,1)S(1)}, u32[]{:S(2)}, u32[]{:S(2)}) %collective-permute-start.32) | collective-permute-done | bytes 589856 | tf_op jit(solution)/shard_map/ppermute | solution.py:959
  386.6 2.2 fusion.12
  390.2 3.4 collective-permute-done.26.refs_0_
  393.6 4.0 collective-permute-done.30.refs_2_
  398.5 3.0 add_convert_fusion.5
  401.4 2.3 collective-permute-start.35
  405.4 2.2 add_convert_fusion.21
  407.6 2.3 collective-permute-start.36
  411.0 2.4 broadcast_select_fusion.5
  414.0 6.7 %collective-permute-done.37.refs_0_ = bf16[400,768]{1,0:T(8,128)(2,1)S(1)} collective-permute-done((bf16[400,768]{1,0:T(8,128)(2,1)S(1)}, bf16[400,768]{1,0:T(8,128)(2,1)S(1)}, u32[]{:S(2)}, u32[]{:S(2)}) %collective-permute-start.37) | collective-permute-done | bytes 614432 | tf_op jit(solution)/shard_map/ppermute | solution.py:963
  422.7 2.3 collective-permute-start.39
  425.1 2.5 collective-permute-done.35.refs_0_
  427.6 2.2 add_convert_fusion.20
  429.8 5.2 %collective-permute-start.38 = (bf16[768,384]{1,0:T(8,128)(2,1)}, bf16[768,384]{1,0:T(8,128)(2,1)}, u32[]{:S(2)}, u32[]{:S(2)}) collective-permute-start(bf16[768,384]{1,0:T(8,128)(2,1)} %add_convert_fusion.20), channel_id=1, source_target_pairs={{2,0},{3,1},{4,6},{5,7},{10,8},{11,9},{12,14},{13,15},{18,16},{19,... | collective-permute-start | bytes 1769480 | tf_op jit(solution)/shard_map/ppermute | solution.py:970
  435.1 2.4 broadcast_select_fusion.4
  442.0 6.3 %collective-permute-done.38.refs_1_ = bf16[768,384]{1,0:T(8,128)(2,1)} collective-permute-done((bf16[768,384]{1,0:T(8,128)(2,1)}, bf16[768,384]{1,0:T(8,128)(2,1)}, u32[]{:S(2)}, u32[]{:S(2)}) %collective-permute-start.38) | collective-permute-done | bytes 589856 | tf_op jit(solution)/shard_map/ppermute | solution.py:970
  452.5 2.5 maximum_convert_fusion.refs_3_
  455.1 3.5 collective-permute-done.41.refs_0_
  459.9 2.3 fusion.15
  467.8 6.3 %collective-permute-start.44 = (bf16[512,768]{1,0:T(8,128)(2,1)}, bf16[512,768]{1,0:T(8,128)(2,1)}, u32[]{:S(2)}, u32[]{:S(2)}) collective-permute-start(bf16[512,768]{1,0:T(8,128)(2,1)} %get-tuple-element.201), channel_id=1, source_target_pairs={{16,0},{17,1},{18,2},{19,3},{20,4},{21,5},{22,6},{23,7},{24,8},{25... | collective-permute-start | bytes 2359304 | tf_op jit(solution)/shard_map/ppermute | solution.py:911
  477.6 2.8 maximum_convert_fusion.1.refs_4_
  480.4 5.2 %collective-permute-done.45 = bf16[512,768]{1,0:T(8,128)(2,1)} collective-permute-done((bf16[512,768]{1,0:T(8,128)(2,1)}, bf16[512,768]{1,0:T(8,128)(2,1)}, u32[]{:S(2)}, u32[]{:S(2)}) %collective-permute-start.45) | collective-permute-done | bytes 786464 | tf_op jit(solution)/shard_map/ppermute | solution.py:907
  485.6 2.1 maximum_select_fusion.3.refs_6_
  488.8 2.4 collective-permute-done.42.refs_1_
  (420 shorter events, 103.3 us)
Async XLA Ops:
  0.7 4.6 collective-permute-start.4
  2.0 11.5 %collective-permute-start.3 = (bf16[256,768]{1,0:T(8,128)(2,1)S(1)}, bf16[256,768]{1,0:T(8,128)(2,1)S(1)}, u32[]{:S(2)}, u32[]{:S(2)}) collective-permute-start(bf16[256,768]{1,0:T(8,128)(2,1)S(1)} %broadcast_select_fusion.13), channel_id=1, source_target_pairs={{0,16},{16,0},{1,17},{17,1},{2,18},{18,2},{3,19},{19,3},{4,20},{20... | collective-permute-start | bytes 1179656 | tf_op jit(solution)/shard_map/ppermute | solution.py:1060
  2.6 2.5 collective-permute-start.5
  2.7 18.5 %collective-permute-start.8 = (bf16[768,1536]{1,0:T(8,128)(2,1)}, bf16[768,1536]{1,0:T(8,128)(2,1)S(1)}, u32[]{:S(2)}, u32[]{:S(2)}) collective-permute-start(bf16[768,1536]{1,0:T(8,128)(2,1)} %bitcast.111), channel_id=1, source_target_pairs={{0,8},{8,0},{1,9},{9,1},{2,10},{10,2},{3,11},{11,3},{4,12},{12,4},... | collective-permute-start | bytes 7077896 | tf_op jit(solution)/shard_map/ppermute | solution.py:903
  3.1 18.1 %collective-permute-start.9 = (bf16[1536,768]{1,0:T(8,128)(2,1)}, bf16[1536,768]{1,0:T(8,128)(2,1)S(1)}, u32[]{:S(2)}, u32[]{:S(2)}) collective-permute-start(bf16[1536,768]{1,0:T(8,128)(2,1)} %bitcast.118), channel_id=1, source_target_pairs={{0,8},{8,0},{1,9},{9,1},{2,10},{10,2},{3,11},{11,3},{4,12},{12,4},... | collective-permute-start | bytes 7077896 | tf_op jit(solution)/shard_map/ppermute | solution.py:903
  4.4 15.7 %copy-start.79 = (bf16[256,768]{1,0:T(8,128)(2,1)}, bf16[256,768]{1,0:T(8,128)(2,1)S(1)}, u32[]{:S(2)}) copy-start(bf16[256,768]{1,0:T(8,128)(2,1)S(1)} %get-tuple-element.242) | copy-start | bytes 1179652
  5.1 15.0 %copy-start.119 = (bf16[768,384]{1,0:T(8,128)(2,1)}, bf16[768,384]{1,0:T(8,128)(2,1)S(1)}, u32[]{:S(2)}) copy-start(bf16[768,384]{1,0:T(8,128)(2,1)S(1)} %get-tuple-element.223) | copy-start | bytes 1769476
  7.4 59.0 %copy-start.124 = (bf16[768,384]{1,0:T(8,128)(2,1)}, bf16[768,384]{1,0:T(8,128)(2,1)S(1)}, u32[]{:S(2)}) copy-start(bf16[768,384]{1,0:T(8,128)(2,1)S(1)} %get-tuple-element.224) | copy-start | bytes 1769476
  7.4 59.0 %copy-start.128 = (bf16[768,384]{1,0:T(8,128)(2,1)}, bf16[768,384]{1,0:T(8,128)(2,1)S(1)}, u32[]{:S(2)}) copy-start(bf16[768,384]{1,0:T(8,128)(2,1)S(1)} %get-tuple-element.225) | copy-start | bytes 1769476
  15.7 5.5 %collective-permute-start.6 = (bf16[512,1536]{1,0:T(8,128)(2,1)S(1)}, bf16[512,1536]{1,0:T(8,128)(2,1)S(1)}, u32[]{:S(2)}, u32[]{:S(2)}) collective-permute-start(bf16[512,1536]{1,0:T(8,128)(2,1)S(1)} %fusion.refs_1_), channel_id=1, source_target_pairs={{0,8},{8,0},{1,9},{9,1},{2,10},{10,2},{3,11},{11,3},{4,12},{12,4},... | collective-permute-start | bytes 4718600 | tf_op jit(solution)/shard_map/ppermute | solution.py:903
  15.8 5.4 %collective-permute-start.7 = (bf16[384,768]{1,0:T(8,128)(2,1)S(1)}, bf16[384,768]{1,0:T(8,128)(2,1)S(1)}, u32[]{:S(2)}, u32[]{:S(2)}) collective-permute-start(bf16[384,768]{1,0:T(8,128)(2,1)S(1)} %bitcast.94), channel_id=1, source_target_pairs={{0,8},{8,0},{1,9},{9,1},{2,10},{10,2},{3,11},{11,3},{4,12},{12,4},... | collective-permute-start | bytes 1769480 | tf_op jit(solution)/shard_map/ppermute | solution.py:903
  16.3 3.7 collective-permute-start
  20.0 76.9 %copy-start.43 = (s32[1,6]{1,0:T(1,128)}, s32[1,6]{1,0:T(1,128)S(1)}, u32[]{:S(2)}) copy-start(s32[1,6]{1,0:T(1,128)S(1)} %collective-permute-done.shift_far) | copy-start | bytes 76
  20.0 1.2 collective-permute-start.1
  21.2 50.9 %copy-start.29 = (f32[1,1536]{1,0:T(1,128)}, f32[1,1536]{1,0:T(1,128)S(1)}, u32[]{:S(2)}) copy-start(f32[1,1536]{1,0:T(1,128)S(1)} %collective-permute-done.1.bup_far) | copy-start | bytes 18436
  44.0 22.3 %copy-start.110 = (bf16[768,384]{1,0:T(8,128)(2,1)S(1)}, bf16[768,384]{1,0:T(8,128)(2,1)}, u32[]{:S(2)}) copy-start(bf16[768,384]{1,0:T(8,128)(2,1)} %copy-done.109) | copy-start | bytes 1769476
  44.0 22.3 %copy-start.115 = (bf16[768,384]{1,0:T(8,128)(2,1)S(1)}, bf16[768,384]{1,0:T(8,128)(2,1)}, u32[]{:S(2)}) copy-start(bf16[768,384]{1,0:T(8,128)(2,1)} %copy-done.114) | copy-start | bytes 1769476
  44.1 22.1 %collective-permute-start.10 = (bf16[512,768]{1,0:T(8,128)(2,1)S(1)}, bf16[512,768]{1,0:T(8,128)(2,1)S(1)}, u32[]{:S(2)}, u32[]{:S(2)}) collective-permute-start(bf16[512,768]{1,0:T(8,128)(2,1)S(1)} %layer_forward.3), channel_id=1, source_target_pairs={{0,16},{1,17},{2,18},{3,19},{4,20},{5,21},{6,22},{7,23},{8,24},{9,... | collective-permute-start | bytes 2359304 | tf_op jit(solution)/shard_map/ppermute | solution.py:907
  45.5 13.5 %collective-permute-start.2 = (bf16[256,768]{1,0:T(8,128)(2,1)S(1)}, bf16[256,768]{1,0:T(8,128)(2,1)S(1)}, u32[]{:S(2)}, u32[]{:S(2)}) collective-permute-start(bf16[256,768]{1,0:T(8,128)(2,1)S(1)} %get-tuple-element.241), channel_id=1, source_target_pairs={{16,0},{17,1},{18,2},{19,3},{20,4},{21,5},{22,6},{23,7},{24,8},{25... | collective-permute-start | bytes 1179656 | tf_op jit(solution)/shard_map/ppermute | solution.py:911
  68.6 3.5 collective-permute-start.11
  95.5 29.5 %copy-start.26 = (f32[6,2,512]{2,1,0:T(2,128)}, f32[6,2,512]{2,1,0:T(2,128)S(1)}, u32[]{:S(2)}) copy-start(f32[6,2,512]{2,1,0:T(2,128)S(1)} %get-tuple-element.116.refs_13_.refs_3_) | copy-start | bytes 73732
  95.6 37.2 %collective-permute-start.14 = (bf16[768,768]{1,0:T(8,128)(2,1)S(1)}, bf16[768,768]{1,0:T(8,128)(2,1)}, u32[]{:S(2)}, u32[]{:S(2)}) collective-permute-start(bf16[768,768]{1,0:T(8,128)(2,1)S(1)} %pad_maximum_fusion.3), channel_id=1, source_target_pairs={{0,16},{1,17},{2,18},{3,19},{4,20},{5,21},{6,22},{7,23},{8,24},{9,... | collective-permute-start | bytes 3538952 | tf_op jit(solution)/shard_map/ppermute | solution.py:907
  126.8 11.4 %collective-permute-start.12 = (bf16[512,1536]{1,0:T(8,128)(2,1)}, bf16[512,1536]{1,0:T(8,128)(2,1)}, u32[]{:S(2)}, u32[]{:S(2)}) collective-permute-start(bf16[512,1536]{1,0:T(8,128)(2,1)} %get-tuple-element.120), channel_id=1, source_target_pairs={{0,8},{8,0},{1,9},{9,1},{2,10},{10,2},{3,11},{11,3},{4,12},{12,4},... | collective-permute-start | bytes 4718600 | tf_op jit(solution)/shard_map/ppermute | solution.py:903
  134.9 15.2 %copy-start.5 = (bf16[512,768]{1,0:T(8,128)(2,1)}, bf16[512,768]{1,0:T(8,128)(2,1)S(1)}, u32[]{:S(2)}) copy-start(bf16[512,768]{1,0:T(8,128)(2,1)S(1)} %slice_select_fusion.refs_3_.refs_6_) | copy-start | bytes 2359300
  137.0 14.7 %collective-permute-start.15 = (bf16[512,1536]{1,0:T(8,128)(2,1)S(1)}, bf16[512,1536]{1,0:T(8,128)(2,1)S(1)}, u32[]{:S(2)}, u32[]{:S(2)}) collective-permute-start(bf16[512,1536]{1,0:T(8,128)(2,1)S(1)} %fusion.2.refs_1_.refs_15_), channel_id=1, source_target_pairs={{0,8},{8,0},{1,9},{9,1},{2,10},{10,2},{3,11},{11,3},{4,12},{12,4},... | collective-permute-start | bytes 4718600 | tf_op jit(solution)/shard_map/ppermute | solution.py:903
  142.1 37.3 %collective-permute-start.13 = (bf16[512,768]{1,0:T(8,128)(2,1)S(1)}, bf16[512,768]{1,0:T(8,128)(2,1)}, u32[]{:S(2)}, u32[]{:S(2)}) collective-permute-start(bf16[512,768]{1,0:T(8,128)(2,1)S(1)} %add_convert_fusion.15), channel_id=1, source_target_pairs={{16,0},{17,1},{18,2},{19,3},{20,4},{21,5},{22,6},{23,7},{24,8},{25... | collective-permute-start | bytes 2359304 | tf_op jit(solution)/shard_map/ppermute | solution.py:911
  181.6 31.5 %copy-start.122 = (bf16[768,384]{1,0:T(8,128)(2,1)S(1)}, bf16[768,384]{1,0:T(8,128)(2,1)}, u32[]{:S(2)}) copy-start(bf16[768,384]{1,0:T(8,128)(2,1)} %copy-done.119) | copy-start | bytes 1769476
  181.7 31.5 %copy-start.135 = (bf16[768,384]{1,0:T(8,128)(2,1)S(1)}, bf16[768,384]{1,0:T(8,128)(2,1)}, u32[]{:S(2)}) copy-start(bf16[768,384]{1,0:T(8,128)(2,1)} %copy-done.132) | copy-start | bytes 1769476
  213.1 3.7 collective-permute-start.16
  221.0 13.9 %copy-start.107 = (bf16[512,768]{1,0:T(8,128)(2,1)}, bf16[512,768]{1,0:T(8,128)(2,1)S(1)}, u32[]{:S(2)}) copy-start(bf16[512,768]{1,0:T(8,128)(2,1)S(1)} %add_convert_fusion.13) | copy-start | bytes 2359300
  221.0 18.7 %collective-permute-start.17 = (bf16[512,768]{1,0:T(8,128)(2,1)S(1)}, bf16[512,768]{1,0:T(8,128)(2,1)S(1)}, u32[]{:S(2)}, u32[]{:S(2)}) collective-permute-start(bf16[512,768]{1,0:T(8,128)(2,1)S(1)} %add_convert_fusion.13), channel_id=1, source_target_pairs={{16,0},{17,1},{18,2},{19,3},{20,4},{21,5},{22,6},{23,7},{24,8},{25... | collective-permute-start | bytes 2359304 | tf_op jit(solution)/shard_map/ppermute | solution.py:911
  222.7 17.0 %copy-start.60 = (bf16[512,768]{1,0:T(8,128)(2,1)S(1)}, bf16[512,768]{1,0:T(8,128)(2,1)}, u32[]{:S(2)}) copy-start(bf16[512,768]{1,0:T(8,128)(2,1)} %get-tuple-element.111.refs_1_.refs_2_) | copy-start | bytes 2359300
  222.7 16.9 %copy-start.81 = (bf16[256,768]{1,0:T(8,128)(2,1)S(1)}, bf16[256,768]{1,0:T(8,128)(2,1)}, u32[]{:S(2)}) copy-start(bf16[256,768]{1,0:T(8,128)(2,1)} %copy-done.80) | copy-start | bytes 1179652
  222.8 16.9 %copy-start.83 = (bf16[256,768]{1,0:T(8,128)(2,1)S(1)}, bf16[256,768]{1,0:T(8,128)(2,1)}, u32[]{:S(2)}) copy-start(bf16[256,768]{1,0:T(8,128)(2,1)} %copy-done.82) | copy-start | bytes 1179652
  245.5 5.0 %collective-permute-start.18 = (bf16[1536,768]{1,0:T(8,128)(2,1)}, bf16[1536,768]{1,0:T(8,128)(2,1)}, u32[]{:S(2)}, u32[]{:S(2)}) collective-permute-start(bf16[1536,768]{1,0:T(8,128)(2,1)} %half_gradient.2.token), channel_id=1, source_target_pairs={{0,8},{8,0},{1,9},{9,1},{2,10},{10,2},{3,11},{11,3},{4,12},{12,4},... | collective-permute-start | bytes 7077896 | tf_op jit(solution)/shard_map/ppermute | solution.py:903
  252.8 19.9 %copy-start.63 = (bf16[1536,768]{1,0:T(8,128)(2,1)}, bf16[1536,768]{1,0:T(8,128)(2,1)S(1)}, u32[]{:S(2)}) copy-start(bf16[1536,768]{1,0:T(8,128)(2,1)S(1)} %add_convert_fusion.1) | copy-start | bytes 7077892
  252.9 28.4 %collective-permute-start.19 = (bf16[768,768]{1,0:T(8,128)(2,1)S(1)}, bf16[768,768]{1,0:T(8,128)(2,1)S(1)}, u32[]{:S(2)}, u32[]{:S(2)}) collective-permute-start(bf16[768,768]{1,0:T(8,128)(2,1)S(1)} %dynamic-slice_bitcast_fusion.1.refs_0_), channel_id=1, source_target_pairs={{0,1},{1,0},{2,3},{3,2},{4,5},{5,4},{6,7},{7,6},{8,9},{9,8},{10,11... | collective-permute-start | bytes 3538952 | tf_op jit(solution)/shard_map/ppermute | solution.py:959
  274.5 57.5 %copy-start.14 = (f32[1,3072]{1,0:T(1,128)}, f32[1,3072]{1,0:T(1,128)S(1)}, u32[]{:S(2)}) copy-start(f32[1,3072]{1,0:T(1,128)S(1)} %get-tuple-element.165.refs_13_.refs_5_) | copy-start | bytes 36868
  282.4 4.9 collective-permute-start.21
  284.4 30.3 %collective-permute-start.20 = (bf16[768,768]{1,0:T(8,128)(2,1)S(1)}, bf16[768,768]{1,0:T(8,128)(2,1)S(1)}, u32[]{:S(2)}, u32[]{:S(2)}) collective-permute-start(bf16[768,768]{1,0:T(8,128)(2,1)S(1)} %fusion.4.refs_0_), channel_id=1, source_target_pairs={{0,2},{1,3},{6,4},{7,5},{8,10},{9,11},{14,12},{15,13},{16,18},{17,... | collective-permute-start | bytes 3538952 | tf_op jit(solution)/shard_map/ppermute | solution.py:963
  289.7 28.1 %collective-permute-start.22 = (bf16[384,1536]{1,0:T(8,128)(2,1)S(1)}, bf16[384,1536]{1,0:T(8,128)(2,1)S(1)}, u32[]{:S(2)}, u32[]{:S(2)}) collective-permute-start(bf16[384,1536]{1,0:T(8,128)(2,1)S(1)} %dynamic-slice_bitcast_fusion.refs_1_), channel_id=1, source_target_pairs={{0,1},{1,0},{2,3},{3,2},{4,5},{5,4},{6,7},{7,6},{8,9},{9,8},{10,11... | collective-permute-start | bytes 3538952 | tf_op jit(solution)/shard_map/ppermute | solution.py:959
  318.8 9.5 %collective-permute-start.25 = (bf16[512,1536]{1,0:T(8,128)(2,1)}, bf16[512,1536]{1,0:T(8,128)(2,1)}, u32[]{:S(2)}, u32[]{:S(2)}) collective-permute-start(bf16[512,1536]{1,0:T(8,128)(2,1)} %get-tuple-element.157), channel_id=1, source_target_pairs={{0,8},{8,0},{1,9},{9,1},{2,10},{10,2},{3,11},{11,3},{4,12},{12,4},... | collective-permute-start | bytes 4718600 | tf_op jit(solution)/shard_map/ppermute | solution.py:903
  321.9 30.6 %collective-permute-start.24 = (bf16[384,1536]{1,0:T(8,128)(2,1)}, bf16[384,1536]{1,0:T(8,128)(2,1)}, u32[]{:S(2)}, u32[]{:S(2)}) collective-permute-start(bf16[384,1536]{1,0:T(8,128)(2,1)} %fusion.3.refs_0_), channel_id=1, source_target_pairs={{0,2},{1,3},{6,4},{7,5},{8,10},{9,11},{14,12},{15,13},{16,18},{17,... | collective-permute-start | bytes 3538952 | tf_op jit(solution)/shard_map/ppermute | solution.py:963
  324.7 30.6 %collective-permute-start.23 = (bf16[768,768]{1,0:T(8,128)(2,1)}, bf16[768,768]{1,0:T(8,128)(2,1)}, u32[]{:S(2)}, u32[]{:S(2)}) collective-permute-start(bf16[768,768]{1,0:T(8,128)(2,1)} %add_convert_fusion.10), channel_id=1, source_target_pairs={{2,4},{3,5},{4,2},{5,3},{10,12},{11,13},{12,10},{13,11},{18,20},{1... | collective-permute-start | bytes 3538952 | tf_op jit(solution)/shard_map/ppermute | solution.py:966
  355.3 13.7 %collective-permute-start.31 = (bf16[1536,384]{1,0:T(8,128)(2,1)}, bf16[1536,384]{1,0:T(8,128)(2,1)S(1)}, u32[]{:S(2)}, u32[]{:S(2)}) collective-permute-start(bf16[1536,384]{1,0:T(8,128)(2,1)} %get-tuple-element.176), channel_id=1, source_target_pairs={{0,8},{8,0},{1,9},{9,1},{2,10},{10,2},{3,11},{11,3},{4,12},{12,4},... | collective-permute-start | bytes 3538952 | tf_op jit(solution)/shard_map/ppermute | solution.py:903
  356.7 13.3 %collective-permute-start.28 = (bf16[768,768]{1,0:T(8,128)(2,1)S(1)}, bf16[768,768]{1,0:T(8,128)(2,1)S(1)}, u32[]{:S(2)}, u32[]{:S(2)}) collective-permute-start(bf16[768,768]{1,0:T(8,128)(2,1)S(1)} %copy-done.106), channel_id=1, source_target_pairs={{0,8},{8,0},{1,9},{9,1},{2,10},{10,2},{3,11},{11,3},{4,12},{12,4},... | collective-permute-start | bytes 3538952 | tf_op jit(solution)/shard_map/ppermute | solution.py:903
  356.7 12.3 %collective-permute-start.29 = (f32[16,768]{1,0:T(8,128)S(1)}, f32[16,768]{1,0:T(8,128)S(1)}, u32[]{:S(2)}, u32[]{:S(2)}) collective-permute-start(f32[16,768]{1,0:T(8,128)S(1)} %copy-done.32), channel_id=1, source_target_pairs={{0,8},{8,0},{1,9},{9,1},{2,10},{10,2},{3,11},{11,3},{4,12},{12,4},... | collective-permute-start | bytes 147464 | tf_op jit(solution)/shard_map/ppermute | solution.py:903
  360.1 30.1 %collective-permute-start.27 = (bf16[384,1536]{1,0:T(8,128)(2,1)}, bf16[384,1536]{1,0:T(8,128)(2,1)}, u32[]{:S(2)}, u32[]{:S(2)}) collective-permute-start(bf16[384,1536]{1,0:T(8,128)(2,1)} %add_convert_fusion.8), channel_id=1, source_target_pairs={{2,4},{3,5},{4,2},{5,3},{10,12},{11,13},{12,10},{13,11},{18,20},{1... | collective-permute-start | bytes 3538952 | tf_op jit(solution)/shard_map/ppermute | solution.py:966
  366.6 27.0 %collective-permute-start.26 = (bf16[768,768]{1,0:T(8,128)(2,1)}, bf16[768,768]{1,0:T(8,128)(2,1)}, u32[]{:S(2)}, u32[]{:S(2)}) collective-permute-start(bf16[768,768]{1,0:T(8,128)(2,1)} %add_convert_fusion.9), channel_id=1, source_target_pairs={{2,0},{3,1},{4,6},{5,7},{10,8},{11,9},{12,14},{13,15},{18,16},{19,... | collective-permute-start | bytes 3538952 | tf_op jit(solution)/shard_map/ppermute | solution.py:970
  369.5 16.3 %collective-permute-start.32 = (bf16[768,384]{1,0:T(8,128)(2,1)S(1)}, bf16[768,384]{1,0:T(8,128)(2,1)S(1)}, u32[]{:S(2)}, u32[]{:S(2)}) collective-permute-start(bf16[768,384]{1,0:T(8,128)(2,1)S(1)} %dynamic-slice_bitcast_fusion.3), channel_id=1, source_target_pairs={{0,1},{1,0},{2,3},{3,2},{4,5},{5,4},{6,7},{7,6},{8,9},{9,8},{10,11... | collective-permute-start | bytes 1769480 | tf_op jit(solution)/shard_map/ppermute | solution.py:959
  371.1 26.5 %collective-permute-start.30 = (bf16[400,768]{1,0:T(8,128)(2,1)S(1)}, bf16[400,768]{1,0:T(8,128)(2,1)S(1)}, u32[]{:S(2)}, u32[]{:S(2)}) collective-permute-start(bf16[400,768]{1,0:T(8,128)(2,1)S(1)} %dynamic-slice_bitcast_fusion.2.refs_2_), channel_id=1, source_target_pairs={{0,1},{1,0},{2,3},{3,2},{4,5},{5,4},{6,7},{7,6},{8,9},{9,8},{10,11... | collective-permute-start | bytes 1843208 | tf_op jit(solution)/shard_map/ppermute | solution.py:959
  388.8 16.6 %collective-permute-start.34 = (bf16[768,384]{1,0:T(8,128)(2,1)}, bf16[768,384]{1,0:T(8,128)(2,1)}, u32[]{:S(2)}, u32[]{:S(2)}) collective-permute-start(bf16[768,384]{1,0:T(8,128)(2,1)} %fusion.12), channel_id=1, source_target_pairs={{0,2},{1,3},{6,4},{7,5},{8,10},{9,11},{14,12},{15,13},{16,18},{17,... | collective-permute-start | bytes 1769480 | tf_op jit(solution)/shard_map/ppermute | solution.py:963
  401.4 26.2 %collective-permute-start.35 = (bf16[384,1536]{1,0:T(8,128)(2,1)}, bf16[384,1536]{1,0:T(8,128)(2,1)}, u32[]{:S(2)}, u32[]{:S(2)}) collective-permute-start(bf16[384,1536]{1,0:T(8,128)(2,1)} %add_convert_fusion.5), channel_id=1, source_target_pairs={{2,0},{3,1},{4,6},{5,7},{10,8},{11,9},{12,14},{13,15},{18,16},{19,... | collective-permute-start | bytes 3538952 | tf_op jit(solution)/shard_map/ppermute | solution.py:970
  404.0 16.7 %collective-permute-start.37 = (bf16[400,768]{1,0:T(8,128)(2,1)S(1)}, bf16[400,768]{1,0:T(8,128)(2,1)S(1)}, u32[]{:S(2)}, u32[]{:S(2)}) collective-permute-start(bf16[400,768]{1,0:T(8,128)(2,1)S(1)} %fusion.11), channel_id=1, source_target_pairs={{0,2},{1,3},{6,4},{7,5},{8,10},{9,11},{14,12},{15,13},{16,18},{17,... | collective-permute-start | bytes 1843208 | tf_op jit(solution)/shard_map/ppermute | solution.py:963
  407.6 17.5 %collective-permute-start.36 = (bf16[768,384]{1,0:T(8,128)(2,1)}, bf16[768,384]{1,0:T(8,128)(2,1)}, u32[]{:S(2)}, u32[]{:S(2)}) collective-permute-start(bf16[768,384]{1,0:T(8,128)(2,1)} %add_convert_fusion.21), channel_id=1, source_target_pairs={{2,4},{3,5},{4,2},{5,3},{10,12},{11,13},{12,10},{13,11},{18,20},{1... | collective-permute-start | bytes 1769480 | tf_op jit(solution)/shard_map/ppermute | solution.py:966
  413.4 28.6 %collective-permute-start.33 = (bf16[768,768]{1,0:T(8,128)(2,1)}, bf16[768,768]{1,0:T(8,128)(2,1)}, u32[]{:S(2)}, u32[]{:S(2)}) collective-permute-start(bf16[768,768]{1,0:T(8,128)(2,1)} %broadcast_select_fusion.5), channel_id=1, source_target_pairs={{0,1},{1,0},{2,3},{3,2},{4,5},{5,4},{6,7},{7,6},{8,9},{9,8},{10,11... | collective-permute-start | bytes 3538952 | tf_op jit(solution)/shard_map/ppermute | solution.py:971
  422.7 15.8 %collective-permute-start.39 = (bf16[400,768]{1,0:T(8,128)(2,1)S(1)}, bf16[400,768]{1,0:T(8,128)(2,1)S(1)}, u32[]{:S(2)}, u32[]{:S(2)}) collective-permute-start(bf16[400,768]{1,0:T(8,128)(2,1)S(1)} %add_convert_fusion.19), channel_id=1, source_target_pairs={{2,4},{3,5},{4,2},{5,3},{10,12},{11,13},{12,10},{13,11},{18,20},{1... | collective-permute-start | bytes 1843208 | tf_op jit(solution)/shard_map/ppermute | solution.py:966
  429.8 18.5 %collective-permute-start.38 = (bf16[768,384]{1,0:T(8,128)(2,1)}, bf16[768,384]{1,0:T(8,128)(2,1)}, u32[]{:S(2)}, u32[]{:S(2)}) collective-permute-start(bf16[768,384]{1,0:T(8,128)(2,1)} %add_convert_fusion.20), channel_id=1, source_target_pairs={{2,0},{3,1},{4,6},{5,7},{10,8},{11,9},{12,14},{13,15},{18,16},{19,... | collective-permute-start | bytes 1769480 | tf_op jit(solution)/shard_map/ppermute | solution.py:970
  437.5 37.3 %collective-permute-start.43 = (bf16[384,1536]{1,0:T(8,128)(2,1)}, bf16[384,1536]{1,0:T(8,128)(2,1)S(1)}, u32[]{:S(2)}, u32[]{:S(2)}) collective-permute-start(bf16[384,1536]{1,0:T(8,128)(2,1)} %broadcast_select_fusion.4), channel_id=1, source_target_pairs={{0,1},{1,0},{2,3},{3,2},{4,5},{5,4},{6,7},{7,6},{8,9},{9,8},{10,11... | collective-permute-start | bytes 3538952 | tf_op jit(solution)/shard_map/ppermute | solution.py:971
  440.6 18.1 %collective-permute-start.41 = (bf16[400,768]{1,0:T(8,128)(2,1)S(1)}, bf16[400,768]{1,0:T(8,128)(2,1)S(1)}, u32[]{:S(2)}, u32[]{:S(2)}) collective-permute-start(bf16[400,768]{1,0:T(8,128)(2,1)S(1)} %add_convert_fusion.18.refs_2_), channel_id=1, source_target_pairs={{2,0},{3,1},{4,6},{5,7},{10,8},{11,9},{12,14},{13,15},{18,16},{19,... | collective-permute-start | bytes 1843208 | tf_op jit(solution)/shard_map/ppermute | solution.py:970
  450.3 38.5 %collective-permute-start.40 = (bf16[768,384]{1,0:T(8,128)(2,1)}, bf16[768,384]{1,0:T(8,128)(2,1)}, u32[]{:S(2)}, u32[]{:S(2)}) collective-permute-start(bf16[768,384]{1,0:T(8,128)(2,1)} %broadcast_select_fusion.12), channel_id=1, source_target_pairs={{0,1},{1,0},{2,3},{3,2},{4,5},{5,4},{6,7},{7,6},{8,9},{9,8},{10,11... | collective-permute-start | bytes 1769480 | tf_op jit(solution)/shard_map/ppermute | solution.py:971
  466.5 19.1 %collective-permute-start.45 = (bf16[512,768]{1,0:T(8,128)(2,1)}, bf16[512,768]{1,0:T(8,128)(2,1)}, u32[]{:S(2)}, u32[]{:S(2)}) collective-permute-start(bf16[512,768]{1,0:T(8,128)(2,1)} %pad_maximum_fusion.7), channel_id=1, source_target_pairs={{0,16},{1,17},{2,18},{3,19},{4,20},{5,21},{6,22},{7,23},{8,24},{9,... | collective-permute-start | bytes 2359304 | tf_op jit(solution)/shard_map/ppermute | solution.py:907
  467.8 20.0 %collective-permute-start.44 = (bf16[512,768]{1,0:T(8,128)(2,1)}, bf16[512,768]{1,0:T(8,128)(2,1)}, u32[]{:S(2)}, u32[]{:S(2)}) collective-permute-start(bf16[512,768]{1,0:T(8,128)(2,1)} %get-tuple-element.201), channel_id=1, source_target_pairs={{16,0},{17,1},{18,2},{19,3},{20,4},{21,5},{22,6},{23,7},{24,8},{25... | collective-permute-start | bytes 2359304 | tf_op jit(solution)/shard_map/ppermute | solution.py:911
  474.2 17.0 %collective-permute-start.42 = (bf16[400,768]{1,0:T(8,128)(2,1)S(1)}, bf16[400,768]{1,0:T(8,128)(2,1)S(1)}, u32[]{:S(2)}, u32[]{:S(2)}) collective-permute-start(bf16[400,768]{1,0:T(8,128)(2,1)S(1)} %broadcast_select_fusion.9), channel_id=1, source_target_pairs={{0,1},{1,0},{2,3},{3,2},{4,5},{5,4},{6,7},{7,6},{8,9},{9,8},{10,11... | collective-permute-start | bytes 1843208 | tf_op jit(solution)/shard_map/ppermute | solution.py:971
  (121 other events, 345.9 us)
